TPU v7x, 512 devices: a whole 4x8x8 slice. The times are simulated.
512 devices in a mesh: dp: 16 (over z, x_lo), section: 4 (over x_hi, core), vocab: 8 (over y).
Axes of the slice: x: 4 (x_hi: 2, x_lo: 2; x = x_hi * 2 + x_lo), y: 8, z: 8, core: 2. Of those that a mesh axis runs over, the one named last changes fastest.
Arguments:
- hidden_rows: bfloat16 [4, 128, 16384], P('section', None, 'dp'), may hold values from -4 to 4
- head: bfloat16 [65536, 16384], P(('section', 'vocab'), 'dp'), may hold values from -0.015822244 to 0.015822244
- unite_gain: float32 [3, 16384], P(None, 'dp'), may hold values from 0.2 to 1
- norm_gain: float32 [16384], P('dp'), may hold values from 0.5 to 1.5
- segment_ids: int32 [128], replicated, may hold values from 0 to 7, never falling along the last dimension, each value on 1 to 32 neighbouring positions
Outputs:
- step_loss: float32 [3], replicated
- grad_unite: float32 [3, 16384], P(None, 'dp')
- grad_norm: float32 [16384], P('dp')
Inputs may be any that keep to these rules, and one draw needn't show every extreme that they name: `segment_ids`: never falling along the tokens; each packed sequence holds 1 to 32 tokens.
All inputs are finite; a program needn't handle non-finite values.
Results may differ from a plain program's by a relative error of at most 0.0019.
Values may be sent and summed in bfloat16 or wider, within the bound.
No kernel may reach another device: no remote copies, remote signals or barrier semaphores. Data moves between devices by JAX's collectives and lax.ppermute only.
A program may use at most 64 MiB of HBM per device.

v0:
```python
import jax
import jax.numpy as jnp
from jax import lax
from jax.sharding import PartitionSpec as P

STEPS = 3


EPS = 1e-06
CONTRACT = (((1,), (1,)), ((), ()))


def joined(part, axis, combine):
    gathered = jax.tree.map(lambda a: lax.all_gather(a, axis), part)

    def take(source):
        return jax.tree.map(lambda a: lax.dynamic_index_in_dim(a, source, 0, False), gathered)

    return lax.fori_loop(
        1, lax.axis_size(axis), lambda source, state: combine(state, take(source)), take(0)
    )


def join_parts(first, second):
    peak = jnp.maximum(first[0], second[0])
    mass = first[1] * jnp.exp(first[0] - peak) + second[1] * jnp.exp(second[0] - peak)
    return (peak, mass)


def local_parts(logits):
    peak = jnp.max(logits, axis=-1)
    mass = jnp.sum(jnp.exp(logits - peak[:, None]), axis=-1)
    return (peak, mass)


def on_device(hidden_rows, head, unite_gain, norm_gain, segment_ids):
    rows = lax.all_gather(hidden_rows, "section", axis=0, tiled=True)
    layers = rows[:3].astype(jnp.float32)
    final = rows[3]
    total_tokens = rows.shape[1]
    width = rows.shape[2] * lax.axis_size("dp")
    shards = lax.axis_size("section") * lax.axis_size("vocab")
    teacher = lax.psum_scatter(
        lax.dot_general(final, head, CONTRACT, preferred_element_type=jnp.float32),
        "dp",
        scatter_dimension=0,
        tiled=True,
    )
    copies = teacher.shape[0] * lax.axis_size("dp") // total_tokens
    top, total = local_parts(teacher)
    top, total = joined((top, total), ("section", "vocab"), join_parts)
    united = jnp.sum(layers * unite_gain[:, None, :], axis=0)
    same = jnp.concatenate(
        [jnp.zeros((1,), jnp.float32), (segment_ids[1:] == segment_ids[:-1]).astype(jnp.float32)]
    )
    carry = jnp.zeros_like(united)
    saved_logits, saved_peak, saved_mass, saved_normed, saved_radius = ([], [], [], [], [])
    for step in range(STEPS):
        xvals = united + carry
        square = lax.psum(jnp.sum(xvals * xvals, axis=-1), "dp")
        radius = jnp.sqrt(square / width + EPS)
        normed = xvals / radius[:, None]
        draft = (normed * norm_gain).astype(jnp.bfloat16)
        logits = lax.psum_scatter(
            lax.dot_general(draft, head, CONTRACT, preferred_element_type=jnp.float32),
            "dp",
            scatter_dimension=0,
            tiled=True,
        )
        peak, mass = local_parts(logits)
        peak, mass = joined((peak, mass), ("section", "vocab"), join_parts)
        saved_logits.append(logits)
        saved_peak.append(peak)
        saved_mass.append(mass)
        saved_normed.append(normed)
        saved_radius.append(radius)
        shifted = jnp.concatenate(
            [jnp.zeros((1, united.shape[1]), jnp.float32), draft[:-1].astype(jnp.float32)], axis=0
        )
        carry = shifted * same[:, None]
    prob = jnp.exp(teacher - top[:, None]) / total[:, None]
    scale = 1.0 / (total_tokens * STEPS)
    grad_norm = jnp.zeros_like(norm_gain)
    grad_unite = jnp.zeros_like(unite_gain)
    local_unite = jnp.zeros_like(unite_gain)
    loss_parts = []
    for step in range(STEPS):
        logits = saved_logits[step]
        peak = saved_peak[step]
        mass = saved_mass[step]
        normed = saved_normed[step]
        radius = saved_radius[step]
        lse = peak + jnp.log(mass)
        loss_parts.append(
            (jnp.sum(lse) / shards - jnp.sum(prob * logits)) / (total_tokens * copies)
        )
        dlogits = ((jnp.exp(logits - peak[:, None]) / mass[:, None] - prob) * scale).astype(
            jnp.bfloat16
        )
        dhidden = jnp.dot(
            lax.all_gather(dlogits, "dp", axis=0, tiled=True),
            head,
            preferred_element_type=jnp.float32,
        )
        norm_part = jnp.sum(dhidden * normed, axis=0)
        centre_part = jnp.sum(dhidden * normed * norm_gain, axis=-1)
        unite_part = jnp.sum(layers * (dhidden / radius[:, None])[None], axis=1) * norm_gain
        centre = lax.psum(centre_part, ("dp", "section", "vocab")) / width
        local_unite = local_unite - jnp.sum(
            layers * (normed * (centre / radius)[:, None])[None], axis=1
        )
        norm_sum, unite_sum = lax.psum((norm_part, unite_part), ("section", "vocab"))
        grad_norm = grad_norm + norm_sum
        grad_unite = grad_unite + unite_sum
    grad_unite = grad_unite + local_unite
    step_loss = lax.psum(jnp.stack(loss_parts), ("dp", "section", "vocab"))
    return (step_loss, grad_unite, grad_norm)


def solution(mesh):
    placed = (P("section", None, "dp"), P(("section", "vocab"), "dp"), P(None, "dp"), P("dp"), P())
    return jax.shard_map(
        on_device,
        mesh=mesh,
        in_specs=placed,
        out_specs=(P(), P(None, "dp"), P("dp")),
        check_vma=False,
    )
```

profile of v0, /device:TPU:1, one launch (start us, length us, event | category | flops | bytes accessed | tf_op | source)
XLA Modules:
  0.0 825.9 jit_solution(12957948623412470070)
XLA Ops:
  7.9 34.2 %all-gather.10.cloned.1.call-done = bf16[4,128,1024]{2,1,0:T(8,128)(2,1)} async-done(((bf16[1,128,1024]{2,1,0:T(8,128)(2,1)}), bf16[4,128,1024]{2,1,0:T(8,128)(2,1)}) %all-gather.10.cloned.1.call-update) | async-done | bytes 1048592 | tf_op jit(solution)/shard_map/all_gather | solution.py:37
  42.1 1.4 fusion.8
  43.6 27.7 %psum.91 = f32[128]{0:T(128)S(1)} all-reduce(f32[128]{0:T(128)S(1)} %multiply_reduce_fusion.5), channel_id=1, replica_groups=mesh['dp'=16,'section'=4,'vocab'=8] {'dp'}, use_global_device_ids=true, to_apply=%region_2.0 | all-reduce | flops 128 | bytes 1024 | tf_op jit(solution)/shard_map/psum | solution.py:60
  72.2 4.7 fusion.21
  77.0 4.7 fusion.18
  81.8 1.3 dynamic-slice
  84.1 24.4 %psum.92 = f32[128]{0:T(128)S(1)} all-reduce(f32[128]{0:T(128)S(1)} %multiply_reduce_fusion.4), channel_id=1, replica_groups=mesh['dp'=16,'section'=4,'vocab'=8] {'dp'}, use_global_device_ids=true, to_apply=%region_16.17 | all-reduce | flops 128 | bytes 1024 | tf_op jit(solution)/shard_map/psum | solution.py:60
  109.2 4.7 fusion.22
  114.0 30.6 %reduce-scatter.5.cloned.1.call-done = f32[8,2048]{1,0:T(8,128)} async-done(((f32[128,2048]{1,0:T(8,128)}), f32[8,2048]{1,0:T(8,128)}) %reduce-scatter.5.cloned.1.call-update) | async-done | bytes 65552 | tf_op jit(solution)/shard_map/reduce_scatter | solution.py:64
  145.9 1.0 exponential_reduce_fusion.3
  147.2 73.2 %reduce-scatter.7.cloned.1.call-done = f32[8,2048]{1,0:T(8,128)} async-done(((f32[128,2048]{1,0:T(8,128)}), f32[8,2048]{1,0:T(8,128)}) %reduce-scatter.7.cloned.1.call-update) | async-done | bytes 65552 | tf_op jit(solution)/shard_map/reduce_scatter | solution.py:43
  221.6 1.0 exponential_reduce_fusion.2
  222.9 68.4 %all-reduce.13 = (f32[256]{0:T(256)S(1)}, f32[256]{0:T(256)S(1)}, f32[256]{0:T(256)S(1)}, f32[256]{0:T(256)S(1)}) all-reduce(f32[256]{0:T(256)S(1)} %dynamic-update-slice, f32[256]{0:T(256)S(1)} %dynamic-update-slice.1, f32[256]{0:T(256)S(1)} %dynamic-update-slice.2, ...), channel_id=2, replica_groups=mesh['dp'=16,'section'=4,'vocab'=8] {'section','vocab'}, use_global_device_ids=true, to_apply=%add.2 | all-reduce | flops 1024 | bytes 8192
  291.7 1.4 while.69
  293.0 1.4 while.68
  295.4 26.2 %all_gather.77 = bf16[128,2048]{1,0:T(8,128)(2,1)S(1)} all-gather(bf16[8,2048]{1,0:T(8,128)(2,1)S(1)} %multiply_convert_fusion.6), channel_id=1, replica_groups=mesh['dp'=16,'section'=4,'vocab'=8] {'dp'}, dimensions={0}, use_global_device_ids=true | all-gather | bytes 557056 | tf_op jit(solution)/shard_map/all_gather | solution.py:101
  321.7 3.7 multiply_reduce_fusion.8
  325.4 25.9 %psum.93 = f32[128]{0:T(128)S(1)} all-reduce(f32[128]{0:T(128)S(1)} %get-tuple-element.555), channel_id=1, replica_groups=mesh['dp'=16,'section'=4,'vocab'=8] {'dp'}, use_global_device_ids=true, to_apply=%region_25.26 | all-reduce | flops 128 | bytes 1024 | tf_op jit(solution)/shard_map/psum | solution.py:60
  353.1 4.7 fusion.17
  360.5 78.6 %reduce-scatter.11.cloned.1.call-done = f32[8,2048]{1,0:T(8,128)} async-done(((f32[128,2048]{1,0:T(8,128)}), f32[8,2048]{1,0:T(8,128)}) %reduce-scatter.11.cloned.1.call-update) | async-done | bytes 65552 | tf_op jit(solution)/shard_map/reduce_scatter | solution.py:64
  440.3 1.7 multiply_reduce_fusion.11
  442.4 68.3 %all-reduce.12 = (f32[256]{0:T(256)S(1)}, f32[256]{0:T(256)S(1)}, f32[256]{0:T(256)S(1)}, f32[256]{0:T(256)S(1)}) all-reduce(f32[256]{0:T(256)S(1)} %dynamic-update-slice.6, f32[256]{0:T(256)S(1)} %dynamic-update-slice.7, f32[256]{0:T(256)S(1)} %dynamic-update-slice.4, ...), channel_id=8, replica_groups=mesh['dp'=16,'section'=4,'vocab'=8] {'section','vocab'}, use_global_device_ids=true, to_apply=%add.8 | all-reduce | flops 1024 | bytes 8192
  511.1 1.4 while.70
  515.1 1.4 while.71
  518.3 1.1 multiply_convert_fusion.5
  519.4 25.9 %all_gather.78 = bf16[128,2048]{1,0:T(8,128)(2,1)S(1)} all-gather(bf16[8,2048]{1,0:T(8,128)(2,1)S(1)} %get-tuple-element.628), channel_id=1, replica_groups=mesh['dp'=16,'section'=4,'vocab'=8] {'dp'}, dimensions={0}, use_global_device_ids=true | all-gather | bytes 557056 | tf_op jit(solution)/shard_map/all_gather | solution.py:101
  545.3 2.9 fusion.23
  548.2 27.3 %all_gather.79 = bf16[128,2048]{1,0:T(8,128)(2,1)S(1)} all-gather(bf16[8,2048]{1,0:T(8,128)(2,1)S(1)} %get-tuple-element.629), channel_id=1, replica_groups=mesh['dp'=16,'section'=4,'vocab'=8] {'dp'}, dimensions={0}, use_global_device_ids=true | all-gather | bytes 557056 | tf_op jit(solution)/shard_map/all_gather | solution.py:101
  575.6 1.8 multiply_reduce_fusion.6
  577.5 118.0 %all-reduce.10 = (f32[3]{0:T(128)}, f32[128]{0:T(128)S(1)}, f32[128]{0:T(128)S(1)}, f32[128]{0:T(128)S(1)}) all-reduce(f32[3]{0:T(128)S(1)} %pad_maximum_fusion, f32[128]{0:T(128)S(1)} %copy-done.19, f32[128]{0:T(128)S(1)} %get-tuple-element.548, ...), channel_id=1, replica_groups=mesh['dp'=16,'section'=4,'vocab'=8] {'dp','section','vocab'}, use_global_device_ids=true, to_apply=%region_33.34 | all-reduce | flops 387 | bytes 3096 | tf_op jit(solution)/shard_map/psum | solution.py:116
  695.9 2.0 fusion.12
  697.9 120.9 %all-reduce.11 = (f32[3,1024]{1,0:T(4,128)S(1)}, f32[1024]{0:T(1024)}) all-reduce(f32[3,1024]{1,0:T(4,128)S(1)} %add_multiply_fusion, f32[1024]{0:T(1024)S(1)} %add_add_fusion), channel_id=1, replica_groups=mesh['dp'=16,'section'=4,'vocab'=8] {'section','vocab'}, use_global_device_ids=true, to_apply=%region_35.36 | all-reduce | flops 4096 | bytes 32768 | tf_op jit(solution)/shard_map/psum | solution.py:112
  (240 shorter events, 18.6 us)
Async XLA Ops:
  7.2 35.0 %all-gather.10.cloned.1.call-start = ((), (), s32[]{:S(2)}) async-start(), calls=%async_computation.4 | async-start | bytes 1310720 | tf_op jit(solution)/shard_map/all_gather | solution.py:37
  7.9 136.8 %reduce-scatter.5.cloned.1.call-start = ((), (), s32[]{:S(2)}) async-start(), calls=%async_computation.5 | async-start | bytes 1114112 | tf_op jit(solution)/shard_map/reduce_scatter | solution.py:64
  43.5 33.5 %copy-start.1 = (bf16[4,128,1024]{2,1,0:T(8,128)(2,1)S(1)}, bf16[4,128,1024]{2,1,0:T(8,128)(2,1)}, u32[]{:S(2)}) copy-start(bf16[4,128,1024]{2,1,0:T(8,128)(2,1)} %all-gather.10.cloned.1.call-done) | copy-start | bytes 3145732
  71.3 10.3 %copy-start.21 = (f32[128]{0:T(128)}, f32[128]{0:T(128)S(1)}, u32[]{:S(2)}) copy-start(f32[128]{0:T(128)S(1)} %psum.91) | copy-start | bytes 1540
  71.3 250.3 %copy-start.9 = (f32[128]{0:T(128)}, f32[128]{0:T(128)S(1)}, u32[]{:S(2)}) copy-start(f32[128]{0:T(128)S(1)} %add_sqrt_fusion.2) | copy-start | bytes 1540
  76.9 6.8 copy-start.20
  76.9 32.1 %copy-start.4 = (f32[1024]{0:T(1024)S(1)}, f32[1024]{0:T(1024)}, u32[]{:S(2)}) copy-start(f32[1024]{0:T(1024)} %param.16) | copy-start | bytes 12292
  76.9 143.4 %reduce-scatter.7.cloned.1.call-start = ((), (), s32[]{:S(2)}) async-start(), calls=%async_computation.6 | async-start | bytes 1114112 | tf_op jit(solution)/shard_map/reduce_scatter | solution.py:43
  81.7 276.2 %reduce-scatter.9.cloned.1.call-start = ((), (), s32[]{:S(2)}) async-start(), calls=%async_computation.7 | async-start | bytes 1114112 | tf_op jit(solution)/shard_map/reduce_scatter | solution.py:64
  83.8 237.8 %copy-start.7 = (f32[128]{0:T(128)}, f32[128]{0:T(128)S(1)}, u32[]{:S(2)}) copy-start(f32[128]{0:T(128)S(1)} %add_convert_fusion) | copy-start | bytes 1540
  108.5 0.5 copy-start.15
  109.0 113.6 %copy-start.11 = (f32[128]{0:T(128)}, f32[128]{0:T(128)S(1)}, u32[]{:S(2)}) copy-start(f32[128]{0:T(128)S(1)} %add_sqrt_fusion.1) | copy-start | bytes 1540
  114.0 325.1 %reduce-scatter.11.cloned.1.call-start = ((), (), s32[]{:S(2)}) async-start(), calls=%async_computation.8 | async-start | bytes 1114112 | tf_op jit(solution)/shard_map/reduce_scatter | solution.py:64
  294.4 31.0 %copy-start.5 = (f32[8]{0:T(128)}, f32[8]{0:T(128)S(1)}, u32[]{:S(2)}) copy-start(f32[8]{0:T(128)S(1)} %get-tuple-element.535) | copy-start | bytes 100
  325.4 114.9 %copy-start.2 = (f32[8,2048]{1,0:T(8,128)S(1)}, f32[8,2048]{1,0:T(8,128)}, u32[]{:S(2)}) copy-start(f32[8,2048]{1,0:T(8,128)} %reduce-scatter.7.cloned.1.call-done) | copy-start | bytes 196612
  325.4 114.9 %copy-start.3 = (f32[8,2048]{1,0:T(8,128)S(1)}, f32[8,2048]{1,0:T(8,128)}, u32[]{:S(2)}) copy-start(f32[8,2048]{1,0:T(8,128)} %reduce-scatter.5.cloned.1.call-done) | copy-start | bytes 196612
  351.3 0.6 copy-start.17
  351.9 0.5 copy-start.13
  353.1 6.0 copy-start.6
  357.9 217.7 %copy-start.12 = (f32[128]{0:T(128)S(1)}, f32[128]{0:T(128)}, u32[]{:S(2)}) copy-start(f32[128]{0:T(128)} %copy-done.11) | copy-start | bytes 1540
  357.9 217.7 %copy-start.14 = (f32[128]{0:T(128)S(1)}, f32[128]{0:T(128)}, u32[]{:S(2)}) copy-start(f32[128]{0:T(128)} %copy-done.13) | copy-start | bytes 1540
  518.3 57.3 %copy-start = (bf16[2048,1024]{1,0:T(8,128)(2,1)S(1)}, bf16[2048,1024]{1,0:T(8,128)(2,1)}, u32[]{:S(2)}) copy-start(bf16[2048,1024]{1,0:T(8,128)(2,1)} %param.14) | copy-start | bytes 12582916
  575.6 1.9 copy-start.19
  575.6 119.8 %copy-start.22 = (f32[128]{0:T(128)S(1)}, f32[128]{0:T(128)}, u32[]{:S(2)}) copy-start(f32[128]{0:T(128)} %copy-done.21) | copy-start | bytes 1540
  575.6 119.8 %copy-start.10 = (f32[128]{0:T(128)S(1)}, f32[128]{0:T(128)}, u32[]{:S(2)}) copy-start(f32[128]{0:T(128)} %copy-done.9) | copy-start | bytes 1540
  575.6 120.0 %copy-start.16 = (f32[128]{0:T(128)S(1)}, f32[128]{0:T(128)}, u32[]{:S(2)}) copy-start(f32[128]{0:T(128)} %copy-done.15) | copy-start | bytes 1540
  575.6 120.0 %copy-start.18 = (f32[128]{0:T(128)S(1)}, f32[128]{0:T(128)}, u32[]{:S(2)}) copy-start(f32[128]{0:T(128)} %copy-done.17) | copy-start | bytes 1540
  575.6 120.2 %copy-start.8 = (f32[1024]{0:T(1024)S(1)}, f32[1024]{0:T(1024)}, u32[]{:S(2)}) copy-start(f32[1024]{0:T(1024)} %get-tuple-element.543) | copy-start | bytes 12292
Sparse Core Ops, SparseCore 0:
  10.1 31.9 all-gather.9
  77.1 67.5 reduce-scatter.4
  147.7 72.6 reduce-scatter.6
  223.0 73.7 reduce-scatter.8
  358.0 81.0 reduce-scatter.10
where the time goes:
time: 836 us; the launch traced here: 826 us
  blocking collectives  533 us (64%)
  waiting for transfers between devices  217 us (26%)
  matrix products  27.3 us (3%)
  other arithmetic  21.7 us (3%)
  between operations  18.7 us (2%)
    unnamed x2, blocking collectives  137 us
    psum x1, blocking collectives, on_device(): lax.psum((norm_part, unite_part), ('section', 'vocab'))  121 us
    psum x1, blocking collectives, on_device(): step_loss = lax.psum(jnp.stack(loss_parts), ('dp', 'section', 'vocab'))  118 us
    reduce_scatter x3, waiting for transfers between devices, on_device(): lax.psum_scatter(lax.dot_general(draft, head, CONTRACT, preferred_element...  109 us
    all_gather x3, blocking collectives, on_device(): lax.all_gather(dlogits, 'dp', axis=0, tiled=True)  79.4 us
    psum x3, blocking collectives, on_device(): square = lax.psum(jnp.sum(xvals * xvals, axis=-1), 'dp')  78 us
    reduce_scatter x1, waiting for transfers between devices, on_device(): lax.psum_scatter(lax.dot_general(final, head, CONTRACT, preferred_element...  73.2 us
    all_gather x1, waiting for transfers between devices, on_device(): rows = lax.all_gather(hidden_rows, 'section', axis=0, tiled=True)  34.2 us
  transfers between devices with their start and end apart: 5, of which 4 were waited for; matrix products, arithmetic and copies ran while one was open for 4% of the time, Pallas kernels for 0%

commit v1 on v0

v1 whole, which is shorter than its diff:
```python
import jax
import jax.numpy as jnp
from jax import lax
from jax.sharding import PartitionSpec as P

STEPS = 3
EPS = 1e-06
CONTRACT = (((1,), (1,)), ((), ()))
F32 = jnp.float32
BF16 = jnp.bfloat16


def later(a, by):
    return jnp.concatenate([jnp.zeros((by,) + a.shape[1:], a.dtype), a[:-by]], axis=0)


def exchange(a, axis):
    n = lax.axis_size(axis)
    return lax.all_to_all(jnp.broadcast_to(a[None], (n,) + a.shape), axis, 0, 0)


def radii_of(sums, same, width):
    q00, q01, q11, q02, q12, q22 = sums

    def radius(square):
        return jnp.sqrt(jnp.maximum(square, 0.0) / width + EPS)

    r1 = radius(q00)
    a2 = same / jnp.concatenate([jnp.ones((1,), F32), r1[:-1]])
    r2 = radius(q00 + 2.0 * a2 * q01 + a2 * a2 * q11)
    a3 = same / jnp.concatenate([jnp.ones((1,), F32), r2[:-1]])
    b3 = a3 * later(a2, 1)
    r3 = radius(
        q00 + 2.0 * a3 * q01 + a3 * a3 * q11 + 2.0 * b3 * q02 + 2.0 * a3 * b3 * q12 + b3 * b3 * q22
    )
    return r1, r2, r3, a2, a3, b3


def on_device(hidden_rows, head, unite_gain, norm_gain, segment_ids):
    rows = lax.all_gather(hidden_rows, "section", axis=0, tiled=True)
    layers = rows[:3].astype(F32)
    final = rows[3]
    tokens, cols = final.shape
    n_dp = lax.axis_size("dp")
    width = cols * n_dp
    shards = lax.axis_size("section") * lax.axis_size("vocab")
    block = tokens // n_dp
    vocab = head.shape[0]
    same = jnp.concatenate([jnp.zeros((1,), F32), (segment_ids[1:] == segment_ids[:-1]).astype(F32)])

    united = jnp.sum(layers * unite_gain[:, None, :], axis=0)
    once = united * norm_gain
    back1 = later(once, 1)
    back2 = later(once * norm_gain, 2)
    stacked = jnp.stack(
        [
            final,
            once.astype(BF16),
            (back1 * norm_gain).astype(BF16),
            (back2 * norm_gain).astype(BF16),
        ],
        axis=0,
    )
    stacked = stacked.reshape(4, n_dp, block, cols).transpose(1, 0, 2, 3).reshape(4 * tokens, cols)
    summed = lax.psum_scatter(
        lax.dot_general(stacked, head, CONTRACT, preferred_element_type=F32),
        "dp",
        scatter_dimension=0,
        tiled=True,
    ).reshape(4, block, vocab)

    sums = jnp.stack(
        [
            jnp.sum(united * united, axis=-1),
            jnp.sum(united * back1, axis=-1),
            jnp.sum(back1 * back1, axis=-1),
            jnp.sum(united * back2, axis=-1),
            jnp.sum(back1 * back2, axis=-1),
            jnp.sum(back2 * back2, axis=-1),
        ]
    )
    sums = jnp.sum(exchange(sums, "dp"), axis=0)
    r1, r2, r3, a2, a3, b3 = radii_of(sums, same, width)

    mine = lax.axis_index("dp") * block
    r1b, r2b, r3b, a2b, a3b, b3b = (
        lax.dynamic_slice_in_dim(v, mine, block)[:, None] for v in (r1, r2, r3, a2, a3, b3)
    )
    teacher, plain, second, third = summed[0], summed[1], summed[2], summed[3]
    logits = jnp.stack(
        [
            plain / r1b,
            (plain + a2b * second) / r2b,
            (plain + a3b * second + b3b * third) / r3b,
        ]
    )

    top = jnp.max(teacher, axis=-1)
    e0 = jnp.exp(teacher - top[:, None])
    peak = jnp.max(logits, axis=-1)
    low = logits - peak[:, :, None]
    e = jnp.exp(low)
    stats = jnp.concatenate(
        [
            top[None],
            jnp.sum(e0, axis=-1)[None],
            peak,
            jnp.sum(e, axis=-1),
            jnp.sum(e * low, axis=-1),
            jnp.sum(e0[None] * low, axis=-1),
        ],
        axis=0,
    )
    every = exchange(stats, ("section", "vocab"))
    tops, totals = every[:, 0], every[:, 1]
    peaks, masses, firsts, crosses = (every[:, 2 + 3 * i : 5 + 3 * i] for i in range(4))
    all_top = jnp.max(tops, axis=0)
    scale0 = jnp.exp(tops - all_top)
    total = jnp.sum(scale0 * totals, axis=0)
    all_peak = jnp.max(peaks, axis=0)
    down = peaks - all_peak
    scale = jnp.exp(down)
    mass = jnp.sum(scale * masses, axis=0)
    under_p = jnp.sum(scale * (firsts + down * masses), axis=0) / mass
    under_q = jnp.sum(scale0[:, None] * (crosses + down * totals[:, None]), axis=0) / total
    loss = jnp.log(mass) - under_q
    count = tokens * STEPS
    centre = (under_p - under_q) / (count * width)

    f = jnp.exp(peak - all_peak) / (mass * count)
    f0 = jnp.exp(top - all_top) / (total * count)
    dlogits = (e * f[:, :, None] - (e0 * f0[:, None])[None]).astype(BF16)

    dall = exchange(dlogits.reshape(STEPS * block, vocab), "dp").reshape(n_dp * STEPS * block, vocab)
    small = exchange(jnp.concatenate([loss, centre], axis=0), "dp")
    step_loss = jnp.sum(small[:, :STEPS], axis=(0, 2)) / tokens
    centre = small[:, STEPS:].transpose(1, 0, 2).reshape(STEPS, tokens)

    dhidden = lax.dot_general(dall, head, (((1,), (0,)), ((), ())), preferred_element_type=F32)
    dhidden = dhidden.reshape(n_dp, STEPS, block, cols)

    xs = (
        united,
        united + a2[:, None] * back1,
        united + a3[:, None] * back1 + b3[:, None] * back2,
    )
    grad_norm = jnp.zeros_like(norm_gain)
    outer = jnp.zeros_like(united)
    for k, (x, r) in enumerate(zip(xs, (r1, r2, r3), strict=True)):
        normed = x / r[:, None]
        dh = dhidden[:, k].reshape(tokens, cols)
        grad_norm = grad_norm + jnp.sum(dh * normed, axis=0)
        outer = outer + (dh * norm_gain - normed * (centre[k] / shards)[:, None]) / r[:, None]
    grads = jnp.concatenate([jnp.sum(layers * outer[None], axis=1), grad_norm[None]], axis=0)
    grads = jnp.sum(lax.all_gather(grads, "section"), axis=0)
    grads = jnp.sum(exchange(grads, "vocab"), axis=0)
    return (step_loss, grads[:3], grads[3])


def solution(mesh):
    placed = (P("section", None, "dp"), P(("section", "vocab"), "dp"), P(None, "dp"), P("dp"), P())
    return jax.shard_map(
        on_device,
        mesh=mesh,
        in_specs=placed,
        out_specs=(P(), P(None, "dp"), P("dp")),
        check_vma=False,
    )
```

time: 836 us -> 272 us (0.33); the launches traced: 826 us -> 272 us
  blocking collectives: 533 us -> 11.8 us
  starting transfers between devices: 0.2 us -> 32.5 us
  waiting for transfers between devices: 217 us -> 188 us
  matrix products: 27.3 us -> 8.75 us
  other arithmetic: 21.7 us -> 8.13 us
    psum x5 -> x0, blocking collectives: 317 us -> none  [the longest x1 121 us: on_device(): lax.psum((norm_part, unite_part), ('section', 'vocab'))]
    unnamed x2 -> x0, blocking collectives: 137 us -> none
    reduce_scatter x4 -> x1, waiting for transfers between devices: 182 us -> 83.8 us  [on_device(): lax.psum_scatter(lax.dot_general(stacked, head, CONTRACT, preferred_eleme...]
    all_to_all x0 -> x5, waiting for transfers between devices: none -> 69.3 us  [exchange(): return lax.all_to_all(jnp.broadcast_to(a[None], (n,) + a.shape), axis, 0, 0)]
    all_gather x3 -> x1, blocking collectives: 79.4 us -> 11.8 us  [on_device(): grads = jnp.sum(lax.all_gather(grads, 'section'), axis=0)]
    all_to_all x0 -> x5, starting transfers between devices: none -> 32.4 us  [exchange(): return lax.all_to_all(jnp.broadcast_to(a[None], (n,) + a.shape), axis, 0, 0)]
    dot_general x7 -> x2, matrix products: 27.3 us -> 8.75 us  [the longest x1 4.46 us: on_device(): lax.dot_general(dall, head, (((1,), (0,)), ((), ())), preferred_element_t...]
  transfers between devices with their start and end apart: 5 -> 7, of which waited for: 4 -> 7; matrix products, arithmetic and copies ran while one was open for 4% -> 1% of each run, Pallas kernels for 0% -> 0%
where the time goes in v1:
time: 272 us
  waiting for transfers between devices  188 us (69%)
  starting transfers between devices  32.5 us (12%)
  between operations  14.3 us (5%)
  blocking collectives  11.8 us (4%)
  matrix products  8.75 us (3%)
  local copies, waits for them, and re-layouts  8.42 us (3%)
  other arithmetic  8.13 us (3%)
    reduce_scatter x1, waiting for transfers between devices, on_device(): lax.psum_scatter(lax.dot_general(stacked, head, CONTRACT, preferred_eleme...  83.8 us
    all_to_all x5, waiting for transfers between devices, exchange(): return lax.all_to_all(jnp.broadcast_to(a[None], (n,) + a.shape), axis, 0, 0)  69.3 us
    all_gather x1, waiting for transfers between devices, on_device(): rows = lax.all_gather(hidden_rows, 'section', axis=0, tiled=True)  34.2 us
    all_to_all x5, starting transfers between devices, exchange(): return lax.all_to_all(jnp.broadcast_to(a[None], (n,) + a.shape), axis, 0, 0)  32.4 us
    all_gather x1, blocking collectives, on_device(): grads = jnp.sum(lax.all_gather(grads, 'section'), axis=0)  11.8 us
  transfers between devices with their start and end apart: 7, of which 7 were waited for; matrix products, arithmetic and copies ran while one was open for 1% of the time, Pallas kernels for 0%

profile of v1, /device:TPU:1, one launch (start us, length us, event | category | flops | bytes accessed | tf_op | source)
XLA Modules:
  0.0 271.9 jit_solution(6974318556953941556)
XLA Ops:
  7.2 0.7 all-gather.4.cloned.1.call-update
  8.0 34.2 %all-gather.4.cloned.1.call-done = bf16[4,128,1024]{2,1,0:T(8,128)(2,1)} async-done(((bf16[1,128,1024]{2,1,0:T(8,128)(2,1)}), bf16[4,128,1024]{2,1,0:T(8,128)(2,1)}) %all-gather.4.cloned.1.call-update) | async-done | bytes 1048592 | tf_op jit(solution)/shard_map/all_gather | solution.py:40
  42.1 1.4 fusion.2
  43.7 0.4 multiply_reduce_fusion.2
  44.2 0.7 copy-done
  45.0 1.1 copy-done.3
  46.2 4.3 %fusion.49 = f32[512,2048]{1,0:T(8,128)} fusion(bf16[512,1024]{1,0:T(8,128)(2,1)S(1)} %bitcast.172, bf16[2048,1024]{1,0:T(8,128)(2,1)S(1)} %copy-done.3), kind=kOutput, calls=%fused_computation.121 | convolution fusion | flops 2147483648 | bytes 9437184 | tf_op jit(solution)/shard_map/dot_general | solution.py:66
  50.5 0.6 broadcast_in_dim.16
  51.1 7.2 %all-to-all-start = ((f32[16,6,128]{2,1,0:T(8,128)}), f32[16,6,128]{2,1,0:T(8,128)S(1)}, u32[]{:S(2)}, u32[]{:S(2)}) async-start(f32[16,6,128]{2,1,0:T(8,128)} %broadcast_in_dim.16), calls=%async_computation.1 | async-start | bytes 131072 | tf_op jit(solution)/shard_map/all_to_all | solution.py:19
  58.4 7.9 %all-to-all-done = f32[16,6,128]{2,1,0:T(8,128)S(1)} async-done(((f32[16,6,128]{2,1,0:T(8,128)}), f32[16,6,128]{2,1,0:T(8,128)S(1)}, u32[]{:S(2)}, u32[]{:S(2)}) %all-to-all-start) | async-done | bytes 49184 | tf_op jit(solution)/shard_map/all_to_all | solution.py:19
  67.1 83.8 %reduce-scatter.2.cloned.1.call-done = f32[32,2048]{1,0:T(8,128)} async-done(((f32[512,2048]{1,0:T(8,128)}), f32[32,2048]{1,0:T(8,128)}) %reduce-scatter.2.cloned.1.call-update) | async-done | bytes 262160 | tf_op jit(solution)/shard_map/reduce_scatter | solution.py:65
  150.9 1.0 slice_reduce_fusion.1
  151.9 1.1 fusion.48
  153.5 0.7 broadcast_in_dim.17
  154.1 12.2 %all-to-all-start.1 = ((f32[32,14,8]{1,2,0:T(8,128)}), f32[32,14,8]{1,2,0:T(8,128)S(1)}, u32[]{:S(2)}, u32[]{:S(2)}) async-start(f32[32,14,8]{1,2,0:T(8,128)} %broadcast_in_dim.17), calls=%async_computation.2 | async-start | bytes 262144 | tf_op jit(solution)/shard_map/all_to_all | solution.py:19
  166.4 11.1 %all-to-all-done.1 = f32[32,14,8]{1,2,0:T(8,128)S(1)} async-done(((f32[32,14,8]{1,2,0:T(8,128)}), f32[32,14,8]{1,2,0:T(8,128)S(1)}, u32[]{:S(2)}, u32[]{:S(2)}) %all-to-all-start.1) | async-done | bytes 14368 | tf_op jit(solution)/shard_map/all_to_all | solution.py:19
  178.7 0.3 fusion.21
  179.3 0.6 broadcast_in_dim.18
  179.9 5.3 %all-to-all-start.2 = ((f32[16,6,8]{2,1,0:T(8,128)}), f32[16,6,8]{2,1,0:T(8,128)S(1)}, u32[]{:S(2)}, u32[]{:S(2)}) async-start(f32[16,6,8]{2,1,0:T(8,128)} %broadcast_in_dim.18), calls=%async_computation.3 | async-start | bytes 131072 | tf_op jit(solution)/shard_map/all_to_all | solution.py:19
  185.6 7.4 %all-to-all-done.2 = f32[16,6,8]{2,1,0:T(8,128)S(1)} async-done(((f32[16,6,8]{2,1,0:T(8,128)}), f32[16,6,8]{2,1,0:T(8,128)S(1)}, u32[]{:S(2)}, u32[]{:S(2)}) %all-to-all-start.2) | async-done | bytes 3104 | tf_op jit(solution)/shard_map/all_to_all | solution.py:19
  193.1 1.3 broadcast_in_dim.19
  194.4 4.4 %all-to-all-start.3 = ((bf16[16,24,2048]{2,1,0:T(8,128)(2,1)}), bf16[16,24,2048]{2,1,0:T(8,128)(2,1)}, u32[]{:S(2)}, u32[]{:S(2)}) async-start(bf16[16,24,2048]{2,1,0:T(8,128)(2,1)} %broadcast_in_dim.19), calls=%async_computation.4 | async-start | bytes 3145728 | tf_op jit(solution)/shard_map/all_to_all | solution.py:19
  199.4 34.8 %all-to-all-done.3 = bf16[16,24,2048]{2,1,0:T(8,128)(2,1)} async-done(((bf16[16,24,2048]{2,1,0:T(8,128)(2,1)}), bf16[16,24,2048]{2,1,0:T(8,128)(2,1)}, u32[]{:S(2)}, u32[]{:S(2)}) %all-to-all-start.3) | async-done | bytes 1572896 | tf_op jit(solution)/shard_map/all_to_all | solution.py:19
  234.2 4.5 %fusion = f32[16,3,8,1024]{3,2,1,0:T(8,128)S(1)} fusion(bf16[2048,1024]{1,0:T(8,128)(2,1)} %param.6, bf16[16,24,2048]{2,1,0:T(8,128)(2,1)} %all-to-all-done.3), kind=kOutput, calls=%fused_computation | convolution fusion | flops 1610612736 | bytes 7340032 | tf_op jit(solution)/shard_map/dot_general | solution.py:139
  238.7 0.6 fusion.9
  239.3 0.3 multiply_reduce_fusion.1
  240.0 11.8 %all-gather.1 = f32[4,4,1024]{2,1,0:T(4,128)S(1)} all-gather(f32[1,4,1024]{2,1,0:T(4,128)S(1)} %maximum_bitcast_fusion), channel_id=2, replica_groups=mesh['dp'=16,'section'=4,'vocab'=8] {'section'}, dimensions={0}, use_global_device_ids=true | all-gather | bytes 81920 | tf_op jit(solution)/shard_map/all_gather | solution.py:155
  251.8 0.7 broadcast_in_dim.20
  252.5 3.4 %all-to-all-start.4 = ((f32[8,4,1024]{2,1,0:T(4,128)}), f32[8,4,1024]{2,1,0:T(4,128)S(1)}, u32[]{:S(2)}, u32[]{:S(2)}) async-start(f32[8,4,1024]{2,1,0:T(4,128)} %broadcast_in_dim.20), calls=%async_computation.5 | async-start | bytes 262144 | tf_op jit(solution)/shard_map/all_to_all | solution.py:19
  255.8 0.5 broadcast_multiply_fusion.3
  256.4 8.0 %all-to-all-done.4 = f32[8,4,1024]{2,1,0:T(4,128)S(1)} async-done(((f32[8,4,1024]{2,1,0:T(4,128)}), f32[8,4,1024]{2,1,0:T(4,128)S(1)}, u32[]{:S(2)}, u32[]{:S(2)}) %all-to-all-start.4) | async-done | bytes 131104 | tf_op jit(solution)/shard_map/all_to_all | solution.py:19
  264.4 0.6 slice.146
  (66 shorter events, 4.7 us)
Async XLA Ops:
  7.2 36.4 %copy-start.1 = (f32[1024]{0:T(1024)S(1)}, f32[1024]{0:T(1024)}, u32[]{:S(2)}) copy-start(f32[1024]{0:T(1024)} %param.8) | copy-start | bytes 12292
  7.2 35.0 %all-gather.4.cloned.1.call-start = ((), (), s32[]{:S(2)}) async-start(), calls=%async_computation.6 | async-start | bytes 1310720 | tf_op jit(solution)/shard_map/all_gather | solution.py:40
  7.9 143.0 %reduce-scatter.2.cloned.1.call-start = ((), (), s32[]{:S(2)}) async-start(), calls=%async_computation.7 | async-start | bytes 4456448 | tf_op jit(solution)/shard_map/reduce_scatter | solution.py:65
  43.6 1.2 copy-start
  43.7 2.5 copy-start.3
  50.5 7.9 %copy-start.4 = (s32[128]{0:T(128)S(1)}, s32[128]{0:T(128)}, u32[]{:S(2)}) copy-start(s32[128]{0:T(128)} %param.9) | copy-start | bytes 1540
  51.1 15.2 %all-to-all-start = ((f32[16,6,128]{2,1,0:T(8,128)}), f32[16,6,128]{2,1,0:T(8,128)S(1)}, u32[]{:S(2)}, u32[]{:S(2)}) async-start(f32[16,6,128]{2,1,0:T(8,128)} %broadcast_in_dim.16), calls=%async_computation.1 | async-start | bytes 131072 | tf_op jit(solution)/shard_map/all_to_all | solution.py:19
  154.1 23.4 %all-to-all-start.1 = ((f32[32,14,8]{1,2,0:T(8,128)}), f32[32,14,8]{1,2,0:T(8,128)S(1)}, u32[]{:S(2)}, u32[]{:S(2)}) async-start(f32[32,14,8]{1,2,0:T(8,128)} %broadcast_in_dim.17), calls=%async_computation.2 | async-start | bytes 262144 | tf_op jit(solution)/shard_map/all_to_all | solution.py:19
  179.9 13.2 %all-to-all-start.2 = ((f32[16,6,8]{2,1,0:T(8,128)}), f32[16,6,8]{2,1,0:T(8,128)S(1)}, u32[]{:S(2)}, u32[]{:S(2)}) async-start(f32[16,6,8]{2,1,0:T(8,128)} %broadcast_in_dim.18), calls=%async_computation.3 | async-start | bytes 131072 | tf_op jit(solution)/shard_map/all_to_all | solution.py:19
  194.4 39.8 %all-to-all-start.3 = ((bf16[16,24,2048]{2,1,0:T(8,128)(2,1)}), bf16[16,24,2048]{2,1,0:T(8,128)(2,1)}, u32[]{:S(2)}, u32[]{:S(2)}) async-start(bf16[16,24,2048]{2,1,0:T(8,128)(2,1)} %broadcast_in_dim.19), calls=%async_computation.4 | async-start | bytes 3145728 | tf_op jit(solution)/shard_map/all_to_all | solution.py:19
  252.5 11.9 %all-to-all-start.4 = ((f32[8,4,1024]{2,1,0:T(4,128)}), f32[8,4,1024]{2,1,0:T(4,128)S(1)}, u32[]{:S(2)}, u32[]{:S(2)}) async-start(f32[8,4,1024]{2,1,0:T(4,128)} %broadcast_in_dim.20), calls=%async_computation.5 | async-start | bytes 262144 | tf_op jit(solution)/shard_map/all_to_all | solution.py:19
  264.4 0.6 copy-start.2
Sparse Core Ops, SparseCore 0:
  10.1 31.9 all-gather.3
  50.6 100.2 reduce-scatter.1

commit v2 on v1

--- a/solution.py
+++ b/solution.py
@@ -8,6 +8,7 @@
 CONTRACT = (((1,), (1,)), ((), ()))
 F32 = jnp.float32
 BF16 = jnp.bfloat16
+PAIR = 2
 
 
 def later(a, by):
@@ -17,6 +18,24 @@
 def exchange(a, axis):
     n = lax.axis_size(axis)
     return lax.all_to_all(jnp.broadcast_to(a[None], (n,) + a.shape), axis, 0, 0)
+
+
+def permute(a, axis, to):
+    return lax.ppermute(a, axis, [(i, to(i)) for i in range(lax.axis_size(axis))])
+
+
+def up(a):
+    n = lax.axis_size("dp")
+    return permute(a, "dp", lambda i: (i + PAIR) % n)
+
+
+def down(a):
+    n = lax.axis_size("dp")
+    return permute(a, "dp", lambda i: (i - PAIR) % n)
+
+
+def swap(a):
+    return permute(a, "dp", lambda i: i ^ 1)
 
 
 def radii_of(sums, same, width):
@@ -36,19 +55,62 @@
     return r1, r2, r3, a2, a3, b3
 
 
+def sum_over_dp(blocks):
+    far = blocks(4)
+    half = far.shape[0] // 2
+    from_below, from_above = up(far[:half]), down(far[half:])
+    three, five = blocks(3), blocks(5)
+    from_below, from_above = (
+        up(jnp.concatenate([three[:half] + from_below, three[half:]], axis=0)),
+        down(jnp.concatenate([five[:half], five[half:] + from_above], axis=0)),
+    )
+    from_below, from_above = up(blocks(2) + from_below), down(blocks(6) + from_above)
+    from_below, from_above = up(blocks(1) + from_below), down(blocks(7) + from_above)
+    own = blocks(0) + from_below + from_above
+    return own[:half] + swap(own[half:])
+
+
+def gather_over_dp(block):
+    half = block.shape[0]
+    own = jnp.concatenate([block, swap(block)], axis=0)
+    seven, one = up(own), down(own)
+    six, two = up(seven), down(one)
+    five, three = up(six), down(two)
+    four = jnp.concatenate([up(five[:half]), down(three[half:])], axis=0)
+    return jnp.concatenate([own, one, two, three, four, five, six, seven], axis=0)
+
+
 def on_device(hidden_rows, head, unite_gain, norm_gain, segment_ids):
-    rows = lax.all_gather(hidden_rows, "section", axis=0, tiled=True)
-    layers = rows[:3].astype(F32)
-    final = rows[3]
-    tokens, cols = final.shape
+    own_rows = hidden_rows[0]
+    tokens, cols = own_rows.shape
     n_dp = lax.axis_size("dp")
+    n_z = n_dp // PAIR
     width = cols * n_dp
     shards = lax.axis_size("section") * lax.axis_size("vocab")
+    n_section = lax.axis_size("section")
     block = tokens // n_dp
     vocab = head.shape[0]
+    place = lax.axis_index("dp")
+    z, x = place // PAIR, place % PAIR
+    section = lax.axis_index("section")
+
+    def relative(a):
+        a = a.reshape((n_z, PAIR, block) + a.shape[1:])
+        a = lax.dynamic_slice_in_dim(jnp.concatenate([a, a], axis=0), z, n_z, axis=0)
+        a = jnp.where(x == 0, a, a[:, ::-1])
+        return a.reshape((tokens,) + a.shape[3:])
+
+    rows = [own_rows] + [permute(own_rows, "section", lambda i, j=j: i ^ j) for j in range(1, n_section)]
+    layer = [section ^ j for j in range(n_section)]
+    gains = jnp.concatenate([unite_gain, jnp.zeros_like(unite_gain[:1])], axis=0)
+    united = sum(
+        rows[j].astype(F32) * lax.dynamic_slice_in_dim(gains, layer[j], 1) for j in range(n_section)
+    )
+    final = rows[0]
+    for j in range(1, n_section):
+        final = jnp.where(layer[j] == n_section - 1, rows[j], final)
+
     same = jnp.concatenate([jnp.zeros((1,), F32), (segment_ids[1:] == segment_ids[:-1]).astype(F32)])
-
-    united = jnp.sum(layers * unite_gain[:, None, :], axis=0)
     once = united * norm_gain
     back1 = later(once, 1)
     back2 = later(once * norm_gain, 2)
@@ -59,15 +121,19 @@
             (back1 * norm_gain).astype(BF16),
             (back2 * norm_gain).astype(BF16),
         ],
-        axis=0,
-    )
-    stacked = stacked.reshape(4, n_dp, block, cols).transpose(1, 0, 2, 3).reshape(4 * tokens, cols)
-    summed = lax.psum_scatter(
-        lax.dot_general(stacked, head, CONTRACT, preferred_element_type=F32),
-        "dp",
-        scatter_dimension=0,
-        tiled=True,
-    ).reshape(4, block, vocab)
+        axis=1,
+    )
+    stacked = relative(stacked).reshape(n_z, PAIR, block, 4, cols).transpose(0, 1, 3, 2, 4)
+    stacked = stacked.reshape(n_z, PAIR * 4 * block, cols)
+
+    def product(a):
+        return lax.dot_general(a, head, CONTRACT, preferred_element_type=F32)
+
+    far = product(stacked[4])
+    order = (3, 5, 2, 6, 1, 7, 0)
+    rest = product(jnp.concatenate([stacked[i] for i in order], axis=0))
+    rest = rest.reshape(len(order), PAIR * 4 * block, vocab)
+    summed = sum_over_dp(lambda i: far if i == 4 else rest[order.index(i)]).reshape(4, block, vocab)
 
     sums = jnp.stack(
         [
@@ -80,11 +146,10 @@
         ]
     )
     sums = jnp.sum(exchange(sums, "dp"), axis=0)
-    r1, r2, r3, a2, a3, b3 = radii_of(sums, same, width)
-
-    mine = lax.axis_index("dp") * block
+    scalars = radii_of(sums, same, width)
+    mine = place * block
     r1b, r2b, r3b, a2b, a3b, b3b = (
-        lax.dynamic_slice_in_dim(v, mine, block)[:, None] for v in (r1, r2, r3, a2, a3, b3)
+        lax.dynamic_slice_in_dim(v, mine, block)[:, None] for v in scalars
     )
     teacher, plain, second, third = summed[0], summed[1], summed[2], summed[3]
     logits = jnp.stack(
@@ -118,11 +183,11 @@
     scale0 = jnp.exp(tops - all_top)
     total = jnp.sum(scale0 * totals, axis=0)
     all_peak = jnp.max(peaks, axis=0)
-    down = peaks - all_peak
-    scale = jnp.exp(down)
+    fall = peaks - all_peak
+    scale = jnp.exp(fall)
     mass = jnp.sum(scale * masses, axis=0)
-    under_p = jnp.sum(scale * (firsts + down * masses), axis=0) / mass
-    under_q = jnp.sum(scale0[:, None] * (crosses + down * totals[:, None]), axis=0) / total
+    under_p = jnp.sum(scale * (firsts + fall * masses), axis=0) / mass
+    under_q = jnp.sum(scale0[:, None] * (crosses + fall * totals[:, None]), axis=0) / total
     loss = jnp.log(mass) - under_q
     count = tokens * STEPS
     centre = (under_p - under_q) / (count * width)
@@ -131,27 +196,31 @@
     f0 = jnp.exp(top - all_top) / (total * count)
     dlogits = (e * f[:, :, None] - (e0 * f0[:, None])[None]).astype(BF16)
 
-    dall = exchange(dlogits.reshape(STEPS * block, vocab), "dp").reshape(n_dp * STEPS * block, vocab)
+    dall = gather_over_dp(dlogits.reshape(STEPS * block, vocab))
     small = exchange(jnp.concatenate([loss, centre], axis=0), "dp")
     step_loss = jnp.sum(small[:, :STEPS], axis=(0, 2)) / tokens
-    centre = small[:, STEPS:].transpose(1, 0, 2).reshape(STEPS, tokens)
+    centre = small[:, STEPS:].transpose(0, 2, 1).reshape(tokens, STEPS)
 
     dhidden = lax.dot_general(dall, head, (((1,), (0,)), ((), ())), preferred_element_type=F32)
     dhidden = dhidden.reshape(n_dp, STEPS, block, cols)
 
-    xs = (
-        united,
-        united + a2[:, None] * back1,
-        united + a3[:, None] * back1 + b3[:, None] * back2,
-    )
+    tall = relative(jnp.concatenate([jnp.stack(scalars, axis=1), centre], axis=1))
+    r1, r2, r3, a2, a3, b3, c1, c2, c3 = (tall[:, i : i + 1] for i in range(9))
+    near, back1, back2 = relative(united), relative(back1), relative(back2)
+    xs = (near, near + a2 * back1, near + a3 * back1 + b3 * back2)
     grad_norm = jnp.zeros_like(norm_gain)
     outer = jnp.zeros_like(united)
-    for k, (x, r) in enumerate(zip(xs, (r1, r2, r3), strict=True)):
-        normed = x / r[:, None]
+    for k, (v, r, c) in enumerate(zip(xs, (r1, r2, r3), (c1, c2, c3), strict=True)):
+        normed = v / r
         dh = dhidden[:, k].reshape(tokens, cols)
         grad_norm = grad_norm + jnp.sum(dh * normed, axis=0)
-        outer = outer + (dh * norm_gain - normed * (centre[k] / shards)[:, None]) / r[:, None]
-    grads = jnp.concatenate([jnp.sum(layers * outer[None], axis=1), grad_norm[None]], axis=0)
+        outer = outer + (dh * norm_gain - normed * (c / shards)) / r
+    by_row = [jnp.sum(relative(rows[j]).astype(F32) * outer, axis=0) for j in range(n_section)]
+    grads = [
+        sum(jnp.where(layer[j] == l, by_row[j], 0.0) for j in range(n_section))
+        for l in range(n_section - 1)
+    ]
+    grads = jnp.stack(grads + [grad_norm])
     grads = jnp.sum(lax.all_gather(grads, "section"), axis=0)
     grads = jnp.sum(exchange(grads, "vocab"), axis=0)
     return (step_loss, grads[:3], grads[3])

time: 272 us -> 236 us (0.87)
  waiting for transfers between devices: 188 us -> 68.4 us
  starting transfers between devices: 32.5 us -> 103 us
  between operations: 14.3 us -> 1.52 us
  other arithmetic: 8.13 us -> 20.7 us
  local copies, waits for them, and re-layouts: 8.42 us -> 18.7 us
    reduce_scatter x1 -> x0, waiting for transfers between devices: 83.8 us -> none  [on_device(): lax.psum_scatter(lax.dot_general(stacked, head, CONTRACT, preferred_eleme...]
    ppermute x0 -> x21, starting transfers between devices: none -> 72.2 us  [permute(): lax.ppermute(a, axis, [(i, to(i)) for i in range(lax.axis_size(axis))])]
    all_to_all x5 -> x4, waiting for transfers between devices: 69.3 us -> 23 us  [exchange(): return lax.all_to_all(jnp.broadcast_to(a[None], (n,) + a.shape), axis, 0, 0)]
    ppermute x0 -> x21, waiting for transfers between devices: none -> 45.4 us  [permute(): lax.ppermute(a, axis, [(i, to(i)) for i in range(lax.axis_size(axis))])]
    all_gather x1 -> x0, waiting for transfers between devices: 34.2 us -> none  [on_device(): rows = lax.all_gather(hidden_rows, 'section', axis=0, tiled=True)]
    unnamed x12 -> x38, local copies, waits for them, and re-layouts: 2.14 us -> 8.84 us
    concatenate x0 -> x13, other arithmetic: none -> 6.47 us  [the longest x8 5.49 us: relative(): jnp.concatenate([a, a], axis=0)]
    add x1 -> x8, other arithmetic: 0.62 us -> 6.94 us  [the longest x1 1.44 us: sum_over_dp(): three[:half] + from_below]
  transfers between devices with their start and end apart: 7 -> 25, of which waited for: 7 -> 13; matrix products, arithmetic and copies ran while one was open for 1% -> 10% of each run, Pallas kernels for 0% -> 0%
where the time goes in v2:
time: 236 us; the launch traced here: 234 us
  starting transfers between devices  103 us (44%)
  waiting for transfers between devices  68.4 us (29%)
  other arithmetic  20.7 us (9%)
  local copies, waits for them, and re-layouts  18.7 us (8%)
  blocking collectives  12.7 us (5%)
  matrix products  9.74 us (4%)
    ppermute x21, starting transfers between devices, permute(): lax.ppermute(a, axis, [(i, to(i)) for i in range(lax.axis_size(axis))])  72.2 us
    ppermute x21, waiting for transfers between devices, permute(): lax.ppermute(a, axis, [(i, to(i)) for i in range(lax.axis_size(axis))])  45.4 us
    all_to_all x4, starting transfers between devices, exchange(): return lax.all_to_all(jnp.broadcast_to(a[None], (n,) + a.shape), axis, 0, 0)  30.3 us
    all_to_all x4, waiting for transfers between devices, exchange(): return lax.all_to_all(jnp.broadcast_to(a[None], (n,) + a.shape), axis, 0, 0)  23 us
    all_gather x1, blocking collectives, on_device(): grads = jnp.sum(lax.all_gather(grads, 'section'), axis=0)  12.7 us
    unnamed x38, local copies, waits for them, and re-layouts  8.84 us
    concatenate x8, other arithmetic, relative(): jnp.concatenate([a, a], axis=0)  5.49 us
    dot_general x2, matrix products, product(): return lax.dot_general(a, head, CONTRACT, preferred_element_type=F32)  5.3 us
  transfers between devices with their start and end apart: 25, of which 13 were waited for; matrix products, arithmetic and copies ran while one was open for 10% of the time, Pallas kernels for 0%

profile of v2, /device:TPU:1, one launch (start us, length us, event | category | flops | bytes accessed | tf_op | source)
XLA Modules:
  0.0 234.4 jit_solution(4241934800678092195)
XLA Ops:
  0.6 6.0 %collective-permute-start = (bf16[128,1024]{1,0:T(8,128)(2,1)}, bf16[128,1024]{1,0:T(8,128)(2,1)S(1)}, u32[]{:S(2)}, u32[]{:S(2)}) collective-permute-start(bf16[128,1024]{1,0:T(8,128)(2,1)} %bitcast.215), channel_id=1, source_target_pairs={{0,24},{8,16},{16,8},{24,0},{1,25},{9,17},{17,9},{25,1},{2,26},{10... | collective-permute-start | bytes 786440 | tf_op jit(solution)/shard_map/ppermute | solution.py:24
  6.7 7.5 %collective-permute-start.1 = (bf16[128,1024]{1,0:T(8,128)(2,1)}, bf16[128,1024]{1,0:T(8,128)(2,1)S(1)}, u32[]{:S(2)}, u32[]{:S(2)}) collective-permute-start(bf16[128,1024]{1,0:T(8,128)(2,1)} %bitcast.216), channel_id=1, source_target_pairs={{0,16},{8,24},{16,0},{24,8},{1,17},{9,25},{17,1},{25,9},{2,18},{10... | collective-permute-start | bytes 786440 | tf_op jit(solution)/shard_map/ppermute | solution.py:24
  14.2 1.9 collective-permute-start.2
  31.5 3.9 %fusion.79 = f32[448,2048]{1,0:T(8,128)} fusion(bf16[448,1024]{1,0:T(8,128)(2,1)S(1)} %constant_dynamic-update-slice_fusion, bf16[2048,1024]{1,0:T(8,128)(2,1)S(1)} %copy-done), kind=kOutput, calls=%fused_computation.253 | convolution fusion | flops 1879048192 | bytes 8781824 | tf_op jit(solution)/shard_map/dot_general | solution.py:130
  35.4 8.3 %collective-permute-start.7 = (f32[32,2048]{1,0:T(8,128)}, f32[32,2048]{1,0:T(8,128)}, u32[]{:S(2)}, u32[]{:S(2)}) collective-permute-start(f32[32,2048]{1,0:T(8,128)} %get-tuple-element.76), channel_id=1, source_target_pairs={{0,448},{32,480},{64,0},{96,32},{128,64},{160,96},{192,128},{224,1... | collective-permute-start | bytes 786440 | tf_op jit(solution)/shard_map/ppermute | solution.py:24
  44.4 5.0 %all-to-all-start = ((f32[16,6,128]{2,1,0:T(8,128)}), f32[16,6,128]{2,1,0:T(8,128)S(1)}, u32[]{:S(2)}, u32[]{:S(2)}) async-start(f32[16,6,128]{2,1,0:T(8,128)} %broadcast_in_dim.28), calls=%async_computation | async-start | bytes 131072 | tf_op jit(solution)/shard_map/all_to_all | solution.py:20
  52.9 3.3 %collective-permute-start.4 = (f32[64,2048]{1,0:T(8,128)S(1)}, f32[64,2048]{1,0:T(8,128)S(1)}, u32[]{:S(2)}, u32[]{:S(2)}) collective-permute-start(f32[64,2048]{1,0:T(8,128)S(1)} %pad_maximum_fusion), channel_id=1, source_target_pairs={{0,64},{32,96},{64,128},{96,160},{128,192},{160,224},{192,256},{22... | collective-permute-start | bytes 1572872 | tf_op jit(solution)/shard_map/ppermute | solution.py:24
  57.4 2.9 %collective-permute-start.8 = (f32[64,2048]{1,0:T(8,128)S(1)}, f32[64,2048]{1,0:T(8,128)S(1)}, u32[]{:S(2)}, u32[]{:S(2)}) collective-permute-start(f32[64,2048]{1,0:T(8,128)S(1)} %pad_maximum_fusion.1), channel_id=1, source_target_pairs={{0,448},{32,480},{64,0},{96,32},{128,64},{160,96},{192,128},{224,1... | collective-permute-start | bytes 1572872 | tf_op jit(solution)/shard_map/ppermute | solution.py:24
  60.3 7.9 %collective-permute-done.4 = f32[64,2048]{1,0:T(8,128)S(1)} collective-permute-done((f32[64,2048]{1,0:T(8,128)S(1)}, f32[64,2048]{1,0:T(8,128)S(1)}, u32[]{:S(2)}, u32[]{:S(2)}) %collective-permute-start.4) | collective-permute-done | bytes 524320 | tf_op jit(solution)/shard_map/ppermute | solution.py:24
  71.3 12.3 %collective-permute-done.5 = f32[64,2048]{1,0:T(8,128)S(1)} collective-permute-done((f32[64,2048]{1,0:T(8,128)S(1)}, f32[64,2048]{1,0:T(8,128)S(1)}, u32[]{:S(2)}, u32[]{:S(2)}) %collective-permute-start.5) | collective-permute-done | bytes 524320 | tf_op jit(solution)/shard_map/ppermute | solution.py:24
  88.1 3.4 %collective-permute-start.6 = (f32[64,2048]{1,0:T(8,128)S(1)}, f32[64,2048]{1,0:T(8,128)S(1)}, u32[]{:S(2)}, u32[]{:S(2)}) collective-permute-start(f32[64,2048]{1,0:T(8,128)S(1)} %get-tuple-element.54), channel_id=1, source_target_pairs={{0,64},{32,96},{64,128},{96,160},{128,192},{160,224},{192,256},{22... | collective-permute-start | bytes 1572872 | tf_op jit(solution)/shard_map/ppermute | solution.py:24
  91.5 5.7 %collective-permute-done.9 = f32[64,2048]{1,0:T(8,128)S(1)} collective-permute-done((f32[64,2048]{1,0:T(8,128)S(1)}, f32[64,2048]{1,0:T(8,128)S(1)}, u32[]{:S(2)}, u32[]{:S(2)}) %collective-permute-start.9) | collective-permute-done | bytes 524320 | tf_op jit(solution)/shard_map/ppermute | solution.py:24
  98.3 3.3 %collective-permute-start.10 = (f32[64,2048]{1,0:T(8,128)S(1)}, f32[64,2048]{1,0:T(8,128)S(1)}, u32[]{:S(2)}, u32[]{:S(2)}) collective-permute-start(f32[64,2048]{1,0:T(8,128)S(1)} %slice_add_fusion.1), channel_id=1, source_target_pairs={{0,448},{32,480},{64,0},{96,32},{128,64},{160,96},{192,128},{224,1... | collective-permute-start | bytes 1572872 | tf_op jit(solution)/shard_map/ppermute | solution.py:24
  101.7 7.9 %collective-permute-done.10 = f32[64,2048]{1,0:T(8,128)S(1)} collective-permute-done((f32[64,2048]{1,0:T(8,128)S(1)}, f32[64,2048]{1,0:T(8,128)S(1)}, u32[]{:S(2)}, u32[]{:S(2)}) %collective-permute-start.10) | collective-permute-done | bytes 524320 | tf_op jit(solution)/shard_map/ppermute | solution.py:24
  110.8 2.1 collective-permute-start.11
  113.5 4.4 %collective-permute-done.11 = f32[32,2048]{1,0:T(8,128)S(1)} collective-permute-done((f32[32,2048]{1,0:T(8,128)S(1)}, f32[32,2048]{1,0:T(8,128)S(1)}, u32[]{:S(2)}, u32[]{:S(2)}) %collective-permute-start.11) | collective-permute-done | bytes 262176 | tf_op jit(solution)/shard_map/ppermute | solution.py:24
  119.4 15.5 %all-to-all-start.1 = ((f32[32,14,8]{1,2,0:T(8,128)}), f32[32,14,8]{1,2,0:T(8,128)S(1)}, u32[]{:S(2)}, u32[]{:S(2)}) async-start(f32[32,14,8]{1,2,0:T(8,128)} %broadcast_in_dim.29), calls=%async_computation.1 | async-start | bytes 262144 | tf_op jit(solution)/shard_map/all_to_all | solution.py:20
  135.0 11.1 %all-to-all-done.1 = f32[32,14,8]{1,2,0:T(8,128)S(1)} async-done(((f32[32,14,8]{1,2,0:T(8,128)}), f32[32,14,8]{1,2,0:T(8,128)S(1)}, u32[]{:S(2)}, u32[]{:S(2)}) %all-to-all-start.1) | async-done | bytes 14368 | tf_op jit(solution)/shard_map/all_to_all | solution.py:20
  148.5 6.4 %all-to-all-start.2 = ((f32[16,6,8]{2,1,0:T(8,128)}), f32[16,6,8]{2,1,0:T(8,128)S(1)}, u32[]{:S(2)}, u32[]{:S(2)}) async-start(f32[16,6,8]{2,1,0:T(8,128)} %broadcast_in_dim.30), calls=%async_computation.2 | async-start | bytes 131072 | tf_op jit(solution)/shard_map/all_to_all | solution.py:20
  156.0 3.3 %collective-permute-start.12 = (bf16[24,2048]{1,0:T(8,128)(2,1)S(1)}, bf16[24,2048]{1,0:T(8,128)(2,1)S(1)}, u32[]{:S(2)}, u32[]{:S(2)}) collective-permute-start(bf16[24,2048]{1,0:T(8,128)(2,1)S(1)} %get-tuple-element.44), channel_id=1, source_target_pairs={{0,32},{32,0},{64,96},{96,64},{128,160},{160,128},{192,224},{224,1... | collective-permute-start | bytes 294920 | tf_op jit(solution)/shard_map/ppermute | solution.py:24
  159.3 3.6 %all-to-all-done.2 = f32[16,6,8]{2,1,0:T(8,128)S(1)} async-done(((f32[16,6,8]{2,1,0:T(8,128)}), f32[16,6,8]{2,1,0:T(8,128)S(1)}, u32[]{:S(2)}, u32[]{:S(2)}) %all-to-all-start.2) | async-done | bytes 3104 | tf_op jit(solution)/shard_map/all_to_all | solution.py:20
  165.0 2.4 %collective-permute-start.13 = (bf16[48,2048]{1,0:T(8,128)(2,1)S(1)}, bf16[48,2048]{1,0:T(8,128)(2,1)S(1)}, u32[]{:S(2)}, u32[]{:S(2)}) collective-permute-start(bf16[48,2048]{1,0:T(8,128)(2,1)S(1)} %pad_maximum_fusion.3), channel_id=1, source_target_pairs={{0,448},{32,480},{64,0},{96,32},{128,64},{160,96},{192,128},{224,1... | collective-permute-start | bytes 589832 | tf_op jit(solution)/shard_map/ppermute | solution.py:24
  167.5 2.9 %collective-permute-start.16 = (bf16[48,2048]{1,0:T(8,128)(2,1)S(1)}, bf16[48,2048]{1,0:T(8,128)(2,1)S(1)}, u32[]{:S(2)}, u32[]{:S(2)}) collective-permute-start(bf16[48,2048]{1,0:T(8,128)(2,1)S(1)} %pad_maximum_fusion.3), channel_id=1, source_target_pairs={{0,64},{32,96},{64,128},{96,160},{128,192},{160,224},{192,256},{22... | collective-permute-start | bytes 589832 | tf_op jit(solution)/shard_map/ppermute | solution.py:24
  171.5 4.0 %collective-permute-start.14 = (bf16[48,2048]{1,0:T(8,128)(2,1)S(1)}, bf16[48,2048]{1,0:T(8,128)(2,1)S(1)}, u32[]{:S(2)}, u32[]{:S(2)}) collective-permute-start(bf16[48,2048]{1,0:T(8,128)(2,1)S(1)} %collective-permute-done.13), channel_id=1, source_target_pairs={{0,448},{32,480},{64,0},{96,32},{128,64},{160,96},{192,128},{224,1... | collective-permute-start | bytes 589832 | tf_op jit(solution)/shard_map/ppermute | solution.py:24
  175.4 2.1 collective-permute-start.17
  178.3 4.8 %collective-permute-start.15 = (bf16[48,2048]{1,0:T(8,128)(2,1)S(1)}, bf16[48,2048]{1,0:T(8,128)(2,1)S(1)}, u32[]{:S(2)}, u32[]{:S(2)}) collective-permute-start(bf16[48,2048]{1,0:T(8,128)(2,1)S(1)} %collective-permute-done.14), channel_id=1, source_target_pairs={{0,448},{32,480},{64,0},{96,32},{128,64},{160,96},{192,128},{224,1... | collective-permute-start | bytes 589832 | tf_op jit(solution)/shard_map/ppermute | solution.py:24
  185.7 5.0 %collective-permute-done.18 = bf16[48,2048]{1,0:T(8,128)(2,1)S(1)} collective-permute-done((bf16[48,2048]{1,0:T(8,128)(2,1)S(1)}, bf16[48,2048]{1,0:T(8,128)(2,1)S(1)}, u32[]{:S(2)}, u32[]{:S(2)}) %collective-permute-start.18) | collective-permute-done | bytes 196640 | tf_op jit(solution)/shard_map/ppermute | solution.py:24
  192.7 4.6 %collective-permute-start.20 = (bf16[24,2048]{1,0:T(8,128)(2,1)S(1)}, bf16[24,2048]{1,0:T(8,128)(2,1)S(1)}, u32[]{:S(2)}, u32[]{:S(2)}) collective-permute-start(bf16[24,2048]{1,0:T(8,128)(2,1)S(1)} %slice.286), channel_id=1, source_target_pairs={{0,448},{32,480},{64,0},{96,32},{128,64},{160,96},{192,128},{224,1... | collective-permute-start | bytes 294920 | tf_op jit(solution)/shard_map/ppermute | solution.py:24
  201.6 4.4 %fusion.81 = f32[384,1024]{1,0:T(8,128)S(1)} fusion(bf16[384,2048]{1,0:T(8,128)(2,1)} %constant_dynamic-update-slice_fusion.7, bf16[2048,1024]{1,0:T(8,128)(2,1)} %param.6), kind=kOutput, calls=%fused_computation.255 | convolution fusion | flops 1610612736 | bytes 7340032 | tf_op jit(solution)/shard_map/dot_general | solution.py:204
  208.5 12.7 %all-gather.1 = f32[4,4,1024]{2,1,0:T(4,128)S(1)} all-gather(f32[1,4,1024]{2,1,0:T(4,128)S(1)} %maximum_bitcast_fusion), channel_id=2, replica_groups=mesh['dp'=16,'section'=4,'vocab'=8] {'section'}, dimensions={0}, use_global_device_ids=true | all-gather | bytes 81920 | tf_op jit(solution)/shard_map/all_gather | solution.py:224
  221.8 3.4 %all-to-all-start.3 = ((f32[8,4,1024]{2,1,0:T(4,128)}), f32[8,4,1024]{2,1,0:T(4,128)S(1)}, u32[]{:S(2)}, u32[]{:S(2)}) async-start(f32[8,4,1024]{2,1,0:T(4,128)} %broadcast_in_dim.32), calls=%async_computation.3 | async-start | bytes 262144 | tf_op jit(solution)/shard_map/all_to_all | solution.py:20
  225.7 8.0 %all-to-all-done.3 = f32[8,4,1024]{2,1,0:T(4,128)S(1)} async-done(((f32[8,4,1024]{2,1,0:T(4,128)}), f32[8,4,1024]{2,1,0:T(4,128)S(1)}, u32[]{:S(2)}, u32[]{:S(2)}) %all-to-all-start.3) | async-done | bytes 131104 | tf_op jit(solution)/shard_map/all_to_all | solution.py:20
  (180 shorter events, 53.0 us)
Async XLA Ops:
  0.6 22.5 %copy-start.6 = (f32[1024]{0:T(1024)S(1)}, f32[1024]{0:T(1024)}, u32[]{:S(2)}) copy-start(f32[1024]{0:T(1024)} %param.8) | copy-start | bytes 12292
  0.6 19.8 %collective-permute-start = (bf16[128,1024]{1,0:T(8,128)(2,1)}, bf16[128,1024]{1,0:T(8,128)(2,1)S(1)}, u32[]{:S(2)}, u32[]{:S(2)}) collective-permute-start(bf16[128,1024]{1,0:T(8,128)(2,1)} %bitcast.215), channel_id=1, source_target_pairs={{0,24},{8,16},{16,8},{24,0},{1,25},{9,17},{17,9},{25,1},{2,26},{10... | collective-permute-start | bytes 786440 | tf_op jit(solution)/shard_map/ppermute | solution.py:24
  6.7 15.2 %collective-permute-start.1 = (bf16[128,1024]{1,0:T(8,128)(2,1)}, bf16[128,1024]{1,0:T(8,128)(2,1)S(1)}, u32[]{:S(2)}, u32[]{:S(2)}) collective-permute-start(bf16[128,1024]{1,0:T(8,128)(2,1)} %bitcast.216), channel_id=1, source_target_pairs={{0,16},{8,24},{16,0},{24,8},{1,17},{9,25},{17,1},{25,9},{2,18},{10... | collective-permute-start | bytes 786440 | tf_op jit(solution)/shard_map/ppermute | solution.py:24
  14.2 7.7 %collective-permute-start.2 = (bf16[128,1024]{1,0:T(8,128)(2,1)}, bf16[128,1024]{1,0:T(8,128)(2,1)S(1)}, u32[]{:S(2)}, u32[]{:S(2)}) collective-permute-start(bf16[128,1024]{1,0:T(8,128)(2,1)} %bitcast.217), channel_id=1, source_target_pairs={{0,8},{8,0},{16,24},{24,16},{1,9},{9,1},{17,25},{25,17},{2,10},{10... | collective-permute-start | bytes 786440 | tf_op jit(solution)/shard_map/ppermute | solution.py:24
  23.2 1.0 copy-start.1
  25.1 2.2 copy-start
  29.5 21.9 %collective-permute-start.3 = (f32[32,2048]{1,0:T(8,128)}, f32[32,2048]{1,0:T(8,128)}, u32[]{:S(2)}, u32[]{:S(2)}) collective-permute-start(f32[32,2048]{1,0:T(8,128)} %get-tuple-element.75), channel_id=1, source_target_pairs={{0,64},{32,96},{64,128},{96,160},{128,192},{160,224},{192,256},{22... | collective-permute-start | bytes 786440 | tf_op jit(solution)/shard_map/ppermute | solution.py:24
  35.4 15.9 %collective-permute-start.7 = (f32[32,2048]{1,0:T(8,128)}, f32[32,2048]{1,0:T(8,128)}, u32[]{:S(2)}, u32[]{:S(2)}) collective-permute-start(f32[32,2048]{1,0:T(8,128)} %get-tuple-element.76), channel_id=1, source_target_pairs={{0,448},{32,480},{64,0},{96,32},{128,64},{160,96},{192,128},{224,1... | collective-permute-start | bytes 786440 | tf_op jit(solution)/shard_map/ppermute | solution.py:24
  44.4 12.9 %all-to-all-start = ((f32[16,6,128]{2,1,0:T(8,128)}), f32[16,6,128]{2,1,0:T(8,128)S(1)}, u32[]{:S(2)}, u32[]{:S(2)}) async-start(f32[16,6,128]{2,1,0:T(8,128)} %broadcast_in_dim.28), calls=%async_computation | async-start | bytes 131072 | tf_op jit(solution)/shard_map/all_to_all | solution.py:20
  52.9 15.3 %collective-permute-start.4 = (f32[64,2048]{1,0:T(8,128)S(1)}, f32[64,2048]{1,0:T(8,128)S(1)}, u32[]{:S(2)}, u32[]{:S(2)}) collective-permute-start(f32[64,2048]{1,0:T(8,128)S(1)} %pad_maximum_fusion), channel_id=1, source_target_pairs={{0,64},{32,96},{64,128},{96,160},{128,192},{160,224},{192,256},{22... | collective-permute-start | bytes 1572872 | tf_op jit(solution)/shard_map/ppermute | solution.py:24
  57.4 14.0 %collective-permute-start.8 = (f32[64,2048]{1,0:T(8,128)S(1)}, f32[64,2048]{1,0:T(8,128)S(1)}, u32[]{:S(2)}, u32[]{:S(2)}) collective-permute-start(f32[64,2048]{1,0:T(8,128)S(1)} %pad_maximum_fusion.1), channel_id=1, source_target_pairs={{0,448},{32,480},{64,0},{96,32},{128,64},{160,96},{192,128},{224,1... | collective-permute-start | bytes 1572872 | tf_op jit(solution)/shard_map/ppermute | solution.py:24
  69.3 14.3 %collective-permute-start.5 = (f32[64,2048]{1,0:T(8,128)S(1)}, f32[64,2048]{1,0:T(8,128)S(1)}, u32[]{:S(2)}, u32[]{:S(2)}) collective-permute-start(f32[64,2048]{1,0:T(8,128)S(1)} %slice_add_fusion.2), channel_id=1, source_target_pairs={{0,64},{32,96},{64,128},{96,160},{128,192},{160,224},{192,256},{22... | collective-permute-start | bytes 1572872 | tf_op jit(solution)/shard_map/ppermute | solution.py:24
  85.0 12.2 %collective-permute-start.9 = (f32[64,2048]{1,0:T(8,128)S(1)}, f32[64,2048]{1,0:T(8,128)S(1)}, u32[]{:S(2)}, u32[]{:S(2)}) collective-permute-start(f32[64,2048]{1,0:T(8,128)S(1)} %get-tuple-element.55), channel_id=1, source_target_pairs={{0,448},{32,480},{64,0},{96,32},{128,64},{160,96},{192,128},{224,1... | collective-permute-start | bytes 1572872 | tf_op jit(solution)/shard_map/ppermute | solution.py:24
  88.1 13.6 %collective-permute-start.6 = (f32[64,2048]{1,0:T(8,128)S(1)}, f32[64,2048]{1,0:T(8,128)S(1)}, u32[]{:S(2)}, u32[]{:S(2)}) collective-permute-start(f32[64,2048]{1,0:T(8,128)S(1)} %get-tuple-element.54), channel_id=1, source_target_pairs={{0,64},{32,96},{64,128},{96,160},{128,192},{160,224},{192,256},{22... | collective-permute-start | bytes 1572872 | tf_op jit(solution)/shard_map/ppermute | solution.py:24
  98.3 11.3 %collective-permute-start.10 = (f32[64,2048]{1,0:T(8,128)S(1)}, f32[64,2048]{1,0:T(8,128)S(1)}, u32[]{:S(2)}, u32[]{:S(2)}) collective-permute-start(f32[64,2048]{1,0:T(8,128)S(1)} %slice_add_fusion.1), channel_id=1, source_target_pairs={{0,448},{32,480},{64,0},{96,32},{128,64},{160,96},{192,128},{224,1... | collective-permute-start | bytes 1572872 | tf_op jit(solution)/shard_map/ppermute | solution.py:24
  110.8 7.1 %collective-permute-start.11 = (f32[32,2048]{1,0:T(8,128)S(1)}, f32[32,2048]{1,0:T(8,128)S(1)}, u32[]{:S(2)}, u32[]{:S(2)}) collective-permute-start(f32[32,2048]{1,0:T(8,128)S(1)} %slice.273), channel_id=1, source_target_pairs={{0,32},{32,0},{64,96},{96,64},{128,160},{160,128},{192,224},{224,1... | collective-permute-start | bytes 786440 | tf_op jit(solution)/shard_map/ppermute | solution.py:24
  119.4 26.7 %all-to-all-start.1 = ((f32[32,14,8]{1,2,0:T(8,128)}), f32[32,14,8]{1,2,0:T(8,128)S(1)}, u32[]{:S(2)}, u32[]{:S(2)}) async-start(f32[32,14,8]{1,2,0:T(8,128)} %broadcast_in_dim.29), calls=%async_computation.1 | async-start | bytes 262144 | tf_op jit(solution)/shard_map/all_to_all | solution.py:20
  148.5 14.3 %all-to-all-start.2 = ((f32[16,6,8]{2,1,0:T(8,128)}), f32[16,6,8]{2,1,0:T(8,128)S(1)}, u32[]{:S(2)}, u32[]{:S(2)}) async-start(f32[16,6,8]{2,1,0:T(8,128)} %broadcast_in_dim.30), calls=%async_computation.2 | async-start | bytes 131072 | tf_op jit(solution)/shard_map/all_to_all | solution.py:20
  156.0 9.0 %collective-permute-start.12 = (bf16[24,2048]{1,0:T(8,128)(2,1)S(1)}, bf16[24,2048]{1,0:T(8,128)(2,1)S(1)}, u32[]{:S(2)}, u32[]{:S(2)}) collective-permute-start(bf16[24,2048]{1,0:T(8,128)(2,1)S(1)} %get-tuple-element.44), channel_id=1, source_target_pairs={{0,32},{32,0},{64,96},{96,64},{128,160},{160,128},{192,224},{224,1... | collective-permute-start | bytes 294920 | tf_op jit(solution)/shard_map/ppermute | solution.py:24
  165.0 6.4 %collective-permute-start.13 = (bf16[48,2048]{1,0:T(8,128)(2,1)S(1)}, bf16[48,2048]{1,0:T(8,128)(2,1)S(1)}, u32[]{:S(2)}, u32[]{:S(2)}) collective-permute-start(bf16[48,2048]{1,0:T(8,128)(2,1)S(1)} %pad_maximum_fusion.3), channel_id=1, source_target_pairs={{0,448},{32,480},{64,0},{96,32},{128,64},{160,96},{192,128},{224,1... | collective-permute-start | bytes 589832 | tf_op jit(solution)/shard_map/ppermute | solution.py:24
  167.5 8.0 %collective-permute-start.16 = (bf16[48,2048]{1,0:T(8,128)(2,1)S(1)}, bf16[48,2048]{1,0:T(8,128)(2,1)S(1)}, u32[]{:S(2)}, u32[]{:S(2)}) collective-permute-start(bf16[48,2048]{1,0:T(8,128)(2,1)S(1)} %pad_maximum_fusion.3), channel_id=1, source_target_pairs={{0,64},{32,96},{64,128},{96,160},{128,192},{160,224},{192,256},{22... | collective-permute-start | bytes 589832 | tf_op jit(solution)/shard_map/ppermute | solution.py:24
  171.5 6.8 %collective-permute-start.14 = (bf16[48,2048]{1,0:T(8,128)(2,1)S(1)}, bf16[48,2048]{1,0:T(8,128)(2,1)S(1)}, u32[]{:S(2)}, u32[]{:S(2)}) collective-permute-start(bf16[48,2048]{1,0:T(8,128)(2,1)S(1)} %collective-permute-done.13), channel_id=1, source_target_pairs={{0,448},{32,480},{64,0},{96,32},{128,64},{160,96},{192,128},{224,1... | collective-permute-start | bytes 589832 | tf_op jit(solution)/shard_map/ppermute | solution.py:24
  175.4 7.6 %collective-permute-start.17 = (bf16[48,2048]{1,0:T(8,128)(2,1)S(1)}, bf16[48,2048]{1,0:T(8,128)(2,1)S(1)}, u32[]{:S(2)}, u32[]{:S(2)}) collective-permute-start(bf16[48,2048]{1,0:T(8,128)(2,1)S(1)} %collective-permute-done.16), channel_id=1, source_target_pairs={{0,64},{32,96},{64,128},{96,160},{128,192},{160,224},{192,256},{22... | collective-permute-start | bytes 589832 | tf_op jit(solution)/shard_map/ppermute | solution.py:24
  178.3 14.4 %collective-permute-start.15 = (bf16[48,2048]{1,0:T(8,128)(2,1)S(1)}, bf16[48,2048]{1,0:T(8,128)(2,1)S(1)}, u32[]{:S(2)}, u32[]{:S(2)}) collective-permute-start(bf16[48,2048]{1,0:T(8,128)(2,1)S(1)} %collective-permute-done.14), channel_id=1, source_target_pairs={{0,448},{32,480},{64,0},{96,32},{128,64},{160,96},{192,128},{224,1... | collective-permute-start | bytes 589832 | tf_op jit(solution)/shard_map/ppermute | solution.py:24
  183.1 7.6 %collective-permute-start.18 = (bf16[48,2048]{1,0:T(8,128)(2,1)S(1)}, bf16[48,2048]{1,0:T(8,128)(2,1)S(1)}, u32[]{:S(2)}, u32[]{:S(2)}) collective-permute-start(bf16[48,2048]{1,0:T(8,128)(2,1)S(1)} %collective-permute-done.17), channel_id=1, source_target_pairs={{0,64},{32,96},{64,128},{96,160},{128,192},{160,224},{192,256},{22... | collective-permute-start | bytes 589832 | tf_op jit(solution)/shard_map/ppermute | solution.py:24
  190.7 7.2 %collective-permute-start.19 = (bf16[24,2048]{1,0:T(8,128)(2,1)S(1)}, bf16[24,2048]{1,0:T(8,128)(2,1)S(1)}, u32[]{:S(2)}, u32[]{:S(2)}) collective-permute-start(bf16[24,2048]{1,0:T(8,128)(2,1)S(1)} %slice.285), channel_id=1, source_target_pairs={{0,64},{32,96},{64,128},{96,160},{128,192},{160,224},{192,256},{22... | collective-permute-start | bytes 294920 | tf_op jit(solution)/shard_map/ppermute | solution.py:24
  192.7 6.2 %collective-permute-start.20 = (bf16[24,2048]{1,0:T(8,128)(2,1)S(1)}, bf16[24,2048]{1,0:T(8,128)(2,1)S(1)}, u32[]{:S(2)}, u32[]{:S(2)}) collective-permute-start(bf16[24,2048]{1,0:T(8,128)(2,1)S(1)} %slice.286), channel_id=1, source_target_pairs={{0,448},{32,480},{64,0},{96,32},{128,64},{160,96},{192,128},{224,1... | collective-permute-start | bytes 294920 | tf_op jit(solution)/shard_map/ppermute | solution.py:24
  206.8 1.0 copy-start.2
  206.8 1.0 copy-start.3
  206.8 1.1 copy-start.4
  206.8 1.2 copy-start.5
  221.8 11.9 %all-to-all-start.3 = ((f32[8,4,1024]{2,1,0:T(4,128)}), f32[8,4,1024]{2,1,0:T(4,128)S(1)}, u32[]{:S(2)}, u32[]{:S(2)}) async-start(f32[8,4,1024]{2,1,0:T(4,128)} %broadcast_in_dim.32), calls=%async_computation.3 | async-start | bytes 262144 | tf_op jit(solution)/shard_map/all_to_all | solution.py:20
  (1 other events, 0.6 us)

commit v3 on v2

v3 whole, which is shorter than its diff:
```python
import jax
import jax.numpy as jnp
from jax import lax
from jax.sharding import PartitionSpec as P

STEPS = 3
EPS = 1e-06
CONTRACT = (((1,), (1,)), ((), ()))
F32 = jnp.float32
BF16 = jnp.bfloat16
LANES = 128
PAIR = 2


def later(a, by):
    return jnp.concatenate([jnp.zeros((by,) + a.shape[1:], a.dtype), a[:-by]], axis=0)


def exchange(a, axis):
    n = lax.axis_size(axis)
    return lax.all_to_all(jnp.broadcast_to(a[None], (n,) + a.shape), axis, 0, 0)


def permute(a, axis, to):
    return lax.ppermute(a, axis, [(i, to(i)) for i in range(lax.axis_size(axis))])


def up(a):
    n = lax.axis_size("dp")
    return permute(a, "dp", lambda i: (i + PAIR) % n)


def down(a):
    n = lax.axis_size("dp")
    return permute(a, "dp", lambda i: (i - PAIR) % n)


def swap(a):
    return permute(a, "dp", lambda i: i ^ 1)


def columns(a):
    return [a[:, i : i + 1] for i in range(a.shape[1])]


def both(below, above):
    return lax.optimization_barrier((up(below), down(above)))


def sum_over_dp(blocks):
    far = blocks(4)
    half = far.shape[0] // 2
    from_below, from_above = both(far[:half], far[half:])
    three, five = blocks(3), blocks(5)
    from_below, from_above = both(
        jnp.concatenate([three[:half] + from_below, three[half:]], axis=0),
        jnp.concatenate([five[:half], five[half:] + from_above], axis=0),
    )
    from_below, from_above = both(blocks(2) + from_below, blocks(6) + from_above)
    from_below, from_above = both(blocks(1) + from_below, blocks(7) + from_above)
    own = blocks(0) + from_below + from_above
    return own[:half] + swap(own[half:])


def gather_over_dp(block):
    half = block.shape[0]
    own = jnp.concatenate([block, swap(block)], axis=0)
    seven, one = both(own, own)
    six, two = both(seven, one)
    five, three = both(six, two)
    four = jnp.concatenate(both(five[:half], three[half:]), axis=0)
    return [own, one, two, three, four, five, six, seven]


def parts(a):
    out = []
    for _ in range(3):
        top = lax.reduce_precision(a, 8, 7)
        out.append(top.astype(BF16))
        a = a - top
    return out


def on_device(hidden_rows, head, unite_gain, norm_gain, segment_ids):
    own_rows = hidden_rows[0]
    tokens, cols = own_rows.shape
    n_dp = lax.axis_size("dp")
    n_z = n_dp // PAIR
    width = cols * n_dp
    shards = lax.axis_size("section") * lax.axis_size("vocab")
    n_section = lax.axis_size("section")
    block = tokens // n_dp
    vocab = head.shape[0]
    place = lax.axis_index("dp")
    z, x = place // PAIR, place % PAIR
    section = lax.axis_index("section")

    def relative(a):
        a = a.reshape((n_z, PAIR, block) + a.shape[1:])
        a = lax.dynamic_slice_in_dim(jnp.concatenate([a, a], axis=0), z, n_z, axis=0)
        a = jnp.where(x == 0, a, a[:, ::-1])
        return a.reshape((tokens,) + a.shape[3:])

    rows = [own_rows] + [permute(own_rows, "section", lambda i, j=j: i ^ j) for j in range(1, n_section)]
    layer = [section ^ j for j in range(n_section)]
    gains = jnp.concatenate([unite_gain, jnp.zeros_like(unite_gain[:1])], axis=0)
    united = sum(
        rows[j].astype(F32) * lax.dynamic_slice_in_dim(gains, layer[j], 1) for j in range(n_section)
    )
    final = rows[0]
    for j in range(1, n_section):
        final = jnp.where(layer[j] == n_section - 1, rows[j], final)

    same = (segment_ids[1:] == segment_ids[:-1]).astype(F32)
    same = jnp.concatenate([jnp.zeros((1,), F32), same])[:, None]
    once = united * norm_gain
    back1 = later(once, 1)
    back2 = later(once * norm_gain, 2)
    stacked = jnp.stack(
        [
            final,
            once.astype(BF16),
            (back1 * norm_gain).astype(BF16),
            (back2 * norm_gain).astype(BF16),
        ],
        axis=1,
    )
    stacked = relative(stacked).reshape(n_z, PAIR, block, 4, cols).transpose(0, 1, 3, 2, 4)
    stacked = stacked.reshape(n_z, PAIR * 4 * block, cols)

    def total_of(a, b):
        return jnp.sum(a * b, axis=-1, keepdims=True)

    q00, q01, q11 = total_of(united, united), total_of(united, back1), total_of(back1, back1)
    q02, q12, q22 = total_of(united, back2), total_of(back1, back2), total_of(back2, back2)
    flags = [same / n_dp, later(same, 1) / n_dp]
    before = [later(q00, 1), later(q01, 1), later(q11, 1), later(q00, 2)]
    extra = jnp.concatenate([q00, q01, q11, q02, q12, q22] + before + flags, axis=1)
    extra = jnp.pad(extra, ((0, 0), (0, LANES - extra.shape[1])))
    extra = relative(extra).reshape(n_z, PAIR, 1, block, LANES)
    extra = jnp.pad(extra, ((0, 0), (0, 0), (0, 3), (0, 0), (0, 0))).reshape(n_z, -1, LANES)

    def product(a):
        return lax.dot_general(a, head, CONTRACT, preferred_element_type=F32)

    far = product(stacked[4])
    order = (3, 5, 2, 6, 1, 7, 0)
    rest = product(jnp.concatenate([stacked[i] for i in order], axis=0))
    rest = rest.reshape(len(order), PAIR * 4 * block, vocab)

    def term(i):
        return jnp.concatenate([far if i == 4 else rest[order.index(i)], extra[i]], axis=1)

    summed = sum_over_dp(term)
    q00, q01, q11, q02, q12, q22, p00, p01, p11, pp00, same0, same1 = columns(
        summed[:block, vocab : vocab + 12]
    )
    summed = summed[:, :vocab].reshape(4, block, vocab)

    def inverse(square):
        return 1.0 / jnp.sqrt(jnp.maximum(square, 0.0) / width + EPS)

    i1 = inverse(q00)
    a2 = same0 * inverse(p00)
    i2 = inverse(q00 + 2.0 * a2 * q01 + a2 * a2 * q11)
    a2p = same1 * inverse(pp00)
    a3 = same0 * inverse(p00 + 2.0 * a2p * p01 + a2p * a2p * p11)
    b3 = a3 * a2p
    i3 = inverse(
        q00 + 2.0 * a3 * q01 + a3 * a3 * q11 + 2.0 * b3 * q02 + 2.0 * a3 * b3 * q12 + b3 * b3 * q22
    )
    teacher, plain, second, third = summed[0], summed[1], summed[2], summed[3]
    logits = jnp.stack(
        [plain * i1, (plain + a2 * second) * i2, (plain + a3 * second + b3 * third) * i3]
    )

    top = jnp.max(teacher, axis=-1)
    e0 = jnp.exp(teacher - top[:, None])
    peak = jnp.max(logits, axis=-1)
    low = logits - peak[:, :, None]
    e = jnp.exp(low)
    stats = jnp.concatenate(
        [
            top[None],
            jnp.sum(e0, axis=-1)[None],
            peak,
            jnp.sum(e, axis=-1),
            jnp.sum(e * low, axis=-1),
            jnp.sum(e0[None] * low, axis=-1),
        ],
        axis=0,
    )
    every = exchange(stats, ("section", "vocab"))
    tops, totals = every[:, 0], every[:, 1]
    peaks, masses, firsts, crosses = (every[:, 2 + 3 * i : 5 + 3 * i] for i in range(4))
    all_top = jnp.max(tops, axis=0)
    scale0 = jnp.exp(tops - all_top)
    total = jnp.sum(scale0 * totals, axis=0)
    all_peak = jnp.max(peaks, axis=0)
    fall = peaks - all_peak
    scale = jnp.exp(fall)
    mass = jnp.sum(scale * masses, axis=0)
    under_p = jnp.sum(scale * (firsts + fall * masses), axis=0) / mass
    under_q = jnp.sum(scale0[:, None] * (crosses + fall * totals[:, None]), axis=0) / total
    loss = jnp.log(mass) - under_q
    count = tokens * STEPS
    centre = (under_p - under_q) / (count * width)

    f = jnp.exp(peak - all_peak) / (mass * count)
    f0 = jnp.exp(top - all_top) / (total * count)
    dlogits = (e * f[:, :, None] - (e0 * f0[:, None])[None]).astype(BF16)

    known = jnp.stack([i1, i2, i3, a2, a3, b3], axis=1).reshape(block, 6)
    known = jnp.concatenate([known, loss.T, centre.T / shards], axis=1)
    known = jnp.pad(known, ((0, 0), (0, LANES - known.shape[1])))
    message = jnp.concatenate(
        [dlogits.reshape(STEPS * block, vocab), jnp.concatenate(parts(known), axis=0)], axis=1
    )
    near, back1, back2 = (relative(a).reshape(n_z, PAIR, block, cols) for a in (united, back1, back2))
    rows = [relative(a).reshape(n_z, PAIR, block, cols) for a in rows]

    grad_norm = 0.0
    by_row = [0.0] * n_section
    losses = []
    for i, arrived in enumerate(gather_over_dp(message)):
        dhidden = lax.dot_general(
            arrived[:, :vocab], head, (((1,), (0,)), ((), ())), preferred_element_type=F32
        ).reshape(PAIR, STEPS, block, cols)
        known = jnp.sum(arrived[:, vocab:].astype(F32).reshape(PAIR, 3, block, LANES), axis=1)
        i1, i2, i3, a2, a3, b3, l1, l2, l3, c1, c2, c3 = (known[:, :, j : j + 1] for j in range(12))
        losses.append(jnp.concatenate([l1, l2, l3], axis=2))
        xs = (near[i], near[i] + a2 * back1[i], near[i] + a3 * back1[i] + b3 * back2[i])
        outer = 0.0
        for k, (v, r, c) in enumerate(zip(xs, (i1, i2, i3), (c1, c2, c3), strict=True)):
            normed = v * r
            grad_norm = grad_norm + jnp.sum(dhidden[:, k] * normed, axis=(0, 1))
            outer = outer + (dhidden[:, k] * norm_gain - normed * c) * r
        for j in range(n_section):
            by_row[j] = by_row[j] + jnp.sum(rows[j][i].astype(F32) * outer, axis=(0, 1))

    losses = jnp.stack(losses)
    losses = lax.dynamic_slice_in_dim(jnp.concatenate([losses, losses], axis=0), n_z - z, n_z, axis=0)
    losses = jnp.where(x == 0, losses, losses[:, ::-1])
    step_loss = jnp.sum(losses, axis=(0, 1, 2)) / tokens
    grads = [
        sum(jnp.where(layer[j] == l, by_row[j], 0.0) for j in range(n_section))
        for l in range(n_section - 1)
    ]
    grads = jnp.stack(grads + [grad_norm])
    grads = jnp.sum(lax.all_gather(grads, "section"), axis=0)
    grads = jnp.sum(exchange(grads, "vocab"), axis=0)
    return (step_loss, grads[:3], grads[3])


def solution(mesh):
    placed = (P("section", None, "dp"), P(("section", "vocab"), "dp"), P(None, "dp"), P("dp"), P())
    return jax.shard_map(
        on_device,
        mesh=mesh,
        in_specs=placed,
        out_specs=(P(), P(None, "dp"), P("dp")),
        check_vma=False,
    )
```

time: 236 us -> 241 us (1.021)
  matrix products: 9.74 us -> 25.4 us
  starting transfers between devices: 103 us -> 95 us
  waiting for transfers between devices: 68.4 us -> 61.9 us
  local copies, waits for them, and re-layouts: 18.7 us -> 21.6 us
    dot_general x1 -> x8, matrix products: 4.45 us -> 20.2 us  [on_device(): lax.dot_general(arrived[:, :vocab], head, (((1,), (0,)), ((), ())), prefe...]
    slice x4 -> x49, local copies, waits for them, and re-layouts: 1.02 us -> 13.4 us  [the longest x24 7.97 us: on_device(): known[:, :, j:j + 1]]
    all_to_all x4 -> x2, starting transfers between devices: 30.3 us -> 18.8 us  [exchange(): return lax.all_to_all(jnp.broadcast_to(a[None], (n,) + a.shape), axis, 0, 0)]
    unnamed x38 -> x116, local copies, waits for them, and re-layouts: 8.84 us -> 3.23 us
    all_to_all x4 -> x2, waiting for transfers between devices: 23 us -> 18.5 us  [exchange(): return lax.all_to_all(jnp.broadcast_to(a[None], (n,) + a.shape), axis, 0, 0)]
    ppermute x21, starting transfers between devices: 72.2 us -> 76.2 us  [permute(): lax.ppermute(a, axis, [(i, to(i)) for i in range(lax.axis_size(axis))])]
    select_n x1 -> x6, other arithmetic: 0.1 us -> 2.58 us  [relative(): a = jnp.where(x == 0, a, a[:, ::-1])]
    concatenate x8 -> x7, other arithmetic: 5.49 us -> 3.59 us  [relative(): jnp.concatenate([a, a], axis=0)]
  transfers between devices with their start and end apart: 25 -> 23, of which waited for: 13 -> 13; matrix products, arithmetic and copies ran while one was open for 10% -> 14% of each run, Pallas kernels for 0% -> 0%
where the time goes in v3:
time: 241 us; the launch traced here: 239 us
  starting transfers between devices  95 us (39%)
  waiting for transfers between devices  61.9 us (26%)
  matrix products  25.4 us (11%)
  other arithmetic  22.5 us (9%)
  local copies, waits for them, and re-layouts  21.6 us (9%)
  blocking collectives  10.7 us (4%)
    ppermute x21, starting transfers between devices, permute(): lax.ppermute(a, axis, [(i, to(i)) for i in range(lax.axis_size(axis))])  76.2 us
    ppermute x21, waiting for transfers between devices, permute(): lax.ppermute(a, axis, [(i, to(i)) for i in range(lax.axis_size(axis))])  43.3 us
    dot_general x8, matrix products, on_device(): lax.dot_general(arrived[:, :vocab], head, (((1,), (0,)), ((), ())), prefe...  20.2 us
    all_to_all x2, starting transfers between devices, exchange(): return lax.all_to_all(jnp.broadcast_to(a[None], (n,) + a.shape), axis, 0, 0)  18.8 us
    all_to_all x2, waiting for transfers between devices, exchange(): return lax.all_to_all(jnp.broadcast_to(a[None], (n,) + a.shape), axis, 0, 0)  18.5 us
    all_gather x1, blocking collectives, on_device(): grads = jnp.sum(lax.all_gather(grads, 'section'), axis=0)  10.7 us
    slice x24, local copies, waits for them, and re-layouts, on_device(): known[:, :, j:j + 1]  7.97 us
    dot_general x2, matrix products, product(): return lax.dot_general(a, head, CONTRACT, preferred_element_type=F32)  5.28 us
  transfers between devices with their start and end apart: 23, of which 13 were waited for; matrix products, arithmetic and copies ran while one was open for 14% of the time, Pallas kernels for 0%

profile of v3, /device:TPU:1, one launch (start us, length us, event | category | flops | bytes accessed | tf_op | source)
XLA Modules:
  0.0 239.3 jit_solution(6317988574432374708)
XLA Ops:
  0.6 6.2 %collective-permute-start = (bf16[128,1024]{1,0:T(8,128)(2,1)}, bf16[128,1024]{1,0:T(8,128)(2,1)S(1)}, u32[]{:S(2)}, u32[]{:S(2)}) collective-permute-start(bf16[128,1024]{1,0:T(8,128)(2,1)} %bitcast.856), channel_id=1, source_target_pairs={{0,24},{8,16},{16,8},{24,0},{1,25},{9,17},{17,9},{25,1},{2,26},{10... | collective-permute-start | bytes 786440 | tf_op jit(solution)/shard_map/ppermute | solution.py:25
  6.8 7.5 %collective-permute-start.1 = (bf16[128,1024]{1,0:T(8,128)(2,1)}, bf16[128,1024]{1,0:T(8,128)(2,1)S(1)}, u32[]{:S(2)}, u32[]{:S(2)}) collective-permute-start(bf16[128,1024]{1,0:T(8,128)(2,1)} %bitcast.857), channel_id=1, source_target_pairs={{0,16},{8,24},{16,0},{24,8},{1,17},{9,25},{17,1},{25,9},{2,18},{10... | collective-permute-start | bytes 786440 | tf_op jit(solution)/shard_map/ppermute | solution.py:25
  19.0 3.1 %collective-permute-done.1 = bf16[128,1024]{1,0:T(8,128)(2,1)S(1)} collective-permute-done((bf16[128,1024]{1,0:T(8,128)(2,1)}, bf16[128,1024]{1,0:T(8,128)(2,1)S(1)}, u32[]{:S(2)}, u32[]{:S(2)}) %collective-permute-start.1) | collective-permute-done | bytes 262176 | tf_op jit(solution)/shard_map/ppermute | solution.py:25
  28.1 3.9 %fusion.150 = f32[448,2048]{1,0:T(8,128)} fusion(bf16[448,1024]{1,0:T(8,128)(2,1)S(1)} %constant_dynamic-update-slice_fusion, bf16[2048,1024]{1,0:T(8,128)(2,1)S(1)} %copy-done), kind=kOutput, calls=%fused_computation.549 | convolution fusion | flops 1879048192 | bytes 8781824 | tf_op jit(solution)/shard_map/dot_general | solution.py:144
  36.0 8.3 %collective-permute-start.4 = (f32[32,2176]{1,0:T(8,128)S(1)}, f32[32,2176]{1,0:T(8,128)S(1)}, u32[]{:S(2)}, u32[]{:S(2)}) collective-permute-start(f32[32,2176]{1,0:T(8,128)S(1)} %get-tuple-element.223), channel_id=1, source_target_pairs={{0,448},{32,480},{64,0},{96,32},{128,64},{160,96},{192,128},{224,1... | collective-permute-start | bytes 835592 | tf_op jit(solution)/shard_map/ppermute | solution.py:25
  44.2 3.3 %fusion.147 = (f32[64,2048]{1,0:T(8,128)S(1)}, f32[64,2048]{1,0:T(8,128)S(1)}, f32[64,2048]{1,0:T(8,128)}, f32[64,2048]{1,0:T(8,128)S(1)}, f32[64,2048]{1,0:T(8,...) fusion(f32[448,2048]{1,0:T(8,128)} %fusion.150), kind=kLoop, calls=%fused_computation.546 | loop fusion | bytes 7340032 | tf_op jit(solution)/shard_map/slice | solution.py:152
  50.6 5.3 %collective-permute-start.6 = (f32[64,2176]{1,0:T(8,128)}, f32[64,2176]{1,0:T(8,128)}, u32[]{:S(2)}, u32[]{:S(2)}) collective-permute-start(f32[64,2176]{1,0:T(8,128)} %pad_maximum_fusion), channel_id=1, source_target_pairs={{0,448},{32,480},{64,0},{96,32},{128,64},{160,96},{192,128},{224,1... | collective-permute-start | bytes 1671176 | tf_op jit(solution)/shard_map/ppermute | solution.py:25
  60.4 6.4 %collective-permute-done.6 = f32[64,2176]{1,0:T(8,128)} collective-permute-done((f32[64,2176]{1,0:T(8,128)}, f32[64,2176]{1,0:T(8,128)}, u32[]{:S(2)}, u32[]{:S(2)}) %collective-permute-start.6) | collective-permute-done | bytes 557088 | tf_op jit(solution)/shard_map/ppermute | solution.py:25
  66.9 5.9 %collective-permute-done.5 = f32[64,2176]{1,0:T(8,128)} collective-permute-done((f32[64,2176]{1,0:T(8,128)}, f32[64,2176]{1,0:T(8,128)}, u32[]{:S(2)}, u32[]{:S(2)}) %collective-permute-start.5) | collective-permute-done | bytes 557088 | tf_op jit(solution)/shard_map/ppermute | solution.py:25
  77.1 3.4 %collective-permute-start.7 = (f32[64,2176]{1,0:T(8,128)S(1)}, f32[64,2176]{1,0:T(8,128)S(1)}, u32[]{:S(2)}, u32[]{:S(2)}) collective-permute-start(f32[64,2176]{1,0:T(8,128)S(1)} %maximum_add_fusion.2), channel_id=1, source_target_pairs={{0,64},{32,96},{64,128},{96,160},{128,192},{160,224},{192,256},{22... | collective-permute-start | bytes 1671176 | tf_op jit(solution)/shard_map/ppermute | solution.py:25
  83.0 4.5 %collective-permute-done.8 = f32[64,2176]{1,0:T(8,128)S(1)} collective-permute-done((f32[64,2176]{1,0:T(8,128)S(1)}, f32[64,2176]{1,0:T(8,128)S(1)}, u32[]{:S(2)}, u32[]{:S(2)}) %collective-permute-start.8) | collective-permute-done | bytes 557088 | tf_op jit(solution)/shard_map/ppermute | solution.py:25
  87.5 4.3 %collective-permute-done.7 = f32[64,2176]{1,0:T(8,128)S(1)} collective-permute-done((f32[64,2176]{1,0:T(8,128)S(1)}, f32[64,2176]{1,0:T(8,128)S(1)}, u32[]{:S(2)}, u32[]{:S(2)}) %collective-permute-start.7) | collective-permute-done | bytes 557088 | tf_op jit(solution)/shard_map/ppermute | solution.py:25
  93.8 3.4 %collective-permute-start.9 = (f32[64,2176]{1,0:T(8,128)S(1)}, f32[64,2176]{1,0:T(8,128)S(1)}, u32[]{:S(2)}, u32[]{:S(2)}) collective-permute-start(f32[64,2176]{1,0:T(8,128)S(1)} %maximum_add_fusion.1), channel_id=1, source_target_pairs={{0,64},{32,96},{64,128},{96,160},{128,192},{160,224},{192,256},{22... | collective-permute-start | bytes 1671176 | tf_op jit(solution)/shard_map/ppermute | solution.py:25
  97.5 7.0 %collective-permute-done.10 = f32[64,2176]{1,0:T(8,128)S(1)} collective-permute-done((f32[64,2176]{1,0:T(8,128)S(1)}, f32[64,2176]{1,0:T(8,128)S(1)}, u32[]{:S(2)}, u32[]{:S(2)}) %collective-permute-start.10) | collective-permute-done | bytes 557088 | tf_op jit(solution)/shard_map/ppermute | solution.py:25
  104.4 3.2 %collective-permute-done.9 = f32[64,2176]{1,0:T(8,128)S(1)} collective-permute-done((f32[64,2176]{1,0:T(8,128)S(1)}, f32[64,2176]{1,0:T(8,128)S(1)}, u32[]{:S(2)}, u32[]{:S(2)}) %collective-permute-start.9) | collective-permute-done | bytes 557088 | tf_op jit(solution)/shard_map/ppermute | solution.py:25
  107.7 3.5 %collective-permute-start.11 = (f32[32,2176]{1,0:T(8,128)S(1)}, f32[32,2176]{1,0:T(8,128)S(1)}, u32[]{:S(2)}, u32[]{:S(2)}) collective-permute-start(f32[32,2176]{1,0:T(8,128)S(1)} %slice.1126), channel_id=1, source_target_pairs={{0,32},{32,0},{64,96},{96,64},{128,160},{160,128},{192,224},{224,1... | collective-permute-start | bytes 835592 | tf_op jit(solution)/shard_map/ppermute | solution.py:25
  112.2 2.9 %collective-permute-done.11 = f32[32,2176]{1,0:T(8,128)S(1)} collective-permute-done((f32[32,2176]{1,0:T(8,128)S(1)}, f32[32,2176]{1,0:T(8,128)S(1)}, u32[]{:S(2)}, u32[]{:S(2)}) %collective-permute-start.11) | collective-permute-done | bytes 278560 | tf_op jit(solution)/shard_map/ppermute | solution.py:25
  117.1 15.4 %all-to-all-start = ((f32[32,14,8]{1,2,0:T(8,128)}), f32[32,14,8]{1,2,0:T(8,128)S(1)}, u32[]{:S(2)}, u32[]{:S(2)}) async-start(f32[32,14,8]{1,2,0:T(8,128)} %broadcast_in_dim.42), calls=%async_computation | async-start | bytes 262144 | tf_op jit(solution)/shard_map/all_to_all | solution.py:21
  132.8 11.0 %all-to-all-done = f32[32,14,8]{1,2,0:T(8,128)S(1)} async-done(((f32[32,14,8]{1,2,0:T(8,128)}), f32[32,14,8]{1,2,0:T(8,128)S(1)}, u32[]{:S(2)}, u32[]{:S(2)}) %all-to-all-start) | async-done | bytes 14368 | tf_op jit(solution)/shard_map/all_to_all | solution.py:21
  148.2 3.7 %collective-permute-done.12 = bf16[24,2176]{1,0:T(8,128)(2,1)S(1)} collective-permute-done((bf16[24,2176]{1,0:T(8,128)(2,1)S(1)}, bf16[24,2176]{1,0:T(8,128)(2,1)S(1)}, u32[]{:S(2)}, u32[]{:S(2)}) %collective-permute-start.12) | collective-permute-done | bytes 104480 | tf_op jit(solution)/shard_map/ppermute | solution.py:25
  154.1 4.3 %collective-permute-start.14 = (bf16[48,2176]{1,0:T(8,128)(2,1)S(1)}, bf16[48,2176]{1,0:T(8,128)(2,1)S(1)}, u32[]{:S(2)}, u32[]{:S(2)}) collective-permute-start(bf16[48,2176]{1,0:T(8,128)(2,1)S(1)} %pad_maximum_fusion.3), channel_id=1, source_target_pairs={{0,448},{32,480},{64,0},{96,32},{128,64},{160,96},{192,128},{224,1... | collective-permute-start | bytes 626696 | tf_op jit(solution)/shard_map/ppermute | solution.py:25
  158.4 3.0 %fusion.26 = f32[48,1024]{1,0:T(8,128)S(1)} fusion(bf16[2048,1024]{1,0:T(8,128)(2,1)} %param.6, bf16[48,2176]{1,0:T(8,128)(2,1)S(1)} %pad_maximum_fusion.3), kind=kOutput, calls=%fused_computation.96 | convolution fusion | flops 201326592 | bytes 4587520 | tf_op jit(solution)/shard_map/dot_general | solution.py:226
  164.8 3.0 %fusion.31 = f32[48,1024]{1,0:T(8,128)S(1)} fusion(bf16[2048,1024]{1,0:T(8,128)(2,1)} %param.6, bf16[48,2176]{1,0:T(8,128)(2,1)S(1)} %collective-permute-done.13), kind=kOutput, calls=%fused_computation.104 | convolution fusion | flops 201326592 | bytes 4587520 | tf_op jit(solution)/shard_map/dot_general | solution.py:226
  167.9 4.6 %collective-permute-start.16 = (bf16[48,2176]{1,0:T(8,128)(2,1)S(1)}, bf16[48,2176]{1,0:T(8,128)(2,1)}, u32[]{:S(2)}, u32[]{:S(2)}) collective-permute-start(bf16[48,2176]{1,0:T(8,128)(2,1)S(1)} %collective-permute-done.14), channel_id=1, source_target_pairs={{0,448},{32,480},{64,0},{96,32},{128,64},{160,96},{192,128},{224,1... | collective-permute-start | bytes 626696 | tf_op jit(solution)/shard_map/ppermute | solution.py:25
  177.4 3.0 %fusion.33 = f32[48,1024]{1,0:T(8,128)S(1)} fusion(bf16[2048,1024]{1,0:T(8,128)(2,1)} %param.6, bf16[48,2176]{1,0:T(8,128)(2,1)S(1)} %collective-permute-done.15), kind=kOutput, calls=%fused_computation.106 | convolution fusion | flops 201326592 | bytes 4587520 | tf_op jit(solution)/shard_map/dot_general | solution.py:226
  180.5 4.8 %collective-permute-start.18 = (bf16[48,2176]{1,0:T(8,128)(2,1)}, bf16[48,2176]{1,0:T(8,128)(2,1)S(1)}, u32[]{:S(2)}, u32[]{:S(2)}) collective-permute-start(bf16[48,2176]{1,0:T(8,128)(2,1)} %collective-permute-done.16), channel_id=1, source_target_pairs={{0,448},{32,480},{64,0},{96,32},{128,64},{160,96},{192,128},{224,1... | collective-permute-start | bytes 626696 | tf_op jit(solution)/shard_map/ppermute | solution.py:25
  190.9 3.5 %fusion.35 = f32[48,1024]{1,0:T(8,128)S(1)} fusion(bf16[2048,1024]{1,0:T(8,128)(2,1)} %param.6, bf16[48,2176]{1,0:T(8,128)(2,1)S(1)} %collective-permute-done.17), kind=kOutput, calls=%fused_computation.108 | convolution fusion | flops 201326592 | bytes 4587520 | tf_op jit(solution)/shard_map/dot_general | solution.py:226
  199.8 4.6 %collective-permute-start.20 = (bf16[24,2176]{1,0:T(8,128)(2,1)}, bf16[24,2176]{1,0:T(8,128)(2,1)}, u32[]{:S(2)}, u32[]{:S(2)}) collective-permute-start(bf16[24,2176]{1,0:T(8,128)(2,1)} %slice.931), channel_id=1, source_target_pairs={{0,448},{32,480},{64,0},{96,32},{128,64},{160,96},{192,128},{224,1... | collective-permute-start | bytes 313352 | tf_op jit(solution)/shard_map/ppermute | solution.py:25
  208.6 3.1 %fusion.24 = f32[48,1024]{1,0:T(8,128)S(1)} fusion(bf16[2048,1024]{1,0:T(8,128)(2,1)} %param.6, bf16[48,2176]{1,0:T(8,128)(2,1)S(1)} %constant_dynamic-update-slice_fusion.13), kind=kOutput, calls=%fused_computation.94 | convolution fusion | flops 201326592 | bytes 4587520 | tf_op jit(solution)/shard_map/dot_general | solution.py:226
  215.3 10.7 %all-gather.1 = f32[4,4,1024]{2,1,0:T(4,128)S(1)} all-gather(f32[1,4,1024]{2,1,0:T(4,128)S(1)} %maximum_bitcast_fusion), channel_id=2, replica_groups=mesh['dp'=16,'section'=4,'vocab'=8] {'section'}, dimensions={0}, use_global_device_ids=true | all-gather | bytes 81920 | tf_op jit(solution)/shard_map/all_gather | solution.py:250
  226.7 3.4 %all-to-all-start.1 = ((f32[8,4,1024]{2,1,0:T(4,128)}), f32[8,4,1024]{2,1,0:T(4,128)S(1)}, u32[]{:S(2)}, u32[]{:S(2)}) async-start(f32[8,4,1024]{2,1,0:T(4,128)} %broadcast_in_dim.44), calls=%async_computation.1 | async-start | bytes 262144 | tf_op jit(solution)/shard_map/all_to_all | solution.py:21
  231.1 7.6 %all-to-all-done.1 = f32[8,4,1024]{2,1,0:T(4,128)S(1)} async-done(((f32[8,4,1024]{2,1,0:T(4,128)}), f32[8,4,1024]{2,1,0:T(4,128)S(1)}, u32[]{:S(2)}, u32[]{:S(2)}) %all-to-all-start.1) | async-done | bytes 131104 | tf_op jit(solution)/shard_map/all_to_all | solution.py:21
  (299 shorter events, 69.3 us)
Async XLA Ops:
  0.6 25.2 %copy-start.4 = (bf16[1,128,1024]{2,1,0:T(8,128)(2,1)S(1)}, bf16[1,128,1024]{2,1,0:T(8,128)(2,1)}, u32[]{:S(2)}) copy-start(bf16[1,128,1024]{2,1,0:T(8,128)(2,1)} %param.5) | copy-start | bytes 786436
  0.6 18.3 %collective-permute-start = (bf16[128,1024]{1,0:T(8,128)(2,1)}, bf16[128,1024]{1,0:T(8,128)(2,1)S(1)}, u32[]{:S(2)}, u32[]{:S(2)}) collective-permute-start(bf16[128,1024]{1,0:T(8,128)(2,1)} %bitcast.856), channel_id=1, source_target_pairs={{0,24},{8,16},{16,8},{24,0},{1,25},{9,17},{17,9},{25,1},{2,26},{10... | collective-permute-start | bytes 786440 | tf_op jit(solution)/shard_map/ppermute | solution.py:25
  6.8 15.2 %collective-permute-start.1 = (bf16[128,1024]{1,0:T(8,128)(2,1)}, bf16[128,1024]{1,0:T(8,128)(2,1)S(1)}, u32[]{:S(2)}, u32[]{:S(2)}) collective-permute-start(bf16[128,1024]{1,0:T(8,128)(2,1)} %bitcast.857), channel_id=1, source_target_pairs={{0,16},{8,24},{16,0},{24,8},{1,17},{9,25},{17,1},{25,9},{2,18},{10... | collective-permute-start | bytes 786440 | tf_op jit(solution)/shard_map/ppermute | solution.py:25
  14.3 7.7 %collective-permute-start.2 = (bf16[128,1024]{1,0:T(8,128)(2,1)}, bf16[128,1024]{1,0:T(8,128)(2,1)S(1)}, u32[]{:S(2)}, u32[]{:S(2)}) collective-permute-start(bf16[128,1024]{1,0:T(8,128)(2,1)} %bitcast.858), channel_id=1, source_target_pairs={{0,8},{8,0},{16,24},{24,16},{1,9},{9,1},{17,25},{25,17},{2,10},{10... | collective-permute-start | bytes 786440 | tf_op jit(solution)/shard_map/ppermute | solution.py:25
  34.0 14.9 %collective-permute-start.3 = (f32[32,2176]{1,0:T(8,128)S(1)}, f32[32,2176]{1,0:T(8,128)S(1)}, u32[]{:S(2)}, u32[]{:S(2)}) collective-permute-start(f32[32,2176]{1,0:T(8,128)S(1)} %get-tuple-element.224), channel_id=1, source_target_pairs={{0,64},{32,96},{64,128},{96,160},{128,192},{160,224},{192,256},{22... | collective-permute-start | bytes 835592 | tf_op jit(solution)/shard_map/ppermute | solution.py:25
  36.0 13.8 %collective-permute-start.4 = (f32[32,2176]{1,0:T(8,128)S(1)}, f32[32,2176]{1,0:T(8,128)S(1)}, u32[]{:S(2)}, u32[]{:S(2)}) collective-permute-start(f32[32,2176]{1,0:T(8,128)S(1)} %get-tuple-element.223), channel_id=1, source_target_pairs={{0,448},{32,480},{64,0},{96,32},{128,64},{160,96},{192,128},{224,1... | collective-permute-start | bytes 835592 | tf_op jit(solution)/shard_map/ppermute | solution.py:25
  50.6 16.2 %collective-permute-start.6 = (f32[64,2176]{1,0:T(8,128)}, f32[64,2176]{1,0:T(8,128)}, u32[]{:S(2)}, u32[]{:S(2)}) collective-permute-start(f32[64,2176]{1,0:T(8,128)} %pad_maximum_fusion), channel_id=1, source_target_pairs={{0,448},{32,480},{64,0},{96,32},{128,64},{160,96},{192,128},{224,1... | collective-permute-start | bytes 1671176 | tf_op jit(solution)/shard_map/ppermute | solution.py:25
  56.8 15.9 %collective-permute-start.5 = (f32[64,2176]{1,0:T(8,128)}, f32[64,2176]{1,0:T(8,128)}, u32[]{:S(2)}, u32[]{:S(2)}) collective-permute-start(f32[64,2176]{1,0:T(8,128)} %fusion.9), channel_id=1, source_target_pairs={{0,64},{32,96},{64,128},{96,160},{128,192},{160,224},{192,256},{22... | collective-permute-start | bytes 1671176 | tf_op jit(solution)/shard_map/ppermute | solution.py:25
  58.8 17.2 %copy-start.5 = (f32[64,2048]{1,0:T(8,128)S(1)}, f32[64,2048]{1,0:T(8,128)}, u32[]{:S(2)}) copy-start(f32[64,2048]{1,0:T(8,128)} %get-tuple-element.211) | copy-start | bytes 1572868
  74.0 13.5 %collective-permute-start.8 = (f32[64,2176]{1,0:T(8,128)S(1)}, f32[64,2176]{1,0:T(8,128)S(1)}, u32[]{:S(2)}, u32[]{:S(2)}) collective-permute-start(f32[64,2176]{1,0:T(8,128)S(1)} %maximum_add_fusion.3), channel_id=1, source_target_pairs={{0,448},{32,480},{64,0},{96,32},{128,64},{160,96},{192,128},{224,1... | collective-permute-start | bytes 1671176 | tf_op jit(solution)/shard_map/ppermute | solution.py:25
  77.1 14.7 %collective-permute-start.7 = (f32[64,2176]{1,0:T(8,128)S(1)}, f32[64,2176]{1,0:T(8,128)S(1)}, u32[]{:S(2)}, u32[]{:S(2)}) collective-permute-start(f32[64,2176]{1,0:T(8,128)S(1)} %maximum_add_fusion.2), channel_id=1, source_target_pairs={{0,64},{32,96},{64,128},{96,160},{128,192},{160,224},{192,256},{22... | collective-permute-start | bytes 1671176 | tf_op jit(solution)/shard_map/ppermute | solution.py:25
  91.8 12.6 %collective-permute-start.10 = (f32[64,2176]{1,0:T(8,128)S(1)}, f32[64,2176]{1,0:T(8,128)S(1)}, u32[]{:S(2)}, u32[]{:S(2)}) collective-permute-start(f32[64,2176]{1,0:T(8,128)S(1)} %maximum_add_fusion.4), channel_id=1, source_target_pairs={{0,448},{32,480},{64,0},{96,32},{128,64},{160,96},{192,128},{224,1... | collective-permute-start | bytes 1671176 | tf_op jit(solution)/shard_map/ppermute | solution.py:25
  93.8 13.8 %collective-permute-start.9 = (f32[64,2176]{1,0:T(8,128)S(1)}, f32[64,2176]{1,0:T(8,128)S(1)}, u32[]{:S(2)}, u32[]{:S(2)}) collective-permute-start(f32[64,2176]{1,0:T(8,128)S(1)} %maximum_add_fusion.1), channel_id=1, source_target_pairs={{0,64},{32,96},{64,128},{96,160},{128,192},{160,224},{192,256},{22... | collective-permute-start | bytes 1671176 | tf_op jit(solution)/shard_map/ppermute | solution.py:25
  107.6 40.5 %copy-start.8 = (bf16[8,2,8,1024]{3,2,1,0:T(8,128)(2,1)S(1)}, bf16[8,2,8,1024]{3,2,1,0:T(8,128)(2,1)}, u32[]{:S(2)}) copy-start(bf16[8,2,8,1024]{3,2,1,0:T(8,128)(2,1)} %get-tuple-element.266) | copy-start | bytes 786436
  107.7 7.4 %collective-permute-start.11 = (f32[32,2176]{1,0:T(8,128)S(1)}, f32[32,2176]{1,0:T(8,128)S(1)}, u32[]{:S(2)}, u32[]{:S(2)}) collective-permute-start(f32[32,2176]{1,0:T(8,128)S(1)} %slice.1126), channel_id=1, source_target_pairs={{0,32},{32,0},{64,96},{96,64},{128,160},{160,128},{192,224},{224,1... | collective-permute-start | bytes 835592 | tf_op jit(solution)/shard_map/ppermute | solution.py:25
  117.1 26.6 %all-to-all-start = ((f32[32,14,8]{1,2,0:T(8,128)}), f32[32,14,8]{1,2,0:T(8,128)S(1)}, u32[]{:S(2)}, u32[]{:S(2)}) async-start(f32[32,14,8]{1,2,0:T(8,128)} %broadcast_in_dim.42), calls=%async_computation | async-start | bytes 262144 | tf_op jit(solution)/shard_map/all_to_all | solution.py:21
  145.9 6.0 %collective-permute-start.12 = (bf16[24,2176]{1,0:T(8,128)(2,1)S(1)}, bf16[24,2176]{1,0:T(8,128)(2,1)S(1)}, u32[]{:S(2)}, u32[]{:S(2)}) collective-permute-start(bf16[24,2176]{1,0:T(8,128)(2,1)S(1)} %maximum_maximum_fusion), channel_id=1, source_target_pairs={{0,32},{32,0},{64,96},{96,64},{128,160},{160,128},{192,224},{224,1... | collective-permute-start | bytes 313352 | tf_op jit(solution)/shard_map/ppermute | solution.py:25
  151.9 10.5 %collective-permute-start.13 = (bf16[48,2176]{1,0:T(8,128)(2,1)S(1)}, bf16[48,2176]{1,0:T(8,128)(2,1)S(1)}, u32[]{:S(2)}, u32[]{:S(2)}) collective-permute-start(bf16[48,2176]{1,0:T(8,128)(2,1)S(1)} %pad_maximum_fusion.3), channel_id=1, source_target_pairs={{0,64},{32,96},{64,128},{96,160},{128,192},{160,224},{192,256},{22... | collective-permute-start | bytes 626696 | tf_op jit(solution)/shard_map/ppermute | solution.py:25
  154.1 8.4 %collective-permute-start.14 = (bf16[48,2176]{1,0:T(8,128)(2,1)S(1)}, bf16[48,2176]{1,0:T(8,128)(2,1)S(1)}, u32[]{:S(2)}, u32[]{:S(2)}) collective-permute-start(bf16[48,2176]{1,0:T(8,128)(2,1)S(1)} %pad_maximum_fusion.3), channel_id=1, source_target_pairs={{0,448},{32,480},{64,0},{96,32},{128,64},{160,96},{192,128},{224,1... | collective-permute-start | bytes 626696 | tf_op jit(solution)/shard_map/ppermute | solution.py:25
  162.5 12.8 %collective-permute-start.15 = (bf16[48,2176]{1,0:T(8,128)(2,1)S(1)}, bf16[48,2176]{1,0:T(8,128)(2,1)S(1)}, u32[]{:S(2)}, u32[]{:S(2)}) collective-permute-start(bf16[48,2176]{1,0:T(8,128)(2,1)S(1)} %collective-permute-done.13), channel_id=1, source_target_pairs={{0,64},{32,96},{64,128},{96,160},{128,192},{160,224},{192,256},{22... | collective-permute-start | bytes 626696 | tf_op jit(solution)/shard_map/ppermute | solution.py:25
  167.9 7.4 %collective-permute-start.16 = (bf16[48,2176]{1,0:T(8,128)(2,1)S(1)}, bf16[48,2176]{1,0:T(8,128)(2,1)}, u32[]{:S(2)}, u32[]{:S(2)}) collective-permute-start(bf16[48,2176]{1,0:T(8,128)(2,1)S(1)} %collective-permute-done.14), channel_id=1, source_target_pairs={{0,448},{32,480},{64,0},{96,32},{128,64},{160,96},{192,128},{224,1... | collective-permute-start | bytes 626696 | tf_op jit(solution)/shard_map/ppermute | solution.py:25
  175.2 15.0 %collective-permute-start.17 = (bf16[48,2176]{1,0:T(8,128)(2,1)S(1)}, bf16[48,2176]{1,0:T(8,128)(2,1)S(1)}, u32[]{:S(2)}, u32[]{:S(2)}) collective-permute-start(bf16[48,2176]{1,0:T(8,128)(2,1)S(1)} %collective-permute-done.15), channel_id=1, source_target_pairs={{0,64},{32,96},{64,128},{96,160},{128,192},{160,224},{192,256},{22... | collective-permute-start | bytes 626696 | tf_op jit(solution)/shard_map/ppermute | solution.py:25
  180.5 9.8 %collective-permute-start.18 = (bf16[48,2176]{1,0:T(8,128)(2,1)}, bf16[48,2176]{1,0:T(8,128)(2,1)S(1)}, u32[]{:S(2)}, u32[]{:S(2)}) collective-permute-start(bf16[48,2176]{1,0:T(8,128)(2,1)} %collective-permute-done.16), channel_id=1, source_target_pairs={{0,448},{32,480},{64,0},{96,32},{128,64},{160,96},{192,128},{224,1... | collective-permute-start | bytes 626696 | tf_op jit(solution)/shard_map/ppermute | solution.py:25
  195.2 16.9 %copy-start.6 = (f32[8,2,8,1024]{3,2,1,0:T(8,128)S(1)}, f32[8,2,8,1024]{3,2,1,0:T(8,128)}, u32[]{:S(2)}) copy-start(f32[8,2,8,1024]{3,2,1,0:T(8,128)} %reverse_select_fusion.1) | copy-start | bytes 1572868
  195.2 16.9 %copy-start.12 = (f32[1024]{0:T(1024)S(1)}, f32[1024]{0:T(1024)}, u32[]{:S(2)}) copy-start(f32[1024]{0:T(1024)} %param.8) | copy-start | bytes 12292
  197.9 8.9 %collective-permute-start.19 = (bf16[24,2176]{1,0:T(8,128)(2,1)}, bf16[24,2176]{1,0:T(8,128)(2,1)}, u32[]{:S(2)}, u32[]{:S(2)}) collective-permute-start(bf16[24,2176]{1,0:T(8,128)(2,1)} %slice.930), channel_id=1, source_target_pairs={{0,64},{32,96},{64,128},{96,160},{128,192},{160,224},{192,256},{22... | collective-permute-start | bytes 313352 | tf_op jit(solution)/shard_map/ppermute | solution.py:25
  199.8 7.0 %collective-permute-start.20 = (bf16[24,2176]{1,0:T(8,128)(2,1)}, bf16[24,2176]{1,0:T(8,128)(2,1)}, u32[]{:S(2)}, u32[]{:S(2)}) collective-permute-start(bf16[24,2176]{1,0:T(8,128)(2,1)} %slice.931), channel_id=1, source_target_pairs={{0,448},{32,480},{64,0},{96,32},{128,64},{160,96},{192,128},{224,1... | collective-permute-start | bytes 313352 | tf_op jit(solution)/shard_map/ppermute | solution.py:25
  213.9 16.3 %copy-start.16 = (f32[2,8,3]{1,0,2:T(2,128)S(1)}, f32[2,8,3]{1,0,2:T(2,128)}, u32[]{:S(2)}) copy-start(f32[2,8,3]{1,0,2:T(2,128)} %copy.282) | copy-start | bytes 580
  214.0 16.3 %copy-start.13 = (f32[2,8,3]{1,0,2:T(2,128)S(1)}, f32[2,8,3]{1,0,2:T(2,128)}, u32[]{:S(2)}) copy-start(f32[2,8,3]{1,0,2:T(2,128)} %copy.283) | copy-start | bytes 580
  214.0 16.3 %copy-start.15 = (f32[2,8,3]{1,0,2:T(2,128)S(1)}, f32[2,8,3]{1,0,2:T(2,128)}, u32[]{:S(2)}) copy-start(f32[2,8,3]{1,0,2:T(2,128)} %copy-done.14) | copy-start | bytes 580
  214.0 16.3 %copy-start.17 = (f32[2,8,3]{1,0,2:T(2,128)S(1)}, f32[2,8,3]{1,0,2:T(2,128)}, u32[]{:S(2)}) copy-start(f32[2,8,3]{1,0,2:T(2,128)} %copy.280) | copy-start | bytes 580
  226.7 11.9 %all-to-all-start.1 = ((f32[8,4,1024]{2,1,0:T(4,128)}), f32[8,4,1024]{2,1,0:T(4,128)S(1)}, u32[]{:S(2)}, u32[]{:S(2)}) async-start(f32[8,4,1024]{2,1,0:T(4,128)} %broadcast_in_dim.44), calls=%async_computation.1 | async-start | bytes 262144 | tf_op jit(solution)/shard_map/all_to_all | solution.py:21
  (36 other events, 162.5 us)

commit v4 on v3

v4 whole, which is shorter than its diff:
```python
import functools

import jax
import jax.numpy as jnp
from jax import lax
from jax.experimental import pallas as pl
from jax.experimental.pallas import tpu as pltpu
from jax.sharding import PartitionSpec as P

STEPS = 3
EPS = 1e-06
CONTRACT = (((1,), (1,)), ((), ()))
F32 = jnp.float32
BF16 = jnp.bfloat16
LANES = 128
PAIR = 2
VMEM_LIMIT = 40 * 1024 * 1024


def exchange(a, axis):
    n = lax.axis_size(axis)
    return lax.all_to_all(jnp.broadcast_to(a[None], (n,) + a.shape), axis, 0, 0)


def permute(a, axis, to):
    return lax.ppermute(a, axis, [(i, to(i)) for i in range(lax.axis_size(axis))])


def ring(a, steps):
    n, m = lax.axis_size("dp"), lax.axis_size("section")
    pairs = [
        (i * m + j, (i + steps * PAIR * (1 - 2 * (j % 2))) % n * m + j)
        for i in range(n)
        for j in range(m)
    ]
    return lax.ppermute(a, ("dp", "section"), pairs)


def swap(a):
    return permute(a, "dp", lambda i: i ^ 1)


def both(below, above):
    return lax.optimization_barrier((ring(below, 1), ring(above, -1)))


def columns(a):
    return [a[:, i : i + 1] for i in range(a.shape[1])]


def sum_over_dp(term, n_z):
    totals = [term(n_z - 1, h) for h in range(PAIR)]
    for i in range(n_z - 2, -1, -1):
        for h in (1, 0):
            totals[h] = term(i, h) + ring(totals[h], 1)
    return totals[0] + swap(totals[1])


def gather_over_dp(block):
    own = jnp.concatenate([block, swap(block)], axis=0)
    seven, one = both(own, own)
    six, two = both(seven, one)
    five, three = both(six, two)
    cut = block.shape[1] // LANES // 2 * LANES
    four = both(five[:, :cut], three[:, cut:])
    return [own, one, two, three, *four, five, six, seven]


def parts(a):
    out = []
    for _ in range(3):
        top = lax.reduce_precision(a, 8, 7)
        out.append(top.astype(BF16))
        a = a - top
    return out


def shifted(a, by):
    at = lax.broadcasted_iota(jnp.int32, a.shape, 0)
    return jnp.where(at < by, 0.0, pltpu.roll(a, by, 0))


def token_of(place_ref, i, h, n_z, block):
    z, x, way = place_ref[1], place_ref[2], place_ref[3]
    other = lax.rem(z + way * i + n_z, n_z)
    return pl.multiple_of((other * PAIR + (x ^ h)) * block, block)


def united_of(place_ref, rows, gains_ref):
    section = place_ref[0]
    return sum(
        rows[j][...].astype(F32) * gains_ref[pl.ds(section ^ j, 1), :] for j in range(len(rows))
    )


def prepare(n_z, block, n_dp, place_ref, gains_ref, gain_ref, same_ref, *refs):
    rows, (lhs_ref, extra_ref, m0, m1, m2, m3, ex) = refs[:-7], refs[-7:]
    section, count = place_ref[0], len(rows)
    united = united_of(place_ref, rows, gains_ref)
    gain = gain_ref[...]
    once = united * gain
    back1 = shifted(once, 1)
    back2 = shifted(once * gain, 2)
    final = 0.0
    for j in range(count):
        final = final + rows[j][...].astype(F32) * ((section ^ j) == count - 1).astype(F32)
    m0[...] = final
    m1[...] = once
    m2[...] = back1 * gain
    m3[...] = back2 * gain

    shape = (united.shape[0], LANES)
    lane = lax.broadcasted_iota(jnp.int32, shape, 1)

    def total(a, b):
        return jnp.broadcast_to(jnp.sum(a * b, axis=1, keepdims=True), shape)

    q00, q01, q11 = total(united, united), total(united, back1), total(back1, back1)
    q02, q12, q22 = total(united, back2), total(back1, back2), total(back2, back2)
    same = jnp.broadcast_to(same_ref[...], shape) * (1.0 / n_dp)
    kept = [q00, q01, q11, q02, q12, q22]
    kept += [shifted(q00, 1), shifted(q01, 1), shifted(q11, 1), shifted(q00, 2)]
    kept += [same, shifted(same, 1)]
    extra = jnp.zeros(shape, F32)
    for i, a in enumerate(kept):
        extra = jnp.where(lane == i, a, extra)
    ex[...] = extra

    size = 4 * block
    for i in range(n_z):
        for h in range(PAIR):
            at = (i * PAIR + h) * size
            mine = pl.ds(token_of(place_ref, i, h, n_z, block), block)
            first = jnp.concatenate([m0[mine, :], m1[mine, :]], axis=0)
            lhs_ref[at : at + 2 * block, :] = first.astype(BF16)
            second = jnp.concatenate([m2[mine, :], m3[mine, :]], axis=0)
            lhs_ref[at + 2 * block : at + size, :] = second.astype(BF16)
            extra_ref[at : at + block, :] = ex[mine, :]
            extra_ref[at + block : at + size, :] = jnp.zeros((size - block, LANES), F32)


def arrange(n_z, block, place_ref, gains_ref, gain_ref, *refs):
    rows, (near_ref, back1_ref, back2_ref, layers_ref, m0, m1, m2, m3) = refs[:-8], refs[-8:]
    united = united_of(place_ref, rows, gains_ref)
    gain = gain_ref[...]
    once = united * gain
    m0[...] = united
    m1[...] = shifted(once, 1)
    m2[...] = shifted(once * gain, 2)

    def ordered(source):
        for i in range(n_z):
            yield (
                slice(i * PAIR * block, (i + 1) * PAIR * block),
                jnp.concatenate(
                    [
                        source[pl.ds(token_of(place_ref, i, h, n_z, block), block), :]
                        for h in range(PAIR)
                    ],
                    axis=0,
                ),
            )

    for source, out in ((m0, near_ref), (m1, back1_ref), (m2, back2_ref)):
        for at, a in ordered(source):
            out[at, :] = a
    for j, row in enumerate(rows):
        m3[...] = row[...].astype(F32)
        for at, a in ordered(m3):
            layers_ref[j, at, :] = a.astype(BF16)


def backward(n_z, block, shards, place_ref, *refs):
    blocks, (head_ref, near_ref, back1_ref, back2_ref, layers_ref, gain_ref) = refs[:9], refs[9:15]
    grads_ref, known_ref, lhs, dh, aux, acc = refs[15:]
    vocab, cols = head_ref.shape
    size = PAIR * STEPS * block
    spots = [0, 1, 2, 3, 4, 4, 5, 6, 7]
    for b, (spot, ref) in enumerate(zip(spots, blocks, strict=True)):
        at = slice(spot * size, (spot + 1) * size)
        if b == 4:
            cut = ref.shape[1]
            lhs[at, :cut] = ref[...]
            continue
        start = cut if b == 5 else 0
        lhs[at, start:] = ref[:, : vocab - start]
        tail = ref[:, vocab - start :].astype(F32)
        for h in range(PAIR):
            three = [tail[(h * 3 + p) * block : (h * 3 + p + 1) * block] for p in range(3)]
            known = three[0] + three[1] + three[2]
            aux[(spot * PAIR + h) * block : (spot * PAIR + h + 1) * block, :] = known
            known_ref[pl.ds(token_of(place_ref, spot, h, n_z, block), block), :] = known

    wide = 256

    @pl.loop(0, cols // wide)
    def _(c):
        at = pl.ds(pl.multiple_of(c * wide, wide), wide)
        dh[:, at] = jnp.dot(lhs[...], head_ref[:, at], preferred_element_type=F32)

    acc[...] = jnp.zeros_like(acc)
    gain = gain_ref[...]
    count = layers_ref.shape[0]

    @pl.loop(0, n_z)
    def _(i):
        pair = pl.multiple_of(i * PAIR * block, PAIR * block)
        layers = [layers_ref[j, pl.ds(pair, PAIR * block), :].astype(F32) for j in range(count)]
        for h in range(PAIR):
            mine = pl.ds(pl.multiple_of(pair + h * block, block), block)
            known = aux[mine, :]
            i1, i2, i3, a2, a3, b3, c1, c2, c3 = (
                known[:, j : j + 1] for j in (0, 1, 2, 3, 4, 5, 9, 10, 11)
            )
            u, v1, v2 = near_ref[mine, :], back1_ref[mine, :], back2_ref[mine, :]
            xs = (u, u + a2 * v1, u + a3 * v1 + b3 * v2)
            outer, to_norm = 0.0, 0.0
            for k, (v, r, c) in enumerate(zip(xs, (i1, i2, i3), (c1, c2, c3), strict=True)):
                start = pl.multiple_of(i * size + (h * STEPS + k) * block, block)
                d = dh[pl.ds(start, block), :]
                normed = v * r
                to_norm = to_norm + d * normed
                outer = outer + (d * gain - normed * (c * (1.0 / shards))) * r
            acc[count * block :, :] += to_norm
            for j in range(count):
                acc[j * block : (j + 1) * block, :] += layers[j][h * block : (h + 1) * block] * outer

    section = place_ref[0]
    for j in range(count + 1):
        row = jnp.sum(acc[j * block : (j + 1) * block, :], axis=0, keepdims=True)
        grads_ref[pl.ds(section ^ j if j < count else count - 1, 1), :] = row


def on_device(hidden_rows, head, unite_gain, norm_gain, segment_ids):
    own_rows = hidden_rows[0]
    tokens, cols = own_rows.shape
    n_dp = lax.axis_size("dp")
    n_z = n_dp // PAIR
    width = cols * n_dp
    shards = lax.axis_size("section") * lax.axis_size("vocab")
    n_section = lax.axis_size("section")
    block = tokens // n_dp
    vocab = head.shape[0]
    place = lax.axis_index("dp")
    z, x = place // PAIR, place % PAIR
    section = lax.axis_index("section")

    sections = [own_rows]
    for j in range(1, n_section):
        sections.append(permute(own_rows, "section", lambda i, j=j: i ^ j))
    rows = sections
    way = 1 - 2 * (section % 2)
    where = jnp.stack([section, z, x, way]).astype(jnp.int32)
    gains = jnp.concatenate([unite_gain, jnp.zeros_like(unite_gain[:1])], axis=0)
    gain = norm_gain[None]
    same = (segment_ids[1:] == segment_ids[:-1]).astype(F32)
    same = jnp.concatenate([jnp.zeros((1,), F32), same])[:, None]

    smem, vmem = pl.BlockSpec(memory_space=pltpu.SMEM), pl.BlockSpec(memory_space=pltpu.VMEM)
    params = pltpu.CompilerParams(vmem_limit_bytes=VMEM_LIMIT)
    whole = pltpu.VMEM((tokens, cols), F32)
    stacked, extra = pl.pallas_call(
        functools.partial(prepare, n_z, block, n_dp),
        out_shape=(
            jax.ShapeDtypeStruct((4 * tokens, cols), BF16),
            jax.ShapeDtypeStruct((4 * tokens, LANES), F32),
        ),
        in_specs=[smem] + [vmem] * (3 + n_section),
        out_specs=(vmem, vmem),
        scratch_shapes=[whole] * 4 + [pltpu.VMEM((tokens, LANES), F32)],
        compiler_params=params,
        name="prepare",
    )(where, gains, gain, same, *rows)

    def product(a):
        return lax.dot_general(a, head, CONTRACT, preferred_element_type=F32)

    size = 4 * block
    split = (n_z - 1) * PAIR * size
    far = product(stacked[split:])
    rest = product(stacked[:split])

    def term(i, h):
        at = (i * PAIR + h) * size
        made = far[at - split : at - split + size] if at >= split else rest[at : at + size]
        return jnp.concatenate([made, extra[at : at + size]], axis=1)

    summed = sum_over_dp(term, n_z)
    q00, q01, q11, q02, q12, q22, p00, p01, p11, pp00, same0, same1 = columns(
        summed[:block, vocab : vocab + 12]
    )
    summed = summed[:, :vocab].reshape(4, block, vocab)

    def inverse(square):
        return 1.0 / jnp.sqrt(jnp.maximum(square, 0.0) / width + EPS)

    i1 = inverse(q00)
    a2 = same0 * inverse(p00)
    i2 = inverse(q00 + 2.0 * a2 * q01 + a2 * a2 * q11)
    a2p = same1 * inverse(pp00)
    a3 = same0 * inverse(p00 + 2.0 * a2p * p01 + a2p * a2p * p11)
    b3 = a3 * a2p
    i3 = inverse(
        q00 + 2.0 * a3 * q01 + a3 * a3 * q11 + 2.0 * b3 * q02 + 2.0 * a3 * b3 * q12 + b3 * b3 * q22
    )
    teacher, plain, second, third = summed[0], summed[1], summed[2], summed[3]
    logits = jnp.stack(
        [plain * i1, (plain + a2 * second) * i2, (plain + a3 * second + b3 * third) * i3]
    )

    top = jnp.max(teacher, axis=-1)
    e0 = jnp.exp(teacher - top[:, None])
    peak = jnp.max(logits, axis=-1)
    low = logits - peak[:, :, None]
    e = jnp.exp(low)
    stats = jnp.concatenate(
        [
            top[None],
            jnp.sum(e0, axis=-1)[None],
            peak,
            jnp.sum(e, axis=-1),
            jnp.sum(e * low, axis=-1),
            jnp.sum(e0[None] * low, axis=-1),
        ],
        axis=0,
    )
    every = exchange(stats, ("section", "vocab"))
    tops, totals = every[:, 0], every[:, 1]
    peaks, masses, firsts, crosses = (every[:, 2 + 3 * i : 5 + 3 * i] for i in range(4))
    all_top = jnp.max(tops, axis=0)
    scale0 = jnp.exp(tops - all_top)
    total = jnp.sum(scale0 * totals, axis=0)
    all_peak = jnp.max(peaks, axis=0)
    fall = peaks - all_peak
    scale = jnp.exp(fall)
    mass = jnp.sum(scale * masses, axis=0)
    under_p = jnp.sum(scale * (firsts + fall * masses), axis=0) / mass
    under_q = jnp.sum(scale0[:, None] * (crosses + fall * totals[:, None]), axis=0) / total
    loss = jnp.log(mass) - under_q
    count = tokens * STEPS
    centre = (under_p - under_q) / (count * width)

    f = jnp.exp(peak - all_peak) / (mass * count)
    f0 = jnp.exp(top - all_top) / (total * count)
    dlogits = (e * f[:, :, None] - (e0 * f0[:, None])[None]).astype(BF16)

    known = jnp.stack([i1, i2, i3, a2, a3, b3], axis=1).reshape(block, 6)
    known = jnp.concatenate([known, loss.T, centre.T], axis=1)
    known = jnp.pad(known, ((0, 0), (0, LANES - known.shape[1])))
    message = jnp.concatenate(
        [dlogits.reshape(STEPS * block, vocab), jnp.concatenate(parts(known), axis=0)], axis=1
    )
    ordered = jax.ShapeDtypeStruct((tokens, cols), F32)
    tied = lax.optimization_barrier((message, *rows))
    near, back1, back2, layers = pl.pallas_call(
        functools.partial(arrange, n_z, block),
        out_shape=(ordered,) * 3 + (jax.ShapeDtypeStruct((n_section, tokens, cols), BF16),),
        in_specs=[smem] + [vmem] * (2 + n_section),
        out_specs=(vmem,) * 4,
        scratch_shapes=[whole] * 4,
        compiler_params=params,
        name="arrange",
    )(where, gains, gain, *tied[1:])

    blocks = gather_over_dp(tied[0])
    grads, known = pl.pallas_call(
        functools.partial(backward, n_z, block, shards),
        out_shape=(
            jax.ShapeDtypeStruct((n_section, cols), F32),
            jax.ShapeDtypeStruct((tokens, LANES), F32),
        ),
        in_specs=[smem] + [vmem] * 15,
        out_specs=(vmem, vmem),
        scratch_shapes=[
            pltpu.VMEM((STEPS * tokens, vocab), BF16),
            pltpu.VMEM((STEPS * tokens, cols), F32),
            pltpu.VMEM((tokens, LANES), F32),
            pltpu.VMEM(((n_section + 1) * block, cols), F32),
        ],
        compiler_params=params,
        name="backward",
    )(where, *blocks, head, near, back1, back2, layers, gain)
    step_loss = jnp.sum(known[:, 6:9], axis=0) / tokens
    grads = jnp.sum(lax.all_gather(grads, "section"), axis=0)
    grads = jnp.sum(exchange(grads, "vocab"), axis=0)
    return (step_loss, grads[:3], grads[3])


def solution(mesh):
    placed = (P("section", None, "dp"), P(("section", "vocab"), "dp"), P(None, "dp"), P("dp"), P())
    return jax.shard_map(
        on_device,
        mesh=mesh,
        in_specs=placed,
        out_specs=(P(), P(None, "dp"), P("dp")),
        check_vma=False,
    )
```

time: 241 us -> 214 us (0.89)
  starting transfers between devices: 95 us -> 128 us
  matrix products: 25.4 us -> 5.68 us
  other arithmetic: 22.5 us -> 4.42 us
  waiting for transfers between devices: 61.9 us -> 48.5 us
  local copies, waits for them, and re-layouts: 21.6 us -> 8.5 us
  Pallas kernels: 0 us -> 7.32 us
    ppermute x0 -> x22, starting transfers between devices: none -> 84.1 us  [ring(): return lax.ppermute(a, ('dp', 'section'), pairs)]
    ppermute x21 -> x5, starting transfers between devices: 76.2 us -> 20.9 us  [permute(): lax.ppermute(a, axis, [(i, to(i)) for i in range(lax.axis_size(axis))])]
    ppermute x21 -> x5, waiting for transfers between devices: 43.3 us -> 11.3 us  [permute(): lax.ppermute(a, axis, [(i, to(i)) for i in range(lax.axis_size(axis))])]
    dot_general x8 -> x0, matrix products: 20.2 us -> none  [on_device(): lax.dot_general(arrived[:, :vocab], head, (((1,), (0,)), ((), ())), prefe...]
    ppermute x0 -> x22, waiting for transfers between devices: none -> 18.2 us  [ring(): return lax.ppermute(a, ('dp', 'section'), pairs)]
    slice x51 -> x5, local copies, waits for them, and re-layouts: 13.5 us -> 0.5 us  [the longest x1 0.42 us: term(): rest[at:at + size]]
    concatenate x18 -> x2, other arithmetic: 8.37 us -> 0.04 us  [term(): return jnp.concatenate([made, extra[at:at + size]], axis=1)]
    pallas_call x0 -> x3, Pallas kernels: none -> 7.32 us  [the longest x1 4.36 us: on_device(): pl.pallas_call(functools.partial(backward, n_z, block, shards), out_shape...]
  transfers between devices with their start and end apart: 23 -> 29, of which waited for: 13 -> 20; matrix products, arithmetic and copies ran while one was open for 14% -> 2% of each run, Pallas kernels for 0% -> 1%
where the time goes in v4:
time: 214 us; the launch traced here: 213 us
  starting transfers between devices  128 us (60%)
  waiting for transfers between devices  48.5 us (23%)
  blocking collectives  9.89 us (5%)
  local copies, waits for them, and re-layouts  8.5 us (4%)
  Pallas kernels  7.32 us (3%)
  matrix products  5.68 us (3%)
  other arithmetic  4.42 us (2%)
    ppermute x22, starting transfers between devices, ring(): return lax.ppermute(a, ('dp', 'section'), pairs)  84.1 us
    all_to_all x2, starting transfers between devices, exchange(): return lax.all_to_all(jnp.broadcast_to(a[None], (n,) + a.shape), axis, 0, 0)  22.6 us
    ppermute x5, starting transfers between devices, permute(): lax.ppermute(a, axis, [(i, to(i)) for i in range(lax.axis_size(axis))])  20.9 us
    all_to_all x2, waiting for transfers between devices, exchange(): return lax.all_to_all(jnp.broadcast_to(a[None], (n,) + a.shape), axis, 0, 0)  18.9 us
    ppermute x22, waiting for transfers between devices, ring(): return lax.ppermute(a, ('dp', 'section'), pairs)  18.2 us
    ppermute x5, waiting for transfers between devices, permute(): lax.ppermute(a, axis, [(i, to(i)) for i in range(lax.axis_size(axis))])  11.3 us
    all_gather x1, blocking collectives, on_device(): grads = jnp.sum(lax.all_gather(grads, 'section'), axis=0)  9.89 us
    dot_general x2, matrix products, product(): return lax.dot_general(a, head, CONTRACT, preferred_element_type=F32)  5.68 us
  transfers between devices with their start and end apart: 29, of which 20 were waited for; matrix products, arithmetic and copies ran while one was open for 2% of the time, Pallas kernels for 1%

profile of v4, /device:TPU:1, one launch (start us, length us, event | category | flops | bytes accessed | tf_op | source)
XLA Modules:
  0.0 213.2 jit_solution(5973571057539496164)
XLA Ops:
  0.6 6.0 %collective-permute-start.2 = (bf16[128,1024]{1,0:T(8,128)(2,1)}, bf16[128,1024]{1,0:T(8,128)(2,1)S(1)}, u32[]{:S(2)}, u32[]{:S(2)}) collective-permute-start(bf16[128,1024]{1,0:T(8,128)(2,1)} %bitcast.63), channel_id=1, source_target_pairs={{0,24},{8,16},{16,8},{24,0},{1,25},{9,17},{17,9},{25,1},{2,26},{10... | collective-permute-start | bytes 786440 | tf_op jit(solution)/shard_map/ppermute | solution.py:26
  6.7 7.5 %collective-permute-start.1 = (bf16[128,1024]{1,0:T(8,128)(2,1)}, bf16[128,1024]{1,0:T(8,128)(2,1)S(1)}, u32[]{:S(2)}, u32[]{:S(2)}) collective-permute-start(bf16[128,1024]{1,0:T(8,128)(2,1)} %bitcast.64), channel_id=1, source_target_pairs={{0,16},{8,24},{16,0},{24,8},{1,17},{9,25},{17,1},{25,9},{2,18},{10... | collective-permute-start | bytes 786440 | tf_op jit(solution)/shard_map/ppermute | solution.py:26
  18.1 3.8 %collective-permute-done.1.refs_2_ = bf16[128,1024]{1,0:T(8,128)(2,1)S(1)} collective-permute-done((bf16[128,1024]{1,0:T(8,128)(2,1)}, bf16[128,1024]{1,0:T(8,128)(2,1)S(1)}, u32[]{:S(2)}, u32[]{:S(2)}) %collective-permute-start.1) | collective-permute-done | bytes 262176 | tf_op jit(solution)/shard_map/ppermute | solution.py:26
  25.1 3.6 %fusion.11 = f32[64,2048]{1,0:T(8,128)S(1)} fusion(bf16[2048,1024]{1,0:T(8,128)(2,1)} %refs_9_.1, bf16[512,1024]{1,0:T(8,128)(2,1)S(1)} %get-tuple-element.24), kind=kOutput, calls=%fused_computation.36 | convolution fusion | flops 268435456 | bytes 4849664 | tf_op jit(solution)/shard_map/dot_general | solution.py:276
  30.9 8.3 %collective-permute-start.10 = (f32[32,2176]{1,0:T(8,128)S(1)}, f32[32,2176]{1,0:T(8,128)S(1)}, u32[]{:S(2)}, u32[]{:S(2)}) collective-permute-start(f32[32,2176]{1,0:T(8,128)S(1)} %pad_maximum_fusion.1), channel_id=1, source_target_pairs={{0,64},{8,456},{16,80},{24,472},{32,96},{40,488},{48,112},{56,504}... | collective-permute-start | bytes 835592 | tf_op jit(solution)/shard_map/ppermute | solution.py:36
  42.7 5.0 %collective-permute-start.11 = (f32[32,2176]{1,0:T(8,128)S(1)}, f32[32,2176]{1,0:T(8,128)S(1)}, u32[]{:S(2)}, u32[]{:S(2)}) collective-permute-start(f32[32,2176]{1,0:T(8,128)S(1)} %maximum_add_fusion.13), channel_id=1, source_target_pairs={{0,64},{8,456},{16,80},{24,472},{32,96},{40,488},{48,112},{56,504}... | collective-permute-start | bytes 835592 | tf_op jit(solution)/shard_map/ppermute | solution.py:36
  47.7 2.9 %collective-permute-start.4 = (f32[32,2176]{1,0:T(8,128)S(1)}, f32[32,2176]{1,0:T(8,128)S(1)}, u32[]{:S(2)}, u32[]{:S(2)}) collective-permute-start(f32[32,2176]{1,0:T(8,128)S(1)} %maximum_add_fusion.6), channel_id=1, source_target_pairs={{0,64},{8,456},{16,80},{24,472},{32,96},{40,488},{48,112},{56,504}... | collective-permute-start | bytes 835592 | tf_op jit(solution)/shard_map/ppermute | solution.py:36
  51.2 5.0 %collective-permute-start.12 = (f32[32,2176]{1,0:T(8,128)S(1)}, f32[32,2176]{1,0:T(8,128)S(1)}, u32[]{:S(2)}, u32[]{:S(2)}) collective-permute-start(f32[32,2176]{1,0:T(8,128)S(1)} %maximum_add_fusion.12), channel_id=1, source_target_pairs={{0,64},{8,456},{16,80},{24,472},{32,96},{40,488},{48,112},{56,504}... | collective-permute-start | bytes 835592 | tf_op jit(solution)/shard_map/ppermute | solution.py:36
  56.3 2.9 %collective-permute-start.5 = (f32[32,2176]{1,0:T(8,128)S(1)}, f32[32,2176]{1,0:T(8,128)S(1)}, u32[]{:S(2)}, u32[]{:S(2)}) collective-permute-start(f32[32,2176]{1,0:T(8,128)S(1)} %maximum_add_fusion.5), channel_id=1, source_target_pairs={{0,64},{8,456},{16,80},{24,472},{32,96},{40,488},{48,112},{56,504}... | collective-permute-start | bytes 835592 | tf_op jit(solution)/shard_map/ppermute | solution.py:36
  59.7 5.0 %collective-permute-start.13 = (f32[32,2176]{1,0:T(8,128)S(1)}, f32[32,2176]{1,0:T(8,128)S(1)}, u32[]{:S(2)}, u32[]{:S(2)}) collective-permute-start(f32[32,2176]{1,0:T(8,128)S(1)} %maximum_add_fusion.11), channel_id=1, source_target_pairs={{0,64},{8,456},{16,80},{24,472},{32,96},{40,488},{48,112},{56,504}... | collective-permute-start | bytes 835592 | tf_op jit(solution)/shard_map/ppermute | solution.py:36
  64.8 2.9 %collective-permute-start.6 = (f32[32,2176]{1,0:T(8,128)S(1)}, f32[32,2176]{1,0:T(8,128)S(1)}, u32[]{:S(2)}, u32[]{:S(2)}) collective-permute-start(f32[32,2176]{1,0:T(8,128)S(1)} %maximum_add_fusion.4), channel_id=1, source_target_pairs={{0,64},{8,456},{16,80},{24,472},{32,96},{40,488},{48,112},{56,504}... | collective-permute-start | bytes 835592 | tf_op jit(solution)/shard_map/ppermute | solution.py:36
  68.3 5.0 %collective-permute-start.14 = (f32[32,2176]{1,0:T(8,128)S(1)}, f32[32,2176]{1,0:T(8,128)S(1)}, u32[]{:S(2)}, u32[]{:S(2)}) collective-permute-start(f32[32,2176]{1,0:T(8,128)S(1)} %maximum_add_fusion.10), channel_id=1, source_target_pairs={{0,64},{8,456},{16,80},{24,472},{32,96},{40,488},{48,112},{56,504}... | collective-permute-start | bytes 835592 | tf_op jit(solution)/shard_map/ppermute | solution.py:36
  73.3 2.9 %collective-permute-start.7 = (f32[32,2176]{1,0:T(8,128)S(1)}, f32[32,2176]{1,0:T(8,128)S(1)}, u32[]{:S(2)}, u32[]{:S(2)}) collective-permute-start(f32[32,2176]{1,0:T(8,128)S(1)} %maximum_add_fusion.3), channel_id=1, source_target_pairs={{0,64},{8,456},{16,80},{24,472},{32,96},{40,488},{48,112},{56,504}... | collective-permute-start | bytes 835592 | tf_op jit(solution)/shard_map/ppermute | solution.py:36
  76.8 5.0 %collective-permute-start.15 = (f32[32,2176]{1,0:T(8,128)S(1)}, f32[32,2176]{1,0:T(8,128)S(1)}, u32[]{:S(2)}, u32[]{:S(2)}) collective-permute-start(f32[32,2176]{1,0:T(8,128)S(1)} %maximum_add_fusion.9), channel_id=1, source_target_pairs={{0,64},{8,456},{16,80},{24,472},{32,96},{40,488},{48,112},{56,504}... | collective-permute-start | bytes 835592 | tf_op jit(solution)/shard_map/ppermute | solution.py:36
  81.9 2.9 %collective-permute-start.8 = (f32[32,2176]{1,0:T(8,128)S(1)}, f32[32,2176]{1,0:T(8,128)S(1)}, u32[]{:S(2)}, u32[]{:S(2)}) collective-permute-start(f32[32,2176]{1,0:T(8,128)S(1)} %maximum_add_fusion.2), channel_id=1, source_target_pairs={{0,64},{8,456},{16,80},{24,472},{32,96},{40,488},{48,112},{56,504}... | collective-permute-start | bytes 835592 | tf_op jit(solution)/shard_map/ppermute | solution.py:36
  85.3 5.2 %collective-permute-start.16 = (f32[32,2176]{1,0:T(8,128)S(1)}, f32[32,2176]{1,0:T(8,128)S(1)}, u32[]{:S(2)}, u32[]{:S(2)}) collective-permute-start(f32[32,2176]{1,0:T(8,128)S(1)} %maximum_add_fusion.8), channel_id=1, source_target_pairs={{0,64},{8,456},{16,80},{24,472},{32,96},{40,488},{48,112},{56,504}... | collective-permute-start | bytes 835592 | tf_op jit(solution)/shard_map/ppermute | solution.py:36
  94.0 3.2 %collective-permute-start.17 = (f32[32,2176]{1,0:T(8,128)S(1)}, f32[32,2176]{1,0:T(8,128)S(1)}, u32[]{:S(2)}, u32[]{:S(2)}) collective-permute-start(f32[32,2176]{1,0:T(8,128)S(1)} %maximum_add_fusion.7), channel_id=1, source_target_pairs={{0,32},{32,0},{64,96},{96,64},{128,160},{160,128},{192,224},{224,1... | collective-permute-start | bytes 835592 | tf_op jit(solution)/shard_map/ppermute | solution.py:26
  97.8 3.7 %collective-permute-done.17 = f32[32,2176]{1,0:T(8,128)S(1)} collective-permute-done((f32[32,2176]{1,0:T(8,128)S(1)}, f32[32,2176]{1,0:T(8,128)S(1)}, u32[]{:S(2)}, u32[]{:S(2)}) %collective-permute-start.17) | collective-permute-done | bytes 278560 | tf_op jit(solution)/shard_map/ppermute | solution.py:26
  103.6 19.3 %all-to-all-start = ((f32[32,14,8]{1,2,0:T(8,128)}), f32[32,14,8]{1,2,0:T(8,128)S(1)}, u32[]{:S(2)}, u32[]{:S(2)}) async-start(f32[32,14,8]{1,2,0:T(8,128)} %broadcast_in_dim.19), calls=%async_computation | async-start | bytes 262144 | tf_op jit(solution)/shard_map/all_to_all | solution.py:22
  123.0 11.0 %all-to-all-done = f32[32,14,8]{1,2,0:T(8,128)S(1)} async-done(((f32[32,14,8]{1,2,0:T(8,128)}), f32[32,14,8]{1,2,0:T(8,128)S(1)}, u32[]{:S(2)}, u32[]{:S(2)}) %all-to-all-start) | async-done | bytes 14368 | tf_op jit(solution)/shard_map/all_to_all | solution.py:22
  138.5 3.8 %collective-permute-done.18 = bf16[24,2176]{1,0:T(8,128)(2,1)S(1)} collective-permute-done((bf16[24,2176]{1,0:T(8,128)(2,1)S(1)}, bf16[24,2176]{1,0:T(8,128)(2,1)S(1)}, u32[]{:S(2)}, u32[]{:S(2)}) %collective-permute-start.18) | collective-permute-done | bytes 104480 | tf_op jit(solution)/shard_map/ppermute | solution.py:26
  144.2 4.6 %collective-permute-start.19 = (bf16[48,2176]{1,0:T(8,128)(2,1)S(1)}, bf16[48,2176]{1,0:T(8,128)(2,1)S(1)}, u32[]{:S(2)}, u32[]{:S(2)}) collective-permute-start(bf16[48,2176]{1,0:T(8,128)(2,1)S(1)} %constant_dynamic-update-slice_fusion.6.refs_0_), channel_id=1, source_target_pairs={{0,64},{8,456},{16,80},{24,472},{32,96},{40,488},{48,112},{56,504}... | collective-permute-start | bytes 626696 | tf_op jit(solution)/shard_map/ppermute | solution.py:36
  150.0 3.0 %collective-permute-done.19.refs_8_ = bf16[48,2176]{1,0:T(8,128)(2,1)S(1)} collective-permute-done((bf16[48,2176]{1,0:T(8,128)(2,1)S(1)}, bf16[48,2176]{1,0:T(8,128)(2,1)S(1)}, u32[]{:S(2)}, u32[]{:S(2)}) %collective-permute-start.19) | collective-permute-done | bytes 208928 | tf_op jit(solution)/shard_map/ppermute | solution.py:36
  154.9 4.6 %collective-permute-start.21 = (bf16[48,2176]{1,0:T(8,128)(2,1)S(1)}, bf16[48,2176]{1,0:T(8,128)(2,1)S(1)}, u32[]{:S(2)}, u32[]{:S(2)}) collective-permute-start(bf16[48,2176]{1,0:T(8,128)(2,1)S(1)} %collective-permute-done.19.refs_8_), channel_id=1, source_target_pairs={{0,64},{8,456},{16,80},{24,472},{32,96},{40,488},{48,112},{56,504}... | collective-permute-start | bytes 626696 | tf_op jit(solution)/shard_map/ppermute | solution.py:36
  160.7 3.1 %collective-permute-done.21.refs_7_ = bf16[48,2176]{1,0:T(8,128)(2,1)S(1)} collective-permute-done((bf16[48,2176]{1,0:T(8,128)(2,1)S(1)}, bf16[48,2176]{1,0:T(8,128)(2,1)S(1)}, u32[]{:S(2)}, u32[]{:S(2)}) %collective-permute-start.21) | collective-permute-done | bytes 208928 | tf_op jit(solution)/shard_map/ppermute | solution.py:36
  166.2 4.1 %collective-permute-start.23 = (bf16[48,2176]{1,0:T(8,128)(2,1)S(1)}, bf16[48,2176]{1,0:T(8,128)(2,1)S(1)}, u32[]{:S(2)}, u32[]{:S(2)}) collective-permute-start(bf16[48,2176]{1,0:T(8,128)(2,1)S(1)} %collective-permute-done.21.refs_7_), channel_id=1, source_target_pairs={{0,64},{8,456},{16,80},{24,472},{32,96},{40,488},{48,112},{56,504}... | collective-permute-start | bytes 626696 | tf_op jit(solution)/shard_map/ppermute | solution.py:36
  171.6 3.1 %collective-permute-done.23.refs_6_ = bf16[48,2176]{1,0:T(8,128)(2,1)S(1)} collective-permute-done((bf16[48,2176]{1,0:T(8,128)(2,1)S(1)}, bf16[48,2176]{1,0:T(8,128)(2,1)S(1)}, u32[]{:S(2)}, u32[]{:S(2)}) %collective-permute-start.23) | collective-permute-done | bytes 208928 | tf_op jit(solution)/shard_map/ppermute | solution.py:36
  177.1 4.1 %collective-permute-start.25 = (bf16[48,1024]{1,0:T(8,128)(2,1)S(1)}, bf16[48,1024]{1,0:T(8,128)(2,1)S(1)}, u32[]{:S(2)}, u32[]{:S(2)}) collective-permute-start(bf16[48,1024]{1,0:T(8,128)(2,1)S(1)} %slice.269), channel_id=1, source_target_pairs={{0,64},{8,456},{16,80},{24,472},{32,96},{40,488},{48,112},{56,504}... | collective-permute-start | bytes 294920 | tf_op jit(solution)/shard_map/ppermute | solution.py:36
  185.7 4.4 %backward.1 = (f32[4,1024]{1,0:T(4,128)S(1)}, f32[128,128]{1,0:T(8,128)S(1)}) custom-call(s32[4]{0:T(128)S(1)} %pad_add_fusion.place_ref, bf16[48,2176]{1,0:T(8,128)(2,1)S(1)} %constant_dynamic-update-slice_fusion.6.refs_0_, bf16[48,2176]{1,0:T(8,128)(2,1)S(1)} %collective-permute-done.20.refs_1_, bf16[48,2176]{1,0:T(8,128)(2,1)S(1)} %collective-permute-done.22.refs_2_, ...), custom_call_target="tpu_custom_call" | custom-call | tf_op jit(solution)/shard_map/backward/pallas_call | solution.py:366
  190.1 9.9 %all-gather.1 = f32[4,4,1024]{2,1,0:T(4,128)S(1)} all-gather(f32[1,4,1024]{2,1,0:T(4,128)S(1)} %bitcast.71), channel_id=2, replica_groups=mesh['dp'=16,'section'=4,'vocab'=8] {'section'}, dimensions={0}, use_global_device_ids=true | all-gather | bytes 81920 | tf_op jit(solution)/shard_map/all_gather | solution.py:384
  200.6 3.4 %all-to-all-start.1 = ((f32[8,4,1024]{2,1,0:T(4,128)}), f32[8,4,1024]{2,1,0:T(4,128)S(1)}, u32[]{:S(2)}, u32[]{:S(2)}) async-start(f32[8,4,1024]{2,1,0:T(4,128)} %broadcast_in_dim.20), calls=%async_computation.1 | async-start | bytes 262144 | tf_op jit(solution)/shard_map/all_to_all | solution.py:22
  204.6 7.9 %all-to-all-done.1 = f32[8,4,1024]{2,1,0:T(4,128)S(1)} async-done(((f32[8,4,1024]{2,1,0:T(4,128)}), f32[8,4,1024]{2,1,0:T(4,128)S(1)}, u32[]{:S(2)}, u32[]{:S(2)}) %all-to-all-start.1) | async-done | bytes 131104 | tf_op jit(solution)/shard_map/all_to_all | solution.py:22
  (118 shorter events, 44.9 us)
Async XLA Ops:
  0.6 17.5 %collective-permute-start.2 = (bf16[128,1024]{1,0:T(8,128)(2,1)}, bf16[128,1024]{1,0:T(8,128)(2,1)S(1)}, u32[]{:S(2)}, u32[]{:S(2)}) collective-permute-start(bf16[128,1024]{1,0:T(8,128)(2,1)} %bitcast.63), channel_id=1, source_target_pairs={{0,24},{8,16},{16,8},{24,0},{1,25},{9,17},{17,9},{25,1},{2,26},{10... | collective-permute-start | bytes 786440 | tf_op jit(solution)/shard_map/ppermute | solution.py:26
  6.7 15.2 %collective-permute-start.1 = (bf16[128,1024]{1,0:T(8,128)(2,1)}, bf16[128,1024]{1,0:T(8,128)(2,1)S(1)}, u32[]{:S(2)}, u32[]{:S(2)}) collective-permute-start(bf16[128,1024]{1,0:T(8,128)(2,1)} %bitcast.64), channel_id=1, source_target_pairs={{0,16},{8,24},{16,0},{24,8},{1,17},{9,25},{17,1},{25,9},{2,18},{10... | collective-permute-start | bytes 786440 | tf_op jit(solution)/shard_map/ppermute | solution.py:26
  14.2 7.7 %collective-permute-start = (bf16[128,1024]{1,0:T(8,128)(2,1)}, bf16[128,1024]{1,0:T(8,128)(2,1)S(1)}, u32[]{:S(2)}, u32[]{:S(2)}) collective-permute-start(bf16[128,1024]{1,0:T(8,128)(2,1)} %bitcast.65), channel_id=1, source_target_pairs={{0,8},{8,0},{16,24},{24,16},{1,9},{9,1},{17,25},{25,17},{2,10},{10... | collective-permute-start | bytes 786440 | tf_op jit(solution)/shard_map/ppermute | solution.py:26
  17.1 11.5 %copy-start = (bf16[2048,1024]{1,0:T(8,128)(2,1)S(1)}, bf16[2048,1024]{1,0:T(8,128)(2,1)}, u32[]{:S(2)}) copy-start(bf16[2048,1024]{1,0:T(8,128)(2,1)} %refs_9_.1) | copy-start | bytes 12582916
  30.9 11.7 %collective-permute-start.10 = (f32[32,2176]{1,0:T(8,128)S(1)}, f32[32,2176]{1,0:T(8,128)S(1)}, u32[]{:S(2)}, u32[]{:S(2)}) collective-permute-start(f32[32,2176]{1,0:T(8,128)S(1)} %pad_maximum_fusion.1), channel_id=1, source_target_pairs={{0,64},{8,456},{16,80},{24,472},{32,96},{40,488},{48,112},{56,504}... | collective-permute-start | bytes 835592 | tf_op jit(solution)/shard_map/ppermute | solution.py:36
  39.2 8.5 %collective-permute-start.3 = (f32[32,2176]{1,0:T(8,128)S(1)}, f32[32,2176]{1,0:T(8,128)S(1)}, u32[]{:S(2)}, u32[]{:S(2)}) collective-permute-start(f32[32,2176]{1,0:T(8,128)S(1)} %pad_maximum_fusion), channel_id=1, source_target_pairs={{0,64},{8,456},{16,80},{24,472},{32,96},{40,488},{48,112},{56,504}... | collective-permute-start | bytes 835592 | tf_op jit(solution)/shard_map/ppermute | solution.py:36
  42.7 8.5 %collective-permute-start.11 = (f32[32,2176]{1,0:T(8,128)S(1)}, f32[32,2176]{1,0:T(8,128)S(1)}, u32[]{:S(2)}, u32[]{:S(2)}) collective-permute-start(f32[32,2176]{1,0:T(8,128)S(1)} %maximum_add_fusion.13), channel_id=1, source_target_pairs={{0,64},{8,456},{16,80},{24,472},{32,96},{40,488},{48,112},{56,504}... | collective-permute-start | bytes 835592 | tf_op jit(solution)/shard_map/ppermute | solution.py:36
  47.7 8.5 %collective-permute-start.4 = (f32[32,2176]{1,0:T(8,128)S(1)}, f32[32,2176]{1,0:T(8,128)S(1)}, u32[]{:S(2)}, u32[]{:S(2)}) collective-permute-start(f32[32,2176]{1,0:T(8,128)S(1)} %maximum_add_fusion.6), channel_id=1, source_target_pairs={{0,64},{8,456},{16,80},{24,472},{32,96},{40,488},{48,112},{56,504}... | collective-permute-start | bytes 835592 | tf_op jit(solution)/shard_map/ppermute | solution.py:36
  51.2 8.5 %collective-permute-start.12 = (f32[32,2176]{1,0:T(8,128)S(1)}, f32[32,2176]{1,0:T(8,128)S(1)}, u32[]{:S(2)}, u32[]{:S(2)}) collective-permute-start(f32[32,2176]{1,0:T(8,128)S(1)} %maximum_add_fusion.12), channel_id=1, source_target_pairs={{0,64},{8,456},{16,80},{24,472},{32,96},{40,488},{48,112},{56,504}... | collective-permute-start | bytes 835592 | tf_op jit(solution)/shard_map/ppermute | solution.py:36
  56.3 8.5 %collective-permute-start.5 = (f32[32,2176]{1,0:T(8,128)S(1)}, f32[32,2176]{1,0:T(8,128)S(1)}, u32[]{:S(2)}, u32[]{:S(2)}) collective-permute-start(f32[32,2176]{1,0:T(8,128)S(1)} %maximum_add_fusion.5), channel_id=1, source_target_pairs={{0,64},{8,456},{16,80},{24,472},{32,96},{40,488},{48,112},{56,504}... | collective-permute-start | bytes 835592 | tf_op jit(solution)/shard_map/ppermute | solution.py:36
  59.7 8.5 %collective-permute-start.13 = (f32[32,2176]{1,0:T(8,128)S(1)}, f32[32,2176]{1,0:T(8,128)S(1)}, u32[]{:S(2)}, u32[]{:S(2)}) collective-permute-start(f32[32,2176]{1,0:T(8,128)S(1)} %maximum_add_fusion.11), channel_id=1, source_target_pairs={{0,64},{8,456},{16,80},{24,472},{32,96},{40,488},{48,112},{56,504}... | collective-permute-start | bytes 835592 | tf_op jit(solution)/shard_map/ppermute | solution.py:36
  64.8 8.5 %collective-permute-start.6 = (f32[32,2176]{1,0:T(8,128)S(1)}, f32[32,2176]{1,0:T(8,128)S(1)}, u32[]{:S(2)}, u32[]{:S(2)}) collective-permute-start(f32[32,2176]{1,0:T(8,128)S(1)} %maximum_add_fusion.4), channel_id=1, source_target_pairs={{0,64},{8,456},{16,80},{24,472},{32,96},{40,488},{48,112},{56,504}... | collective-permute-start | bytes 835592 | tf_op jit(solution)/shard_map/ppermute | solution.py:36
  68.3 8.5 %collective-permute-start.14 = (f32[32,2176]{1,0:T(8,128)S(1)}, f32[32,2176]{1,0:T(8,128)S(1)}, u32[]{:S(2)}, u32[]{:S(2)}) collective-permute-start(f32[32,2176]{1,0:T(8,128)S(1)} %maximum_add_fusion.10), channel_id=1, source_target_pairs={{0,64},{8,456},{16,80},{24,472},{32,96},{40,488},{48,112},{56,504}... | collective-permute-start | bytes 835592 | tf_op jit(solution)/shard_map/ppermute | solution.py:36
  73.3 8.5 %collective-permute-start.7 = (f32[32,2176]{1,0:T(8,128)S(1)}, f32[32,2176]{1,0:T(8,128)S(1)}, u32[]{:S(2)}, u32[]{:S(2)}) collective-permute-start(f32[32,2176]{1,0:T(8,128)S(1)} %maximum_add_fusion.3), channel_id=1, source_target_pairs={{0,64},{8,456},{16,80},{24,472},{32,96},{40,488},{48,112},{56,504}... | collective-permute-start | bytes 835592 | tf_op jit(solution)/shard_map/ppermute | solution.py:36
  76.8 8.5 %collective-permute-start.15 = (f32[32,2176]{1,0:T(8,128)S(1)}, f32[32,2176]{1,0:T(8,128)S(1)}, u32[]{:S(2)}, u32[]{:S(2)}) collective-permute-start(f32[32,2176]{1,0:T(8,128)S(1)} %maximum_add_fusion.9), channel_id=1, source_target_pairs={{0,64},{8,456},{16,80},{24,472},{32,96},{40,488},{48,112},{56,504}... | collective-permute-start | bytes 835592 | tf_op jit(solution)/shard_map/ppermute | solution.py:36
  81.9 8.6 %collective-permute-start.8 = (f32[32,2176]{1,0:T(8,128)S(1)}, f32[32,2176]{1,0:T(8,128)S(1)}, u32[]{:S(2)}, u32[]{:S(2)}) collective-permute-start(f32[32,2176]{1,0:T(8,128)S(1)} %maximum_add_fusion.2), channel_id=1, source_target_pairs={{0,64},{8,456},{16,80},{24,472},{32,96},{40,488},{48,112},{56,504}... | collective-permute-start | bytes 835592 | tf_op jit(solution)/shard_map/ppermute | solution.py:36
  85.3 95.9 %copy-start.3 = (bf16[1,128,1024]{2,1,0:T(8,128)(2,1)S(1)}, bf16[1,128,1024]{2,1,0:T(8,128)(2,1)}, u32[]{:S(2)}) copy-start(bf16[1,128,1024]{2,1,0:T(8,128)(2,1)} %param.5) | copy-start | bytes 786436
  85.3 95.9 %copy-start.5 = (f32[1024]{0:T(1024)S(1)}, f32[1024]{0:T(1024)}, u32[]{:S(2)}) copy-start(f32[1024]{0:T(1024)} %param.8) | copy-start | bytes 12292
  85.3 8.6 %collective-permute-start.16 = (f32[32,2176]{1,0:T(8,128)S(1)}, f32[32,2176]{1,0:T(8,128)S(1)}, u32[]{:S(2)}, u32[]{:S(2)}) collective-permute-start(f32[32,2176]{1,0:T(8,128)S(1)} %maximum_add_fusion.8), channel_id=1, source_target_pairs={{0,64},{8,456},{16,80},{24,472},{32,96},{40,488},{48,112},{56,504}... | collective-permute-start | bytes 835592 | tf_op jit(solution)/shard_map/ppermute | solution.py:36
  90.6 7.3 %collective-permute-start.9 = (f32[32,2176]{1,0:T(8,128)S(1)}, f32[32,2176]{1,0:T(8,128)S(1)}, u32[]{:S(2)}, u32[]{:S(2)}) collective-permute-start(f32[32,2176]{1,0:T(8,128)S(1)} %maximum_add_fusion.1), channel_id=1, source_target_pairs={{0,64},{8,456},{16,80},{24,472},{32,96},{40,488},{48,112},{56,504}... | collective-permute-start | bytes 835592 | tf_op jit(solution)/shard_map/ppermute | solution.py:36
  94.0 7.6 %collective-permute-start.17 = (f32[32,2176]{1,0:T(8,128)S(1)}, f32[32,2176]{1,0:T(8,128)S(1)}, u32[]{:S(2)}, u32[]{:S(2)}) collective-permute-start(f32[32,2176]{1,0:T(8,128)S(1)} %maximum_add_fusion.7), channel_id=1, source_target_pairs={{0,32},{32,0},{64,96},{96,64},{128,160},{160,128},{192,224},{224,1... | collective-permute-start | bytes 835592 | tf_op jit(solution)/shard_map/ppermute | solution.py:26
  103.6 30.5 %all-to-all-start = ((f32[32,14,8]{1,2,0:T(8,128)}), f32[32,14,8]{1,2,0:T(8,128)S(1)}, u32[]{:S(2)}, u32[]{:S(2)}) async-start(f32[32,14,8]{1,2,0:T(8,128)} %broadcast_in_dim.19), calls=%async_computation | async-start | bytes 262144 | tf_op jit(solution)/shard_map/all_to_all | solution.py:22
  136.2 6.0 %collective-permute-start.18 = (bf16[24,2176]{1,0:T(8,128)(2,1)S(1)}, bf16[24,2176]{1,0:T(8,128)(2,1)S(1)}, u32[]{:S(2)}, u32[]{:S(2)}) collective-permute-start(bf16[24,2176]{1,0:T(8,128)(2,1)S(1)} %maximum_maximum_fusion), channel_id=1, source_target_pairs={{0,32},{32,0},{64,96},{96,64},{128,160},{160,128},{192,224},{224,1... | collective-permute-start | bytes 313352 | tf_op jit(solution)/shard_map/ppermute | solution.py:26
  142.3 7.8 %collective-permute-start.20 = (bf16[48,2176]{1,0:T(8,128)(2,1)S(1)}, bf16[48,2176]{1,0:T(8,128)(2,1)S(1)}, u32[]{:S(2)}, u32[]{:S(2)}) collective-permute-start(bf16[48,2176]{1,0:T(8,128)(2,1)S(1)} %constant_dynamic-update-slice_fusion.6.refs_0_), channel_id=1, source_target_pairs={{0,448},{8,72},{16,464},{24,88},{32,480},{40,104},{48,496},{56,120... | collective-permute-start | bytes 626696 | tf_op jit(solution)/shard_map/ppermute | solution.py:36
  144.2 8.8 %collective-permute-start.19 = (bf16[48,2176]{1,0:T(8,128)(2,1)S(1)}, bf16[48,2176]{1,0:T(8,128)(2,1)S(1)}, u32[]{:S(2)}, u32[]{:S(2)}) collective-permute-start(bf16[48,2176]{1,0:T(8,128)(2,1)S(1)} %constant_dynamic-update-slice_fusion.6.refs_0_), channel_id=1, source_target_pairs={{0,64},{8,456},{16,80},{24,472},{32,96},{40,488},{48,112},{56,504}... | collective-permute-start | bytes 626696 | tf_op jit(solution)/shard_map/ppermute | solution.py:36
  153.0 7.7 %collective-permute-start.22 = (bf16[48,2176]{1,0:T(8,128)(2,1)S(1)}, bf16[48,2176]{1,0:T(8,128)(2,1)S(1)}, u32[]{:S(2)}, u32[]{:S(2)}) collective-permute-start(bf16[48,2176]{1,0:T(8,128)(2,1)S(1)} %collective-permute-done.20.refs_1_), channel_id=1, source_target_pairs={{0,448},{8,72},{16,464},{24,88},{32,480},{40,104},{48,496},{56,120... | collective-permute-start | bytes 626696 | tf_op jit(solution)/shard_map/ppermute | solution.py:36
  154.9 8.9 %collective-permute-start.21 = (bf16[48,2176]{1,0:T(8,128)(2,1)S(1)}, bf16[48,2176]{1,0:T(8,128)(2,1)S(1)}, u32[]{:S(2)}, u32[]{:S(2)}) collective-permute-start(bf16[48,2176]{1,0:T(8,128)(2,1)S(1)} %collective-permute-done.19.refs_8_), channel_id=1, source_target_pairs={{0,64},{8,456},{16,80},{24,472},{32,96},{40,488},{48,112},{56,504}... | collective-permute-start | bytes 626696 | tf_op jit(solution)/shard_map/ppermute | solution.py:36
  163.8 7.7 %collective-permute-start.24 = (bf16[48,2176]{1,0:T(8,128)(2,1)S(1)}, bf16[48,2176]{1,0:T(8,128)(2,1)S(1)}, u32[]{:S(2)}, u32[]{:S(2)}) collective-permute-start(bf16[48,2176]{1,0:T(8,128)(2,1)S(1)} %collective-permute-done.22.refs_2_), channel_id=1, source_target_pairs={{0,448},{8,72},{16,464},{24,88},{32,480},{40,104},{48,496},{56,120... | collective-permute-start | bytes 626696 | tf_op jit(solution)/shard_map/ppermute | solution.py:36
  166.2 8.4 %collective-permute-start.23 = (bf16[48,2176]{1,0:T(8,128)(2,1)S(1)}, bf16[48,2176]{1,0:T(8,128)(2,1)S(1)}, u32[]{:S(2)}, u32[]{:S(2)}) collective-permute-start(bf16[48,2176]{1,0:T(8,128)(2,1)S(1)} %collective-permute-done.21.refs_7_), channel_id=1, source_target_pairs={{0,64},{8,456},{16,80},{24,472},{32,96},{40,488},{48,112},{56,504}... | collective-permute-start | bytes 626696 | tf_op jit(solution)/shard_map/ppermute | solution.py:36
  174.7 8.8 %collective-permute-start.26 = (bf16[48,1152]{1,0:T(8,128)(2,1)S(1)}, bf16[48,1152]{1,0:T(8,128)(2,1)S(1)}, u32[]{:S(2)}, u32[]{:S(2)}) collective-permute-start(bf16[48,1152]{1,0:T(8,128)(2,1)S(1)} %slice.270), channel_id=1, source_target_pairs={{0,448},{8,72},{16,464},{24,88},{32,480},{40,104},{48,496},{56,120... | collective-permute-start | bytes 331784 | tf_op jit(solution)/shard_map/ppermute | solution.py:36
  177.1 6.4 %collective-permute-start.25 = (bf16[48,1024]{1,0:T(8,128)(2,1)S(1)}, bf16[48,1024]{1,0:T(8,128)(2,1)S(1)}, u32[]{:S(2)}, u32[]{:S(2)}) collective-permute-start(bf16[48,1024]{1,0:T(8,128)(2,1)S(1)} %slice.269), channel_id=1, source_target_pairs={{0,64},{8,456},{16,80},{24,472},{32,96},{40,488},{48,112},{56,504}... | collective-permute-start | bytes 294920 | tf_op jit(solution)/shard_map/ppermute | solution.py:36
  200.6 11.9 %all-to-all-start.1 = ((f32[8,4,1024]{2,1,0:T(4,128)}), f32[8,4,1024]{2,1,0:T(4,128)S(1)}, u32[]{:S(2)}, u32[]{:S(2)}) async-start(f32[8,4,1024]{2,1,0:T(4,128)} %broadcast_in_dim.20), calls=%async_computation.1 | async-start | bytes 262144 | tf_op jit(solution)/shard_map/all_to_all | solution.py:22
  (4 other events, 4.4 us)

commit v5 on v4

--- a/solution.py
+++ b/solution.py
@@ -27,42 +27,38 @@
 
 
 def ring(a, steps):
-    n, m = lax.axis_size("dp"), lax.axis_size("section")
-    pairs = [
-        (i * m + j, (i + steps * PAIR * (1 - 2 * (j % 2))) % n * m + j)
-        for i in range(n)
-        for j in range(m)
-    ]
-    return lax.ppermute(a, ("dp", "section"), pairs)
+    n = lax.axis_size("dp")
+    return permute(a, "dp", lambda i: (i + steps * PAIR) % n)
 
 
 def swap(a):
     return permute(a, "dp", lambda i: i ^ 1)
 
 
-def both(below, above):
-    return lax.optimization_barrier((ring(below, 1), ring(above, -1)))
-
-
 def columns(a):
     return [a[:, i : i + 1] for i in range(a.shape[1])]
 
 
 def sum_over_dp(term, n_z):
-    totals = [term(n_z - 1, h) for h in range(PAIR)]
-    for i in range(n_z - 2, -1, -1):
-        for h in (1, 0):
-            totals[h] = term(i, h) + ring(totals[h], 1)
-    return totals[0] + swap(totals[1])
+    far = n_z // 2
+    ups, downs = [None, None], [None, None]
+    ups[0], downs[1] = ring(term(far, 0), 1), ring(term(far, 1), -1)
+    for hops in range(far - 1, 0, -1):
+        for h in range(PAIR):
+            for held, sign in ((ups, 1), (downs, -1)):
+                made = term(sign * hops % n_z, h)
+                held[h] = ring(made if held[h] is None else made + held[h], sign)
+    own, other = (term(0, h) + ups[h] + downs[h] for h in range(PAIR))
+    return own + swap(other)
 
 
 def gather_over_dp(block):
     own = jnp.concatenate([block, swap(block)], axis=0)
-    seven, one = both(own, own)
-    six, two = both(seven, one)
-    five, three = both(six, two)
+    seven, one = ring(own, 1), ring(own, -1)
+    six, two = ring(seven, 1), ring(one, -1)
+    five, three = ring(six, 1), ring(two, -1)
     cut = block.shape[1] // LANES // 2 * LANES
-    four = both(five[:, :cut], three[:, cut:])
+    four = ring(five[:, :cut], 1), ring(three[:, cut:], -1)
     return [own, one, two, three, *four, five, six, seven]
 
 
@@ -81,8 +77,8 @@
 
 
 def token_of(place_ref, i, h, n_z, block):
-    z, x, way = place_ref[1], place_ref[2], place_ref[3]
-    other = lax.rem(z + way * i + n_z, n_z)
+    z, x = place_ref[1], place_ref[2]
+    other = lax.rem(z + i, n_z)
     return pl.multiple_of((other * PAIR + (x ^ h)) * block, block)
 
 
@@ -249,8 +245,7 @@
     for j in range(1, n_section):
         sections.append(permute(own_rows, "section", lambda i, j=j: i ^ j))
     rows = sections
-    way = 1 - 2 * (section % 2)
-    where = jnp.stack([section, z, x, way]).astype(jnp.int32)
+    where = jnp.stack([section, z, x]).astype(jnp.int32)
     gains = jnp.concatenate([unite_gain, jnp.zeros_like(unite_gain[:1])], axis=0)
     gain = norm_gain[None]
     same = (segment_ids[1:] == segment_ids[:-1]).astype(F32)
@@ -276,13 +271,18 @@
         return lax.dot_general(a, head, CONTRACT, preferred_element_type=F32)
 
     size = 4 * block
-    split = (n_z - 1) * PAIR * size
-    far = product(stacked[split:])
-    rest = product(stacked[:split])
+    first = n_z // 2 * PAIR * size
+    last = first + PAIR * size
+    far = product(stacked[first:last])
+    rest = product(jnp.concatenate([stacked[:first], stacked[last:]], axis=0))
 
     def term(i, h):
         at = (i * PAIR + h) * size
-        made = far[at - split : at - split + size] if at >= split else rest[at : at + size]
+        if first <= at < last:
+            made = far[at - first : at - first + size]
+        else:
+            at_rest = at if at < first else at - PAIR * size
+            made = rest[at_rest : at_rest + size]
         return jnp.concatenate([made, extra[at : at + size]], axis=1)
 
     summed = sum_over_dp(term, n_z)
@@ -308,25 +308,17 @@
         [plain * i1, (plain + a2 * second) * i2, (plain + a3 * second + b3 * third) * i3]
     )
 
-    top = jnp.max(teacher, axis=-1)
-    e0 = jnp.exp(teacher - top[:, None])
-    peak = jnp.max(logits, axis=-1)
-    low = logits - peak[:, :, None]
+    top = jnp.max(teacher, axis=-1, keepdims=True)
+    e0 = jnp.exp(teacher - top)
+    peak = jnp.max(logits, axis=-1, keepdims=True)
+    low = logits - peak
     e = jnp.exp(low)
-    stats = jnp.concatenate(
-        [
-            top[None],
-            jnp.sum(e0, axis=-1)[None],
-            peak,
-            jnp.sum(e, axis=-1),
-            jnp.sum(e * low, axis=-1),
-            jnp.sum(e0[None] * low, axis=-1),
-        ],
-        axis=0,
-    )
-    every = exchange(stats, ("section", "vocab"))
-    tops, totals = every[:, 0], every[:, 1]
-    peaks, masses, firsts, crosses = (every[:, 2 + 3 * i : 5 + 3 * i] for i in range(4))
+    stats = [top, jnp.sum(e0, axis=-1, keepdims=True), *peak]
+    stats += [*jnp.sum(e, axis=-1, keepdims=True), *jnp.sum(e * low, axis=-1, keepdims=True)]
+    stats += [*jnp.sum(e0[None] * low, axis=-1, keepdims=True)]
+    every = exchange(jnp.concatenate(stats, axis=1), ("section", "vocab"))
+    tops, totals = every[:, :, :1], every[:, :, 1:2]
+    peaks, masses, firsts, crosses = (every[:, :, 2 + 3 * i : 5 + 3 * i] for i in range(4))
     all_top = jnp.max(tops, axis=0)
     scale0 = jnp.exp(tops - all_top)
     total = jnp.sum(scale0 * totals, axis=0)
@@ -335,20 +327,20 @@
     scale = jnp.exp(fall)
     mass = jnp.sum(scale * masses, axis=0)
     under_p = jnp.sum(scale * (firsts + fall * masses), axis=0) / mass
-    under_q = jnp.sum(scale0[:, None] * (crosses + fall * totals[:, None]), axis=0) / total
+    under_q = jnp.sum(scale0 * (crosses + fall * totals), axis=0) / total
     loss = jnp.log(mass) - under_q
     count = tokens * STEPS
     centre = (under_p - under_q) / (count * width)
 
-    f = jnp.exp(peak - all_peak) / (mass * count)
-    f0 = jnp.exp(top - all_top) / (total * count)
-    dlogits = (e * f[:, :, None] - (e0 * f0[:, None])[None]).astype(BF16)
-
-    known = jnp.stack([i1, i2, i3, a2, a3, b3], axis=1).reshape(block, 6)
-    known = jnp.concatenate([known, loss.T, centre.T], axis=1)
+    f0 = e0 * (jnp.exp(top - all_top) / (total * count))
+    dlogits = []
+    for k in range(STEPS):
+        f = jnp.exp(peak[k] - all_peak[:, k : k + 1]) / (mass[:, k : k + 1] * count)
+        dlogits.append((e[k] * f - f0).astype(BF16))
+    known = jnp.concatenate([i1, i2, i3, a2, a3, b3, loss, centre], axis=1)
     known = jnp.pad(known, ((0, 0), (0, LANES - known.shape[1])))
     message = jnp.concatenate(
-        [dlogits.reshape(STEPS * block, vocab), jnp.concatenate(parts(known), axis=0)], axis=1
+        [jnp.concatenate(dlogits, axis=0), jnp.concatenate(parts(known), axis=0)], axis=1
     )
     ordered = jax.ShapeDtypeStruct((tokens, cols), F32)
     tied = lax.optimization_barrier((message, *rows))

time: 214 us -> 203 us (0.949)
  blocking collectives: 9.89 us -> 40 us
  starting transfers between devices: 128 us -> 103 us
  waiting for transfers between devices: 48.5 us -> 31.8 us
    ppermute x22 -> x0, starting transfers between devices: 84.1 us -> none  [ring(): return lax.ppermute(a, ('dp', 'section'), pairs)]
    ppermute x5 -> x27, starting transfers between devices: 20.9 us -> 99.8 us  [permute(): lax.ppermute(a, axis, [(i, to(i)) for i in range(lax.axis_size(axis))])]
    all_to_all x0 -> x1, blocking collectives: none -> 27.6 us  [exchange(): return lax.all_to_all(jnp.broadcast_to(a[None], (n,) + a.shape), axis, 0, 0)]
    all_to_all x2 -> x1, starting transfers between devices: 22.6 us -> 3.37 us  [exchange(): return lax.all_to_all(jnp.broadcast_to(a[None], (n,) + a.shape), axis, 0, 0)]
    ppermute x22 -> x0, waiting for transfers between devices: 18.2 us -> none  [ring(): return lax.ppermute(a, ('dp', 'section'), pairs)]
    ppermute x5 -> x27, waiting for transfers between devices: 11.3 us -> 23.8 us  [permute(): lax.ppermute(a, axis, [(i, to(i)) for i in range(lax.axis_size(axis))])]
    all_to_all x2 -> x1, waiting for transfers between devices: 18.9 us -> 7.93 us  [exchange(): return lax.all_to_all(jnp.broadcast_to(a[None], (n,) + a.shape), axis, 0, 0)]
    all_gather x1, blocking collectives: 9.89 us -> 12.4 us  [on_device(): grads = jnp.sum(lax.all_gather(grads, 'section'), axis=0)]
  transfers between devices with their start and end apart: 29 -> 28, of which waited for: 20 -> 13; matrix products, arithmetic and copies ran while one was open for 2% -> 3% of each run, Pallas kernels for 1% -> 1%
where the time goes in v5:
time: 203 us; the launch traced here: 201 us
  starting transfers between devices  103 us (51%)
  blocking collectives  40 us (20%)
  waiting for transfers between devices  31.8 us (16%)
  local copies, waits for them, and re-layouts  7.88 us (4%)
  Pallas kernels  7.33 us (4%)
  matrix products  5.83 us (3%)
  other arithmetic  4.34 us (2%)
    ppermute x27, starting transfers between devices, permute(): lax.ppermute(a, axis, [(i, to(i)) for i in range(lax.axis_size(axis))])  99.8 us
    all_to_all x1, blocking collectives, exchange(): return lax.all_to_all(jnp.broadcast_to(a[None], (n,) + a.shape), axis, 0, 0)  27.6 us
    ppermute x27, waiting for transfers between devices, permute(): lax.ppermute(a, axis, [(i, to(i)) for i in range(lax.axis_size(axis))])  23.8 us
    all_gather x1, blocking collectives, on_device(): grads = jnp.sum(lax.all_gather(grads, 'section'), axis=0)  12.4 us
    all_to_all x1, waiting for transfers between devices, exchange(): return lax.all_to_all(jnp.broadcast_to(a[None], (n,) + a.shape), axis, 0, 0)  7.93 us
    dot_general x2, matrix products, product(): return lax.dot_general(a, head, CONTRACT, preferred_element_type=F32)  5.83 us
    unnamed x22, local copies, waits for them, and re-layouts  4.72 us
    pallas_call x1, Pallas kernels, on_device(): pl.pallas_call(functools.partial(backward, n_z, block, shards), out_shape...  4.38 us
  transfers between devices with their start and end apart: 28, of which 13 were waited for; matrix products, arithmetic and copies ran while one was open for 3% of the time, Pallas kernels for 1%

profile of v5, /device:TPU:1, one launch (start us, length us, event | category | flops | bytes accessed | tf_op | source)
XLA Modules:
  0.0 201.5 jit_solution(15447584609228920332)
XLA Ops:
  0.6 6.0 %collective-permute-start.2 = (bf16[128,1024]{1,0:T(8,128)(2,1)}, bf16[128,1024]{1,0:T(8,128)(2,1)S(1)}, u32[]{:S(2)}, u32[]{:S(2)}) collective-permute-start(bf16[128,1024]{1,0:T(8,128)(2,1)} %bitcast.83), channel_id=1, source_target_pairs={{0,24},{8,16},{16,8},{24,0},{1,25},{9,17},{17,9},{25,1},{2,26},{10... | collective-permute-start | bytes 786440 | tf_op jit(solution)/shard_map/ppermute | solution.py:26
  6.7 7.5 %collective-permute-start.1 = (bf16[128,1024]{1,0:T(8,128)(2,1)}, bf16[128,1024]{1,0:T(8,128)(2,1)S(1)}, u32[]{:S(2)}, u32[]{:S(2)}) collective-permute-start(bf16[128,1024]{1,0:T(8,128)(2,1)} %bitcast.84), channel_id=1, source_target_pairs={{0,16},{8,24},{16,0},{24,8},{1,17},{9,25},{17,1},{25,9},{2,18},{10... | collective-permute-start | bytes 786440 | tf_op jit(solution)/shard_map/ppermute | solution.py:26
  14.2 1.9 collective-permute-start
  17.9 4.0 %collective-permute-done.1.refs_2_ = bf16[128,1024]{1,0:T(8,128)(2,1)S(1)} collective-permute-done((bf16[128,1024]{1,0:T(8,128)(2,1)}, bf16[128,1024]{1,0:T(8,128)(2,1)S(1)}, u32[]{:S(2)}, u32[]{:S(2)}) %collective-permute-start.1) | collective-permute-done | bytes 262176 | tf_op jit(solution)/shard_map/ppermute | solution.py:26
  25.2 3.7 %fusion.7 = f32[64,2048]{1,0:T(8,128)S(1)} fusion(bf16[2048,1024]{1,0:T(8,128)(2,1)} %refs_9_.1, bf16[512,1024]{1,0:T(8,128)(2,1)S(1)} %get-tuple-element.16), kind=kOutput, calls=%fused_computation.27 | convolution fusion | flops 268435456 | bytes 4849664 | tf_op jit(solution)/shard_map/dot_general | solution.py:271
  29.0 8.3 %collective-permute-start.13 = (f32[32,2176]{1,0:T(8,128)S(1)}, f32[32,2176]{1,0:T(8,128)S(1)}, u32[]{:S(2)}, u32[]{:S(2)}) collective-permute-start(f32[32,2176]{1,0:T(8,128)S(1)} %pad_maximum_fusion.3), channel_id=1, source_target_pairs={{0,448},{32,480},{64,0},{96,32},{128,64},{160,96},{192,128},{224,1... | collective-permute-start | bytes 835592 | tf_op jit(solution)/shard_map/ppermute | solution.py:26
  37.3 1.9 collective-permute-start.3
  39.3 2.1 %fusion = f32[448,2048]{1,0:T(8,128)S(1)} fusion(bf16[2048,1024]{1,0:T(8,128)(2,1)S(1)} %copy-done, bf16[192,1024]{1,0:T(8,128)(2,1)S(1)} %slice.261, bf16[256,1024]{1,0:T(8,128)(2,1)S(1)} %slice.260), kind=kOutput, calls=%fused_computation | convolution fusion | flops 1880883200 | bytes 8781824 | tf_op jit(solution)/shard_map/dot_general | solution.py:271
  41.8 4.6 %collective-permute-start.7 = (f32[32,2176]{1,0:T(8,128)S(1)}, f32[32,2176]{1,0:T(8,128)S(1)}, u32[]{:S(2)}, u32[]{:S(2)}) collective-permute-start(f32[32,2176]{1,0:T(8,128)S(1)} %pad_maximum_fusion.1), channel_id=1, source_target_pairs={{0,448},{32,480},{64,0},{96,32},{128,64},{160,96},{192,128},{224,1... | collective-permute-start | bytes 835592 | tf_op jit(solution)/shard_map/ppermute | solution.py:26
  46.4 1.9 collective-permute-start.10
  48.4 2.9 %collective-permute-done.7 = f32[32,2176]{1,0:T(8,128)S(1)} collective-permute-done((f32[32,2176]{1,0:T(8,128)S(1)}, f32[32,2176]{1,0:T(8,128)S(1)}, u32[]{:S(2)}, u32[]{:S(2)}) %collective-permute-start.7) | collective-permute-done | bytes 278560 | tf_op jit(solution)/shard_map/ppermute | solution.py:26
  51.3 5.3 %collective-permute-start.8 = (f32[32,2176]{1,0:T(8,128)S(1)}, f32[32,2176]{1,0:T(8,128)S(1)}, u32[]{:S(2)}, u32[]{:S(2)}) collective-permute-start(f32[32,2176]{1,0:T(8,128)S(1)} %maximum_add_fusion.5), channel_id=1, source_target_pairs={{0,448},{32,480},{64,0},{96,32},{128,64},{160,96},{192,128},{224,1... | collective-permute-start | bytes 835592 | tf_op jit(solution)/shard_map/ppermute | solution.py:26
  58.7 4.6 %collective-permute-start.14 = (f32[32,2176]{1,0:T(8,128)S(1)}, f32[32,2176]{1,0:T(8,128)S(1)}, u32[]{:S(2)}, u32[]{:S(2)}) collective-permute-start(f32[32,2176]{1,0:T(8,128)S(1)} %maximum_add_fusion.11), channel_id=1, source_target_pairs={{0,448},{32,480},{64,0},{96,32},{128,64},{160,96},{192,128},{224,1... | collective-permute-start | bytes 835592 | tf_op jit(solution)/shard_map/ppermute | solution.py:26
  65.3 4.6 %collective-permute-start.9 = (f32[32,2176]{1,0:T(8,128)S(1)}, f32[32,2176]{1,0:T(8,128)S(1)}, u32[]{:S(2)}, u32[]{:S(2)}) collective-permute-start(f32[32,2176]{1,0:T(8,128)S(1)} %maximum_add_fusion.4), channel_id=1, source_target_pairs={{0,448},{32,480},{64,0},{96,32},{128,64},{160,96},{192,128},{224,1... | collective-permute-start | bytes 835592 | tf_op jit(solution)/shard_map/ppermute | solution.py:26
  71.9 4.6 %collective-permute-start.15 = (f32[32,2176]{1,0:T(8,128)S(1)}, f32[32,2176]{1,0:T(8,128)S(1)}, u32[]{:S(2)}, u32[]{:S(2)}) collective-permute-start(f32[32,2176]{1,0:T(8,128)S(1)} %maximum_add_fusion.10), channel_id=1, source_target_pairs={{0,448},{32,480},{64,0},{96,32},{128,64},{160,96},{192,128},{224,1... | collective-permute-start | bytes 835592 | tf_op jit(solution)/shard_map/ppermute | solution.py:26
  80.0 5.0 %collective-permute-start.16 = (f32[32,2176]{1,0:T(8,128)S(1)}, f32[32,2176]{1,0:T(8,128)S(1)}, u32[]{:S(2)}, u32[]{:S(2)}) collective-permute-start(f32[32,2176]{1,0:T(8,128)S(1)} %maximum_add_fusion.9), channel_id=1, source_target_pairs={{0,448},{32,480},{64,0},{96,32},{128,64},{160,96},{192,128},{224,1... | collective-permute-start | bytes 835592 | tf_op jit(solution)/shard_map/ppermute | solution.py:26
  85.3 1.9 collective-permute-start.6
  88.5 3.4 %collective-permute-start.17 = (f32[32,2176]{1,0:T(8,128)S(1)}, f32[32,2176]{1,0:T(8,128)S(1)}, u32[]{:S(2)}, u32[]{:S(2)}) collective-permute-start(f32[32,2176]{1,0:T(8,128)S(1)} %fusion.6), channel_id=1, source_target_pairs={{0,32},{32,0},{64,96},{96,64},{128,160},{160,128},{192,224},{224,1... | collective-permute-start | bytes 835592 | tf_op jit(solution)/shard_map/ppermute | solution.py:26
  93.8 2.2 %collective-permute-done.17 = f32[32,2176]{1,0:T(8,128)S(1)} collective-permute-done((f32[32,2176]{1,0:T(8,128)S(1)}, f32[32,2176]{1,0:T(8,128)S(1)}, u32[]{:S(2)}, u32[]{:S(2)}) %collective-permute-start.17) | collective-permute-done | bytes 278560 | tf_op jit(solution)/shard_map/ppermute | solution.py:26
  97.5 27.6 %all_to_all.10 = f32[32,8,14]{2,1,0:T(8,128)S(1)} all-to-all(f32[32,8,14]{2,1,0:T(8,128)S(1)} %broadcast_in_dim.19), channel_id=1, replica_groups=mesh['dp'=16,'section'=4,'vocab'=8] {'section','vocab'}, dimensions={0} | all-to-all | bytes 28672 | tf_op jit(solution)/shard_map/all_to_all | solution.py:22
  127.2 2.2 %collective-permute-start.18 = (bf16[24,2176]{1,0:T(8,128)(2,1)S(1)}, bf16[24,2176]{1,0:T(8,128)(2,1)S(1)}, u32[]{:S(2)}, u32[]{:S(2)}) collective-permute-start(bf16[24,2176]{1,0:T(8,128)(2,1)S(1)} %maximum_maximum_fusion), channel_id=1, source_target_pairs={{0,32},{32,0},{64,96},{96,64},{128,160},{160,128},{192,224},{224,1... | collective-permute-start | bytes 313352 | tf_op jit(solution)/shard_map/ppermute | solution.py:26
  129.4 3.8 %collective-permute-done.18 = bf16[24,2176]{1,0:T(8,128)(2,1)S(1)} collective-permute-done((bf16[24,2176]{1,0:T(8,128)(2,1)S(1)}, bf16[24,2176]{1,0:T(8,128)(2,1)S(1)}, u32[]{:S(2)}, u32[]{:S(2)}) %collective-permute-start.18) | collective-permute-done | bytes 104480 | tf_op jit(solution)/shard_map/ppermute | solution.py:26
  133.3 5.3 %collective-permute-start.19 = (bf16[48,2176]{1,0:T(8,128)(2,1)S(1)}, bf16[48,2176]{1,0:T(8,128)(2,1)S(1)}, u32[]{:S(2)}, u32[]{:S(2)}) collective-permute-start(bf16[48,2176]{1,0:T(8,128)(2,1)S(1)} %constant_dynamic-update-slice_fusion.refs_0_), channel_id=1, source_target_pairs={{0,448},{32,480},{64,0},{96,32},{128,64},{160,96},{192,128},{224,1... | collective-permute-start | bytes 626696 | tf_op jit(solution)/shard_map/ppermute | solution.py:26
  141.8 5.3 %collective-permute-start.20 = (bf16[48,2176]{1,0:T(8,128)(2,1)S(1)}, bf16[48,2176]{1,0:T(8,128)(2,1)S(1)}, u32[]{:S(2)}, u32[]{:S(2)}) collective-permute-start(bf16[48,2176]{1,0:T(8,128)(2,1)S(1)} %collective-permute-done.19.refs_1_), channel_id=1, source_target_pairs={{0,448},{32,480},{64,0},{96,32},{128,64},{160,96},{192,128},{224,1... | collective-permute-start | bytes 626696 | tf_op jit(solution)/shard_map/ppermute | solution.py:26
  149.9 5.0 %collective-permute-start.21 = (bf16[48,2176]{1,0:T(8,128)(2,1)S(1)}, bf16[48,2176]{1,0:T(8,128)(2,1)S(1)}, u32[]{:S(2)}, u32[]{:S(2)}) collective-permute-start(bf16[48,2176]{1,0:T(8,128)(2,1)S(1)} %collective-permute-done.20.refs_2_), channel_id=1, source_target_pairs={{0,448},{32,480},{64,0},{96,32},{128,64},{160,96},{192,128},{224,1... | collective-permute-start | bytes 626696 | tf_op jit(solution)/shard_map/ppermute | solution.py:26
  157.6 5.0 %collective-permute-start.26 = (bf16[48,1152]{1,0:T(8,128)(2,1)S(1)}, bf16[48,1152]{1,0:T(8,128)(2,1)S(1)}, u32[]{:S(2)}, u32[]{:S(2)}) collective-permute-start(bf16[48,1152]{1,0:T(8,128)(2,1)S(1)} %slice.374), channel_id=1, source_target_pairs={{0,448},{32,480},{64,0},{96,32},{128,64},{160,96},{192,128},{224,1... | collective-permute-start | bytes 331784 | tf_op jit(solution)/shard_map/ppermute | solution.py:26
  166.0 3.2 %collective-permute-done.25.refs_4_ = bf16[48,1024]{1,0:T(8,128)(2,1)S(1)} collective-permute-done((bf16[48,1024]{1,0:T(8,128)(2,1)S(1)}, bf16[48,1024]{1,0:T(8,128)(2,1)S(1)}, u32[]{:S(2)}, u32[]{:S(2)}) %collective-permute-start.25) | collective-permute-done | bytes 98336 | tf_op jit(solution)/shard_map/ppermute | solution.py:26
  169.3 2.2 %copy-done.1 = bf16[2048,1024]{1,0:T(8,128)(2,1)S(1)} copy-done((bf16[2048,1024]{1,0:T(8,128)(2,1)S(1)}, bf16[2048,1024]{1,0:T(8,128)(2,1)}, u32[]{:S(2)}) %copy-start.1) | copy-done | bytes 4194328
  171.4 4.4 %backward.1 = (f32[4,1024]{1,0:T(4,128)S(1)}, f32[128,128]{1,0:T(8,128)S(1)}) custom-call(s32[3]{0:T(128)S(1)} %pad_add_fusion.place_ref, bf16[48,2176]{1,0:T(8,128)(2,1)S(1)} %constant_dynamic-update-slice_fusion.refs_0_, bf16[48,2176]{1,0:T(8,128)(2,1)S(1)} %collective-permute-done.19.refs_1_, bf16[48,2176]{1,0:T(8,128)(2,1)S(1)} %collective-permute-done.20.refs_2_, ...), custom_call_target="tpu_custom_call" | custom-call | tf_op jit(solution)/shard_map/backward/pallas_call | solution.py:358
  175.8 12.4 %all-gather.1 = f32[4,4,1024]{2,1,0:T(4,128)S(1)} all-gather(f32[1,4,1024]{2,1,0:T(4,128)S(1)} %bitcast.91), channel_id=2, replica_groups=mesh['dp'=16,'section'=4,'vocab'=8] {'section'}, dimensions={0}, use_global_device_ids=true | all-gather | bytes 81920 | tf_op jit(solution)/shard_map/all_gather | solution.py:376
  188.9 3.4 %all-to-all-start.1 = ((f32[8,4,1024]{2,1,0:T(4,128)}), f32[8,4,1024]{2,1,0:T(4,128)S(1)}, u32[]{:S(2)}, u32[]{:S(2)}) async-start(f32[8,4,1024]{2,1,0:T(4,128)} %broadcast_in_dim.40), calls=%async_computation.1 | async-start | bytes 262144 | tf_op jit(solution)/shard_map/all_to_all | solution.py:22
  192.9 7.9 %all-to-all-done.1 = f32[8,4,1024]{2,1,0:T(4,128)S(1)} async-done(((f32[8,4,1024]{2,1,0:T(4,128)}), f32[8,4,1024]{2,1,0:T(4,128)S(1)}, u32[]{:S(2)}, u32[]{:S(2)}) %all-to-all-start.1) | async-done | bytes 131104 | tf_op jit(solution)/shard_map/all_to_all | solution.py:22
  (114 shorter events, 36.1 us)
Async XLA Ops:
  0.6 17.3 %collective-permute-start.2 = (bf16[128,1024]{1,0:T(8,128)(2,1)}, bf16[128,1024]{1,0:T(8,128)(2,1)S(1)}, u32[]{:S(2)}, u32[]{:S(2)}) collective-permute-start(bf16[128,1024]{1,0:T(8,128)(2,1)} %bitcast.83), channel_id=1, source_target_pairs={{0,24},{8,16},{16,8},{24,0},{1,25},{9,17},{17,9},{25,1},{2,26},{10... | collective-permute-start | bytes 786440 | tf_op jit(solution)/shard_map/ppermute | solution.py:26
  6.7 15.2 %collective-permute-start.1 = (bf16[128,1024]{1,0:T(8,128)(2,1)}, bf16[128,1024]{1,0:T(8,128)(2,1)S(1)}, u32[]{:S(2)}, u32[]{:S(2)}) collective-permute-start(bf16[128,1024]{1,0:T(8,128)(2,1)} %bitcast.84), channel_id=1, source_target_pairs={{0,16},{8,24},{16,0},{24,8},{1,17},{9,25},{17,1},{25,9},{2,18},{10... | collective-permute-start | bytes 786440 | tf_op jit(solution)/shard_map/ppermute | solution.py:26
  14.2 7.7 %collective-permute-start = (bf16[128,1024]{1,0:T(8,128)(2,1)}, bf16[128,1024]{1,0:T(8,128)(2,1)S(1)}, u32[]{:S(2)}, u32[]{:S(2)}) collective-permute-start(bf16[128,1024]{1,0:T(8,128)(2,1)} %bitcast.85), channel_id=1, source_target_pairs={{0,8},{8,0},{16,24},{24,16},{1,9},{9,1},{17,25},{25,17},{2,10},{10... | collective-permute-start | bytes 786440 | tf_op jit(solution)/shard_map/ppermute | solution.py:26
  25.1 14.1 %copy-start = (bf16[2048,1024]{1,0:T(8,128)(2,1)S(1)}, bf16[2048,1024]{1,0:T(8,128)(2,1)}, u32[]{:S(2)}) copy-start(bf16[2048,1024]{1,0:T(8,128)(2,1)} %refs_9_.1) | copy-start | bytes 12582916
  29.0 29.6 %collective-permute-start.13 = (f32[32,2176]{1,0:T(8,128)S(1)}, f32[32,2176]{1,0:T(8,128)S(1)}, u32[]{:S(2)}, u32[]{:S(2)}) collective-permute-start(f32[32,2176]{1,0:T(8,128)S(1)} %pad_maximum_fusion.3), channel_id=1, source_target_pairs={{0,448},{32,480},{64,0},{96,32},{128,64},{160,96},{192,128},{224,1... | collective-permute-start | bytes 835592 | tf_op jit(solution)/shard_map/ppermute | solution.py:26
  37.3 26.0 %collective-permute-start.3 = (f32[32,2176]{1,0:T(8,128)S(1)}, f32[32,2176]{1,0:T(8,128)S(1)}, u32[]{:S(2)}, u32[]{:S(2)}) collective-permute-start(f32[32,2176]{1,0:T(8,128)S(1)} %pad_maximum_fusion), channel_id=1, source_target_pairs={{0,64},{32,96},{64,128},{96,160},{128,192},{160,224},{192,256},{22... | collective-permute-start | bytes 835592 | tf_op jit(solution)/shard_map/ppermute | solution.py:26
  41.8 9.5 %collective-permute-start.7 = (f32[32,2176]{1,0:T(8,128)S(1)}, f32[32,2176]{1,0:T(8,128)S(1)}, u32[]{:S(2)}, u32[]{:S(2)}) collective-permute-start(f32[32,2176]{1,0:T(8,128)S(1)} %pad_maximum_fusion.1), channel_id=1, source_target_pairs={{0,448},{32,480},{64,0},{96,32},{128,64},{160,96},{192,128},{224,1... | collective-permute-start | bytes 835592 | tf_op jit(solution)/shard_map/ppermute | solution.py:26
  46.4 10.2 %collective-permute-start.10 = (f32[32,2176]{1,0:T(8,128)S(1)}, f32[32,2176]{1,0:T(8,128)S(1)}, u32[]{:S(2)}, u32[]{:S(2)}) collective-permute-start(f32[32,2176]{1,0:T(8,128)S(1)} %pad_maximum_fusion.2), channel_id=1, source_target_pairs={{0,64},{32,96},{64,128},{96,160},{128,192},{160,224},{192,256},{22... | collective-permute-start | bytes 835592 | tf_op jit(solution)/shard_map/ppermute | solution.py:26
  51.3 13.9 %collective-permute-start.8 = (f32[32,2176]{1,0:T(8,128)S(1)}, f32[32,2176]{1,0:T(8,128)S(1)}, u32[]{:S(2)}, u32[]{:S(2)}) collective-permute-start(f32[32,2176]{1,0:T(8,128)S(1)} %maximum_add_fusion.5), channel_id=1, source_target_pairs={{0,448},{32,480},{64,0},{96,32},{128,64},{160,96},{192,128},{224,1... | collective-permute-start | bytes 835592 | tf_op jit(solution)/shard_map/ppermute | solution.py:26
  56.7 13.2 %collective-permute-start.11 = (f32[32,2176]{1,0:T(8,128)S(1)}, f32[32,2176]{1,0:T(8,128)S(1)}, u32[]{:S(2)}, u32[]{:S(2)}) collective-permute-start(f32[32,2176]{1,0:T(8,128)S(1)} %maximum_add_fusion.8), channel_id=1, source_target_pairs={{0,64},{32,96},{64,128},{96,160},{128,192},{160,224},{192,256},{22... | collective-permute-start | bytes 835592 | tf_op jit(solution)/shard_map/ppermute | solution.py:26
  58.7 13.2 %collective-permute-start.14 = (f32[32,2176]{1,0:T(8,128)S(1)}, f32[32,2176]{1,0:T(8,128)S(1)}, u32[]{:S(2)}, u32[]{:S(2)}) collective-permute-start(f32[32,2176]{1,0:T(8,128)S(1)} %maximum_add_fusion.11), channel_id=1, source_target_pairs={{0,448},{32,480},{64,0},{96,32},{128,64},{160,96},{192,128},{224,1... | collective-permute-start | bytes 835592 | tf_op jit(solution)/shard_map/ppermute | solution.py:26
  63.3 13.2 %collective-permute-start.4 = (f32[32,2176]{1,0:T(8,128)S(1)}, f32[32,2176]{1,0:T(8,128)S(1)}, u32[]{:S(2)}, u32[]{:S(2)}) collective-permute-start(f32[32,2176]{1,0:T(8,128)S(1)} %maximum_add_fusion.3), channel_id=1, source_target_pairs={{0,64},{32,96},{64,128},{96,160},{128,192},{160,224},{192,256},{22... | collective-permute-start | bytes 835592 | tf_op jit(solution)/shard_map/ppermute | solution.py:26
  65.3 26.6 %collective-permute-start.9 = (f32[32,2176]{1,0:T(8,128)S(1)}, f32[32,2176]{1,0:T(8,128)S(1)}, u32[]{:S(2)}, u32[]{:S(2)}) collective-permute-start(f32[32,2176]{1,0:T(8,128)S(1)} %maximum_add_fusion.4), channel_id=1, source_target_pairs={{0,448},{32,480},{64,0},{96,32},{128,64},{160,96},{192,128},{224,1... | collective-permute-start | bytes 835592 | tf_op jit(solution)/shard_map/ppermute | solution.py:26
  69.9 17.3 %collective-permute-start.12 = (f32[32,2176]{1,0:T(8,128)S(1)}, f32[32,2176]{1,0:T(8,128)S(1)}, u32[]{:S(2)}, u32[]{:S(2)}) collective-permute-start(f32[32,2176]{1,0:T(8,128)S(1)} %maximum_add_fusion.7), channel_id=1, source_target_pairs={{0,64},{32,96},{64,128},{96,160},{128,192},{160,224},{192,256},{22... | collective-permute-start | bytes 835592 | tf_op jit(solution)/shard_map/ppermute | solution.py:26
  71.9 8.1 %collective-permute-start.15 = (f32[32,2176]{1,0:T(8,128)S(1)}, f32[32,2176]{1,0:T(8,128)S(1)}, u32[]{:S(2)}, u32[]{:S(2)}) collective-permute-start(f32[32,2176]{1,0:T(8,128)S(1)} %maximum_add_fusion.10), channel_id=1, source_target_pairs={{0,448},{32,480},{64,0},{96,32},{128,64},{160,96},{192,128},{224,1... | collective-permute-start | bytes 835592 | tf_op jit(solution)/shard_map/ppermute | solution.py:26
  76.5 8.7 %collective-permute-start.5 = (f32[32,2176]{1,0:T(8,128)S(1)}, f32[32,2176]{1,0:T(8,128)S(1)}, u32[]{:S(2)}, u32[]{:S(2)}) collective-permute-start(f32[32,2176]{1,0:T(8,128)S(1)} %maximum_add_fusion.2), channel_id=1, source_target_pairs={{0,64},{32,96},{64,128},{96,160},{128,192},{160,224},{192,256},{22... | collective-permute-start | bytes 835592 | tf_op jit(solution)/shard_map/ppermute | solution.py:26
  80.0 8.5 %collective-permute-start.16 = (f32[32,2176]{1,0:T(8,128)S(1)}, f32[32,2176]{1,0:T(8,128)S(1)}, u32[]{:S(2)}, u32[]{:S(2)}) collective-permute-start(f32[32,2176]{1,0:T(8,128)S(1)} %maximum_add_fusion.9), channel_id=1, source_target_pairs={{0,448},{32,480},{64,0},{96,32},{128,64},{160,96},{192,128},{224,1... | collective-permute-start | bytes 835592 | tf_op jit(solution)/shard_map/ppermute | solution.py:26
  85.3 8.5 %collective-permute-start.6 = (f32[32,2176]{1,0:T(8,128)S(1)}, f32[32,2176]{1,0:T(8,128)S(1)}, u32[]{:S(2)}, u32[]{:S(2)}) collective-permute-start(f32[32,2176]{1,0:T(8,128)S(1)} %maximum_add_fusion.1), channel_id=1, source_target_pairs={{0,64},{32,96},{64,128},{96,160},{128,192},{160,224},{192,256},{22... | collective-permute-start | bytes 835592 | tf_op jit(solution)/shard_map/ppermute | solution.py:26
  88.5 76.1 %copy-start.3 = (bf16[1,128,1024]{2,1,0:T(8,128)(2,1)S(1)}, bf16[1,128,1024]{2,1,0:T(8,128)(2,1)}, u32[]{:S(2)}) copy-start(bf16[1,128,1024]{2,1,0:T(8,128)(2,1)} %param.5) | copy-start | bytes 786436
  88.5 76.1 %copy-start.5 = (f32[1024]{0:T(1024)S(1)}, f32[1024]{0:T(1024)}, u32[]{:S(2)}) copy-start(f32[1024]{0:T(1024)} %param.8) | copy-start | bytes 12292
  88.5 7.4 %collective-permute-start.17 = (f32[32,2176]{1,0:T(8,128)S(1)}, f32[32,2176]{1,0:T(8,128)S(1)}, u32[]{:S(2)}, u32[]{:S(2)}) collective-permute-start(f32[32,2176]{1,0:T(8,128)S(1)} %fusion.6), channel_id=1, source_target_pairs={{0,32},{32,0},{64,96},{96,64},{128,160},{160,128},{192,224},{224,1... | collective-permute-start | bytes 835592 | tf_op jit(solution)/shard_map/ppermute | solution.py:26
  127.2 6.0 %collective-permute-start.18 = (bf16[24,2176]{1,0:T(8,128)(2,1)S(1)}, bf16[24,2176]{1,0:T(8,128)(2,1)S(1)}, u32[]{:S(2)}, u32[]{:S(2)}) collective-permute-start(bf16[24,2176]{1,0:T(8,128)(2,1)S(1)} %maximum_maximum_fusion), channel_id=1, source_target_pairs={{0,32},{32,0},{64,96},{96,64},{128,160},{160,128},{192,224},{224,1... | collective-permute-start | bytes 313352 | tf_op jit(solution)/shard_map/ppermute | solution.py:26
  133.3 8.6 %collective-permute-start.19 = (bf16[48,2176]{1,0:T(8,128)(2,1)S(1)}, bf16[48,2176]{1,0:T(8,128)(2,1)S(1)}, u32[]{:S(2)}, u32[]{:S(2)}) collective-permute-start(bf16[48,2176]{1,0:T(8,128)(2,1)S(1)} %constant_dynamic-update-slice_fusion.refs_0_), channel_id=1, source_target_pairs={{0,448},{32,480},{64,0},{96,32},{128,64},{160,96},{192,128},{224,1... | collective-permute-start | bytes 626696 | tf_op jit(solution)/shard_map/ppermute | solution.py:26
  138.6 8.6 %collective-permute-start.22 = (bf16[48,2176]{1,0:T(8,128)(2,1)S(1)}, bf16[48,2176]{1,0:T(8,128)(2,1)S(1)}, u32[]{:S(2)}, u32[]{:S(2)}) collective-permute-start(bf16[48,2176]{1,0:T(8,128)(2,1)S(1)} %constant_dynamic-update-slice_fusion.refs_0_), channel_id=1, source_target_pairs={{0,64},{32,96},{64,128},{96,160},{128,192},{160,224},{192,256},{22... | collective-permute-start | bytes 626696 | tf_op jit(solution)/shard_map/ppermute | solution.py:26
  141.8 8.0 %collective-permute-start.20 = (bf16[48,2176]{1,0:T(8,128)(2,1)S(1)}, bf16[48,2176]{1,0:T(8,128)(2,1)S(1)}, u32[]{:S(2)}, u32[]{:S(2)}) collective-permute-start(bf16[48,2176]{1,0:T(8,128)(2,1)S(1)} %collective-permute-done.19.refs_1_), channel_id=1, source_target_pairs={{0,448},{32,480},{64,0},{96,32},{128,64},{160,96},{192,128},{224,1... | collective-permute-start | bytes 626696 | tf_op jit(solution)/shard_map/ppermute | solution.py:26
  147.1 7.8 %collective-permute-start.23 = (bf16[48,2176]{1,0:T(8,128)(2,1)S(1)}, bf16[48,2176]{1,0:T(8,128)(2,1)S(1)}, u32[]{:S(2)}, u32[]{:S(2)}) collective-permute-start(bf16[48,2176]{1,0:T(8,128)(2,1)S(1)} %collective-permute-done.22.refs_8_), channel_id=1, source_target_pairs={{0,64},{32,96},{64,128},{96,160},{128,192},{160,224},{192,256},{22... | collective-permute-start | bytes 626696 | tf_op jit(solution)/shard_map/ppermute | solution.py:26
  149.9 7.7 %collective-permute-start.21 = (bf16[48,2176]{1,0:T(8,128)(2,1)S(1)}, bf16[48,2176]{1,0:T(8,128)(2,1)S(1)}, u32[]{:S(2)}, u32[]{:S(2)}) collective-permute-start(bf16[48,2176]{1,0:T(8,128)(2,1)S(1)} %collective-permute-done.20.refs_2_), channel_id=1, source_target_pairs={{0,448},{32,480},{64,0},{96,32},{128,64},{160,96},{192,128},{224,1... | collective-permute-start | bytes 626696 | tf_op jit(solution)/shard_map/ppermute | solution.py:26
  154.9 7.8 %collective-permute-start.24 = (bf16[48,2176]{1,0:T(8,128)(2,1)S(1)}, bf16[48,2176]{1,0:T(8,128)(2,1)S(1)}, u32[]{:S(2)}, u32[]{:S(2)}) collective-permute-start(bf16[48,2176]{1,0:T(8,128)(2,1)S(1)} %collective-permute-done.23.refs_7_), channel_id=1, source_target_pairs={{0,64},{32,96},{64,128},{96,160},{128,192},{160,224},{192,256},{22... | collective-permute-start | bytes 626696 | tf_op jit(solution)/shard_map/ppermute | solution.py:26
  157.6 11.6 %collective-permute-start.26 = (bf16[48,1152]{1,0:T(8,128)(2,1)S(1)}, bf16[48,1152]{1,0:T(8,128)(2,1)S(1)}, u32[]{:S(2)}, u32[]{:S(2)}) collective-permute-start(bf16[48,1152]{1,0:T(8,128)(2,1)S(1)} %slice.374), channel_id=1, source_target_pairs={{0,448},{32,480},{64,0},{96,32},{128,64},{160,96},{192,128},{224,1... | collective-permute-start | bytes 331784 | tf_op jit(solution)/shard_map/ppermute | solution.py:26
  162.7 6.6 %collective-permute-start.25 = (bf16[48,1024]{1,0:T(8,128)(2,1)S(1)}, bf16[48,1024]{1,0:T(8,128)(2,1)S(1)}, u32[]{:S(2)}, u32[]{:S(2)}) collective-permute-start(bf16[48,1024]{1,0:T(8,128)(2,1)S(1)} %slice.373), channel_id=1, source_target_pairs={{0,64},{32,96},{64,128},{96,160},{128,192},{160,224},{192,256},{22... | collective-permute-start | bytes 294920 | tf_op jit(solution)/shard_map/ppermute | solution.py:26
  169.3 2.2 %copy-start.1 = (bf16[2048,1024]{1,0:T(8,128)(2,1)S(1)}, bf16[2048,1024]{1,0:T(8,128)(2,1)}, u32[]{:S(2)}) copy-start(bf16[2048,1024]{1,0:T(8,128)(2,1)} %refs_9_.1) | copy-start | bytes 12582916
  188.9 11.9 %all-to-all-start.1 = ((f32[8,4,1024]{2,1,0:T(4,128)}), f32[8,4,1024]{2,1,0:T(4,128)S(1)}, u32[]{:S(2)}, u32[]{:S(2)}) async-start(f32[8,4,1024]{2,1,0:T(4,128)} %broadcast_in_dim.40), calls=%async_computation.1 | async-start | bytes 262144 | tf_op jit(solution)/shard_map/all_to_all | solution.py:22
  (3 other events, 2.2 us)

commit v6 on v5

--- a/solution.py
+++ b/solution.py
@@ -13,8 +13,9 @@
 F32 = jnp.float32
 BF16 = jnp.bfloat16
 LANES = 128
+TILES = 4
 PAIR = 2
-VMEM_LIMIT = 40 * 1024 * 1024
+MIB = 1024 * 1024
 
 
 def exchange(a, axis):
@@ -89,8 +90,24 @@
     )
 
 
-def prepare(n_z, block, n_dp, place_ref, gains_ref, gain_ref, same_ref, *refs):
-    rows, (lhs_ref, extra_ref, m0, m1, m2, m3, ex) = refs[:-7], refs[-7:]
+def brought(head_ref, held, sems, tiles):
+    copies = [
+        pltpu.make_async_copy(head_ref.at[at], held.at[at], sems.at[c])
+        for c, at in enumerate(tiles)
+    ]
+    for copy in copies:
+        copy.start()
+    return copies
+
+
+def forward(n_z, block, n_dp, place_ref, head_ref, gains_ref, gain_ref, same_ref, *refs):
+    split = len(refs) - 8 - n_z * PAIR
+    rows, outs = refs[:split], refs[split : split + n_z * PAIR]
+    m0, m1, m2, m3, ex, lhs, held, sems = refs[split + n_z * PAIR :]
+    vocab = head_ref.shape[0]
+    tall = vocab // TILES
+    tiles = [pl.ds(c * tall, tall) for c in range(TILES)]
+    copies = brought(head_ref, held, sems, tiles)
     section, count = place_ref[0], len(rows)
     united = united_of(place_ref, rows, gains_ref)
     gain = gain_ref[...]
@@ -128,11 +145,21 @@
             at = (i * PAIR + h) * size
             mine = pl.ds(token_of(place_ref, i, h, n_z, block), block)
             first = jnp.concatenate([m0[mine, :], m1[mine, :]], axis=0)
-            lhs_ref[at : at + 2 * block, :] = first.astype(BF16)
+            lhs[at : at + 2 * block, :] = first.astype(BF16)
             second = jnp.concatenate([m2[mine, :], m3[mine, :]], axis=0)
-            lhs_ref[at + 2 * block : at + size, :] = second.astype(BF16)
-            extra_ref[at : at + block, :] = ex[mine, :]
-            extra_ref[at + block : at + size, :] = jnp.zeros((size - block, LANES), F32)
+            lhs[at + 2 * block : at + size, :] = second.astype(BF16)
+
+    for q, out in enumerate(outs):
+        mine = pl.ds(token_of(place_ref, q // PAIR, q % PAIR, n_z, block), block)
+        out[:block, vocab:] = ex[mine, :]
+        out[block:, vocab:] = jnp.zeros((size - block, LANES), F32)
+    for c, copy in enumerate(copies):
+        copy.wait()
+        made = lax.dot_general(
+            lhs[...], held[c * tall : (c + 1) * tall, :], CONTRACT, preferred_element_type=F32
+        )
+        for q, out in enumerate(outs):
+            out[:, c * tall : (c + 1) * tall] = made[q * size : (q + 1) * size]
 
 
 def arrange(n_z, block, place_ref, gains_ref, gain_ref, *refs):
@@ -168,8 +195,11 @@
 
 def backward(n_z, block, shards, place_ref, *refs):
     blocks, (head_ref, near_ref, back1_ref, back2_ref, layers_ref, gain_ref) = refs[:9], refs[9:15]
-    grads_ref, known_ref, lhs, dh, aux, acc = refs[15:]
+    grads_ref, known_ref, lhs, dh, aux, acc, held, sems = refs[15:]
     vocab, cols = head_ref.shape
+    wide = cols // TILES
+    tiles = [(slice(None), pl.ds(c * wide, wide)) for c in range(TILES)]
+    copies = brought(head_ref, held, sems, tiles)
     size = PAIR * STEPS * block
     spots = [0, 1, 2, 3, 4, 4, 5, 6, 7]
     for b, (spot, ref) in enumerate(zip(spots, blocks, strict=True)):
@@ -187,12 +217,10 @@
             aux[(spot * PAIR + h) * block : (spot * PAIR + h + 1) * block, :] = known
             known_ref[pl.ds(token_of(place_ref, spot, h, n_z, block), block), :] = known
 
-    wide = 256
-
-    @pl.loop(0, cols // wide)
-    def _(c):
-        at = pl.ds(pl.multiple_of(c * wide, wide), wide)
-        dh[:, at] = jnp.dot(lhs[...], head_ref[:, at], preferred_element_type=F32)
+    for c, copy in enumerate(copies):
+        copy.wait()
+        at = slice(c * wide, (c + 1) * wide)
+        dh[:, at] = jnp.dot(lhs[...], held[:, at], preferred_element_type=F32)
 
     acc[...] = jnp.zeros_like(acc)
     gain = gain_ref[...]
@@ -241,51 +269,37 @@
     z, x = place // PAIR, place % PAIR
     section = lax.axis_index("section")
 
-    sections = [own_rows]
+    rows = [own_rows]
     for j in range(1, n_section):
-        sections.append(permute(own_rows, "section", lambda i, j=j: i ^ j))
-    rows = sections
+        rows.append(permute(own_rows, "section", lambda i, j=j: i ^ j))
+    near_by = lax.optimization_barrier(
+        tuple(jnp.where(section >= 0, a, 0) for a in (own_rows, norm_gain[None]))
+    )
+    rows[0], gain = near_by
     where = jnp.stack([section, z, x]).astype(jnp.int32)
     gains = jnp.concatenate([unite_gain, jnp.zeros_like(unite_gain[:1])], axis=0)
-    gain = norm_gain[None]
     same = (segment_ids[1:] == segment_ids[:-1]).astype(F32)
     same = jnp.concatenate([jnp.zeros((1,), F32), same])[:, None]
 
     smem, vmem = pl.BlockSpec(memory_space=pltpu.SMEM), pl.BlockSpec(memory_space=pltpu.VMEM)
-    params = pltpu.CompilerParams(vmem_limit_bytes=VMEM_LIMIT)
+    hbm = pl.BlockSpec(memory_space=pltpu.MemorySpace.HBM)
     whole = pltpu.VMEM((tokens, cols), F32)
-    stacked, extra = pl.pallas_call(
-        functools.partial(prepare, n_z, block, n_dp),
-        out_shape=(
-            jax.ShapeDtypeStruct((4 * tokens, cols), BF16),
-            jax.ShapeDtypeStruct((4 * tokens, LANES), F32),
-        ),
-        in_specs=[smem] + [vmem] * (3 + n_section),
-        out_specs=(vmem, vmem),
-        scratch_shapes=[whole] * 4 + [pltpu.VMEM((tokens, LANES), F32)],
-        compiler_params=params,
-        name="prepare",
-    )(where, gains, gain, same, *rows)
-
-    def product(a):
-        return lax.dot_general(a, head, CONTRACT, preferred_element_type=F32)
-
     size = 4 * block
-    first = n_z // 2 * PAIR * size
-    last = first + PAIR * size
-    far = product(stacked[first:last])
-    rest = product(jnp.concatenate([stacked[:first], stacked[last:]], axis=0))
-
-    def term(i, h):
-        at = (i * PAIR + h) * size
-        if first <= at < last:
-            made = far[at - first : at - first + size]
-        else:
-            at_rest = at if at < first else at - PAIR * size
-            made = rest[at_rest : at_rest + size]
-        return jnp.concatenate([made, extra[at : at + size]], axis=1)
-
-    summed = sum_over_dp(term, n_z)
+    across = vocab + LANES
+    held = [pltpu.VMEM(head.shape, BF16), pltpu.SemaphoreType.DMA((TILES,))]
+    terms = pl.pallas_call(
+        functools.partial(forward, n_z, block, n_dp),
+        out_shape=[jax.ShapeDtypeStruct((size, across), F32)] * (n_z * PAIR),
+        in_specs=[smem, hbm] + [vmem] * (3 + n_section),
+        out_specs=[vmem] * (n_z * PAIR),
+        scratch_shapes=[whole] * 4
+        + [pltpu.VMEM((tokens, LANES), F32), pltpu.VMEM((4 * tokens, cols), BF16)]
+        + held,
+        compiler_params=pltpu.CompilerParams(vmem_limit_bytes=50 * MIB),
+        name="forward",
+    )(where, head, gains, gain, same, *rows)
+
+    summed = sum_over_dp(lambda i, h: terms[i * PAIR + h], n_z)
     q00, q01, q11, q02, q12, q22, p00, p01, p11, pp00, same0, same1 = columns(
         summed[:block, vocab : vocab + 12]
     )
@@ -350,7 +364,7 @@
         in_specs=[smem] + [vmem] * (2 + n_section),
         out_specs=(vmem,) * 4,
         scratch_shapes=[whole] * 4,
-        compiler_params=params,
+        compiler_params=pltpu.CompilerParams(vmem_limit_bytes=16 * MIB),
         name="arrange",
     )(where, gains, gain, *tied[1:])
 
@@ -361,15 +375,16 @@
             jax.ShapeDtypeStruct((n_section, cols), F32),
             jax.ShapeDtypeStruct((tokens, LANES), F32),
         ),
-        in_specs=[smem] + [vmem] * 15,
+        in_specs=[smem] + [vmem] * 9 + [hbm] + [vmem] * 5,
         out_specs=(vmem, vmem),
         scratch_shapes=[
             pltpu.VMEM((STEPS * tokens, vocab), BF16),
             pltpu.VMEM((STEPS * tokens, cols), F32),
             pltpu.VMEM((tokens, LANES), F32),
             pltpu.VMEM(((n_section + 1) * block, cols), F32),
+            *held,
         ],
-        compiler_params=params,
+        compiler_params=pltpu.CompilerParams(vmem_limit_bytes=48 * MIB),
         name="backward",
     )(where, *blocks, head, near, back1, back2, layers, gain)
     step_loss = jnp.sum(known[:, 6:9], axis=0) / tokens

time: 203 us -> 193 us (0.951)
  Pallas kernels: 7.33 us -> 15 us
  matrix products: 5.83 us -> 0 us
  starting transfers between devices: 103 us -> 98.3 us
  other arithmetic: 4.34 us -> 8.79 us
  local copies, waits for them, and re-layouts: 7.88 us -> 3.49 us
  blocking collectives: 40 us -> 35.8 us
    dot_general x2 -> x0, matrix products: 5.83 us -> none  [product(): return lax.dot_general(a, head, CONTRACT, preferred_element_type=F32)]
    pallas_call x1, Pallas kernels: 1.54 us -> 6.55 us  [on_device(): pl.pallas_call(functools.partial(forward, n_z, block, n_dp), out_shape=[j...]
    ppermute x27, starting transfers between devices: 99.8 us -> 94.9 us  [permute(): lax.ppermute(a, axis, [(i, to(i)) for i in range(lax.axis_size(axis))])]
    all_to_all x1, blocking collectives: 27.6 us -> 23.3 us  [exchange(): return lax.all_to_all(jnp.broadcast_to(a[None], (n,) + a.shape), axis, 0, 0)]
    unnamed x22 -> x14, local copies, waits for them, and re-layouts: 4.72 us -> 0.89 us
    add x10, other arithmetic: 0.33 us -> 3.2 us  [sum_over_dp(): held[h] = ring(made if held[h] is None else made + held[h], sign)]
    pallas_call x1, Pallas kernels: 4.38 us -> 6.99 us  [on_device(): pl.pallas_call(functools.partial(backward, n_z, block, shards), out_shape...]
  transfers between devices with their start and end apart: 28 -> 28, of which waited for: 13 -> 12; matrix products, arithmetic and copies ran while one was open for 3% -> 4% of each run, Pallas kernels for 1% -> 1%
where the time goes in v6:
time: 193 us; the launch traced here: 192 us
  starting transfers between devices  98.3 us (51%)
  blocking collectives  35.8 us (19%)
  waiting for transfers between devices  29.8 us (15%)
  Pallas kernels  15 us (8%)
  other arithmetic  8.79 us (5%)
  local copies, waits for them, and re-layouts  3.49 us (2%)
    ppermute x27, starting transfers between devices, permute(): lax.ppermute(a, axis, [(i, to(i)) for i in range(lax.axis_size(axis))])  94.9 us
    all_to_all x1, blocking collectives, exchange(): return lax.all_to_all(jnp.broadcast_to(a[None], (n,) + a.shape), axis, 0, 0)  23.3 us
    ppermute x27, waiting for transfers between devices, permute(): lax.ppermute(a, axis, [(i, to(i)) for i in range(lax.axis_size(axis))])  21.9 us
    all_gather x1, blocking collectives, on_device(): grads = jnp.sum(lax.all_gather(grads, 'section'), axis=0)  12.4 us
    all_to_all x1, waiting for transfers between devices, exchange(): return lax.all_to_all(jnp.broadcast_to(a[None], (n,) + a.shape), axis, 0, 0)  7.93 us
    pallas_call x1, Pallas kernels, on_device(): pl.pallas_call(functools.partial(backward, n_z, block, shards), out_shape...  6.99 us
    pallas_call x1, Pallas kernels, on_device(): pl.pallas_call(functools.partial(forward, n_z, block, n_dp), out_shape=[j...  6.55 us
  transfers between devices with their start and end apart: 28, of which 12 were waited for; matrix products, arithmetic and copies ran while one was open for 4% of the time, Pallas kernels for 1%

profile of v6, /device:TPU:1, one launch (start us, length us, event | category | flops | bytes accessed | tf_op | source)
XLA Modules:
  0.0 192.3 jit_solution(5102523189477984507)
XLA Ops:
  0.6 5.5 %collective-permute-start.1 = (bf16[128,1024]{1,0:T(8,128)(2,1)}, bf16[128,1024]{1,0:T(8,128)(2,1)S(1)}, u32[]{:S(2)}, u32[]{:S(2)}) collective-permute-start(bf16[128,1024]{1,0:T(8,128)(2,1)} %bitcast.86), channel_id=1, source_target_pairs={{0,16},{8,24},{16,0},{24,8},{1,17},{9,25},{17,1},{25,9},{2,18},{10... | collective-permute-start | bytes 786440 | tf_op jit(solution)/shard_map/ppermute | solution.py:27
  6.1 5.2 %collective-permute-start = (bf16[128,1024]{1,0:T(8,128)(2,1)}, bf16[128,1024]{1,0:T(8,128)(2,1)S(1)}, u32[]{:S(2)}, u32[]{:S(2)}) collective-permute-start(bf16[128,1024]{1,0:T(8,128)(2,1)} %bitcast.87), channel_id=1, source_target_pairs={{0,8},{8,0},{16,24},{24,16},{1,9},{9,1},{17,25},{25,17},{2,10},{10... | collective-permute-start | bytes 786440 | tf_op jit(solution)/shard_map/ppermute | solution.py:27
  11.4 5.0 %collective-permute-start.2 = (bf16[128,1024]{1,0:T(8,128)(2,1)}, bf16[128,1024]{1,0:T(8,128)(2,1)S(1)}, u32[]{:S(2)}, u32[]{:S(2)}) collective-permute-start(bf16[128,1024]{1,0:T(8,128)(2,1)} %bitcast.88), channel_id=1, source_target_pairs={{0,24},{8,16},{16,8},{24,0},{1,25},{9,17},{17,9},{25,1},{2,26},{10... | collective-permute-start | bytes 786440 | tf_op jit(solution)/shard_map/ppermute | solution.py:27
  19.9 3.4 %collective-permute-done.2.refs_3_ = bf16[128,1024]{1,0:T(8,128)(2,1)S(1)} collective-permute-done((bf16[128,1024]{1,0:T(8,128)(2,1)}, bf16[128,1024]{1,0:T(8,128)(2,1)S(1)}, u32[]{:S(2)}, u32[]{:S(2)}) %collective-permute-start.2) | collective-permute-done | bytes 262176 | tf_op jit(solution)/shard_map/ppermute | solution.py:27
  23.3 6.5 %forward.1 = (f32[32,2176]{1,0:T(8,128)S(1)}, f32[32,2176]{1,0:T(8,128)S(1)}, f32[32,2176]{1,0:T(8,128)S(1)}, f32[32,2176]{1,0:T(8,128)S(1)}, f32[32,2176]{1,0:T...) custom-call(s32[3]{0:T(128)S(1)} %pad_add_fusion.place_ref, ...), custom_call_target="tpu_custom_call" | custom-call | tf_op jit(solution)/shard_map/forward/pallas_call | solution.py:290
  29.9 8.1 %collective-permute-start.13 = (f32[32,2176]{1,0:T(8,128)S(1)}, f32[32,2176]{1,0:T(8,128)S(1)}, u32[]{:S(2)}, u32[]{:S(2)}) collective-permute-start(f32[32,2176]{1,0:T(8,128)S(1)} %get-tuple-element.49), channel_id=1, source_target_pairs={{0,448},{32,480},{64,0},{96,32},{128,64},{160,96},{192,128},{224,1... | collective-permute-start | bytes 835592 | tf_op jit(solution)/shard_map/ppermute | solution.py:27
  37.9 1.9 collective-permute-start.3
  39.9 1.9 collective-permute-start.10
  41.8 2.1 %collective-permute-done.13 = f32[32,2176]{1,0:T(8,128)S(1)} collective-permute-done((f32[32,2176]{1,0:T(8,128)S(1)}, f32[32,2176]{1,0:T(8,128)S(1)}, u32[]{:S(2)}, u32[]{:S(2)}) %collective-permute-start.13) | collective-permute-done | bytes 278560 | tf_op jit(solution)/shard_map/ppermute | solution.py:27
  44.9 5.3 %collective-permute-start.14 = (f32[32,2176]{1,0:T(8,128)S(1)}, f32[32,2176]{1,0:T(8,128)S(1)}, u32[]{:S(2)}, u32[]{:S(2)}) collective-permute-start(f32[32,2176]{1,0:T(8,128)S(1)} %add.125), channel_id=1, source_target_pairs={{0,448},{32,480},{64,0},{96,32},{128,64},{160,96},{192,128},{224,1... | collective-permute-start | bytes 835592 | tf_op jit(solution)/shard_map/ppermute | solution.py:27
  52.2 3.4 %collective-permute-start.4 = (f32[32,2176]{1,0:T(8,128)S(1)}, f32[32,2176]{1,0:T(8,128)S(1)}, u32[]{:S(2)}, u32[]{:S(2)}) collective-permute-start(f32[32,2176]{1,0:T(8,128)S(1)} %add.115), channel_id=1, source_target_pairs={{0,64},{32,96},{64,128},{96,160},{128,192},{160,224},{192,256},{22... | collective-permute-start | bytes 835592 | tf_op jit(solution)/shard_map/ppermute | solution.py:27
  58.6 4.6 %collective-permute-start.15 = (f32[32,2176]{1,0:T(8,128)S(1)}, f32[32,2176]{1,0:T(8,128)S(1)}, u32[]{:S(2)}, u32[]{:S(2)}) collective-permute-start(f32[32,2176]{1,0:T(8,128)S(1)} %add.126), channel_id=1, source_target_pairs={{0,448},{32,480},{64,0},{96,32},{128,64},{160,96},{192,128},{224,1... | collective-permute-start | bytes 835592 | tf_op jit(solution)/shard_map/ppermute | solution.py:27
  64.2 3.5 %collective-permute-start.8 = (f32[32,2176]{1,0:T(8,128)S(1)}, f32[32,2176]{1,0:T(8,128)S(1)}, u32[]{:S(2)}, u32[]{:S(2)}) collective-permute-start(f32[32,2176]{1,0:T(8,128)S(1)} %add.119), channel_id=1, source_target_pairs={{0,448},{32,480},{64,0},{96,32},{128,64},{160,96},{192,128},{224,1... | collective-permute-start | bytes 835592 | tf_op jit(solution)/shard_map/ppermute | solution.py:27
  67.7 1.9 collective-permute-start.5
  71.7 4.6 %collective-permute-start.16 = (f32[32,2176]{1,0:T(8,128)S(1)}, f32[32,2176]{1,0:T(8,128)S(1)}, u32[]{:S(2)}, u32[]{:S(2)}) collective-permute-start(f32[32,2176]{1,0:T(8,128)S(1)} %add.127), channel_id=1, source_target_pairs={{0,448},{32,480},{64,0},{96,32},{128,64},{160,96},{192,128},{224,1... | collective-permute-start | bytes 835592 | tf_op jit(solution)/shard_map/ppermute | solution.py:27
  76.3 3.4 %collective-permute-start.9 = (f32[32,2176]{1,0:T(8,128)S(1)}, f32[32,2176]{1,0:T(8,128)S(1)}, u32[]{:S(2)}, u32[]{:S(2)}) collective-permute-start(f32[32,2176]{1,0:T(8,128)S(1)} %add.120), channel_id=1, source_target_pairs={{0,448},{32,480},{64,0},{96,32},{128,64},{160,96},{192,128},{224,1... | collective-permute-start | bytes 835592 | tf_op jit(solution)/shard_map/ppermute | solution.py:27
  79.7 1.9 collective-permute-start.6
  83.0 2.2 %collective-permute-start.17 = (f32[32,2176]{1,0:T(8,128)S(1)}, f32[32,2176]{1,0:T(8,128)S(1)}, u32[]{:S(2)}, u32[]{:S(2)}) collective-permute-start(f32[32,2176]{1,0:T(8,128)S(1)} %add_add_fusion), channel_id=1, source_target_pairs={{0,32},{32,0},{64,96},{96,64},{128,160},{160,128},{192,224},{224,1... | collective-permute-start | bytes 835592 | tf_op jit(solution)/shard_map/ppermute | solution.py:27
  86.1 2.1 %collective-permute-done.6 = f32[32,2176]{1,0:T(8,128)S(1)} collective-permute-done((f32[32,2176]{1,0:T(8,128)S(1)}, f32[32,2176]{1,0:T(8,128)S(1)}, u32[]{:S(2)}, u32[]{:S(2)}) %collective-permute-start.6) | collective-permute-done | bytes 278560 | tf_op jit(solution)/shard_map/ppermute | solution.py:27
  88.2 2.3 %collective-permute-done.17 = f32[32,2176]{1,0:T(8,128)S(1)} collective-permute-done((f32[32,2176]{1,0:T(8,128)S(1)}, f32[32,2176]{1,0:T(8,128)S(1)}, u32[]{:S(2)}, u32[]{:S(2)}) %collective-permute-start.17) | collective-permute-done | bytes 278560 | tf_op jit(solution)/shard_map/ppermute | solution.py:27
  92.0 23.3 %all_to_all.10 = f32[32,8,14]{2,1,0:T(8,128)S(1)} all-to-all(f32[32,8,14]{2,1,0:T(8,128)S(1)} %broadcast_in_dim.46), channel_id=1, replica_groups=mesh['dp'=16,'section'=4,'vocab'=8] {'section','vocab'}, dimensions={0} | all-to-all | bytes 28672 | tf_op jit(solution)/shard_map/all_to_all | solution.py:23
  117.6 2.4 %collective-permute-start.18 = (bf16[24,2176]{1,0:T(8,128)(2,1)S(1)}, bf16[24,2176]{1,0:T(8,128)(2,1)S(1)}, u32[]{:S(2)}, u32[]{:S(2)}) collective-permute-start(bf16[24,2176]{1,0:T(8,128)(2,1)S(1)} %maximum_maximum_fusion), channel_id=1, source_target_pairs={{0,32},{32,0},{64,96},{96,64},{128,160},{160,128},{192,224},{224,1... | collective-permute-start | bytes 313352 | tf_op jit(solution)/shard_map/ppermute | solution.py:27
  120.0 3.6 %collective-permute-done.18 = bf16[24,2176]{1,0:T(8,128)(2,1)S(1)} collective-permute-done((bf16[24,2176]{1,0:T(8,128)(2,1)S(1)}, bf16[24,2176]{1,0:T(8,128)(2,1)S(1)}, u32[]{:S(2)}, u32[]{:S(2)}) %collective-permute-start.18) | collective-permute-done | bytes 104480 | tf_op jit(solution)/shard_map/ppermute | solution.py:27
  123.6 5.3 %collective-permute-start.19 = (bf16[48,2176]{1,0:T(8,128)(2,1)S(1)}, bf16[48,2176]{1,0:T(8,128)(2,1)S(1)}, u32[]{:S(2)}, u32[]{:S(2)}) collective-permute-start(bf16[48,2176]{1,0:T(8,128)(2,1)S(1)} %constant_dynamic-update-slice_fusion.refs_0_), channel_id=1, source_target_pairs={{0,448},{32,480},{64,0},{96,32},{128,64},{160,96},{192,128},{224,1... | collective-permute-start | bytes 626696 | tf_op jit(solution)/shard_map/ppermute | solution.py:27
  132.2 5.3 %collective-permute-start.20 = (bf16[48,2176]{1,0:T(8,128)(2,1)S(1)}, bf16[48,2176]{1,0:T(8,128)(2,1)S(1)}, u32[]{:S(2)}, u32[]{:S(2)}) collective-permute-start(bf16[48,2176]{1,0:T(8,128)(2,1)S(1)} %collective-permute-done.19.refs_1_), channel_id=1, source_target_pairs={{0,448},{32,480},{64,0},{96,32},{128,64},{160,96},{192,128},{224,1... | collective-permute-start | bytes 626696 | tf_op jit(solution)/shard_map/ppermute | solution.py:27
  140.2 5.0 %collective-permute-start.21 = (bf16[48,2176]{1,0:T(8,128)(2,1)S(1)}, bf16[48,2176]{1,0:T(8,128)(2,1)S(1)}, u32[]{:S(2)}, u32[]{:S(2)}) collective-permute-start(bf16[48,2176]{1,0:T(8,128)(2,1)S(1)} %collective-permute-done.20.refs_2_), channel_id=1, source_target_pairs={{0,448},{32,480},{64,0},{96,32},{128,64},{160,96},{192,128},{224,1... | collective-permute-start | bytes 626696 | tf_op jit(solution)/shard_map/ppermute | solution.py:27
  148.0 5.0 %collective-permute-start.26 = (bf16[48,1152]{1,0:T(8,128)(2,1)S(1)}, bf16[48,1152]{1,0:T(8,128)(2,1)S(1)}, u32[]{:S(2)}, u32[]{:S(2)}) collective-permute-start(bf16[48,1152]{1,0:T(8,128)(2,1)S(1)} %slice.218), channel_id=1, source_target_pairs={{0,448},{32,480},{64,0},{96,32},{128,64},{160,96},{192,128},{224,1... | collective-permute-start | bytes 331784 | tf_op jit(solution)/shard_map/ppermute | solution.py:27
  156.4 3.2 %collective-permute-done.25.refs_4_ = bf16[48,1024]{1,0:T(8,128)(2,1)S(1)} collective-permute-done((bf16[48,1024]{1,0:T(8,128)(2,1)S(1)}, bf16[48,1024]{1,0:T(8,128)(2,1)S(1)}, u32[]{:S(2)}, u32[]{:S(2)}) %collective-permute-start.25) | collective-permute-done | bytes 98336 | tf_op jit(solution)/shard_map/ppermute | solution.py:27
  159.6 7.0 %backward.1 = (f32[4,1024]{1,0:T(4,128)S(1)}, f32[128,128]{1,0:T(8,128)S(1)}) custom-call(s32[3]{0:T(128)S(1)} %pad_add_fusion.place_ref, bf16[48,2176]{1,0:T(8,128)(2,1)S(1)} %constant_dynamic-update-slice_fusion.refs_0_, bf16[48,2176]{1,0:T(8,128)(2,1)S(1)} %collective-permute-done.19.refs_1_, bf16[48,2176]{1,0:T(8,128)(2,1)S(1)} %collective-permute-done.20.refs_2_, ...), custom_call_target="tpu_custom_call" | custom-call | tf_op jit(solution)/shard_map/backward/pallas_call | solution.py:372
  166.6 12.4 %all-gather.1 = f32[4,4,1024]{2,1,0:T(4,128)S(1)} all-gather(f32[1,4,1024]{2,1,0:T(4,128)S(1)} %bitcast.85), channel_id=2, replica_groups=mesh['dp'=16,'section'=4,'vocab'=8] {'section'}, dimensions={0}, use_global_device_ids=true | all-gather | bytes 81920 | tf_op jit(solution)/shard_map/all_gather | solution.py:391
  179.7 3.4 %all-to-all-start.1 = ((f32[8,4,1024]{2,1,0:T(4,128)}), f32[8,4,1024]{2,1,0:T(4,128)S(1)}, u32[]{:S(2)}, u32[]{:S(2)}) async-start(f32[8,4,1024]{2,1,0:T(4,128)} %broadcast_in_dim.47), calls=%async_computation.1 | async-start | bytes 262144 | tf_op jit(solution)/shard_map/all_to_all | solution.py:23
  183.7 7.9 %all-to-all-done.1 = f32[8,4,1024]{2,1,0:T(4,128)S(1)} async-done(((f32[8,4,1024]{2,1,0:T(4,128)}), f32[8,4,1024]{2,1,0:T(4,128)S(1)}, u32[]{:S(2)}, u32[]{:S(2)}) %all-to-all-start.1) | async-done | bytes 131104 | tf_op jit(solution)/shard_map/all_to_all | solution.py:23
  (97 shorter events, 32.3 us)
Async XLA Ops:
  0.6 19.3 %collective-permute-start.1 = (bf16[128,1024]{1,0:T(8,128)(2,1)}, bf16[128,1024]{1,0:T(8,128)(2,1)S(1)}, u32[]{:S(2)}, u32[]{:S(2)}) collective-permute-start(bf16[128,1024]{1,0:T(8,128)(2,1)} %bitcast.86), channel_id=1, source_target_pairs={{0,16},{8,24},{16,0},{24,8},{1,17},{9,25},{17,1},{25,9},{2,18},{10... | collective-permute-start | bytes 786440 | tf_op jit(solution)/shard_map/ppermute | solution.py:27
  6.1 13.8 %collective-permute-start = (bf16[128,1024]{1,0:T(8,128)(2,1)}, bf16[128,1024]{1,0:T(8,128)(2,1)S(1)}, u32[]{:S(2)}, u32[]{:S(2)}) collective-permute-start(bf16[128,1024]{1,0:T(8,128)(2,1)} %bitcast.87), channel_id=1, source_target_pairs={{0,8},{8,0},{16,24},{24,16},{1,9},{9,1},{17,25},{25,17},{2,10},{10... | collective-permute-start | bytes 786440 | tf_op jit(solution)/shard_map/ppermute | solution.py:27
  11.4 11.9 %collective-permute-start.2 = (bf16[128,1024]{1,0:T(8,128)(2,1)}, bf16[128,1024]{1,0:T(8,128)(2,1)S(1)}, u32[]{:S(2)}, u32[]{:S(2)}) collective-permute-start(bf16[128,1024]{1,0:T(8,128)(2,1)} %bitcast.88), channel_id=1, source_target_pairs={{0,24},{8,16},{16,8},{24,0},{1,25},{9,17},{17,9},{25,1},{2,26},{10... | collective-permute-start | bytes 786440 | tf_op jit(solution)/shard_map/ppermute | solution.py:27
  29.8 41.8 %copy-start.1 = (f32[32,2176]{1,0:T(8,128)S(1)}, f32[32,2176]{1,0:T(8,128)}, u32[]{:S(2)}) copy-start(f32[32,2176]{1,0:T(8,128)} %get-tuple-element.46) | copy-start | bytes 835588
  29.8 46.4 %copy-start = (f32[32,2176]{1,0:T(8,128)S(1)}, f32[32,2176]{1,0:T(8,128)}, u32[]{:S(2)}) copy-start(f32[32,2176]{1,0:T(8,128)} %get-tuple-element.39) | copy-start | bytes 835588
  29.9 14.1 %collective-permute-start.13 = (f32[32,2176]{1,0:T(8,128)S(1)}, f32[32,2176]{1,0:T(8,128)S(1)}, u32[]{:S(2)}, u32[]{:S(2)}) collective-permute-start(f32[32,2176]{1,0:T(8,128)S(1)} %get-tuple-element.49), channel_id=1, source_target_pairs={{0,448},{32,480},{64,0},{96,32},{128,64},{160,96},{192,128},{224,1... | collective-permute-start | bytes 835592 | tf_op jit(solution)/shard_map/ppermute | solution.py:27
  37.9 14.3 %collective-permute-start.3 = (f32[32,2176]{1,0:T(8,128)S(1)}, f32[32,2176]{1,0:T(8,128)S(1)}, u32[]{:S(2)}, u32[]{:S(2)}) collective-permute-start(f32[32,2176]{1,0:T(8,128)S(1)} %get-tuple-element.38), channel_id=1, source_target_pairs={{0,64},{32,96},{64,128},{96,160},{128,192},{160,224},{192,256},{22... | collective-permute-start | bytes 835592 | tf_op jit(solution)/shard_map/ppermute | solution.py:27
  39.9 15.7 %collective-permute-start.10 = (f32[32,2176]{1,0:T(8,128)S(1)}, f32[32,2176]{1,0:T(8,128)S(1)}, u32[]{:S(2)}, u32[]{:S(2)}) collective-permute-start(f32[32,2176]{1,0:T(8,128)S(1)} %get-tuple-element.45), channel_id=1, source_target_pairs={{0,64},{32,96},{64,128},{96,160},{128,192},{160,224},{192,256},{22... | collective-permute-start | bytes 835592 | tf_op jit(solution)/shard_map/ppermute | solution.py:27
  44.9 12.7 %collective-permute-start.14 = (f32[32,2176]{1,0:T(8,128)S(1)}, f32[32,2176]{1,0:T(8,128)S(1)}, u32[]{:S(2)}, u32[]{:S(2)}) collective-permute-start(f32[32,2176]{1,0:T(8,128)S(1)} %add.125), channel_id=1, source_target_pairs={{0,448},{32,480},{64,0},{96,32},{128,64},{160,96},{192,128},{224,1... | collective-permute-start | bytes 835592 | tf_op jit(solution)/shard_map/ppermute | solution.py:27
  50.2 12.9 %collective-permute-start.7 = (f32[32,2176]{1,0:T(8,128)}, f32[32,2176]{1,0:T(8,128)S(1)}, u32[]{:S(2)}, u32[]{:S(2)}) collective-permute-start(f32[32,2176]{1,0:T(8,128)} %get-tuple-element.41), channel_id=1, source_target_pairs={{0,448},{32,480},{64,0},{96,32},{128,64},{160,96},{192,128},{224,1... | collective-permute-start | bytes 835592 | tf_op jit(solution)/shard_map/ppermute | solution.py:27
  52.2 15.4 %collective-permute-start.4 = (f32[32,2176]{1,0:T(8,128)S(1)}, f32[32,2176]{1,0:T(8,128)S(1)}, u32[]{:S(2)}, u32[]{:S(2)}) collective-permute-start(f32[32,2176]{1,0:T(8,128)S(1)} %add.115), channel_id=1, source_target_pairs={{0,64},{32,96},{64,128},{96,160},{128,192},{160,224},{192,256},{22... | collective-permute-start | bytes 835592 | tf_op jit(solution)/shard_map/ppermute | solution.py:27
  55.6 14.0 %collective-permute-start.11 = (f32[32,2176]{1,0:T(8,128)S(1)}, f32[32,2176]{1,0:T(8,128)S(1)}, u32[]{:S(2)}, u32[]{:S(2)}) collective-permute-start(f32[32,2176]{1,0:T(8,128)S(1)} %add.122), channel_id=1, source_target_pairs={{0,64},{32,96},{64,128},{96,160},{128,192},{160,224},{192,256},{22... | collective-permute-start | bytes 835592 | tf_op jit(solution)/shard_map/ppermute | solution.py:27
  58.6 13.0 %collective-permute-start.15 = (f32[32,2176]{1,0:T(8,128)S(1)}, f32[32,2176]{1,0:T(8,128)S(1)}, u32[]{:S(2)}, u32[]{:S(2)}) collective-permute-start(f32[32,2176]{1,0:T(8,128)S(1)} %add.126), channel_id=1, source_target_pairs={{0,448},{32,480},{64,0},{96,32},{128,64},{160,96},{192,128},{224,1... | collective-permute-start | bytes 835592 | tf_op jit(solution)/shard_map/ppermute | solution.py:27
  64.2 12.1 %collective-permute-start.8 = (f32[32,2176]{1,0:T(8,128)S(1)}, f32[32,2176]{1,0:T(8,128)S(1)}, u32[]{:S(2)}, u32[]{:S(2)}) collective-permute-start(f32[32,2176]{1,0:T(8,128)S(1)} %add.119), channel_id=1, source_target_pairs={{0,448},{32,480},{64,0},{96,32},{128,64},{160,96},{192,128},{224,1... | collective-permute-start | bytes 835592 | tf_op jit(solution)/shard_map/ppermute | solution.py:27
  67.7 12.0 %collective-permute-start.5 = (f32[32,2176]{1,0:T(8,128)S(1)}, f32[32,2176]{1,0:T(8,128)S(1)}, u32[]{:S(2)}, u32[]{:S(2)}) collective-permute-start(f32[32,2176]{1,0:T(8,128)S(1)} %add.116), channel_id=1, source_target_pairs={{0,64},{32,96},{64,128},{96,160},{128,192},{160,224},{192,256},{22... | collective-permute-start | bytes 835592 | tf_op jit(solution)/shard_map/ppermute | solution.py:27
  69.7 13.2 %collective-permute-start.12 = (f32[32,2176]{1,0:T(8,128)S(1)}, f32[32,2176]{1,0:T(8,128)S(1)}, u32[]{:S(2)}, u32[]{:S(2)}) collective-permute-start(f32[32,2176]{1,0:T(8,128)S(1)} %add.123), channel_id=1, source_target_pairs={{0,64},{32,96},{64,128},{96,160},{128,192},{160,224},{192,256},{22... | collective-permute-start | bytes 835592 | tf_op jit(solution)/shard_map/ppermute | solution.py:27
  71.7 11.2 %collective-permute-start.16 = (f32[32,2176]{1,0:T(8,128)S(1)}, f32[32,2176]{1,0:T(8,128)S(1)}, u32[]{:S(2)}, u32[]{:S(2)}) collective-permute-start(f32[32,2176]{1,0:T(8,128)S(1)} %add.127), channel_id=1, source_target_pairs={{0,448},{32,480},{64,0},{96,32},{128,64},{160,96},{192,128},{224,1... | collective-permute-start | bytes 835592 | tf_op jit(solution)/shard_map/ppermute | solution.py:27
  76.3 9.8 %collective-permute-start.9 = (f32[32,2176]{1,0:T(8,128)S(1)}, f32[32,2176]{1,0:T(8,128)S(1)}, u32[]{:S(2)}, u32[]{:S(2)}) collective-permute-start(f32[32,2176]{1,0:T(8,128)S(1)} %add.120), channel_id=1, source_target_pairs={{0,448},{32,480},{64,0},{96,32},{128,64},{160,96},{192,128},{224,1... | collective-permute-start | bytes 835592 | tf_op jit(solution)/shard_map/ppermute | solution.py:27
  79.7 8.5 %collective-permute-start.6 = (f32[32,2176]{1,0:T(8,128)S(1)}, f32[32,2176]{1,0:T(8,128)S(1)}, u32[]{:S(2)}, u32[]{:S(2)}) collective-permute-start(f32[32,2176]{1,0:T(8,128)S(1)} %add.117), channel_id=1, source_target_pairs={{0,64},{32,96},{64,128},{96,160},{128,192},{160,224},{192,256},{22... | collective-permute-start | bytes 835592 | tf_op jit(solution)/shard_map/ppermute | solution.py:27
  83.0 7.6 %collective-permute-start.17 = (f32[32,2176]{1,0:T(8,128)S(1)}, f32[32,2176]{1,0:T(8,128)S(1)}, u32[]{:S(2)}, u32[]{:S(2)}) collective-permute-start(f32[32,2176]{1,0:T(8,128)S(1)} %add_add_fusion), channel_id=1, source_target_pairs={{0,32},{32,0},{64,96},{96,64},{128,160},{160,128},{192,224},{224,1... | collective-permute-start | bytes 835592 | tf_op jit(solution)/shard_map/ppermute | solution.py:27
  117.6 6.0 %collective-permute-start.18 = (bf16[24,2176]{1,0:T(8,128)(2,1)S(1)}, bf16[24,2176]{1,0:T(8,128)(2,1)S(1)}, u32[]{:S(2)}, u32[]{:S(2)}) collective-permute-start(bf16[24,2176]{1,0:T(8,128)(2,1)S(1)} %maximum_maximum_fusion), channel_id=1, source_target_pairs={{0,32},{32,0},{64,96},{96,64},{128,160},{160,128},{192,224},{224,1... | collective-permute-start | bytes 313352 | tf_op jit(solution)/shard_map/ppermute | solution.py:27
  123.6 8.6 %collective-permute-start.19 = (bf16[48,2176]{1,0:T(8,128)(2,1)S(1)}, bf16[48,2176]{1,0:T(8,128)(2,1)S(1)}, u32[]{:S(2)}, u32[]{:S(2)}) collective-permute-start(bf16[48,2176]{1,0:T(8,128)(2,1)S(1)} %constant_dynamic-update-slice_fusion.refs_0_), channel_id=1, source_target_pairs={{0,448},{32,480},{64,0},{96,32},{128,64},{160,96},{192,128},{224,1... | collective-permute-start | bytes 626696 | tf_op jit(solution)/shard_map/ppermute | solution.py:27
  128.9 8.6 %collective-permute-start.22 = (bf16[48,2176]{1,0:T(8,128)(2,1)S(1)}, bf16[48,2176]{1,0:T(8,128)(2,1)S(1)}, u32[]{:S(2)}, u32[]{:S(2)}) collective-permute-start(bf16[48,2176]{1,0:T(8,128)(2,1)S(1)} %constant_dynamic-update-slice_fusion.refs_0_), channel_id=1, source_target_pairs={{0,64},{32,96},{64,128},{96,160},{128,192},{160,224},{192,256},{22... | collective-permute-start | bytes 626696 | tf_op jit(solution)/shard_map/ppermute | solution.py:27
  132.2 8.0 %collective-permute-start.20 = (bf16[48,2176]{1,0:T(8,128)(2,1)S(1)}, bf16[48,2176]{1,0:T(8,128)(2,1)S(1)}, u32[]{:S(2)}, u32[]{:S(2)}) collective-permute-start(bf16[48,2176]{1,0:T(8,128)(2,1)S(1)} %collective-permute-done.19.refs_1_), channel_id=1, source_target_pairs={{0,448},{32,480},{64,0},{96,32},{128,64},{160,96},{192,128},{224,1... | collective-permute-start | bytes 626696 | tf_op jit(solution)/shard_map/ppermute | solution.py:27
  137.5 7.8 %collective-permute-start.23 = (bf16[48,2176]{1,0:T(8,128)(2,1)S(1)}, bf16[48,2176]{1,0:T(8,128)(2,1)S(1)}, u32[]{:S(2)}, u32[]{:S(2)}) collective-permute-start(bf16[48,2176]{1,0:T(8,128)(2,1)S(1)} %collective-permute-done.22.refs_8_), channel_id=1, source_target_pairs={{0,64},{32,96},{64,128},{96,160},{128,192},{160,224},{192,256},{22... | collective-permute-start | bytes 626696 | tf_op jit(solution)/shard_map/ppermute | solution.py:27
  140.2 7.7 %collective-permute-start.21 = (bf16[48,2176]{1,0:T(8,128)(2,1)S(1)}, bf16[48,2176]{1,0:T(8,128)(2,1)S(1)}, u32[]{:S(2)}, u32[]{:S(2)}) collective-permute-start(bf16[48,2176]{1,0:T(8,128)(2,1)S(1)} %collective-permute-done.20.refs_2_), channel_id=1, source_target_pairs={{0,448},{32,480},{64,0},{96,32},{128,64},{160,96},{192,128},{224,1... | collective-permute-start | bytes 626696 | tf_op jit(solution)/shard_map/ppermute | solution.py:27
  145.3 7.8 %collective-permute-start.24 = (bf16[48,2176]{1,0:T(8,128)(2,1)S(1)}, bf16[48,2176]{1,0:T(8,128)(2,1)S(1)}, u32[]{:S(2)}, u32[]{:S(2)}) collective-permute-start(bf16[48,2176]{1,0:T(8,128)(2,1)S(1)} %collective-permute-done.23.refs_7_), channel_id=1, source_target_pairs={{0,64},{32,96},{64,128},{96,160},{128,192},{160,224},{192,256},{22... | collective-permute-start | bytes 626696 | tf_op jit(solution)/shard_map/ppermute | solution.py:27
  148.0 11.6 %collective-permute-start.26 = (bf16[48,1152]{1,0:T(8,128)(2,1)S(1)}, bf16[48,1152]{1,0:T(8,128)(2,1)S(1)}, u32[]{:S(2)}, u32[]{:S(2)}) collective-permute-start(bf16[48,1152]{1,0:T(8,128)(2,1)S(1)} %slice.218), channel_id=1, source_target_pairs={{0,448},{32,480},{64,0},{96,32},{128,64},{160,96},{192,128},{224,1... | collective-permute-start | bytes 331784 | tf_op jit(solution)/shard_map/ppermute | solution.py:27
  153.0 6.6 %collective-permute-start.25 = (bf16[48,1024]{1,0:T(8,128)(2,1)S(1)}, bf16[48,1024]{1,0:T(8,128)(2,1)S(1)}, u32[]{:S(2)}, u32[]{:S(2)}) collective-permute-start(bf16[48,1024]{1,0:T(8,128)(2,1)S(1)} %slice.217), channel_id=1, source_target_pairs={{0,64},{32,96},{64,128},{96,160},{128,192},{160,224},{192,256},{22... | collective-permute-start | bytes 294920 | tf_op jit(solution)/shard_map/ppermute | solution.py:27
  179.7 11.9 %all-to-all-start.1 = ((f32[8,4,1024]{2,1,0:T(4,128)}), f32[8,4,1024]{2,1,0:T(4,128)S(1)}, u32[]{:S(2)}, u32[]{:S(2)}) async-start(f32[8,4,1024]{2,1,0:T(4,128)} %broadcast_in_dim.47), calls=%async_computation.1 | async-start | bytes 262144 | tf_op jit(solution)/shard_map/all_to_all | solution.py:23
  191.7 0.6 copy-start.2

commit v7 on v6

--- a/solution.py
+++ b/solution.py
@@ -51,16 +51,6 @@
                 held[h] = ring(made if held[h] is None else made + held[h], sign)
     own, other = (term(0, h) + ups[h] + downs[h] for h in range(PAIR))
     return own + swap(other)
-
-
-def gather_over_dp(block):
-    own = jnp.concatenate([block, swap(block)], axis=0)
-    seven, one = ring(own, 1), ring(own, -1)
-    six, two = ring(seven, 1), ring(one, -1)
-    five, three = ring(six, 1), ring(two, -1)
-    cut = block.shape[1] // LANES // 2 * LANES
-    four = ring(five[:, :cut], 1), ring(three[:, cut:], -1)
-    return [own, one, two, three, *four, five, six, seven]
 
 
 def parts(a):
@@ -162,85 +152,58 @@
             out[:, c * tall : (c + 1) * tall] = made[q * size : (q + 1) * size]
 
 
-def arrange(n_z, block, place_ref, gains_ref, gain_ref, *refs):
-    rows, (near_ref, back1_ref, back2_ref, layers_ref, m0, m1, m2, m3) = refs[:-8], refs[-8:]
+def backward(block, shards, place_ref, blocks_ref, head_ref, gains_ref, gain_ref, *refs):
+    rows, (grads_ref, known_ref, near, back1, back2, dh, acc, held, sems) = refs[:-9], refs[-9:]
+    vocab, cols = head_ref.shape
+    tall = vocab // TILES
+    copies = [
+        pltpu.make_async_copy(
+            head_ref.at[pl.ds(c * tall, tall)], held.at[pl.ds(c * tall, tall)], sems.at[c]
+        )
+        for c in range(TILES)
+    ]
+    copies[0].start()
+    copies[1].start()
     united = united_of(place_ref, rows, gains_ref)
     gain = gain_ref[...]
     once = united * gain
-    m0[...] = united
-    m1[...] = shifted(once, 1)
-    m2[...] = shifted(once * gain, 2)
-
-    def ordered(source):
-        for i in range(n_z):
-            yield (
-                slice(i * PAIR * block, (i + 1) * PAIR * block),
-                jnp.concatenate(
-                    [
-                        source[pl.ds(token_of(place_ref, i, h, n_z, block), block), :]
-                        for h in range(PAIR)
-                    ],
-                    axis=0,
-                ),
-            )
-
-    for source, out in ((m0, near_ref), (m1, back1_ref), (m2, back2_ref)):
-        for at, a in ordered(source):
-            out[at, :] = a
-    for j, row in enumerate(rows):
-        m3[...] = row[...].astype(F32)
-        for at, a in ordered(m3):
-            layers_ref[j, at, :] = a.astype(BF16)
-
-
-def backward(n_z, block, shards, place_ref, *refs):
-    blocks, (head_ref, near_ref, back1_ref, back2_ref, layers_ref, gain_ref) = refs[:9], refs[9:15]
-    grads_ref, known_ref, lhs, dh, aux, acc, held, sems = refs[15:]
-    vocab, cols = head_ref.shape
-    wide = cols // TILES
-    tiles = [(slice(None), pl.ds(c * wide, wide)) for c in range(TILES)]
-    copies = brought(head_ref, held, sems, tiles)
-    size = PAIR * STEPS * block
-    spots = [0, 1, 2, 3, 4, 4, 5, 6, 7]
-    for b, (spot, ref) in enumerate(zip(spots, blocks, strict=True)):
-        at = slice(spot * size, (spot + 1) * size)
-        if b == 4:
-            cut = ref.shape[1]
-            lhs[at, :cut] = ref[...]
-            continue
-        start = cut if b == 5 else 0
-        lhs[at, start:] = ref[:, : vocab - start]
-        tail = ref[:, vocab - start :].astype(F32)
-        for h in range(PAIR):
-            three = [tail[(h * 3 + p) * block : (h * 3 + p + 1) * block] for p in range(3)]
-            known = three[0] + three[1] + three[2]
-            aux[(spot * PAIR + h) * block : (spot * PAIR + h + 1) * block, :] = known
-            known_ref[pl.ds(token_of(place_ref, spot, h, n_z, block), block), :] = known
+    near[...] = united
+    back1[...] = shifted(once, 1)
+    back2[...] = shifted(once * gain, 2)
+    tail = blocks_ref[:, vocab:].astype(F32)
+    for j in range(near.shape[0] // block):
+        three = [tail[(j * STEPS + p) * block : (j * STEPS + p + 1) * block] for p in range(STEPS)]
+        known_ref[j * block : (j + 1) * block, :] = three[0] + three[1] + three[2]
 
     for c, copy in enumerate(copies):
         copy.wait()
-        at = slice(c * wide, (c + 1) * wide)
-        dh[:, at] = jnp.dot(lhs[...], held[:, at], preferred_element_type=F32)
+        if c + 2 < TILES:
+            copies[c + 2].start()
+        at = slice(c * tall, (c + 1) * tall)
+        made = jnp.dot(blocks_ref[:, at], held[at, :], preferred_element_type=F32)
+        if c == 0:
+            dh[...] = made
+        else:
+            dh[...] += made
 
     acc[...] = jnp.zeros_like(acc)
-    gain = gain_ref[...]
-    count = layers_ref.shape[0]
-
-    @pl.loop(0, n_z)
+    count = len(rows)
+
+    @pl.loop(0, near.shape[0] // (PAIR * block))
     def _(i):
         pair = pl.multiple_of(i * PAIR * block, PAIR * block)
-        layers = [layers_ref[j, pl.ds(pair, PAIR * block), :].astype(F32) for j in range(count)]
+        layers = [row[pl.ds(pair, PAIR * block), :].astype(F32) for row in rows]
         for h in range(PAIR):
             mine = pl.ds(pl.multiple_of(pair + h * block, block), block)
-            known = aux[mine, :]
+            known = known_ref[mine, :]
             i1, i2, i3, a2, a3, b3, c1, c2, c3 = (
                 known[:, j : j + 1] for j in (0, 1, 2, 3, 4, 5, 9, 10, 11)
             )
-            u, v1, v2 = near_ref[mine, :], back1_ref[mine, :], back2_ref[mine, :]
+            u, v1, v2 = near[mine, :], back1[mine, :], back2[mine, :]
             xs = (u, u + a2 * v1, u + a3 * v1 + b3 * v2)
             outer, to_norm = 0.0, 0.0
             for k, (v, r, c) in enumerate(zip(xs, (i1, i2, i3), (c1, c2, c3), strict=True)):
-                start = pl.multiple_of(i * size + (h * STEPS + k) * block, block)
+                start = pl.multiple_of(((i * PAIR + h) * STEPS + k) * block, block)
                 d = dh[pl.ds(start, block), :]
                 normed = v * r
                 to_norm = to_norm + d * normed
@@ -356,37 +319,24 @@
     message = jnp.concatenate(
         [jnp.concatenate(dlogits, axis=0), jnp.concatenate(parts(known), axis=0)], axis=1
     )
-    ordered = jax.ShapeDtypeStruct((tokens, cols), F32)
-    tied = lax.optimization_barrier((message, *rows))
-    near, back1, back2, layers = pl.pallas_call(
-        functools.partial(arrange, n_z, block),
-        out_shape=(ordered,) * 3 + (jax.ShapeDtypeStruct((n_section, tokens, cols), BF16),),
-        in_specs=[smem] + [vmem] * (2 + n_section),
-        out_specs=(vmem,) * 4,
-        scratch_shapes=[whole] * 4,
-        compiler_params=pltpu.CompilerParams(vmem_limit_bytes=16 * MIB),
-        name="arrange",
-    )(where, gains, gain, *tied[1:])
-
-    blocks = gather_over_dp(tied[0])
+    blocks = exchange(message, "dp").reshape(STEPS * tokens, across)
     grads, known = pl.pallas_call(
-        functools.partial(backward, n_z, block, shards),
+        functools.partial(backward, block, shards),
         out_shape=(
             jax.ShapeDtypeStruct((n_section, cols), F32),
             jax.ShapeDtypeStruct((tokens, LANES), F32),
         ),
-        in_specs=[smem] + [vmem] * 9 + [hbm] + [vmem] * 5,
+        in_specs=[smem, vmem, hbm] + [vmem] * (2 + n_section),
         out_specs=(vmem, vmem),
-        scratch_shapes=[
-            pltpu.VMEM((STEPS * tokens, vocab), BF16),
+        scratch_shapes=[whole] * 3
+        + [
             pltpu.VMEM((STEPS * tokens, cols), F32),
-            pltpu.VMEM((tokens, LANES), F32),
             pltpu.VMEM(((n_section + 1) * block, cols), F32),
-            *held,
-        ],
+        ]
+        + held,
         compiler_params=pltpu.CompilerParams(vmem_limit_bytes=48 * MIB),
         name="backward",
-    )(where, *blocks, head, near, back1, back2, layers, gain)
+    )(where, blocks, head, gains, gain, *rows)
     step_loss = jnp.sum(known[:, 6:9], axis=0) / tokens
     grads = jnp.sum(lax.all_gather(grads, "section"), axis=0)
     grads = jnp.sum(exchange(grads, "vocab"), axis=0)

time: 193 us -> 191 us (0.990)
  blocking collectives: 35.8 us -> 77.9 us
  starting transfers between devices: 98.3 us -> 68.6 us
  waiting for transfers between devices: 29.8 us -> 20.1 us
  Pallas kernels: 15 us -> 12 us
    all_to_all x1 -> x2, blocking collectives: 23.3 us -> 69.5 us  [exchange(): return lax.all_to_all(jnp.broadcast_to(a[None], (n,) + a.shape), axis, 0, 0)]
    ppermute x27 -> x18, starting transfers between devices: 94.9 us -> 65.2 us  [permute(): lax.ppermute(a, axis, [(i, to(i)) for i in range(lax.axis_size(axis))])]
    ppermute x27 -> x18, waiting for transfers between devices: 21.9 us -> 12.2 us  [permute(): lax.ppermute(a, axis, [(i, to(i)) for i in range(lax.axis_size(axis))])]
    all_gather x1, blocking collectives: 12.4 us -> 8.43 us  [on_device(): grads = jnp.sum(lax.all_gather(grads, 'section'), axis=0)]
    pallas_call x2 -> x1, Pallas kernels: 8.41 us -> 5.44 us  [on_device(): pl.pallas_call(functools.partial(backward, block, shards), out_shape=(jax...]
  transfers between devices with their start and end apart: 28 -> 19, of which waited for: 12 -> 7; matrix products, arithmetic and copies ran while one was open for 4% -> 3% of each run, Pallas kernels for 1% -> 0%
where the time goes in v7:
time: 191 us; the launch traced here: 190 us
  blocking collectives  77.9 us (41%)
  starting transfers between devices  68.6 us (36%)
  waiting for transfers between devices  20.1 us (11%)
  Pallas kernels  12 us (6%)
  other arithmetic  6.91 us (4%)
  local copies, waits for them, and re-layouts  3.58 us (2%)
    all_to_all x2, blocking collectives, exchange(): return lax.all_to_all(jnp.broadcast_to(a[None], (n,) + a.shape), axis, 0, 0)  69.5 us
    ppermute x18, starting transfers between devices, permute(): lax.ppermute(a, axis, [(i, to(i)) for i in range(lax.axis_size(axis))])  65.2 us
    ppermute x18, waiting for transfers between devices, permute(): lax.ppermute(a, axis, [(i, to(i)) for i in range(lax.axis_size(axis))])  12.2 us
    all_gather x1, blocking collectives, on_device(): grads = jnp.sum(lax.all_gather(grads, 'section'), axis=0)  8.43 us
    all_to_all x1, waiting for transfers between devices, exchange(): return lax.all_to_all(jnp.broadcast_to(a[None], (n,) + a.shape), axis, 0, 0)  7.93 us
    pallas_call x1, Pallas kernels, on_device(): pl.pallas_call(functools.partial(forward, n_z, block, n_dp), out_shape=[j...  6.55 us
    pallas_call x1, Pallas kernels, on_device(): pl.pallas_call(functools.partial(backward, block, shards), out_shape=(jax...  5.44 us
  transfers between devices with their start and end apart: 19, of which 7 were waited for; matrix products, arithmetic and copies ran while one was open for 3% of the time, Pallas kernels for 0%

profile of v7, /device:TPU:1, one launch (start us, length us, event | category | flops | bytes accessed | tf_op | source)
XLA Modules:
  0.0 190.1 jit_solution(5166446555616274184)
XLA Ops:
  0.6 5.5 %collective-permute-start.1 = (bf16[128,1024]{1,0:T(8,128)(2,1)}, bf16[128,1024]{1,0:T(8,128)(2,1)S(1)}, u32[]{:S(2)}, u32[]{:S(2)}) collective-permute-start(bf16[128,1024]{1,0:T(8,128)(2,1)} %bitcast.87), channel_id=1, source_target_pairs={{0,16},{8,24},{16,0},{24,8},{1,17},{9,25},{17,1},{25,9},{2,18},{10... | collective-permute-start | bytes 786440 | tf_op jit(solution)/shard_map/ppermute | solution.py:27
  6.1 5.2 %collective-permute-start = (bf16[128,1024]{1,0:T(8,128)(2,1)}, bf16[128,1024]{1,0:T(8,128)(2,1)S(1)}, u32[]{:S(2)}, u32[]{:S(2)}) collective-permute-start(bf16[128,1024]{1,0:T(8,128)(2,1)} %bitcast.88), channel_id=1, source_target_pairs={{0,8},{8,0},{16,24},{24,16},{1,9},{9,1},{17,25},{25,17},{2,10},{10... | collective-permute-start | bytes 786440 | tf_op jit(solution)/shard_map/ppermute | solution.py:27
  11.4 5.0 %collective-permute-start.2 = (bf16[128,1024]{1,0:T(8,128)(2,1)}, bf16[128,1024]{1,0:T(8,128)(2,1)S(1)}, u32[]{:S(2)}, u32[]{:S(2)}) collective-permute-start(bf16[128,1024]{1,0:T(8,128)(2,1)} %bitcast.89), channel_id=1, source_target_pairs={{0,24},{8,16},{16,8},{24,0},{1,25},{9,17},{17,9},{25,1},{2,26},{10... | collective-permute-start | bytes 786440 | tf_op jit(solution)/shard_map/ppermute | solution.py:27
  19.9 3.4 %collective-permute-done.2.refs_3_ = bf16[128,1024]{1,0:T(8,128)(2,1)S(1)} collective-permute-done((bf16[128,1024]{1,0:T(8,128)(2,1)}, bf16[128,1024]{1,0:T(8,128)(2,1)S(1)}, u32[]{:S(2)}, u32[]{:S(2)}) %collective-permute-start.2) | collective-permute-done | bytes 262176 | tf_op jit(solution)/shard_map/ppermute | solution.py:27
  23.3 6.5 %forward.1 = (f32[32,2176]{1,0:T(8,128)S(1)}, f32[32,2176]{1,0:T(8,128)S(1)}, f32[32,2176]{1,0:T(8,128)S(1)}, f32[32,2176]{1,0:T(8,128)S(1)}, f32[32,2176]{1,0:T...) custom-call(s32[3]{0:T(128)S(1)} %pad_add_fusion.place_ref, ...), custom_call_target="tpu_custom_call" | custom-call | tf_op jit(solution)/shard_map/forward/pallas_call | solution.py:253
  29.8 8.1 %collective-permute-start.13 = (f32[32,2176]{1,0:T(8,128)S(1)}, f32[32,2176]{1,0:T(8,128)S(1)}, u32[]{:S(2)}, u32[]{:S(2)}) collective-permute-start(f32[32,2176]{1,0:T(8,128)S(1)} %get-tuple-element.40), channel_id=1, source_target_pairs={{0,448},{32,480},{64,0},{96,32},{128,64},{160,96},{192,128},{224,1... | collective-permute-start | bytes 835592 | tf_op jit(solution)/shard_map/ppermute | solution.py:27
  37.9 1.9 %collective-permute-start.3 = (f32[32,2176]{1,0:T(8,128)S(1)}, f32[32,2176]{1,0:T(8,128)S(1)}, u32[]{:S(2)}, u32[]{:S(2)}) collective-permute-start(f32[32,2176]{1,0:T(8,128)S(1)} %get-tuple-element.29), channel_id=1, source_target_pairs={{0,64},{32,96},{64,128},{96,160},{128,192},{160,224},{192,256},{22... | collective-permute-start | bytes 835592 | tf_op jit(solution)/shard_map/ppermute | solution.py:27
  39.8 1.9 %collective-permute-start.10 = (f32[32,2176]{1,0:T(8,128)S(1)}, f32[32,2176]{1,0:T(8,128)S(1)}, u32[]{:S(2)}, u32[]{:S(2)}) collective-permute-start(f32[32,2176]{1,0:T(8,128)S(1)} %get-tuple-element.36), channel_id=1, source_target_pairs={{0,64},{32,96},{64,128},{96,160},{128,192},{160,224},{192,256},{22... | collective-permute-start | bytes 835592 | tf_op jit(solution)/shard_map/ppermute | solution.py:27
  41.8 2.1 %collective-permute-done.13 = f32[32,2176]{1,0:T(8,128)S(1)} collective-permute-done((f32[32,2176]{1,0:T(8,128)S(1)}, f32[32,2176]{1,0:T(8,128)S(1)}, u32[]{:S(2)}, u32[]{:S(2)}) %collective-permute-start.13) | collective-permute-done | bytes 278560 | tf_op jit(solution)/shard_map/ppermute | solution.py:27
  43.9 1.0 add.125
  45.0 5.3 %collective-permute-start.14 = (f32[32,2176]{1,0:T(8,128)S(1)}, f32[32,2176]{1,0:T(8,128)S(1)}, u32[]{:S(2)}, u32[]{:S(2)}) collective-permute-start(f32[32,2176]{1,0:T(8,128)S(1)} %add.125), channel_id=1, source_target_pairs={{0,448},{32,480},{64,0},{96,32},{128,64},{160,96},{192,128},{224,1... | collective-permute-start | bytes 835592 | tf_op jit(solution)/shard_map/ppermute | solution.py:27
  50.3 1.9 %collective-permute-start.7 = (f32[32,2176]{1,0:T(8,128)}, f32[32,2176]{1,0:T(8,128)S(1)}, u32[]{:S(2)}, u32[]{:S(2)}) collective-permute-start(f32[32,2176]{1,0:T(8,128)} %get-tuple-element.32), channel_id=1, source_target_pairs={{0,448},{32,480},{64,0},{96,32},{128,64},{160,96},{192,128},{224,1... | collective-permute-start | bytes 835592 | tf_op jit(solution)/shard_map/ppermute | solution.py:27
  52.3 3.4 %collective-permute-start.4 = (f32[32,2176]{1,0:T(8,128)S(1)}, f32[32,2176]{1,0:T(8,128)S(1)}, u32[]{:S(2)}, u32[]{:S(2)}) collective-permute-start(f32[32,2176]{1,0:T(8,128)S(1)} %add.115), channel_id=1, source_target_pairs={{0,64},{32,96},{64,128},{96,160},{128,192},{160,224},{192,256},{22... | collective-permute-start | bytes 835592 | tf_op jit(solution)/shard_map/ppermute | solution.py:27
  55.7 1.9 %collective-permute-start.11 = (f32[32,2176]{1,0:T(8,128)S(1)}, f32[32,2176]{1,0:T(8,128)S(1)}, u32[]{:S(2)}, u32[]{:S(2)}) collective-permute-start(f32[32,2176]{1,0:T(8,128)S(1)} %add.122), channel_id=1, source_target_pairs={{0,64},{32,96},{64,128},{96,160},{128,192},{160,224},{192,256},{22... | collective-permute-start | bytes 835592 | tf_op jit(solution)/shard_map/ppermute | solution.py:27
  57.7 4.7 %collective-permute-start.15 = (f32[32,2176]{1,0:T(8,128)S(1)}, f32[32,2176]{1,0:T(8,128)S(1)}, u32[]{:S(2)}, u32[]{:S(2)}) collective-permute-start(f32[32,2176]{1,0:T(8,128)S(1)} %add.126), channel_id=1, source_target_pairs={{0,448},{32,480},{64,0},{96,32},{128,64},{160,96},{192,128},{224,1... | collective-permute-start | bytes 835592 | tf_op jit(solution)/shard_map/ppermute | solution.py:27
  62.5 4.4 %collective-permute-start.8 = (f32[32,2176]{1,0:T(8,128)S(1)}, f32[32,2176]{1,0:T(8,128)S(1)}, u32[]{:S(2)}, u32[]{:S(2)}) collective-permute-start(f32[32,2176]{1,0:T(8,128)S(1)} %add.119), channel_id=1, source_target_pairs={{0,448},{32,480},{64,0},{96,32},{128,64},{160,96},{192,128},{224,1... | collective-permute-start | bytes 835592 | tf_op jit(solution)/shard_map/ppermute | solution.py:27
  66.9 1.9 %collective-permute-start.5 = (f32[32,2176]{1,0:T(8,128)S(1)}, f32[32,2176]{1,0:T(8,128)S(1)}, u32[]{:S(2)}, u32[]{:S(2)}) collective-permute-start(f32[32,2176]{1,0:T(8,128)S(1)} %add.116), channel_id=1, source_target_pairs={{0,64},{32,96},{64,128},{96,160},{128,192},{160,224},{192,256},{22... | collective-permute-start | bytes 835592 | tf_op jit(solution)/shard_map/ppermute | solution.py:27
  68.9 1.9 %collective-permute-start.12 = (f32[32,2176]{1,0:T(8,128)S(1)}, f32[32,2176]{1,0:T(8,128)S(1)}, u32[]{:S(2)}, u32[]{:S(2)}) collective-permute-start(f32[32,2176]{1,0:T(8,128)S(1)} %add.123), channel_id=1, source_target_pairs={{0,64},{32,96},{64,128},{96,160},{128,192},{160,224},{192,256},{22... | collective-permute-start | bytes 835592 | tf_op jit(solution)/shard_map/ppermute | solution.py:27
  70.9 4.6 %collective-permute-start.16 = (f32[32,2176]{1,0:T(8,128)S(1)}, f32[32,2176]{1,0:T(8,128)S(1)}, u32[]{:S(2)}, u32[]{:S(2)}) collective-permute-start(f32[32,2176]{1,0:T(8,128)S(1)} %add.127), channel_id=1, source_target_pairs={{0,448},{32,480},{64,0},{96,32},{128,64},{160,96},{192,128},{224,1... | collective-permute-start | bytes 835592 | tf_op jit(solution)/shard_map/ppermute | solution.py:27
  75.5 3.4 %collective-permute-start.9 = (f32[32,2176]{1,0:T(8,128)S(1)}, f32[32,2176]{1,0:T(8,128)S(1)}, u32[]{:S(2)}, u32[]{:S(2)}) collective-permute-start(f32[32,2176]{1,0:T(8,128)S(1)} %add.120), channel_id=1, source_target_pairs={{0,448},{32,480},{64,0},{96,32},{128,64},{160,96},{192,128},{224,1... | collective-permute-start | bytes 835592 | tf_op jit(solution)/shard_map/ppermute | solution.py:27
  78.9 1.9 %collective-permute-start.6 = (f32[32,2176]{1,0:T(8,128)S(1)}, f32[32,2176]{1,0:T(8,128)S(1)}, u32[]{:S(2)}, u32[]{:S(2)}) collective-permute-start(f32[32,2176]{1,0:T(8,128)S(1)} %add.117), channel_id=1, source_target_pairs={{0,64},{32,96},{64,128},{96,160},{128,192},{160,224},{192,256},{22... | collective-permute-start | bytes 835592 | tf_op jit(solution)/shard_map/ppermute | solution.py:27
  80.9 1.3 collective-permute-done.12
  82.2 2.2 %collective-permute-start.17 = (f32[32,2176]{1,0:T(8,128)S(1)}, f32[32,2176]{1,0:T(8,128)S(1)}, u32[]{:S(2)}, u32[]{:S(2)}) collective-permute-start(f32[32,2176]{1,0:T(8,128)S(1)} %add_add_fusion), channel_id=1, source_target_pairs={{0,32},{32,0},{64,96},{96,64},{128,160},{160,128},{192,224},{224,1... | collective-permute-start | bytes 835592 | tf_op jit(solution)/shard_map/ppermute | solution.py:27
  84.4 1.2 collective-permute-done.9
  85.6 1.8 collective-permute-done.6
  87.4 2.3 %collective-permute-done.17 = f32[32,2176]{1,0:T(8,128)S(1)} collective-permute-done((f32[32,2176]{1,0:T(8,128)S(1)}, f32[32,2176]{1,0:T(8,128)S(1)}, u32[]{:S(2)}, u32[]{:S(2)}) %collective-permute-start.17) | collective-permute-done | bytes 278560 | tf_op jit(solution)/shard_map/ppermute | solution.py:27
  91.2 22.7 %all_to_all.15 = f32[32,8,14]{2,1,0:T(8,128)S(1)} all-to-all(f32[32,8,14]{2,1,0:T(8,128)S(1)} %broadcast_in_dim.52), channel_id=1, replica_groups=mesh['dp'=16,'section'=4,'vocab'=8] {'section','vocab'}, dimensions={0} | all-to-all | bytes 28672 | tf_op jit(solution)/shard_map/all_to_all | solution.py:23
  116.2 46.8 %all_to_all.16 = bf16[16,24,2176]{2,1,0:T(8,128)(2,1)S(1)} all-to-all(bf16[16,24,2176]{2,1,0:T(8,128)(2,1)S(1)} %broadcast_in_dim.53), channel_id=1, replica_groups=mesh['dp'=16,'section'=4,'vocab'=8] {'dp'}, dimensions={0} | all-to-all | bytes 3342336 | tf_op jit(solution)/shard_map/all_to_all | solution.py:23
  163.0 5.4 %backward.1 = (f32[4,1024]{1,0:T(4,128)S(1)}, f32[128,128]{1,0:T(8,128)S(1)}) custom-call(s32[3]{0:T(128)S(1)} %pad_add_fusion.place_ref, bf16[384,2176]{1,0:T(8,128)(2,1)S(1)} %bitcast.83, bf16[2048,1024]{1,0:T(8,128)(2,1)} %head_ref.3, f32[4,1024]{1,0:T(4,128)S(1)} %concatenate.22.gains_ref, f32[1,1024]{1,0:T(1,128)S(1)} %bitcast.85, ...), custom_call_target="tpu_custom_call" | custom-call | tf_op jit(solution)/shard_map/backward/pallas_call | solution.py:323
  168.5 8.4 %all-gather.1 = f32[4,4,1024]{2,1,0:T(4,128)S(1)} all-gather(f32[1,4,1024]{2,1,0:T(4,128)S(1)} %bitcast.86), channel_id=2, replica_groups=mesh['dp'=16,'section'=4,'vocab'=8] {'section'}, dimensions={0}, use_global_device_ids=true | all-gather | bytes 81920 | tf_op jit(solution)/shard_map/all_gather | solution.py:341
  177.6 3.4 %all-to-all-start.2 = ((f32[8,4,1024]{2,1,0:T(4,128)}), f32[8,4,1024]{2,1,0:T(4,128)S(1)}, u32[]{:S(2)}, u32[]{:S(2)}) async-start(f32[8,4,1024]{2,1,0:T(4,128)} %broadcast_in_dim.54), calls=%async_computation.2 | async-start | bytes 262144 | tf_op jit(solution)/shard_map/all_to_all | solution.py:23
  181.6 7.9 %all-to-all-done.2 = f32[8,4,1024]{2,1,0:T(4,128)S(1)} async-done(((f32[8,4,1024]{2,1,0:T(4,128)}), f32[8,4,1024]{2,1,0:T(4,128)S(1)}, u32[]{:S(2)}, u32[]{:S(2)}) %all-to-all-start.2) | async-done | bytes 131104 | tf_op jit(solution)/shard_map/all_to_all | solution.py:23
  (80 shorter events, 9.5 us)
Async XLA Ops:
  0.6 19.3 %collective-permute-start.1 = (bf16[128,1024]{1,0:T(8,128)(2,1)}, bf16[128,1024]{1,0:T(8,128)(2,1)S(1)}, u32[]{:S(2)}, u32[]{:S(2)}) collective-permute-start(bf16[128,1024]{1,0:T(8,128)(2,1)} %bitcast.87), channel_id=1, source_target_pairs={{0,16},{8,24},{16,0},{24,8},{1,17},{9,25},{17,1},{25,9},{2,18},{10... | collective-permute-start | bytes 786440 | tf_op jit(solution)/shard_map/ppermute | solution.py:27
  6.1 13.8 %collective-permute-start = (bf16[128,1024]{1,0:T(8,128)(2,1)}, bf16[128,1024]{1,0:T(8,128)(2,1)S(1)}, u32[]{:S(2)}, u32[]{:S(2)}) collective-permute-start(bf16[128,1024]{1,0:T(8,128)(2,1)} %bitcast.88), channel_id=1, source_target_pairs={{0,8},{8,0},{16,24},{24,16},{1,9},{9,1},{17,25},{25,17},{2,10},{10... | collective-permute-start | bytes 786440 | tf_op jit(solution)/shard_map/ppermute | solution.py:27
  11.4 11.9 %collective-permute-start.2 = (bf16[128,1024]{1,0:T(8,128)(2,1)}, bf16[128,1024]{1,0:T(8,128)(2,1)S(1)}, u32[]{:S(2)}, u32[]{:S(2)}) collective-permute-start(bf16[128,1024]{1,0:T(8,128)(2,1)} %bitcast.89), channel_id=1, source_target_pairs={{0,24},{8,16},{16,8},{24,0},{1,25},{9,17},{17,9},{25,1},{2,26},{10... | collective-permute-start | bytes 786440 | tf_op jit(solution)/shard_map/ppermute | solution.py:27
  29.8 27.8 %copy-start.3 = (f32[32,2176]{1,0:T(8,128)S(1)}, f32[32,2176]{1,0:T(8,128)}, u32[]{:S(2)}) copy-start(f32[32,2176]{1,0:T(8,128)} %get-tuple-element.38) | copy-start | bytes 835588
  29.8 14.1 %collective-permute-start.13 = (f32[32,2176]{1,0:T(8,128)S(1)}, f32[32,2176]{1,0:T(8,128)S(1)}, u32[]{:S(2)}, u32[]{:S(2)}) collective-permute-start(f32[32,2176]{1,0:T(8,128)S(1)} %get-tuple-element.40), channel_id=1, source_target_pairs={{0,448},{32,480},{64,0},{96,32},{128,64},{160,96},{192,128},{224,1... | collective-permute-start | bytes 835592 | tf_op jit(solution)/shard_map/ppermute | solution.py:27
  37.9 14.3 %collective-permute-start.3 = (f32[32,2176]{1,0:T(8,128)S(1)}, f32[32,2176]{1,0:T(8,128)S(1)}, u32[]{:S(2)}, u32[]{:S(2)}) collective-permute-start(f32[32,2176]{1,0:T(8,128)S(1)} %get-tuple-element.29), channel_id=1, source_target_pairs={{0,64},{32,96},{64,128},{96,160},{128,192},{160,224},{192,256},{22... | collective-permute-start | bytes 835592 | tf_op jit(solution)/shard_map/ppermute | solution.py:27
  39.8 15.8 %collective-permute-start.10 = (f32[32,2176]{1,0:T(8,128)S(1)}, f32[32,2176]{1,0:T(8,128)S(1)}, u32[]{:S(2)}, u32[]{:S(2)}) collective-permute-start(f32[32,2176]{1,0:T(8,128)S(1)} %get-tuple-element.36), channel_id=1, source_target_pairs={{0,64},{32,96},{64,128},{96,160},{128,192},{160,224},{192,256},{22... | collective-permute-start | bytes 835592 | tf_op jit(solution)/shard_map/ppermute | solution.py:27
  43.9 18.5 %copy-start.2 = (f32[32,2176]{1,0:T(8,128)S(1)}, f32[32,2176]{1,0:T(8,128)}, u32[]{:S(2)}) copy-start(f32[32,2176]{1,0:T(8,128)} %get-tuple-element.31) | copy-start | bytes 835588
  45.0 12.7 %collective-permute-start.14 = (f32[32,2176]{1,0:T(8,128)S(1)}, f32[32,2176]{1,0:T(8,128)S(1)}, u32[]{:S(2)}, u32[]{:S(2)}) collective-permute-start(f32[32,2176]{1,0:T(8,128)S(1)} %add.125), channel_id=1, source_target_pairs={{0,448},{32,480},{64,0},{96,32},{128,64},{160,96},{192,128},{224,1... | collective-permute-start | bytes 835592 | tf_op jit(solution)/shard_map/ppermute | solution.py:27
  50.3 12.1 %collective-permute-start.7 = (f32[32,2176]{1,0:T(8,128)}, f32[32,2176]{1,0:T(8,128)S(1)}, u32[]{:S(2)}, u32[]{:S(2)}) collective-permute-start(f32[32,2176]{1,0:T(8,128)} %get-tuple-element.32), channel_id=1, source_target_pairs={{0,448},{32,480},{64,0},{96,32},{128,64},{160,96},{192,128},{224,1... | collective-permute-start | bytes 835592 | tf_op jit(solution)/shard_map/ppermute | solution.py:27
  52.3 14.6 %collective-permute-start.4 = (f32[32,2176]{1,0:T(8,128)S(1)}, f32[32,2176]{1,0:T(8,128)S(1)}, u32[]{:S(2)}, u32[]{:S(2)}) collective-permute-start(f32[32,2176]{1,0:T(8,128)S(1)} %add.115), channel_id=1, source_target_pairs={{0,64},{32,96},{64,128},{96,160},{128,192},{160,224},{192,256},{22... | collective-permute-start | bytes 835592 | tf_op jit(solution)/shard_map/ppermute | solution.py:27
  55.7 13.2 %collective-permute-start.11 = (f32[32,2176]{1,0:T(8,128)S(1)}, f32[32,2176]{1,0:T(8,128)S(1)}, u32[]{:S(2)}, u32[]{:S(2)}) collective-permute-start(f32[32,2176]{1,0:T(8,128)S(1)} %add.122), channel_id=1, source_target_pairs={{0,64},{32,96},{64,128},{96,160},{128,192},{160,224},{192,256},{22... | collective-permute-start | bytes 835592 | tf_op jit(solution)/shard_map/ppermute | solution.py:27
  57.6 13.2 %copy-start.1 = (f32[32,2176]{1,0:T(8,128)S(1)}, f32[32,2176]{1,0:T(8,128)}, u32[]{:S(2)}) copy-start(f32[32,2176]{1,0:T(8,128)} %get-tuple-element.37) | copy-start | bytes 835588
  57.7 13.1 %collective-permute-start.15 = (f32[32,2176]{1,0:T(8,128)S(1)}, f32[32,2176]{1,0:T(8,128)S(1)}, u32[]{:S(2)}, u32[]{:S(2)}) collective-permute-start(f32[32,2176]{1,0:T(8,128)S(1)} %add.126), channel_id=1, source_target_pairs={{0,448},{32,480},{64,0},{96,32},{128,64},{160,96},{192,128},{224,1... | collective-permute-start | bytes 835592 | tf_op jit(solution)/shard_map/ppermute | solution.py:27
  62.4 13.1 %copy-start = (f32[32,2176]{1,0:T(8,128)S(1)}, f32[32,2176]{1,0:T(8,128)}, u32[]{:S(2)}) copy-start(f32[32,2176]{1,0:T(8,128)} %get-tuple-element.30) | copy-start | bytes 835588
  62.5 13.0 %collective-permute-start.8 = (f32[32,2176]{1,0:T(8,128)S(1)}, f32[32,2176]{1,0:T(8,128)S(1)}, u32[]{:S(2)}, u32[]{:S(2)}) collective-permute-start(f32[32,2176]{1,0:T(8,128)S(1)} %add.119), channel_id=1, source_target_pairs={{0,448},{32,480},{64,0},{96,32},{128,64},{160,96},{192,128},{224,1... | collective-permute-start | bytes 835592 | tf_op jit(solution)/shard_map/ppermute | solution.py:27
  66.9 12.0 %collective-permute-start.5 = (f32[32,2176]{1,0:T(8,128)S(1)}, f32[32,2176]{1,0:T(8,128)S(1)}, u32[]{:S(2)}, u32[]{:S(2)}) collective-permute-start(f32[32,2176]{1,0:T(8,128)S(1)} %add.116), channel_id=1, source_target_pairs={{0,64},{32,96},{64,128},{96,160},{128,192},{160,224},{192,256},{22... | collective-permute-start | bytes 835592 | tf_op jit(solution)/shard_map/ppermute | solution.py:27
  68.9 13.2 %collective-permute-start.12 = (f32[32,2176]{1,0:T(8,128)S(1)}, f32[32,2176]{1,0:T(8,128)S(1)}, u32[]{:S(2)}, u32[]{:S(2)}) collective-permute-start(f32[32,2176]{1,0:T(8,128)S(1)} %add.123), channel_id=1, source_target_pairs={{0,64},{32,96},{64,128},{96,160},{128,192},{160,224},{192,256},{22... | collective-permute-start | bytes 835592 | tf_op jit(solution)/shard_map/ppermute | solution.py:27
  70.9 11.2 %collective-permute-start.16 = (f32[32,2176]{1,0:T(8,128)S(1)}, f32[32,2176]{1,0:T(8,128)S(1)}, u32[]{:S(2)}, u32[]{:S(2)}) collective-permute-start(f32[32,2176]{1,0:T(8,128)S(1)} %add.127), channel_id=1, source_target_pairs={{0,448},{32,480},{64,0},{96,32},{128,64},{160,96},{192,128},{224,1... | collective-permute-start | bytes 835592 | tf_op jit(solution)/shard_map/ppermute | solution.py:27
  75.5 10.1 %collective-permute-start.9 = (f32[32,2176]{1,0:T(8,128)S(1)}, f32[32,2176]{1,0:T(8,128)S(1)}, u32[]{:S(2)}, u32[]{:S(2)}) collective-permute-start(f32[32,2176]{1,0:T(8,128)S(1)} %add.120), channel_id=1, source_target_pairs={{0,448},{32,480},{64,0},{96,32},{128,64},{160,96},{192,128},{224,1... | collective-permute-start | bytes 835592 | tf_op jit(solution)/shard_map/ppermute | solution.py:27
  78.9 8.5 %collective-permute-start.6 = (f32[32,2176]{1,0:T(8,128)S(1)}, f32[32,2176]{1,0:T(8,128)S(1)}, u32[]{:S(2)}, u32[]{:S(2)}) collective-permute-start(f32[32,2176]{1,0:T(8,128)S(1)} %add.117), channel_id=1, source_target_pairs={{0,64},{32,96},{64,128},{96,160},{128,192},{160,224},{192,256},{22... | collective-permute-start | bytes 835592 | tf_op jit(solution)/shard_map/ppermute | solution.py:27
  82.2 7.6 %collective-permute-start.17 = (f32[32,2176]{1,0:T(8,128)S(1)}, f32[32,2176]{1,0:T(8,128)S(1)}, u32[]{:S(2)}, u32[]{:S(2)}) collective-permute-start(f32[32,2176]{1,0:T(8,128)S(1)} %add_add_fusion), channel_id=1, source_target_pairs={{0,32},{32,0},{64,96},{96,64},{128,160},{160,128},{192,224},{224,1... | collective-permute-start | bytes 835592 | tf_op jit(solution)/shard_map/ppermute | solution.py:27
  177.6 11.9 %all-to-all-start.2 = ((f32[8,4,1024]{2,1,0:T(4,128)}), f32[8,4,1024]{2,1,0:T(4,128)S(1)}, u32[]{:S(2)}, u32[]{:S(2)}) async-start(f32[8,4,1024]{2,1,0:T(4,128)} %broadcast_in_dim.54), calls=%async_computation.2 | async-start | bytes 262144 | tf_op jit(solution)/shard_map/all_to_all | solution.py:23
  189.5 0.6 copy-start.4

commit v8 on v7

--- a/solution.py
+++ b/solution.py
@@ -27,9 +27,13 @@
     return lax.ppermute(a, axis, [(i, to(i)) for i in range(lax.axis_size(axis))])
 
 
-def ring(a, steps):
+def next_pair(a):
+    return permute(a, "dp", lambda i: i ^ PAIR)
+
+
+def other_pair(a):
     n = lax.axis_size("dp")
-    return permute(a, "dp", lambda i: (i + steps * PAIR) % n)
+    return permute(a, "dp", lambda i: ((i - PAIR) % n ^ PAIR) + PAIR & n - 1)
 
 
 def swap(a):
@@ -40,16 +44,21 @@
     return [a[:, i : i + 1] for i in range(a.shape[1])]
 
 
-def sum_over_dp(term, n_z):
+def sum_over_dp(term, n_z, odd):
     far = n_z // 2
-    ups, downs = [None, None], [None, None]
-    ups[0], downs[1] = ring(term(far, 0), 1), ring(term(far, 1), -1)
+    ahead, back = [None, None], [None, None]
+    ahead[0], back[1] = next_pair(term(far, 0)), other_pair(term(far, 1))
     for hops in range(far - 1, 0, -1):
+        came_ahead, came_back = ahead[:], back[:]
         for h in range(PAIR):
-            for held, sign in ((ups, 1), (downs, -1)):
-                made = term(sign * hops % n_z, h)
-                held[h] = ring(made if held[h] is None else made + held[h], sign)
-    own, other = (term(0, h) + ups[h] + downs[h] for h in range(PAIR))
+            made = term(hops, h)
+            got = came_back[1 - h]
+            ahead[h] = next_pair(made if got is None else made + got)
+            made = term(-hops % n_z, 1 - h)
+            got = came_ahead[h]
+            back[1 - h] = other_pair(made if got is None else made + got)
+    whole = [term(0, h) + back[1 - h] + ahead[1 - h] for h in range(PAIR)]
+    own, other = jnp.where(odd, whole[1], whole[0]), jnp.where(odd, whole[0], whole[1])
     return own + swap(other)
 
 
@@ -68,8 +77,8 @@
 
 
 def token_of(place_ref, i, h, n_z, block):
-    z, x = place_ref[1], place_ref[2]
-    other = lax.rem(z + i, n_z)
+    z, x, way = place_ref[1], place_ref[2], place_ref[3]
+    other = lax.rem(z + way * i + n_z, n_z)
     return pl.multiple_of((other * PAIR + (x ^ h)) * block, block)
 
 
@@ -232,14 +241,15 @@
     z, x = place // PAIR, place % PAIR
     section = lax.axis_index("section")
 
-    rows = [own_rows]
-    for j in range(1, n_section):
-        rows.append(permute(own_rows, "section", lambda i, j=j: i ^ j))
+    across_x = permute(own_rows, "section", lambda i: i ^ 2)
+    other_core = permute(own_rows, "section", lambda i: i ^ 1)
+    rows = [own_rows, other_core, across_x, permute(across_x, "section", lambda i: i ^ 1)]
     near_by = lax.optimization_barrier(
         tuple(jnp.where(section >= 0, a, 0) for a in (own_rows, norm_gain[None]))
     )
     rows[0], gain = near_by
-    where = jnp.stack([section, z, x]).astype(jnp.int32)
+    odd = z % 2
+    where = jnp.stack([section, z, x ^ odd, 1 - 2 * odd]).astype(jnp.int32)
     gains = jnp.concatenate([unite_gain, jnp.zeros_like(unite_gain[:1])], axis=0)
     same = (segment_ids[1:] == segment_ids[:-1]).astype(F32)
     same = jnp.concatenate([jnp.zeros((1,), F32), same])[:, None]
@@ -262,7 +272,7 @@
         name="forward",
     )(where, head, gains, gain, same, *rows)
 
-    summed = sum_over_dp(lambda i, h: terms[i * PAIR + h], n_z)
+    summed = sum_over_dp(lambda i, h: terms[i * PAIR + h], n_z, odd == 1)
     q00, q01, q11, q02, q12, q22, p00, p01, p11, pp00, same0, same1 = columns(
         summed[:block, vocab : vocab + 12]
     )

time: 191 us -> 196 us (1.026)
  starting transfers between devices: 68.6 us -> 59 us
  waiting for transfers between devices: 20.1 us -> 29.2 us
  blocking collectives: 77.9 us -> 81.4 us
    ppermute x18, starting transfers between devices: 65.2 us -> 55.6 us  [permute(): lax.ppermute(a, axis, [(i, to(i)) for i in range(lax.axis_size(axis))])]
    ppermute x18, waiting for transfers between devices: 12.2 us -> 21.2 us  [permute(): lax.ppermute(a, axis, [(i, to(i)) for i in range(lax.axis_size(axis))])]
    all_to_all x2, blocking collectives: 69.5 us -> 72.9 us  [exchange(): return lax.all_to_all(jnp.broadcast_to(a[None], (n,) + a.shape), axis, 0, 0)]
  transfers between devices with their start and end apart: 19 -> 19, of which waited for: 7 -> 8; matrix products, arithmetic and copies ran while one was open for 3% -> 3% of each run, Pallas kernels for 0% -> 0%
where the time goes in v8:
time: 196 us; the launch traced here: 195 us
  blocking collectives  81.4 us (42%)
  starting transfers between devices  59 us (30%)
  waiting for transfers between devices  29.2 us (15%)
  Pallas kernels  12.2 us (6%)
  other arithmetic  8.4 us (4%)
  local copies, waits for them, and re-layouts  3.58 us (2%)
    all_to_all x2, blocking collectives, exchange(): return lax.all_to_all(jnp.broadcast_to(a[None], (n,) + a.shape), axis, 0, 0)  72.9 us
    ppermute x18, starting transfers between devices, permute(): lax.ppermute(a, axis, [(i, to(i)) for i in range(lax.axis_size(axis))])  55.6 us
    ppermute x18, waiting for transfers between devices, permute(): lax.ppermute(a, axis, [(i, to(i)) for i in range(lax.axis_size(axis))])  21.2 us
    all_gather x1, blocking collectives, on_device(): grads = jnp.sum(lax.all_gather(grads, 'section'), axis=0)  8.43 us
    all_to_all x1, waiting for transfers between devices, exchange(): return lax.all_to_all(jnp.broadcast_to(a[None], (n,) + a.shape), axis, 0, 0)  7.93 us
    pallas_call x1, Pallas kernels, on_device(): pl.pallas_call(functools.partial(forward, n_z, block, n_dp), out_shape=[j...  6.76 us
    pallas_call x1, Pallas kernels, on_device(): pl.pallas_call(functools.partial(backward, block, shards), out_shape=(jax...  5.44 us
  transfers between devices with their start and end apart: 19, of which 8 were waited for; matrix products, arithmetic and copies ran while one was open for 3% of the time, Pallas kernels for 0%

profile of v8, /device:TPU:1, one launch (start us, length us, event | category | flops | bytes accessed | tf_op | source)
XLA Modules:
  0.0 194.7 jit_solution(11455468959342169656)
XLA Ops:
  0.6 8.8 %collective-permute-start = (bf16[128,1024]{1,0:T(8,128)(2,1)}, bf16[128,1024]{1,0:T(8,128)(2,1)S(1)}, u32[]{:S(2)}, u32[]{:S(2)}) collective-permute-start(bf16[128,1024]{1,0:T(8,128)(2,1)} %bitcast.88), channel_id=1, source_target_pairs={{0,8},{8,0},{16,24},{24,16},{1,9},{9,1},{17,25},{25,17},{2,10},{10... | collective-permute-start | bytes 786440 | tf_op jit(solution)/shard_map/ppermute | solution.py:27
  9.4 1.9 collective-permute-start.1
  13.3 7.6 %collective-permute-done.1.refs_2_ = bf16[128,1024]{1,0:T(8,128)(2,1)S(1)} collective-permute-done((bf16[128,1024]{1,0:T(8,128)(2,1)}, bf16[128,1024]{1,0:T(8,128)(2,1)S(1)}, u32[]{:S(2)}, u32[]{:S(2)}) %collective-permute-start.1) | collective-permute-done | bytes 262176 | tf_op jit(solution)/shard_map/ppermute | solution.py:27
  21.0 2.7 %collective-permute-start.2 = (bf16[128,1024]{1,0:T(8,128)(2,1)S(1)}, bf16[128,1024]{1,0:T(8,128)(2,1)S(1)}, u32[]{:S(2)}, u32[]{:S(2)}) collective-permute-start(bf16[128,1024]{1,0:T(8,128)(2,1)S(1)} %collective-permute-done.1.refs_2_), channel_id=1, source_target_pairs={{0,8},{8,0},{16,24},{24,16},{1,9},{9,1},{17,25},{25,17},{2,10},{10... | collective-permute-start | bytes 786440 | tf_op jit(solution)/shard_map/ppermute | solution.py:27
  25.2 6.8 %forward.1 = (f32[32,2176]{1,0:T(8,128)S(1)}, f32[32,2176]{1,0:T(8,128)S(1)}, f32[32,2176]{1,0:T(8,128)S(1)}, f32[32,2176]{1,0:T(8,128)S(1)}, f32[32,2176]{1,0:T...) custom-call(s32[4]{0:T(128)S(1)} %pad_add_fusion.place_ref, ...), custom_call_target="tpu_custom_call" | custom-call | tf_op jit(solution)/shard_map/forward/pallas_call | solution.py:263
  31.9 5.4 %collective-permute-start.6 = (f32[32,2176]{1,0:T(8,128)S(1)}, f32[32,2176]{1,0:T(8,128)S(1)}, u32[]{:S(2)}, u32[]{:S(2)}) collective-permute-start(f32[32,2176]{1,0:T(8,128)S(1)} %get-tuple-element.32), channel_id=1, source_target_pairs={{0,448},{32,480},{64,128},{96,160},{128,64},{160,96},{192,256},{22... | collective-permute-start | bytes 835592 | tf_op jit(solution)/shard_map/ppermute | solution.py:27
  37.4 1.9 collective-permute-start.10
  39.3 2.4 %collective-permute-start.3 = (f32[32,2176]{1,0:T(8,128)}, f32[32,2176]{1,0:T(8,128)S(1)}, u32[]{:S(2)}, u32[]{:S(2)}) collective-permute-start(f32[32,2176]{1,0:T(8,128)} %get-tuple-element.28), channel_id=1, source_target_pairs={{0,448},{32,480},{64,128},{96,160},{128,64},{160,96},{192,256},{22... | collective-permute-start | bytes 835592 | tf_op jit(solution)/shard_map/ppermute | solution.py:27
  41.8 2.8 %collective-permute-start.14 = (f32[32,2176]{1,0:T(8,128)S(1)}, f32[32,2176]{1,0:T(8,128)S(1)}, u32[]{:S(2)}, u32[]{:S(2)}) collective-permute-start(f32[32,2176]{1,0:T(8,128)S(1)} %get-tuple-element.40), channel_id=1, source_target_pairs={{0,64},{32,96},{64,0},{96,32},{128,192},{160,224},{192,128},{224,1... | collective-permute-start | bytes 835592 | tf_op jit(solution)/shard_map/ppermute | solution.py:27
  44.7 2.6 %collective-permute-start.7 = (f32[32,2176]{1,0:T(8,128)S(1)}, f32[32,2176]{1,0:T(8,128)S(1)}, u32[]{:S(2)}, u32[]{:S(2)}) collective-permute-start(f32[32,2176]{1,0:T(8,128)S(1)} %add.122), channel_id=1, source_target_pairs={{0,64},{32,96},{64,0},{96,32},{128,192},{160,224},{192,128},{224,1... | collective-permute-start | bytes 835592 | tf_op jit(solution)/shard_map/ppermute | solution.py:27
  47.3 1.0 add.126
  48.3 4.0 %collective-permute-start.11 = (f32[32,2176]{1,0:T(8,128)S(1)}, f32[32,2176]{1,0:T(8,128)S(1)}, u32[]{:S(2)}, u32[]{:S(2)}) collective-permute-start(f32[32,2176]{1,0:T(8,128)S(1)} %add.126), channel_id=1, source_target_pairs={{0,448},{32,480},{64,128},{96,160},{128,64},{160,96},{192,256},{22... | collective-permute-start | bytes 835592 | tf_op jit(solution)/shard_map/ppermute | solution.py:27
  52.4 2.3 %collective-permute-start.4 = (f32[32,2176]{1,0:T(8,128)S(1)}, f32[32,2176]{1,0:T(8,128)S(1)}, u32[]{:S(2)}, u32[]{:S(2)}) collective-permute-start(f32[32,2176]{1,0:T(8,128)S(1)} %add.119), channel_id=1, source_target_pairs={{0,64},{32,96},{64,0},{96,32},{128,192},{160,224},{192,128},{224,1... | collective-permute-start | bytes 835592 | tf_op jit(solution)/shard_map/ppermute | solution.py:27
  54.7 2.7 %collective-permute-start.15 = (f32[32,2176]{1,0:T(8,128)S(1)}, f32[32,2176]{1,0:T(8,128)S(1)}, u32[]{:S(2)}, u32[]{:S(2)}) collective-permute-start(f32[32,2176]{1,0:T(8,128)S(1)} %add.130), channel_id=1, source_target_pairs={{0,448},{32,480},{64,128},{96,160},{128,64},{160,96},{192,256},{22... | collective-permute-start | bytes 835592 | tf_op jit(solution)/shard_map/ppermute | solution.py:27
  57.4 1.8 collective-permute-done.7
  59.2 2.1 %collective-permute-start.8 = (f32[32,2176]{1,0:T(8,128)S(1)}, f32[32,2176]{1,0:T(8,128)S(1)}, u32[]{:S(2)}, u32[]{:S(2)}) collective-permute-start(f32[32,2176]{1,0:T(8,128)S(1)} %add.123), channel_id=1, source_target_pairs={{0,448},{32,480},{64,128},{96,160},{128,64},{160,96},{192,256},{22... | collective-permute-start | bytes 835592 | tf_op jit(solution)/shard_map/ppermute | solution.py:27
  61.4 2.2 %collective-permute-start.12 = (f32[32,2176]{1,0:T(8,128)S(1)}, f32[32,2176]{1,0:T(8,128)S(1)}, u32[]{:S(2)}, u32[]{:S(2)}) collective-permute-start(f32[32,2176]{1,0:T(8,128)S(1)} %add.127), channel_id=1, source_target_pairs={{0,64},{32,96},{64,0},{96,32},{128,192},{160,224},{192,128},{224,1... | collective-permute-start | bytes 835592 | tf_op jit(solution)/shard_map/ppermute | solution.py:27
  63.6 1.6 collective-permute-done.4
  65.2 2.7 %collective-permute-start.5 = (f32[32,2176]{1,0:T(8,128)S(1)}, f32[32,2176]{1,0:T(8,128)S(1)}, u32[]{:S(2)}, u32[]{:S(2)}) collective-permute-start(f32[32,2176]{1,0:T(8,128)S(1)} %add.120), channel_id=1, source_target_pairs={{0,448},{32,480},{64,128},{96,160},{128,64},{160,96},{192,256},{22... | collective-permute-start | bytes 835592 | tf_op jit(solution)/shard_map/ppermute | solution.py:27
  67.9 1.9 collective-permute-start.16
  69.9 1.2 collective-permute-done.8
  71.8 2.2 %collective-permute-start.9 = (f32[32,2176]{1,0:T(8,128)}, f32[32,2176]{1,0:T(8,128)S(1)}, u32[]{:S(2)}, u32[]{:S(2)}) collective-permute-start(f32[32,2176]{1,0:T(8,128)} %add.124), channel_id=1, source_target_pairs={{0,64},{32,96},{64,0},{96,32},{128,192},{160,224},{192,128},{224,1... | collective-permute-start | bytes 835592 | tf_op jit(solution)/shard_map/ppermute | solution.py:27
  74.7 3.8 %collective-permute-start.13 = (f32[32,2176]{1,0:T(8,128)}, f32[32,2176]{1,0:T(8,128)S(1)}, u32[]{:S(2)}, u32[]{:S(2)}) collective-permute-start(f32[32,2176]{1,0:T(8,128)} %add.128), channel_id=1, source_target_pairs={{0,448},{32,480},{64,128},{96,160},{128,64},{160,96},{192,256},{22... | collective-permute-start | bytes 835592 | tf_op jit(solution)/shard_map/ppermute | solution.py:27
  78.5 4.0 %collective-permute-done.9 = f32[32,2176]{1,0:T(8,128)S(1)} collective-permute-done((f32[32,2176]{1,0:T(8,128)}, f32[32,2176]{1,0:T(8,128)S(1)}, u32[]{:S(2)}, u32[]{:S(2)}) %collective-permute-start.9) | collective-permute-done | bytes 278560 | tf_op jit(solution)/shard_map/ppermute | solution.py:27
  83.5 3.1 %collective-permute-start.17 = (f32[32,2176]{1,0:T(8,128)S(1)}, f32[32,2176]{1,0:T(8,128)S(1)}, u32[]{:S(2)}, u32[]{:S(2)}) collective-permute-start(f32[32,2176]{1,0:T(8,128)S(1)} %broadcast_select_fusion.1), channel_id=1, source_target_pairs={{0,32},{32,0},{64,96},{96,64},{128,160},{160,128},{192,224},{224,1... | collective-permute-start | bytes 835592 | tf_op jit(solution)/shard_map/ppermute | solution.py:27
  86.7 4.2 %collective-permute-done.17 = f32[32,2176]{1,0:T(8,128)S(1)} collective-permute-done((f32[32,2176]{1,0:T(8,128)S(1)}, f32[32,2176]{1,0:T(8,128)S(1)}, u32[]{:S(2)}, u32[]{:S(2)}) %collective-permute-start.17) | collective-permute-done | bytes 278560 | tf_op jit(solution)/shard_map/ppermute | solution.py:27
  92.4 27.1 %all_to_all.15 = f32[32,8,14]{2,1,0:T(8,128)S(1)} all-to-all(f32[32,8,14]{2,1,0:T(8,128)S(1)} %broadcast_in_dim.52), channel_id=1, replica_groups=mesh['dp'=16,'section'=4,'vocab'=8] {'section','vocab'}, dimensions={0} | all-to-all | bytes 28672 | tf_op jit(solution)/shard_map/all_to_all | solution.py:23
  121.7 45.9 %all_to_all.16 = bf16[16,24,2176]{2,1,0:T(8,128)(2,1)S(1)} all-to-all(bf16[16,24,2176]{2,1,0:T(8,128)(2,1)S(1)} %broadcast_in_dim.53), channel_id=1, replica_groups=mesh['dp'=16,'section'=4,'vocab'=8] {'dp'}, dimensions={0} | all-to-all | bytes 3342336 | tf_op jit(solution)/shard_map/all_to_all | solution.py:23
  167.6 5.4 %backward.1 = (f32[4,1024]{1,0:T(4,128)S(1)}, f32[128,128]{1,0:T(8,128)S(1)}) custom-call(s32[4]{0:T(128)S(1)} %pad_add_fusion.place_ref, bf16[384,2176]{1,0:T(8,128)(2,1)S(1)} %bitcast.84, bf16[2048,1024]{1,0:T(8,128)(2,1)} %head_ref.3, f32[4,1024]{1,0:T(4,128)S(1)} %concatenate.22.gains_ref, f32[1,1024]{1,0:T(1,128)S(1)} %bitcast.86, ...), custom_call_target="tpu_custom_call" | custom-call | tf_op jit(solution)/shard_map/backward/pallas_call | solution.py:333
  173.1 8.4 %all-gather.1 = f32[4,4,1024]{2,1,0:T(4,128)S(1)} all-gather(f32[1,4,1024]{2,1,0:T(4,128)S(1)} %bitcast.87), channel_id=2, replica_groups=mesh['dp'=16,'section'=4,'vocab'=8] {'section'}, dimensions={0}, use_global_device_ids=true | all-gather | bytes 81920 | tf_op jit(solution)/shard_map/all_gather | solution.py:351
  182.2 3.4 %all-to-all-start.2 = ((f32[8,4,1024]{2,1,0:T(4,128)}), f32[8,4,1024]{2,1,0:T(4,128)S(1)}, u32[]{:S(2)}, u32[]{:S(2)}) async-start(f32[8,4,1024]{2,1,0:T(4,128)} %broadcast_in_dim.54), calls=%async_computation.2 | async-start | bytes 262144 | tf_op jit(solution)/shard_map/all_to_all | solution.py:23
  186.2 7.9 %all-to-all-done.2 = f32[8,4,1024]{2,1,0:T(4,128)S(1)} async-done(((f32[8,4,1024]{2,1,0:T(4,128)}), f32[8,4,1024]{2,1,0:T(4,128)S(1)}, u32[]{:S(2)}, u32[]{:S(2)}) %all-to-all-start.2) | async-done | bytes 131104 | tf_op jit(solution)/shard_map/all_to_all | solution.py:23
  (80 shorter events, 11.9 us)
Async XLA Ops:
  0.6 24.5 %collective-permute-start = (bf16[128,1024]{1,0:T(8,128)(2,1)}, bf16[128,1024]{1,0:T(8,128)(2,1)S(1)}, u32[]{:S(2)}, u32[]{:S(2)}) collective-permute-start(bf16[128,1024]{1,0:T(8,128)(2,1)} %bitcast.88), channel_id=1, source_target_pairs={{0,8},{8,0},{16,24},{24,16},{1,9},{9,1},{17,25},{25,17},{2,10},{10... | collective-permute-start | bytes 786440 | tf_op jit(solution)/shard_map/ppermute | solution.py:27
  9.4 11.5 %collective-permute-start.1 = (bf16[128,1024]{1,0:T(8,128)(2,1)}, bf16[128,1024]{1,0:T(8,128)(2,1)S(1)}, u32[]{:S(2)}, u32[]{:S(2)}) collective-permute-start(bf16[128,1024]{1,0:T(8,128)(2,1)} %bitcast.89), channel_id=1, source_target_pairs={{0,16},{8,24},{16,0},{24,8},{1,17},{9,25},{17,1},{25,9},{2,18},{10... | collective-permute-start | bytes 786440 | tf_op jit(solution)/shard_map/ppermute | solution.py:27
  21.0 4.2 %collective-permute-start.2 = (bf16[128,1024]{1,0:T(8,128)(2,1)S(1)}, bf16[128,1024]{1,0:T(8,128)(2,1)S(1)}, u32[]{:S(2)}, u32[]{:S(2)}) collective-permute-start(bf16[128,1024]{1,0:T(8,128)(2,1)S(1)} %collective-permute-done.1.refs_2_), channel_id=1, source_target_pairs={{0,8},{8,0},{16,24},{24,16},{1,9},{9,1},{17,25},{25,17},{2,10},{10... | collective-permute-start | bytes 786440 | tf_op jit(solution)/shard_map/ppermute | solution.py:27
  31.9 22.7 %copy-start.3 = (f32[32,2176]{1,0:T(8,128)S(1)}, f32[32,2176]{1,0:T(8,128)}, u32[]{:S(2)}) copy-start(f32[32,2176]{1,0:T(8,128)} %get-tuple-element.39) | copy-start | bytes 835588
  31.9 12.7 %collective-permute-start.6 = (f32[32,2176]{1,0:T(8,128)S(1)}, f32[32,2176]{1,0:T(8,128)S(1)}, u32[]{:S(2)}, u32[]{:S(2)}) collective-permute-start(f32[32,2176]{1,0:T(8,128)S(1)} %get-tuple-element.32), channel_id=1, source_target_pairs={{0,448},{32,480},{64,128},{96,160},{128,64},{160,96},{192,256},{22... | collective-permute-start | bytes 835592 | tf_op jit(solution)/shard_map/ppermute | solution.py:27
  37.4 9.9 %collective-permute-start.10 = (f32[32,2176]{1,0:T(8,128)S(1)}, f32[32,2176]{1,0:T(8,128)S(1)}, u32[]{:S(2)}, u32[]{:S(2)}) collective-permute-start(f32[32,2176]{1,0:T(8,128)S(1)} %get-tuple-element.37), channel_id=1, source_target_pairs={{0,64},{32,96},{64,0},{96,32},{128,192},{160,224},{192,128},{224,1... | collective-permute-start | bytes 835592 | tf_op jit(solution)/shard_map/ppermute | solution.py:27
  39.3 13.0 %collective-permute-start.3 = (f32[32,2176]{1,0:T(8,128)}, f32[32,2176]{1,0:T(8,128)S(1)}, u32[]{:S(2)}, u32[]{:S(2)}) collective-permute-start(f32[32,2176]{1,0:T(8,128)} %get-tuple-element.28), channel_id=1, source_target_pairs={{0,448},{32,480},{64,128},{96,160},{128,64},{160,96},{192,256},{22... | collective-permute-start | bytes 835592 | tf_op jit(solution)/shard_map/ppermute | solution.py:27
  41.8 12.9 %collective-permute-start.14 = (f32[32,2176]{1,0:T(8,128)S(1)}, f32[32,2176]{1,0:T(8,128)S(1)}, u32[]{:S(2)}, u32[]{:S(2)}) collective-permute-start(f32[32,2176]{1,0:T(8,128)S(1)} %get-tuple-element.40), channel_id=1, source_target_pairs={{0,64},{32,96},{64,0},{96,32},{128,192},{160,224},{192,128},{224,1... | collective-permute-start | bytes 835592 | tf_op jit(solution)/shard_map/ppermute | solution.py:27
  44.6 14.6 %copy-start.2 = (f32[32,2176]{1,0:T(8,128)S(1)}, f32[32,2176]{1,0:T(8,128)}, u32[]{:S(2)}) copy-start(f32[32,2176]{1,0:T(8,128)} %get-tuple-element.30) | copy-start | bytes 835588
  44.7 14.5 %collective-permute-start.7 = (f32[32,2176]{1,0:T(8,128)S(1)}, f32[32,2176]{1,0:T(8,128)S(1)}, u32[]{:S(2)}, u32[]{:S(2)}) collective-permute-start(f32[32,2176]{1,0:T(8,128)S(1)} %add.122), channel_id=1, source_target_pairs={{0,64},{32,96},{64,0},{96,32},{128,192},{160,224},{192,128},{224,1... | collective-permute-start | bytes 835592 | tf_op jit(solution)/shard_map/ppermute | solution.py:27
  48.3 13.1 %collective-permute-start.11 = (f32[32,2176]{1,0:T(8,128)S(1)}, f32[32,2176]{1,0:T(8,128)S(1)}, u32[]{:S(2)}, u32[]{:S(2)}) collective-permute-start(f32[32,2176]{1,0:T(8,128)S(1)} %add.126), channel_id=1, source_target_pairs={{0,448},{32,480},{64,128},{96,160},{128,64},{160,96},{192,256},{22... | collective-permute-start | bytes 835592 | tf_op jit(solution)/shard_map/ppermute | solution.py:27
  52.3 12.8 %copy-start.1 = (f32[32,2176]{1,0:T(8,128)S(1)}, f32[32,2176]{1,0:T(8,128)}, u32[]{:S(2)}) copy-start(f32[32,2176]{1,0:T(8,128)} %get-tuple-element.26) | copy-start | bytes 835588
  52.4 12.8 %collective-permute-start.4 = (f32[32,2176]{1,0:T(8,128)S(1)}, f32[32,2176]{1,0:T(8,128)S(1)}, u32[]{:S(2)}, u32[]{:S(2)}) collective-permute-start(f32[32,2176]{1,0:T(8,128)S(1)} %add.119), channel_id=1, source_target_pairs={{0,64},{32,96},{64,0},{96,32},{128,192},{160,224},{192,128},{224,1... | collective-permute-start | bytes 835592 | tf_op jit(solution)/shard_map/ppermute | solution.py:27
  54.7 13.2 %collective-permute-start.15 = (f32[32,2176]{1,0:T(8,128)S(1)}, f32[32,2176]{1,0:T(8,128)S(1)}, u32[]{:S(2)}, u32[]{:S(2)}) collective-permute-start(f32[32,2176]{1,0:T(8,128)S(1)} %add.130), channel_id=1, source_target_pairs={{0,448},{32,480},{64,128},{96,160},{128,64},{160,96},{192,256},{22... | collective-permute-start | bytes 835592 | tf_op jit(solution)/shard_map/ppermute | solution.py:27
  59.2 11.8 %collective-permute-start.8 = (f32[32,2176]{1,0:T(8,128)S(1)}, f32[32,2176]{1,0:T(8,128)S(1)}, u32[]{:S(2)}, u32[]{:S(2)}) collective-permute-start(f32[32,2176]{1,0:T(8,128)S(1)} %add.123), channel_id=1, source_target_pairs={{0,448},{32,480},{64,128},{96,160},{128,64},{160,96},{192,256},{22... | collective-permute-start | bytes 835592 | tf_op jit(solution)/shard_map/ppermute | solution.py:27
  61.4 12.6 %copy-start = (f32[32,2176]{1,0:T(8,128)S(1)}, f32[32,2176]{1,0:T(8,128)}, u32[]{:S(2)}) copy-start(f32[32,2176]{1,0:T(8,128)} %get-tuple-element.34) | copy-start | bytes 835588
  61.4 12.6 %collective-permute-start.12 = (f32[32,2176]{1,0:T(8,128)S(1)}, f32[32,2176]{1,0:T(8,128)S(1)}, u32[]{:S(2)}, u32[]{:S(2)}) collective-permute-start(f32[32,2176]{1,0:T(8,128)S(1)} %add.127), channel_id=1, source_target_pairs={{0,64},{32,96},{64,0},{96,32},{128,192},{160,224},{192,128},{224,1... | collective-permute-start | bytes 835592 | tf_op jit(solution)/shard_map/ppermute | solution.py:27
  65.2 13.3 %collective-permute-start.5 = (f32[32,2176]{1,0:T(8,128)S(1)}, f32[32,2176]{1,0:T(8,128)S(1)}, u32[]{:S(2)}, u32[]{:S(2)}) collective-permute-start(f32[32,2176]{1,0:T(8,128)S(1)} %add.120), channel_id=1, source_target_pairs={{0,448},{32,480},{64,128},{96,160},{128,64},{160,96},{192,256},{22... | collective-permute-start | bytes 835592 | tf_op jit(solution)/shard_map/ppermute | solution.py:27
  67.9 10.6 %collective-permute-start.16 = (f32[32,2176]{1,0:T(8,128)S(1)}, f32[32,2176]{1,0:T(8,128)S(1)}, u32[]{:S(2)}, u32[]{:S(2)}) collective-permute-start(f32[32,2176]{1,0:T(8,128)S(1)} %add.131), channel_id=1, source_target_pairs={{0,64},{32,96},{64,0},{96,32},{128,192},{160,224},{192,128},{224,1... | collective-permute-start | bytes 835592 | tf_op jit(solution)/shard_map/ppermute | solution.py:27
  71.8 10.8 %collective-permute-start.9 = (f32[32,2176]{1,0:T(8,128)}, f32[32,2176]{1,0:T(8,128)S(1)}, u32[]{:S(2)}, u32[]{:S(2)}) collective-permute-start(f32[32,2176]{1,0:T(8,128)} %add.124), channel_id=1, source_target_pairs={{0,64},{32,96},{64,0},{96,32},{128,192},{160,224},{192,128},{224,1... | collective-permute-start | bytes 835592 | tf_op jit(solution)/shard_map/ppermute | solution.py:27
  74.7 8.7 %collective-permute-start.13 = (f32[32,2176]{1,0:T(8,128)}, f32[32,2176]{1,0:T(8,128)S(1)}, u32[]{:S(2)}, u32[]{:S(2)}) collective-permute-start(f32[32,2176]{1,0:T(8,128)} %add.128), channel_id=1, source_target_pairs={{0,448},{32,480},{64,128},{96,160},{128,64},{160,96},{192,256},{22... | collective-permute-start | bytes 835592 | tf_op jit(solution)/shard_map/ppermute | solution.py:27
  83.5 7.3 %collective-permute-start.17 = (f32[32,2176]{1,0:T(8,128)S(1)}, f32[32,2176]{1,0:T(8,128)S(1)}, u32[]{:S(2)}, u32[]{:S(2)}) collective-permute-start(f32[32,2176]{1,0:T(8,128)S(1)} %broadcast_select_fusion.1), channel_id=1, source_target_pairs={{0,32},{32,0},{64,96},{96,64},{128,160},{160,128},{192,224},{224,1... | collective-permute-start | bytes 835592 | tf_op jit(solution)/shard_map/ppermute | solution.py:27
  182.2 11.9 %all-to-all-start.2 = ((f32[8,4,1024]{2,1,0:T(4,128)}), f32[8,4,1024]{2,1,0:T(4,128)S(1)}, u32[]{:S(2)}, u32[]{:S(2)}) async-start(f32[8,4,1024]{2,1,0:T(4,128)} %broadcast_in_dim.54), calls=%async_computation.2 | async-start | bytes 262144 | tf_op jit(solution)/shard_map/all_to_all | solution.py:23
  194.1 0.6 copy-start.4

commit v9 on v7

--- a/solution.py
+++ b/solution.py
@@ -43,14 +43,23 @@
 def sum_over_dp(term, n_z):
     far = n_z // 2
     ups, downs = [None, None], [None, None]
-    ups[0], downs[1] = ring(term(far, 0), 1), ring(term(far, 1), -1)
-    for hops in range(far - 1, 0, -1):
-        for h in range(PAIR):
-            for held, sign in ((ups, 1), (downs, -1)):
-                made = term(sign * hops % n_z, h)
-                held[h] = ring(made if held[h] is None else made + held[h], sign)
-    own, other = (term(0, h) + ups[h] + downs[h] for h in range(PAIR))
-    return own + swap(other)
+    ups[1], downs[1] = ring(term(far - 1, 1), 1), ring(term(far + 1, 1), -1)
+    half_way = swap(term(far, 1)) + term(far, 0)
+    downs[0] = ring(term(far + 1, 0), -1)
+    ups[0] = ring(half_way, 1)
+    for hops in range(far - 2, 0, -1):
+        for h in (1, 0):
+            ups[h] = ups[h] + term(hops + 1 - h, h)
+            downs[h] = downs[h] + term(n_z - hops, h)
+            if h == 1 and hops == 1:
+                ups[1], downs[1] = swap(ups[1]), swap(downs[1])
+            elif h == 0 and hops == 1:
+                downs[0] = ring(downs[0] + downs[1], -1)
+                ups[0] = ring(ups[0], 1)
+            else:
+                ups[h], downs[h] = ring(ups[h], 1), ring(downs[h], -1)
+    ups[0] = ring(ups[0] + term(1, 0) + ups[1], 1)
+    return term(0, 0) + swap(term(0, 1)) + ups[0] + downs[0]
 
 
 def parts(a):

time: 191 us -> 192 us (level)
  waiting for transfers between devices: 20.1 us -> 22.9 us
    ppermute x18, waiting for transfers between devices: 12.2 us -> 14.9 us  [permute(): lax.ppermute(a, axis, [(i, to(i)) for i in range(lax.axis_size(axis))])]
  transfers between devices with their start and end apart: 19 -> 19, of which waited for: 7 -> 5; matrix products, arithmetic and copies ran while one was open for 3% -> 3% of each run, Pallas kernels for 0% -> 0%
where the time goes in v9:
time: 192 us; the launch traced here: 191 us
  blocking collectives  77.1 us (40%)
  starting transfers between devices  67.7 us (35%)
  waiting for transfers between devices  22.9 us (12%)
  Pallas kernels  12 us (6%)
  other arithmetic  6.89 us (4%)
  local copies, waits for them, and re-layouts  3.57 us (2%)
    all_to_all x2, blocking collectives, exchange(): return lax.all_to_all(jnp.broadcast_to(a[None], (n,) + a.shape), axis, 0, 0)  68.7 us
    ppermute x18, starting transfers between devices, permute(): lax.ppermute(a, axis, [(i, to(i)) for i in range(lax.axis_size(axis))])  64.3 us
    ppermute x18, waiting for transfers between devices, permute(): lax.ppermute(a, axis, [(i, to(i)) for i in range(lax.axis_size(axis))])  14.9 us
    all_gather x1, blocking collectives, on_device(): grads = jnp.sum(lax.all_gather(grads, 'section'), axis=0)  8.37 us
    all_to_all x1, waiting for transfers between devices, exchange(): return lax.all_to_all(jnp.broadcast_to(a[None], (n,) + a.shape), axis, 0, 0)  7.93 us
    pallas_call x1, Pallas kernels, on_device(): pl.pallas_call(functools.partial(forward, n_z, block, n_dp), out_shape=[j...  6.55 us
    pallas_call x1, Pallas kernels, on_device(): pl.pallas_call(functools.partial(backward, block, shards), out_shape=(jax...  5.44 us
  transfers between devices with their start and end apart: 19, of which 5 were waited for; matrix products, arithmetic and copies ran while one was open for 3% of the time, Pallas kernels for 0%

profile of v9, /device:TPU:1, one launch (start us, length us, event | category | flops | bytes accessed | tf_op | source)
XLA Modules:
  0.0 191.2 jit_solution(7635879178810713461)
XLA Ops:
  0.6 5.5 %collective-permute-start.1 = (bf16[128,1024]{1,0:T(8,128)(2,1)}, bf16[128,1024]{1,0:T(8,128)(2,1)S(1)}, u32[]{:S(2)}, u32[]{:S(2)}) collective-permute-start(bf16[128,1024]{1,0:T(8,128)(2,1)} %bitcast.87), channel_id=1, source_target_pairs={{0,16},{8,24},{16,0},{24,8},{1,17},{9,25},{17,1},{25,9},{2,18},{10... | collective-permute-start | bytes 786440 | tf_op jit(solution)/shard_map/ppermute | solution.py:27
  6.1 5.2 %collective-permute-start = (bf16[128,1024]{1,0:T(8,128)(2,1)}, bf16[128,1024]{1,0:T(8,128)(2,1)S(1)}, u32[]{:S(2)}, u32[]{:S(2)}) collective-permute-start(bf16[128,1024]{1,0:T(8,128)(2,1)} %bitcast.88), channel_id=1, source_target_pairs={{0,8},{8,0},{16,24},{24,16},{1,9},{9,1},{17,25},{25,17},{2,10},{10... | collective-permute-start | bytes 786440 | tf_op jit(solution)/shard_map/ppermute | solution.py:27
  11.4 5.0 %collective-permute-start.2 = (bf16[128,1024]{1,0:T(8,128)(2,1)}, bf16[128,1024]{1,0:T(8,128)(2,1)S(1)}, u32[]{:S(2)}, u32[]{:S(2)}) collective-permute-start(bf16[128,1024]{1,0:T(8,128)(2,1)} %bitcast.89), channel_id=1, source_target_pairs={{0,24},{8,16},{16,8},{24,0},{1,25},{9,17},{17,9},{25,1},{2,26},{10... | collective-permute-start | bytes 786440 | tf_op jit(solution)/shard_map/ppermute | solution.py:27
  16.4 0.8 slice_compare_fusion
  17.4 1.0 broadcast_select_fusion.refs_0_
  19.1 0.7 concatenate.22.gains_ref
  19.9 3.4 %collective-permute-done.2.refs_3_ = bf16[128,1024]{1,0:T(8,128)(2,1)S(1)} collective-permute-done((bf16[128,1024]{1,0:T(8,128)(2,1)}, bf16[128,1024]{1,0:T(8,128)(2,1)S(1)}, u32[]{:S(2)}, u32[]{:S(2)}) %collective-permute-start.2) | collective-permute-done | bytes 262176 | tf_op jit(solution)/shard_map/ppermute | solution.py:27
  23.3 6.5 %forward.1 = (f32[32,2176]{1,0:T(8,128)S(1)}, f32[32,2176]{1,0:T(8,128)S(1)}, f32[32,2176]{1,0:T(8,128)S(1)}, f32[32,2176]{1,0:T(8,128)S(1)}, f32[32,2176]{1,0:T...) custom-call(s32[3]{0:T(128)S(1)} %pad_add_fusion.place_ref, ...), custom_call_target="tpu_custom_call" | custom-call | tf_op jit(solution)/shard_map/forward/pallas_call | solution.py:262
  29.8 2.1 %collective-permute-start.4 = (f32[32,2176]{1,0:T(8,128)S(1)}, f32[32,2176]{1,0:T(8,128)S(1)}, u32[]{:S(2)}, u32[]{:S(2)}) collective-permute-start(f32[32,2176]{1,0:T(8,128)S(1)} %get-tuple-element.27), channel_id=1, source_target_pairs={{0,32},{32,0},{64,96},{96,64},{128,160},{160,128},{192,224},{224,1... | collective-permute-start | bytes 835592 | tf_op jit(solution)/shard_map/ppermute | solution.py:27
  31.9 8.2 %collective-permute-start.14 = (f32[32,2176]{1,0:T(8,128)}, f32[32,2176]{1,0:T(8,128)S(1)}, u32[]{:S(2)}, u32[]{:S(2)}) collective-permute-start(f32[32,2176]{1,0:T(8,128)} %get-tuple-element.38), channel_id=1, source_target_pairs={{0,448},{32,480},{64,0},{96,32},{128,64},{160,96},{192,128},{224,1... | collective-permute-start | bytes 835592 | tf_op jit(solution)/shard_map/ppermute | solution.py:27
  40.1 1.9 %collective-permute-start.8 = (f32[32,2176]{1,0:T(8,128)S(1)}, f32[32,2176]{1,0:T(8,128)S(1)}, u32[]{:S(2)}, u32[]{:S(2)}) collective-permute-start(f32[32,2176]{1,0:T(8,128)S(1)} %get-tuple-element.32), channel_id=1, source_target_pairs={{0,64},{32,96},{64,128},{96,160},{128,192},{160,224},{192,256},{22... | collective-permute-start | bytes 835592 | tf_op jit(solution)/shard_map/ppermute | solution.py:27
  42.1 4.6 %collective-permute-start.12 = (f32[32,2176]{1,0:T(8,128)}, f32[32,2176]{1,0:T(8,128)S(1)}, u32[]{:S(2)}, u32[]{:S(2)}) collective-permute-start(f32[32,2176]{1,0:T(8,128)} %get-tuple-element.35), channel_id=1, source_target_pairs={{0,448},{32,480},{64,0},{96,32},{128,64},{160,96},{192,128},{224,1... | collective-permute-start | bytes 835592 | tf_op jit(solution)/shard_map/ppermute | solution.py:27
  46.7 1.9 %collective-permute-start.5 = (f32[32,2176]{1,0:T(8,128)S(1)}, f32[32,2176]{1,0:T(8,128)S(1)}, u32[]{:S(2)}, u32[]{:S(2)}) collective-permute-start(f32[32,2176]{1,0:T(8,128)S(1)} %add.116), channel_id=1, source_target_pairs={{0,64},{32,96},{64,128},{96,160},{128,192},{160,224},{192,256},{22... | collective-permute-start | bytes 835592 | tf_op jit(solution)/shard_map/ppermute | solution.py:27
  48.6 1.0 add.126
  49.7 4.6 %collective-permute-start.15 = (f32[32,2176]{1,0:T(8,128)S(1)}, f32[32,2176]{1,0:T(8,128)S(1)}, u32[]{:S(2)}, u32[]{:S(2)}) collective-permute-start(f32[32,2176]{1,0:T(8,128)S(1)} %add.126), channel_id=1, source_target_pairs={{0,448},{32,480},{64,0},{96,32},{128,64},{160,96},{192,128},{224,1... | collective-permute-start | bytes 835592 | tf_op jit(solution)/shard_map/ppermute | solution.py:27
  54.3 1.9 %collective-permute-start.9 = (f32[32,2176]{1,0:T(8,128)S(1)}, f32[32,2176]{1,0:T(8,128)S(1)}, u32[]{:S(2)}, u32[]{:S(2)}) collective-permute-start(f32[32,2176]{1,0:T(8,128)S(1)} %add.120), channel_id=1, source_target_pairs={{0,64},{32,96},{64,128},{96,160},{128,192},{160,224},{192,256},{22... | collective-permute-start | bytes 835592 | tf_op jit(solution)/shard_map/ppermute | solution.py:27
  56.8 2.1 %collective-permute-start.6 = (f32[32,2176]{1,0:T(8,128)S(1)}, f32[32,2176]{1,0:T(8,128)S(1)}, u32[]{:S(2)}, u32[]{:S(2)}) collective-permute-start(f32[32,2176]{1,0:T(8,128)S(1)} %add.117), channel_id=1, source_target_pairs={{0,64},{32,96},{64,128},{96,160},{128,192},{160,224},{192,256},{22... | collective-permute-start | bytes 835592 | tf_op jit(solution)/shard_map/ppermute | solution.py:27
  58.9 4.6 %collective-permute-start.13 = (f32[32,2176]{1,0:T(8,128)S(1)}, f32[32,2176]{1,0:T(8,128)S(1)}, u32[]{:S(2)}, u32[]{:S(2)}) collective-permute-start(f32[32,2176]{1,0:T(8,128)S(1)} %add.124), channel_id=1, source_target_pairs={{0,448},{32,480},{64,0},{96,32},{128,64},{160,96},{192,128},{224,1... | collective-permute-start | bytes 835592 | tf_op jit(solution)/shard_map/ppermute | solution.py:27
  63.5 3.1 %collective-permute-start.16 = (f32[32,2176]{1,0:T(8,128)S(1)}, f32[32,2176]{1,0:T(8,128)S(1)}, u32[]{:S(2)}, u32[]{:S(2)}) collective-permute-start(f32[32,2176]{1,0:T(8,128)S(1)} %add.127), channel_id=1, source_target_pairs={{0,32},{32,0},{64,96},{96,64},{128,160},{160,128},{192,224},{224,1... | collective-permute-start | bytes 835592 | tf_op jit(solution)/shard_map/ppermute | solution.py:27
  66.6 2.2 %collective-permute-start.3 = (f32[32,2176]{1,0:T(8,128)S(1)}, f32[32,2176]{1,0:T(8,128)S(1)}, u32[]{:S(2)}, u32[]{:S(2)}) collective-permute-start(f32[32,2176]{1,0:T(8,128)S(1)} %get-tuple-element.26), channel_id=1, source_target_pairs={{0,32},{32,0},{64,96},{96,64},{128,160},{160,128},{192,224},{224,1... | collective-permute-start | bytes 835592 | tf_op jit(solution)/shard_map/ppermute | solution.py:27
  68.8 3.1 %collective-permute-start.10 = (f32[32,2176]{1,0:T(8,128)S(1)}, f32[32,2176]{1,0:T(8,128)S(1)}, u32[]{:S(2)}, u32[]{:S(2)}) collective-permute-start(f32[32,2176]{1,0:T(8,128)S(1)} %add.121), channel_id=1, source_target_pairs={{0,32},{32,0},{64,96},{96,64},{128,160},{160,128},{192,224},{224,1... | collective-permute-start | bytes 835592 | tf_op jit(solution)/shard_map/ppermute | solution.py:27
  72.0 1.9 %collective-permute-start.7 = (f32[32,2176]{1,0:T(8,128)S(1)}, f32[32,2176]{1,0:T(8,128)S(1)}, u32[]{:S(2)}, u32[]{:S(2)}) collective-permute-start(f32[32,2176]{1,0:T(8,128)S(1)} %add.118), channel_id=1, source_target_pairs={{0,64},{32,96},{64,128},{96,160},{128,192},{160,224},{192,256},{22... | collective-permute-start | bytes 835592 | tf_op jit(solution)/shard_map/ppermute | solution.py:27
  74.0 4.6 %collective-permute-start.17 = (f32[32,2176]{1,0:T(8,128)S(1)}, f32[32,2176]{1,0:T(8,128)S(1)}, u32[]{:S(2)}, u32[]{:S(2)}) collective-permute-start(f32[32,2176]{1,0:T(8,128)S(1)} %add_add_fusion), channel_id=1, source_target_pairs={{0,448},{32,480},{64,0},{96,32},{128,64},{160,96},{192,128},{224,1... | collective-permute-start | bytes 835592 | tf_op jit(solution)/shard_map/ppermute | solution.py:27
  78.6 4.5 %collective-permute-done.10 = f32[32,2176]{1,0:T(8,128)S(1)} collective-permute-done((f32[32,2176]{1,0:T(8,128)S(1)}, f32[32,2176]{1,0:T(8,128)S(1)}, u32[]{:S(2)}, u32[]{:S(2)}) %collective-permute-start.10) | collective-permute-done | bytes 278560 | tf_op jit(solution)/shard_map/ppermute | solution.py:27
  83.1 1.9 %collective-permute-start.11 = (f32[32,2176]{1,0:T(8,128)S(1)}, f32[32,2176]{1,0:T(8,128)S(1)}, u32[]{:S(2)}, u32[]{:S(2)}) collective-permute-start(f32[32,2176]{1,0:T(8,128)S(1)} %add_add_fusion.2), channel_id=1, source_target_pairs={{0,64},{32,96},{64,128},{96,160},{128,192},{160,224},{192,256},{22... | collective-permute-start | bytes 835592 | tf_op jit(solution)/shard_map/ppermute | solution.py:27
  85.1 6.6 %collective-permute-done.11 = f32[32,2176]{1,0:T(8,128)S(1)} collective-permute-done((f32[32,2176]{1,0:T(8,128)S(1)}, f32[32,2176]{1,0:T(8,128)S(1)}, u32[]{:S(2)}, u32[]{:S(2)}) %collective-permute-start.11) | collective-permute-done | bytes 278560 | tf_op jit(solution)/shard_map/ppermute | solution.py:27
  93.1 24.2 %all_to_all.15 = f32[32,8,14]{2,1,0:T(8,128)S(1)} all-to-all(f32[32,8,14]{2,1,0:T(8,128)S(1)} %broadcast_in_dim.52), channel_id=1, replica_groups=mesh['dp'=16,'section'=4,'vocab'=8] {'section','vocab'}, dimensions={0} | all-to-all | bytes 28672 | tf_op jit(solution)/shard_map/all_to_all | solution.py:23
  119.6 44.5 %all_to_all.16 = bf16[16,24,2176]{2,1,0:T(8,128)(2,1)S(1)} all-to-all(bf16[16,24,2176]{2,1,0:T(8,128)(2,1)S(1)} %broadcast_in_dim.53), channel_id=1, replica_groups=mesh['dp'=16,'section'=4,'vocab'=8] {'dp'}, dimensions={0} | all-to-all | bytes 3342336 | tf_op jit(solution)/shard_map/all_to_all | solution.py:23
  164.1 5.4 %backward.1 = (f32[4,1024]{1,0:T(4,128)S(1)}, f32[128,128]{1,0:T(8,128)S(1)}) custom-call(s32[3]{0:T(128)S(1)} %pad_add_fusion.place_ref, bf16[384,2176]{1,0:T(8,128)(2,1)S(1)} %bitcast.83, bf16[2048,1024]{1,0:T(8,128)(2,1)} %head_ref.3, f32[4,1024]{1,0:T(4,128)S(1)} %concatenate.22.gains_ref, f32[1,1024]{1,0:T(1,128)S(1)} %bitcast.85, ...), custom_call_target="tpu_custom_call" | custom-call | tf_op jit(solution)/shard_map/backward/pallas_call | solution.py:332
  169.6 8.4 %all-gather.1 = f32[4,4,1024]{2,1,0:T(4,128)S(1)} all-gather(f32[1,4,1024]{2,1,0:T(4,128)S(1)} %bitcast.86), channel_id=2, replica_groups=mesh['dp'=16,'section'=4,'vocab'=8] {'section'}, dimensions={0}, use_global_device_ids=true | all-gather | bytes 81920 | tf_op jit(solution)/shard_map/all_gather | solution.py:350
  178.6 3.4 %all-to-all-start.2 = ((f32[8,4,1024]{2,1,0:T(4,128)}), f32[8,4,1024]{2,1,0:T(4,128)S(1)}, u32[]{:S(2)}, u32[]{:S(2)}) async-start(f32[8,4,1024]{2,1,0:T(4,128)} %broadcast_in_dim.54), calls=%async_computation.2 | async-start | bytes 262144 | tf_op jit(solution)/shard_map/all_to_all | solution.py:23
  182.6 7.9 %all-to-all-done.2 = f32[8,4,1024]{2,1,0:T(4,128)S(1)} async-done(((f32[8,4,1024]{2,1,0:T(4,128)}), f32[8,4,1024]{2,1,0:T(4,128)S(1)}, u32[]{:S(2)}, u32[]{:S(2)}) %all-to-all-start.2) | async-done | bytes 131104 | tf_op jit(solution)/shard_map/all_to_all | solution.py:23
  (77 shorter events, 7.4 us)
Async XLA Ops:
  0.6 19.3 %collective-permute-start.1 = (bf16[128,1024]{1,0:T(8,128)(2,1)}, bf16[128,1024]{1,0:T(8,128)(2,1)S(1)}, u32[]{:S(2)}, u32[]{:S(2)}) collective-permute-start(bf16[128,1024]{1,0:T(8,128)(2,1)} %bitcast.87), channel_id=1, source_target_pairs={{0,16},{8,24},{16,0},{24,8},{1,17},{9,25},{17,1},{25,9},{2,18},{10... | collective-permute-start | bytes 786440 | tf_op jit(solution)/shard_map/ppermute | solution.py:27
  6.1 13.8 %collective-permute-start = (bf16[128,1024]{1,0:T(8,128)(2,1)}, bf16[128,1024]{1,0:T(8,128)(2,1)S(1)}, u32[]{:S(2)}, u32[]{:S(2)}) collective-permute-start(bf16[128,1024]{1,0:T(8,128)(2,1)} %bitcast.88), channel_id=1, source_target_pairs={{0,8},{8,0},{16,24},{24,16},{1,9},{9,1},{17,25},{25,17},{2,10},{10... | collective-permute-start | bytes 786440 | tf_op jit(solution)/shard_map/ppermute | solution.py:27
  11.4 11.9 %collective-permute-start.2 = (bf16[128,1024]{1,0:T(8,128)(2,1)}, bf16[128,1024]{1,0:T(8,128)(2,1)S(1)}, u32[]{:S(2)}, u32[]{:S(2)}) collective-permute-start(bf16[128,1024]{1,0:T(8,128)(2,1)} %bitcast.89), channel_id=1, source_target_pairs={{0,24},{8,16},{16,8},{24,0},{1,25},{9,17},{17,9},{25,1},{2,26},{10... | collective-permute-start | bytes 786440 | tf_op jit(solution)/shard_map/ppermute | solution.py:27
  29.8 26.4 %copy-start.2 = (f32[32,2176]{1,0:T(8,128)S(1)}, f32[32,2176]{1,0:T(8,128)}, u32[]{:S(2)}) copy-start(f32[32,2176]{1,0:T(8,128)} %get-tuple-element.36) | copy-start | bytes 835588
  29.8 16.8 %collective-permute-start.4 = (f32[32,2176]{1,0:T(8,128)S(1)}, f32[32,2176]{1,0:T(8,128)S(1)}, u32[]{:S(2)}, u32[]{:S(2)}) collective-permute-start(f32[32,2176]{1,0:T(8,128)S(1)} %get-tuple-element.27), channel_id=1, source_target_pairs={{0,32},{32,0},{64,96},{96,64},{128,160},{160,128},{192,224},{224,1... | collective-permute-start | bytes 835592 | tf_op jit(solution)/shard_map/ppermute | solution.py:27
  31.9 16.7 %collective-permute-start.14 = (f32[32,2176]{1,0:T(8,128)}, f32[32,2176]{1,0:T(8,128)S(1)}, u32[]{:S(2)}, u32[]{:S(2)}) collective-permute-start(f32[32,2176]{1,0:T(8,128)} %get-tuple-element.38), channel_id=1, source_target_pairs={{0,448},{32,480},{64,0},{96,32},{128,64},{160,96},{192,128},{224,1... | collective-permute-start | bytes 835592 | tf_op jit(solution)/shard_map/ppermute | solution.py:27
  40.1 14.1 %collective-permute-start.8 = (f32[32,2176]{1,0:T(8,128)S(1)}, f32[32,2176]{1,0:T(8,128)S(1)}, u32[]{:S(2)}, u32[]{:S(2)}) collective-permute-start(f32[32,2176]{1,0:T(8,128)S(1)} %get-tuple-element.32), channel_id=1, source_target_pairs={{0,64},{32,96},{64,128},{96,160},{128,192},{160,224},{192,256},{22... | collective-permute-start | bytes 835592 | tf_op jit(solution)/shard_map/ppermute | solution.py:27
  42.1 14.2 %collective-permute-start.12 = (f32[32,2176]{1,0:T(8,128)}, f32[32,2176]{1,0:T(8,128)S(1)}, u32[]{:S(2)}, u32[]{:S(2)}) collective-permute-start(f32[32,2176]{1,0:T(8,128)} %get-tuple-element.35), channel_id=1, source_target_pairs={{0,448},{32,480},{64,0},{96,32},{128,64},{160,96},{192,128},{224,1... | collective-permute-start | bytes 835592 | tf_op jit(solution)/shard_map/ppermute | solution.py:27
  46.7 10.1 %collective-permute-start.5 = (f32[32,2176]{1,0:T(8,128)S(1)}, f32[32,2176]{1,0:T(8,128)S(1)}, u32[]{:S(2)}, u32[]{:S(2)}) collective-permute-start(f32[32,2176]{1,0:T(8,128)S(1)} %add.116), channel_id=1, source_target_pairs={{0,64},{32,96},{64,128},{96,160},{128,192},{160,224},{192,256},{22... | collective-permute-start | bytes 835592 | tf_op jit(solution)/shard_map/ppermute | solution.py:27
  48.6 14.8 %copy-start.1 = (f32[32,2176]{1,0:T(8,128)S(1)}, f32[32,2176]{1,0:T(8,128)}, u32[]{:S(2)}) copy-start(f32[32,2176]{1,0:T(8,128)} %get-tuple-element.40) | copy-start | bytes 835588
  49.7 13.8 %collective-permute-start.15 = (f32[32,2176]{1,0:T(8,128)S(1)}, f32[32,2176]{1,0:T(8,128)S(1)}, u32[]{:S(2)}, u32[]{:S(2)}) collective-permute-start(f32[32,2176]{1,0:T(8,128)S(1)} %add.126), channel_id=1, source_target_pairs={{0,448},{32,480},{64,0},{96,32},{128,64},{160,96},{192,128},{224,1... | collective-permute-start | bytes 835592 | tf_op jit(solution)/shard_map/ppermute | solution.py:27
  54.3 14.5 %collective-permute-start.9 = (f32[32,2176]{1,0:T(8,128)S(1)}, f32[32,2176]{1,0:T(8,128)S(1)}, u32[]{:S(2)}, u32[]{:S(2)}) collective-permute-start(f32[32,2176]{1,0:T(8,128)S(1)} %add.120), channel_id=1, source_target_pairs={{0,64},{32,96},{64,128},{96,160},{128,192},{160,224},{192,256},{22... | collective-permute-start | bytes 835592 | tf_op jit(solution)/shard_map/ppermute | solution.py:27
  56.8 17.2 %copy-start = (f32[32,2176]{1,0:T(8,128)S(1)}, f32[32,2176]{1,0:T(8,128)}, u32[]{:S(2)}) copy-start(f32[32,2176]{1,0:T(8,128)} %get-tuple-element.37) | copy-start | bytes 835588
  56.8 15.1 %collective-permute-start.6 = (f32[32,2176]{1,0:T(8,128)S(1)}, f32[32,2176]{1,0:T(8,128)S(1)}, u32[]{:S(2)}, u32[]{:S(2)}) collective-permute-start(f32[32,2176]{1,0:T(8,128)S(1)} %add.117), channel_id=1, source_target_pairs={{0,64},{32,96},{64,128},{96,160},{128,192},{160,224},{192,256},{22... | collective-permute-start | bytes 835592 | tf_op jit(solution)/shard_map/ppermute | solution.py:27
  58.9 15.0 %collective-permute-start.13 = (f32[32,2176]{1,0:T(8,128)S(1)}, f32[32,2176]{1,0:T(8,128)S(1)}, u32[]{:S(2)}, u32[]{:S(2)}) collective-permute-start(f32[32,2176]{1,0:T(8,128)S(1)} %add.124), channel_id=1, source_target_pairs={{0,448},{32,480},{64,0},{96,32},{128,64},{160,96},{192,128},{224,1... | collective-permute-start | bytes 835592 | tf_op jit(solution)/shard_map/ppermute | solution.py:27
  63.5 10.4 %collective-permute-start.16 = (f32[32,2176]{1,0:T(8,128)S(1)}, f32[32,2176]{1,0:T(8,128)S(1)}, u32[]{:S(2)}, u32[]{:S(2)}) collective-permute-start(f32[32,2176]{1,0:T(8,128)S(1)} %add.127), channel_id=1, source_target_pairs={{0,32},{32,0},{64,96},{96,64},{128,160},{160,128},{192,224},{224,1... | collective-permute-start | bytes 835592 | tf_op jit(solution)/shard_map/ppermute | solution.py:27
  66.6 18.5 %collective-permute-start.3 = (f32[32,2176]{1,0:T(8,128)S(1)}, f32[32,2176]{1,0:T(8,128)S(1)}, u32[]{:S(2)}, u32[]{:S(2)}) collective-permute-start(f32[32,2176]{1,0:T(8,128)S(1)} %get-tuple-element.26), channel_id=1, source_target_pairs={{0,32},{32,0},{64,96},{96,64},{128,160},{160,128},{192,224},{224,1... | collective-permute-start | bytes 835592 | tf_op jit(solution)/shard_map/ppermute | solution.py:27
  68.8 14.2 %collective-permute-start.10 = (f32[32,2176]{1,0:T(8,128)S(1)}, f32[32,2176]{1,0:T(8,128)S(1)}, u32[]{:S(2)}, u32[]{:S(2)}) collective-permute-start(f32[32,2176]{1,0:T(8,128)S(1)} %add.121), channel_id=1, source_target_pairs={{0,32},{32,0},{64,96},{96,64},{128,160},{160,128},{192,224},{224,1... | collective-permute-start | bytes 835592 | tf_op jit(solution)/shard_map/ppermute | solution.py:27
  72.0 11.1 %collective-permute-start.7 = (f32[32,2176]{1,0:T(8,128)S(1)}, f32[32,2176]{1,0:T(8,128)S(1)}, u32[]{:S(2)}, u32[]{:S(2)}) collective-permute-start(f32[32,2176]{1,0:T(8,128)S(1)} %add.118), channel_id=1, source_target_pairs={{0,64},{32,96},{64,128},{96,160},{128,192},{160,224},{192,256},{22... | collective-permute-start | bytes 835592 | tf_op jit(solution)/shard_map/ppermute | solution.py:27
  74.0 11.1 %collective-permute-start.17 = (f32[32,2176]{1,0:T(8,128)S(1)}, f32[32,2176]{1,0:T(8,128)S(1)}, u32[]{:S(2)}, u32[]{:S(2)}) collective-permute-start(f32[32,2176]{1,0:T(8,128)S(1)} %add_add_fusion), channel_id=1, source_target_pairs={{0,448},{32,480},{64,0},{96,32},{128,64},{160,96},{192,128},{224,1... | collective-permute-start | bytes 835592 | tf_op jit(solution)/shard_map/ppermute | solution.py:27
  83.1 8.5 %collective-permute-start.11 = (f32[32,2176]{1,0:T(8,128)S(1)}, f32[32,2176]{1,0:T(8,128)S(1)}, u32[]{:S(2)}, u32[]{:S(2)}) collective-permute-start(f32[32,2176]{1,0:T(8,128)S(1)} %add_add_fusion.2), channel_id=1, source_target_pairs={{0,64},{32,96},{64,128},{96,160},{128,192},{160,224},{192,256},{22... | collective-permute-start | bytes 835592 | tf_op jit(solution)/shard_map/ppermute | solution.py:27
  178.6 11.9 %all-to-all-start.2 = ((f32[8,4,1024]{2,1,0:T(4,128)}), f32[8,4,1024]{2,1,0:T(4,128)S(1)}, u32[]{:S(2)}, u32[]{:S(2)}) async-start(f32[8,4,1024]{2,1,0:T(4,128)} %broadcast_in_dim.54), calls=%async_computation.2 | async-start | bytes 262144 | tf_op jit(solution)/shard_map/all_to_all | solution.py:23
  190.6 0.6 copy-start.3

commit v10 on v9

--- a/solution.py
+++ b/solution.py
@@ -45,9 +45,12 @@
     ups, downs = [None, None], [None, None]
     ups[1], downs[1] = ring(term(far - 1, 1), 1), ring(term(far + 1, 1), -1)
     half_way = swap(term(far, 1)) + term(far, 0)
+    mine = swap(term(0, 1))
     downs[0] = ring(term(far + 1, 0), -1)
     ups[0] = ring(half_way, 1)
     for hops in range(far - 2, 0, -1):
+        if hops == 1:
+            downs[1], mine = lax.optimization_barrier((downs[1], mine))
         for h in (1, 0):
             ups[h] = ups[h] + term(hops + 1 - h, h)
             downs[h] = downs[h] + term(n_z - hops, h)
@@ -59,7 +62,7 @@
             else:
                 ups[h], downs[h] = ring(ups[h], 1), ring(downs[h], -1)
     ups[0] = ring(ups[0] + term(1, 0) + ups[1], 1)
-    return term(0, 0) + swap(term(0, 1)) + ups[0] + downs[0]
+    return term(0, 0) + mine + ups[0] + downs[0]
 
 
 def parts(a):

time: 192 us -> 191 us (level)
  transfers between devices with their start and end apart: 19 -> 19, of which waited for: 5 -> 6; matrix products, arithmetic and copies ran while one was open for 3% -> 3% of each run, Pallas kernels for 0% -> 0%
where the time goes in v10:
time: 191 us; the launch traced here: 190 us
  blocking collectives  77.8 us (41%)
  starting transfers between devices  67.7 us (35%)
  waiting for transfers between devices  21 us (11%)
  Pallas kernels  12 us (6%)
  other arithmetic  6.89 us (4%)
  local copies, waits for them, and re-layouts  3.57 us (2%)
    all_to_all x2, blocking collectives, exchange(): return lax.all_to_all(jnp.broadcast_to(a[None], (n,) + a.shape), axis, 0, 0)  69.4 us
    ppermute x18, starting transfers between devices, permute(): lax.ppermute(a, axis, [(i, to(i)) for i in range(lax.axis_size(axis))])  64.3 us
    ppermute x18, waiting for transfers between devices, permute(): lax.ppermute(a, axis, [(i, to(i)) for i in range(lax.axis_size(axis))])  13 us
    all_gather x1, blocking collectives, on_device(): grads = jnp.sum(lax.all_gather(grads, 'section'), axis=0)  8.37 us
    all_to_all x1, waiting for transfers between devices, exchange(): return lax.all_to_all(jnp.broadcast_to(a[None], (n,) + a.shape), axis, 0, 0)  7.93 us
    pallas_call x1, Pallas kernels, on_device(): pl.pallas_call(functools.partial(forward, n_z, block, n_dp), out_shape=[j...  6.55 us
    pallas_call x1, Pallas kernels, on_device(): pl.pallas_call(functools.partial(backward, block, shards), out_shape=(jax...  5.45 us
  transfers between devices with their start and end apart: 19, of which 6 were waited for; matrix products, arithmetic and copies ran while one was open for 3% of the time, Pallas kernels for 0%

profile of v10, /device:TPU:1, one launch (start us, length us, event | category | flops | bytes accessed | tf_op | source)
XLA Modules:
  0.0 190.0 jit_solution(1985564574873241209)
XLA Ops:
  0.6 5.5 %collective-permute-start.1 = (bf16[128,1024]{1,0:T(8,128)(2,1)}, bf16[128,1024]{1,0:T(8,128)(2,1)S(1)}, u32[]{:S(2)}, u32[]{:S(2)}) collective-permute-start(bf16[128,1024]{1,0:T(8,128)(2,1)} %bitcast.87), channel_id=1, source_target_pairs={{0,16},{8,24},{16,0},{24,8},{1,17},{9,25},{17,1},{25,9},{2,18},{10... | collective-permute-start | bytes 786440 | tf_op jit(solution)/shard_map/ppermute | solution.py:27
  6.1 5.2 %collective-permute-start = (bf16[128,1024]{1,0:T(8,128)(2,1)}, bf16[128,1024]{1,0:T(8,128)(2,1)S(1)}, u32[]{:S(2)}, u32[]{:S(2)}) collective-permute-start(bf16[128,1024]{1,0:T(8,128)(2,1)} %bitcast.88), channel_id=1, source_target_pairs={{0,8},{8,0},{16,24},{24,16},{1,9},{9,1},{17,25},{25,17},{2,10},{10... | collective-permute-start | bytes 786440 | tf_op jit(solution)/shard_map/ppermute | solution.py:27
  11.4 5.0 %collective-permute-start.2 = (bf16[128,1024]{1,0:T(8,128)(2,1)}, bf16[128,1024]{1,0:T(8,128)(2,1)S(1)}, u32[]{:S(2)}, u32[]{:S(2)}) collective-permute-start(bf16[128,1024]{1,0:T(8,128)(2,1)} %bitcast.89), channel_id=1, source_target_pairs={{0,24},{8,16},{16,8},{24,0},{1,25},{9,17},{17,9},{25,1},{2,26},{10... | collective-permute-start | bytes 786440 | tf_op jit(solution)/shard_map/ppermute | solution.py:27
  16.4 0.8 slice_compare_fusion
  17.4 1.0 broadcast_select_fusion.refs_0_
  19.9 3.4 %collective-permute-done.2.refs_3_ = bf16[128,1024]{1,0:T(8,128)(2,1)S(1)} collective-permute-done((bf16[128,1024]{1,0:T(8,128)(2,1)}, bf16[128,1024]{1,0:T(8,128)(2,1)S(1)}, u32[]{:S(2)}, u32[]{:S(2)}) %collective-permute-start.2) | collective-permute-done | bytes 262176 | tf_op jit(solution)/shard_map/ppermute | solution.py:27
  23.3 6.5 %forward.1 = (f32[32,2176]{1,0:T(8,128)S(1)}, f32[32,2176]{1,0:T(8,128)S(1)}, f32[32,2176]{1,0:T(8,128)S(1)}, f32[32,2176]{1,0:T(8,128)S(1)}, f32[32,2176]{1,0:T...) custom-call(s32[3]{0:T(128)S(1)} %pad_add_fusion.place_ref, ...), custom_call_target="tpu_custom_call" | custom-call | tf_op jit(solution)/shard_map/forward/pallas_call | solution.py:265
  29.8 2.1 %collective-permute-start.6 = (f32[32,2176]{1,0:T(8,128)S(1)}, f32[32,2176]{1,0:T(8,128)S(1)}, u32[]{:S(2)}, u32[]{:S(2)}) collective-permute-start(f32[32,2176]{1,0:T(8,128)S(1)} %get-tuple-element.32), channel_id=1, source_target_pairs={{0,32},{32,0},{64,96},{96,64},{128,160},{160,128},{192,224},{224,1... | collective-permute-start | bytes 835592 | tf_op jit(solution)/shard_map/ppermute | solution.py:27
  31.9 8.2 %collective-permute-start.3 = (f32[32,2176]{1,0:T(8,128)}, f32[32,2176]{1,0:T(8,128)S(1)}, u32[]{:S(2)}, u32[]{:S(2)}) collective-permute-start(f32[32,2176]{1,0:T(8,128)} %get-tuple-element.28), channel_id=1, source_target_pairs={{0,448},{32,480},{64,0},{96,32},{128,64},{160,96},{192,128},{224,1... | collective-permute-start | bytes 835592 | tf_op jit(solution)/shard_map/ppermute | solution.py:27
  40.1 1.9 %collective-permute-start.10 = (f32[32,2176]{1,0:T(8,128)S(1)}, f32[32,2176]{1,0:T(8,128)S(1)}, u32[]{:S(2)}, u32[]{:S(2)}) collective-permute-start(f32[32,2176]{1,0:T(8,128)S(1)} %get-tuple-element.37), channel_id=1, source_target_pairs={{0,64},{32,96},{64,128},{96,160},{128,192},{160,224},{192,256},{22... | collective-permute-start | bytes 835592 | tf_op jit(solution)/shard_map/ppermute | solution.py:27
  42.1 4.6 %collective-permute-start.14 = (f32[32,2176]{1,0:T(8,128)}, f32[32,2176]{1,0:T(8,128)S(1)}, u32[]{:S(2)}, u32[]{:S(2)}) collective-permute-start(f32[32,2176]{1,0:T(8,128)} %get-tuple-element.40), channel_id=1, source_target_pairs={{0,448},{32,480},{64,0},{96,32},{128,64},{160,96},{192,128},{224,1... | collective-permute-start | bytes 835592 | tf_op jit(solution)/shard_map/ppermute | solution.py:27
  46.7 1.9 %collective-permute-start.7 = (f32[32,2176]{1,0:T(8,128)S(1)}, f32[32,2176]{1,0:T(8,128)S(1)}, u32[]{:S(2)}, u32[]{:S(2)}) collective-permute-start(f32[32,2176]{1,0:T(8,128)S(1)} %add.117), channel_id=1, source_target_pairs={{0,64},{32,96},{64,128},{96,160},{128,192},{160,224},{192,256},{22... | collective-permute-start | bytes 835592 | tf_op jit(solution)/shard_map/ppermute | solution.py:27
  48.6 3.1 %collective-permute-start.5 = (f32[32,2176]{1,0:T(8,128)S(1)}, f32[32,2176]{1,0:T(8,128)S(1)}, u32[]{:S(2)}, u32[]{:S(2)}) collective-permute-start(f32[32,2176]{1,0:T(8,128)S(1)} %get-tuple-element.30), channel_id=1, source_target_pairs={{0,32},{32,0},{64,96},{96,64},{128,160},{160,128},{192,224},{224,1... | collective-permute-start | bytes 835592 | tf_op jit(solution)/shard_map/ppermute | solution.py:27
  51.7 1.0 add.115
  52.8 4.6 %collective-permute-start.4 = (f32[32,2176]{1,0:T(8,128)S(1)}, f32[32,2176]{1,0:T(8,128)S(1)}, u32[]{:S(2)}, u32[]{:S(2)}) collective-permute-start(f32[32,2176]{1,0:T(8,128)S(1)} %add.115), channel_id=1, source_target_pairs={{0,448},{32,480},{64,0},{96,32},{128,64},{160,96},{192,128},{224,1... | collective-permute-start | bytes 835592 | tf_op jit(solution)/shard_map/ppermute | solution.py:27
  57.4 1.9 %collective-permute-start.11 = (f32[32,2176]{1,0:T(8,128)S(1)}, f32[32,2176]{1,0:T(8,128)S(1)}, u32[]{:S(2)}, u32[]{:S(2)}) collective-permute-start(f32[32,2176]{1,0:T(8,128)S(1)} %add.121), channel_id=1, source_target_pairs={{0,64},{32,96},{64,128},{96,160},{128,192},{160,224},{192,256},{22... | collective-permute-start | bytes 835592 | tf_op jit(solution)/shard_map/ppermute | solution.py:27
  59.4 4.6 %collective-permute-start.15 = (f32[32,2176]{1,0:T(8,128)S(1)}, f32[32,2176]{1,0:T(8,128)S(1)}, u32[]{:S(2)}, u32[]{:S(2)}) collective-permute-start(f32[32,2176]{1,0:T(8,128)S(1)} %add.125), channel_id=1, source_target_pairs={{0,448},{32,480},{64,0},{96,32},{128,64},{160,96},{192,128},{224,1... | collective-permute-start | bytes 835592 | tf_op jit(solution)/shard_map/ppermute | solution.py:27
  64.0 2.1 %collective-permute-start.8 = (f32[32,2176]{1,0:T(8,128)S(1)}, f32[32,2176]{1,0:T(8,128)S(1)}, u32[]{:S(2)}, u32[]{:S(2)}) collective-permute-start(f32[32,2176]{1,0:T(8,128)S(1)} %add.118), channel_id=1, source_target_pairs={{0,64},{32,96},{64,128},{96,160},{128,192},{160,224},{192,256},{22... | collective-permute-start | bytes 835592 | tf_op jit(solution)/shard_map/ppermute | solution.py:27
  66.1 2.2 %collective-permute-start.16 = (f32[32,2176]{1,0:T(8,128)S(1)}, f32[32,2176]{1,0:T(8,128)S(1)}, u32[]{:S(2)}, u32[]{:S(2)}) collective-permute-start(f32[32,2176]{1,0:T(8,128)S(1)} %add.127), channel_id=1, source_target_pairs={{0,32},{32,0},{64,96},{96,64},{128,160},{160,128},{192,224},{224,1... | collective-permute-start | bytes 835592 | tf_op jit(solution)/shard_map/ppermute | solution.py:27
  68.4 3.1 %collective-permute-start.12 = (f32[32,2176]{1,0:T(8,128)S(1)}, f32[32,2176]{1,0:T(8,128)S(1)}, u32[]{:S(2)}, u32[]{:S(2)}) collective-permute-start(f32[32,2176]{1,0:T(8,128)S(1)} %add.122), channel_id=1, source_target_pairs={{0,32},{32,0},{64,96},{96,64},{128,160},{160,128},{192,224},{224,1... | collective-permute-start | bytes 835592 | tf_op jit(solution)/shard_map/ppermute | solution.py:27
  71.5 1.2 collective-permute-done.8
  72.7 1.9 %collective-permute-start.9 = (f32[32,2176]{1,0:T(8,128)S(1)}, f32[32,2176]{1,0:T(8,128)S(1)}, u32[]{:S(2)}, u32[]{:S(2)}) collective-permute-start(f32[32,2176]{1,0:T(8,128)S(1)} %add.119), channel_id=1, source_target_pairs={{0,64},{32,96},{64,128},{96,160},{128,192},{160,224},{192,256},{22... | collective-permute-start | bytes 835592 | tf_op jit(solution)/shard_map/ppermute | solution.py:27
  74.7 4.6 %collective-permute-start.17 = (f32[32,2176]{1,0:T(8,128)S(1)}, f32[32,2176]{1,0:T(8,128)S(1)}, u32[]{:S(2)}, u32[]{:S(2)}) collective-permute-start(f32[32,2176]{1,0:T(8,128)S(1)} %add_add_fusion), channel_id=1, source_target_pairs={{0,448},{32,480},{64,0},{96,32},{128,64},{160,96},{192,128},{224,1... | collective-permute-start | bytes 835592 | tf_op jit(solution)/shard_map/ppermute | solution.py:27
  79.6 1.6 collective-permute-done.9
  81.2 1.9 %collective-permute-start.13 = (f32[32,2176]{1,0:T(8,128)S(1)}, f32[32,2176]{1,0:T(8,128)S(1)}, u32[]{:S(2)}, u32[]{:S(2)}) collective-permute-start(f32[32,2176]{1,0:T(8,128)S(1)} %add_add_fusion.2), channel_id=1, source_target_pairs={{0,64},{32,96},{64,128},{96,160},{128,192},{160,224},{192,256},{22... | collective-permute-start | bytes 835592 | tf_op jit(solution)/shard_map/ppermute | solution.py:27
  83.2 6.6 %collective-permute-done.13 = f32[32,2176]{1,0:T(8,128)S(1)} collective-permute-done((f32[32,2176]{1,0:T(8,128)S(1)}, f32[32,2176]{1,0:T(8,128)S(1)}, u32[]{:S(2)}, u32[]{:S(2)}) %collective-permute-start.13) | collective-permute-done | bytes 278560 | tf_op jit(solution)/shard_map/ppermute | solution.py:27
  91.2 24.9 %all_to_all.15 = f32[32,8,14]{2,1,0:T(8,128)S(1)} all-to-all(f32[32,8,14]{2,1,0:T(8,128)S(1)} %broadcast_in_dim.52), channel_id=1, replica_groups=mesh['dp'=16,'section'=4,'vocab'=8] {'section','vocab'}, dimensions={0} | all-to-all | bytes 28672 | tf_op jit(solution)/shard_map/all_to_all | solution.py:23
  118.4 44.5 %all_to_all.16 = bf16[16,24,2176]{2,1,0:T(8,128)(2,1)S(1)} all-to-all(bf16[16,24,2176]{2,1,0:T(8,128)(2,1)S(1)} %broadcast_in_dim.53), channel_id=1, replica_groups=mesh['dp'=16,'section'=4,'vocab'=8] {'dp'}, dimensions={0} | all-to-all | bytes 3342336 | tf_op jit(solution)/shard_map/all_to_all | solution.py:23
  163.0 5.4 %backward.1 = (f32[4,1024]{1,0:T(4,128)S(1)}, f32[128,128]{1,0:T(8,128)S(1)}) custom-call(s32[3]{0:T(128)S(1)} %pad_add_fusion.place_ref, bf16[384,2176]{1,0:T(8,128)(2,1)S(1)} %bitcast.83, bf16[2048,1024]{1,0:T(8,128)(2,1)} %head_ref.3, f32[4,1024]{1,0:T(4,128)S(1)} %concatenate.22.gains_ref, f32[1,1024]{1,0:T(1,128)S(1)} %bitcast.85, ...), custom_call_target="tpu_custom_call" | custom-call | tf_op jit(solution)/shard_map/backward/pallas_call | solution.py:335
  168.4 8.4 %all-gather.1 = f32[4,4,1024]{2,1,0:T(4,128)S(1)} all-gather(f32[1,4,1024]{2,1,0:T(4,128)S(1)} %bitcast.86), channel_id=2, replica_groups=mesh['dp'=16,'section'=4,'vocab'=8] {'section'}, dimensions={0}, use_global_device_ids=true | all-gather | bytes 81920 | tf_op jit(solution)/shard_map/all_gather | solution.py:353
  177.5 3.4 %all-to-all-start.2 = ((f32[8,4,1024]{2,1,0:T(4,128)}), f32[8,4,1024]{2,1,0:T(4,128)S(1)}, u32[]{:S(2)}, u32[]{:S(2)}) async-start(f32[8,4,1024]{2,1,0:T(4,128)} %broadcast_in_dim.54), calls=%async_computation.2 | async-start | bytes 262144 | tf_op jit(solution)/shard_map/all_to_all | solution.py:23
  181.5 7.9 %all-to-all-done.2 = f32[8,4,1024]{2,1,0:T(4,128)S(1)} async-done(((f32[8,4,1024]{2,1,0:T(4,128)}), f32[8,4,1024]{2,1,0:T(4,128)S(1)}, u32[]{:S(2)}, u32[]{:S(2)}) %all-to-all-start.2) | async-done | bytes 131104 | tf_op jit(solution)/shard_map/all_to_all | solution.py:23
  (77 shorter events, 8.0 us)
Async XLA Ops:
  0.6 19.3 %collective-permute-start.1 = (bf16[128,1024]{1,0:T(8,128)(2,1)}, bf16[128,1024]{1,0:T(8,128)(2,1)S(1)}, u32[]{:S(2)}, u32[]{:S(2)}) collective-permute-start(bf16[128,1024]{1,0:T(8,128)(2,1)} %bitcast.87), channel_id=1, source_target_pairs={{0,16},{8,24},{16,0},{24,8},{1,17},{9,25},{17,1},{25,9},{2,18},{10... | collective-permute-start | bytes 786440 | tf_op jit(solution)/shard_map/ppermute | solution.py:27
  6.1 13.8 %collective-permute-start = (bf16[128,1024]{1,0:T(8,128)(2,1)}, bf16[128,1024]{1,0:T(8,128)(2,1)S(1)}, u32[]{:S(2)}, u32[]{:S(2)}) collective-permute-start(bf16[128,1024]{1,0:T(8,128)(2,1)} %bitcast.88), channel_id=1, source_target_pairs={{0,8},{8,0},{16,24},{24,16},{1,9},{9,1},{17,25},{25,17},{2,10},{10... | collective-permute-start | bytes 786440 | tf_op jit(solution)/shard_map/ppermute | solution.py:27
  11.4 11.9 %collective-permute-start.2 = (bf16[128,1024]{1,0:T(8,128)(2,1)}, bf16[128,1024]{1,0:T(8,128)(2,1)S(1)}, u32[]{:S(2)}, u32[]{:S(2)}) collective-permute-start(bf16[128,1024]{1,0:T(8,128)(2,1)} %bitcast.89), channel_id=1, source_target_pairs={{0,24},{8,16},{16,8},{24,0},{1,25},{9,17},{17,9},{25,1},{2,26},{10... | collective-permute-start | bytes 786440 | tf_op jit(solution)/shard_map/ppermute | solution.py:27
  29.8 29.5 %copy-start.2 = (f32[32,2176]{1,0:T(8,128)S(1)}, f32[32,2176]{1,0:T(8,128)}, u32[]{:S(2)}) copy-start(f32[32,2176]{1,0:T(8,128)} %get-tuple-element.41) | copy-start | bytes 835588
  29.8 16.8 %collective-permute-start.6 = (f32[32,2176]{1,0:T(8,128)S(1)}, f32[32,2176]{1,0:T(8,128)S(1)}, u32[]{:S(2)}, u32[]{:S(2)}) collective-permute-start(f32[32,2176]{1,0:T(8,128)S(1)} %get-tuple-element.32), channel_id=1, source_target_pairs={{0,32},{32,0},{64,96},{96,64},{128,160},{160,128},{192,224},{224,1... | collective-permute-start | bytes 835592 | tf_op jit(solution)/shard_map/ppermute | solution.py:27
  31.9 19.8 %collective-permute-start.3 = (f32[32,2176]{1,0:T(8,128)}, f32[32,2176]{1,0:T(8,128)S(1)}, u32[]{:S(2)}, u32[]{:S(2)}) collective-permute-start(f32[32,2176]{1,0:T(8,128)} %get-tuple-element.28), channel_id=1, source_target_pairs={{0,448},{32,480},{64,0},{96,32},{128,64},{160,96},{192,128},{224,1... | collective-permute-start | bytes 835592 | tf_op jit(solution)/shard_map/ppermute | solution.py:27
  40.1 17.2 %collective-permute-start.10 = (f32[32,2176]{1,0:T(8,128)S(1)}, f32[32,2176]{1,0:T(8,128)S(1)}, u32[]{:S(2)}, u32[]{:S(2)}) collective-permute-start(f32[32,2176]{1,0:T(8,128)S(1)} %get-tuple-element.37), channel_id=1, source_target_pairs={{0,64},{32,96},{64,128},{96,160},{128,192},{160,224},{192,256},{22... | collective-permute-start | bytes 835592 | tf_op jit(solution)/shard_map/ppermute | solution.py:27
  42.1 17.3 %collective-permute-start.14 = (f32[32,2176]{1,0:T(8,128)}, f32[32,2176]{1,0:T(8,128)S(1)}, u32[]{:S(2)}, u32[]{:S(2)}) collective-permute-start(f32[32,2176]{1,0:T(8,128)} %get-tuple-element.40), channel_id=1, source_target_pairs={{0,448},{32,480},{64,0},{96,32},{128,64},{160,96},{192,128},{224,1... | collective-permute-start | bytes 835592 | tf_op jit(solution)/shard_map/ppermute | solution.py:27
  46.7 17.3 %collective-permute-start.7 = (f32[32,2176]{1,0:T(8,128)S(1)}, f32[32,2176]{1,0:T(8,128)S(1)}, u32[]{:S(2)}, u32[]{:S(2)}) collective-permute-start(f32[32,2176]{1,0:T(8,128)S(1)} %add.117), channel_id=1, source_target_pairs={{0,64},{32,96},{64,128},{96,160},{128,192},{160,224},{192,256},{22... | collective-permute-start | bytes 835592 | tf_op jit(solution)/shard_map/ppermute | solution.py:27
  48.6 17.5 %collective-permute-start.5 = (f32[32,2176]{1,0:T(8,128)S(1)}, f32[32,2176]{1,0:T(8,128)S(1)}, u32[]{:S(2)}, u32[]{:S(2)}) collective-permute-start(f32[32,2176]{1,0:T(8,128)S(1)} %get-tuple-element.30), channel_id=1, source_target_pairs={{0,32},{32,0},{64,96},{96,64},{128,160},{160,128},{192,224},{224,1... | collective-permute-start | bytes 835592 | tf_op jit(solution)/shard_map/ppermute | solution.py:27
  51.7 14.4 %copy-start.1 = (f32[32,2176]{1,0:T(8,128)S(1)}, f32[32,2176]{1,0:T(8,128)}, u32[]{:S(2)}) copy-start(f32[32,2176]{1,0:T(8,128)} %get-tuple-element.44) | copy-start | bytes 835588
  52.8 13.3 %collective-permute-start.4 = (f32[32,2176]{1,0:T(8,128)S(1)}, f32[32,2176]{1,0:T(8,128)S(1)}, u32[]{:S(2)}, u32[]{:S(2)}) collective-permute-start(f32[32,2176]{1,0:T(8,128)S(1)} %add.115), channel_id=1, source_target_pairs={{0,448},{32,480},{64,0},{96,32},{128,64},{160,96},{192,128},{224,1... | collective-permute-start | bytes 835592 | tf_op jit(solution)/shard_map/ppermute | solution.py:27
  57.4 11.0 %collective-permute-start.11 = (f32[32,2176]{1,0:T(8,128)S(1)}, f32[32,2176]{1,0:T(8,128)S(1)}, u32[]{:S(2)}, u32[]{:S(2)}) collective-permute-start(f32[32,2176]{1,0:T(8,128)S(1)} %add.121), channel_id=1, source_target_pairs={{0,64},{32,96},{64,128},{96,160},{128,192},{160,224},{192,256},{22... | collective-permute-start | bytes 835592 | tf_op jit(solution)/shard_map/ppermute | solution.py:27
  59.4 15.2 %collective-permute-start.15 = (f32[32,2176]{1,0:T(8,128)S(1)}, f32[32,2176]{1,0:T(8,128)S(1)}, u32[]{:S(2)}, u32[]{:S(2)}) collective-permute-start(f32[32,2176]{1,0:T(8,128)S(1)} %add.125), channel_id=1, source_target_pairs={{0,448},{32,480},{64,0},{96,32},{128,64},{160,96},{192,128},{224,1... | collective-permute-start | bytes 835592 | tf_op jit(solution)/shard_map/ppermute | solution.py:27
  64.0 10.7 %copy-start = (f32[32,2176]{1,0:T(8,128)S(1)}, f32[32,2176]{1,0:T(8,128)}, u32[]{:S(2)}) copy-start(f32[32,2176]{1,0:T(8,128)} %get-tuple-element.42) | copy-start | bytes 835588
  64.0 8.6 %collective-permute-start.8 = (f32[32,2176]{1,0:T(8,128)S(1)}, f32[32,2176]{1,0:T(8,128)S(1)}, u32[]{:S(2)}, u32[]{:S(2)}) collective-permute-start(f32[32,2176]{1,0:T(8,128)S(1)} %add.118), channel_id=1, source_target_pairs={{0,64},{32,96},{64,128},{96,160},{128,192},{160,224},{192,256},{22... | collective-permute-start | bytes 835592 | tf_op jit(solution)/shard_map/ppermute | solution.py:27
  66.1 8.5 %collective-permute-start.16 = (f32[32,2176]{1,0:T(8,128)S(1)}, f32[32,2176]{1,0:T(8,128)S(1)}, u32[]{:S(2)}, u32[]{:S(2)}) collective-permute-start(f32[32,2176]{1,0:T(8,128)S(1)} %add.127), channel_id=1, source_target_pairs={{0,32},{32,0},{64,96},{96,64},{128,160},{160,128},{192,224},{224,1... | collective-permute-start | bytes 835592 | tf_op jit(solution)/shard_map/ppermute | solution.py:27
  68.4 11.2 %collective-permute-start.12 = (f32[32,2176]{1,0:T(8,128)S(1)}, f32[32,2176]{1,0:T(8,128)S(1)}, u32[]{:S(2)}, u32[]{:S(2)}) collective-permute-start(f32[32,2176]{1,0:T(8,128)S(1)} %add.122), channel_id=1, source_target_pairs={{0,32},{32,0},{64,96},{96,64},{128,160},{160,128},{192,224},{224,1... | collective-permute-start | bytes 835592 | tf_op jit(solution)/shard_map/ppermute | solution.py:27
  72.7 8.5 %collective-permute-start.9 = (f32[32,2176]{1,0:T(8,128)S(1)}, f32[32,2176]{1,0:T(8,128)S(1)}, u32[]{:S(2)}, u32[]{:S(2)}) collective-permute-start(f32[32,2176]{1,0:T(8,128)S(1)} %add.119), channel_id=1, source_target_pairs={{0,64},{32,96},{64,128},{96,160},{128,192},{160,224},{192,256},{22... | collective-permute-start | bytes 835592 | tf_op jit(solution)/shard_map/ppermute | solution.py:27
  74.7 8.5 %collective-permute-start.17 = (f32[32,2176]{1,0:T(8,128)S(1)}, f32[32,2176]{1,0:T(8,128)S(1)}, u32[]{:S(2)}, u32[]{:S(2)}) collective-permute-start(f32[32,2176]{1,0:T(8,128)S(1)} %add_add_fusion), channel_id=1, source_target_pairs={{0,448},{32,480},{64,0},{96,32},{128,64},{160,96},{192,128},{224,1... | collective-permute-start | bytes 835592 | tf_op jit(solution)/shard_map/ppermute | solution.py:27
  81.2 8.5 %collective-permute-start.13 = (f32[32,2176]{1,0:T(8,128)S(1)}, f32[32,2176]{1,0:T(8,128)S(1)}, u32[]{:S(2)}, u32[]{:S(2)}) collective-permute-start(f32[32,2176]{1,0:T(8,128)S(1)} %add_add_fusion.2), channel_id=1, source_target_pairs={{0,64},{32,96},{64,128},{96,160},{128,192},{160,224},{192,256},{22... | collective-permute-start | bytes 835592 | tf_op jit(solution)/shard_map/ppermute | solution.py:27
  177.5 11.9 %all-to-all-start.2 = ((f32[8,4,1024]{2,1,0:T(4,128)}), f32[8,4,1024]{2,1,0:T(4,128)S(1)}, u32[]{:S(2)}, u32[]{:S(2)}) async-start(f32[8,4,1024]{2,1,0:T(4,128)} %broadcast_in_dim.54), calls=%async_computation.2 | async-start | bytes 262144 | tf_op jit(solution)/shard_map/all_to_all | solution.py:23
  189.4 0.6 copy-start.3

commit v11 on v10

--- a/solution.py
+++ b/solution.py
@@ -51,6 +51,8 @@
     for hops in range(far - 2, 0, -1):
         if hops == 1:
             downs[1], mine = lax.optimization_barrier((downs[1], mine))
+        else:
+            ups[0], downs[0] = lax.optimization_barrier((ups[0], downs[0]))
         for h in (1, 0):
             ups[h] = ups[h] + term(hops + 1 - h, h)
             downs[h] = downs[h] + term(n_z - hops, h)

time: 191 us -> 195 us (1.021)
  waiting for transfers between devices: 21 us -> 24.6 us
    ppermute x18, waiting for transfers between devices: 13 us -> 16.7 us  [permute(): lax.ppermute(a, axis, [(i, to(i)) for i in range(lax.axis_size(axis))])]
where the time goes in v11:
time: 195 us; the launch traced here: 194 us
  blocking collectives  79.5 us (41%)
  starting transfers between devices  66.5 us (34%)
  waiting for transfers between devices  24.6 us (13%)
  Pallas kernels  12 us (6%)
  other arithmetic  6.89 us (4%)
  local copies, waits for them, and re-layouts  3.57 us (2%)
    all_to_all x2, blocking collectives, exchange(): return lax.all_to_all(jnp.broadcast_to(a[None], (n,) + a.shape), axis, 0, 0)  71.1 us
    ppermute x18, starting transfers between devices, permute(): lax.ppermute(a, axis, [(i, to(i)) for i in range(lax.axis_size(axis))])  63.1 us
    ppermute x18, waiting for transfers between devices, permute(): lax.ppermute(a, axis, [(i, to(i)) for i in range(lax.axis_size(axis))])  16.7 us
    all_gather x1, blocking collectives, on_device(): grads = jnp.sum(lax.all_gather(grads, 'section'), axis=0)  8.37 us
    all_to_all x1, waiting for transfers between devices, exchange(): return lax.all_to_all(jnp.broadcast_to(a[None], (n,) + a.shape), axis, 0, 0)  7.93 us
    pallas_call x1, Pallas kernels, on_device(): pl.pallas_call(functools.partial(forward, n_z, block, n_dp), out_shape=[j...  6.55 us
    pallas_call x1, Pallas kernels, on_device(): pl.pallas_call(functools.partial(backward, block, shards), out_shape=(jax...  5.45 us
  transfers between devices with their start and end apart: 19, of which 6 were waited for; matrix products, arithmetic and copies ran while one was open for 3% of the time, Pallas kernels for 0%

profile of v11, /device:TPU:1, one launch (start us, length us, event | category | flops | bytes accessed | tf_op | source)
XLA Modules:
  0.0 194.1 jit_solution(17119510917862095779)
XLA Ops:
  0.6 5.5 %collective-permute-start.1 = (bf16[128,1024]{1,0:T(8,128)(2,1)}, bf16[128,1024]{1,0:T(8,128)(2,1)S(1)}, u32[]{:S(2)}, u32[]{:S(2)}) collective-permute-start(bf16[128,1024]{1,0:T(8,128)(2,1)} %bitcast.87), channel_id=1, source_target_pairs={{0,16},{8,24},{16,0},{24,8},{1,17},{9,25},{17,1},{25,9},{2,18},{10... | collective-permute-start | bytes 786440 | tf_op jit(solution)/shard_map/ppermute | solution.py:27
  6.1 5.2 %collective-permute-start = (bf16[128,1024]{1,0:T(8,128)(2,1)}, bf16[128,1024]{1,0:T(8,128)(2,1)S(1)}, u32[]{:S(2)}, u32[]{:S(2)}) collective-permute-start(bf16[128,1024]{1,0:T(8,128)(2,1)} %bitcast.88), channel_id=1, source_target_pairs={{0,8},{8,0},{16,24},{24,16},{1,9},{9,1},{17,25},{25,17},{2,10},{10... | collective-permute-start | bytes 786440 | tf_op jit(solution)/shard_map/ppermute | solution.py:27
  11.4 5.0 %collective-permute-start.2 = (bf16[128,1024]{1,0:T(8,128)(2,1)}, bf16[128,1024]{1,0:T(8,128)(2,1)S(1)}, u32[]{:S(2)}, u32[]{:S(2)}) collective-permute-start(bf16[128,1024]{1,0:T(8,128)(2,1)} %bitcast.89), channel_id=1, source_target_pairs={{0,24},{8,16},{16,8},{24,0},{1,25},{9,17},{17,9},{25,1},{2,26},{10... | collective-permute-start | bytes 786440 | tf_op jit(solution)/shard_map/ppermute | solution.py:27
  17.4 1.0 broadcast_select_fusion.refs_0_
  19.9 3.4 %collective-permute-done.2.refs_3_ = bf16[128,1024]{1,0:T(8,128)(2,1)S(1)} collective-permute-done((bf16[128,1024]{1,0:T(8,128)(2,1)}, bf16[128,1024]{1,0:T(8,128)(2,1)S(1)}, u32[]{:S(2)}, u32[]{:S(2)}) %collective-permute-start.2) | collective-permute-done | bytes 262176 | tf_op jit(solution)/shard_map/ppermute | solution.py:27
  23.3 6.5 %forward.1 = (f32[32,2176]{1,0:T(8,128)S(1)}, f32[32,2176]{1,0:T(8,128)S(1)}, f32[32,2176]{1,0:T(8,128)S(1)}, f32[32,2176]{1,0:T(8,128)S(1)}, f32[32,2176]{1,0:T...) custom-call(s32[3]{0:T(128)S(1)} %pad_add_fusion.place_ref, ...), custom_call_target="tpu_custom_call" | custom-call | tf_op jit(solution)/shard_map/forward/pallas_call | solution.py:267
  29.8 7.9 %collective-permute-start.3 = (f32[32,2176]{1,0:T(8,128)}, f32[32,2176]{1,0:T(8,128)S(1)}, u32[]{:S(2)}, u32[]{:S(2)}) collective-permute-start(f32[32,2176]{1,0:T(8,128)} %get-tuple-element.30), channel_id=1, source_target_pairs={{0,448},{32,480},{64,0},{96,32},{128,64},{160,96},{192,128},{224,1... | collective-permute-start | bytes 835592 | tf_op jit(solution)/shard_map/ppermute | solution.py:27
  37.8 2.2 %collective-permute-start.6 = (f32[32,2176]{1,0:T(8,128)S(1)}, f32[32,2176]{1,0:T(8,128)S(1)}, u32[]{:S(2)}, u32[]{:S(2)}) collective-permute-start(f32[32,2176]{1,0:T(8,128)S(1)} %get-tuple-element.34), channel_id=1, source_target_pairs={{0,32},{32,0},{64,96},{96,64},{128,160},{160,128},{192,224},{224,1... | collective-permute-start | bytes 835592 | tf_op jit(solution)/shard_map/ppermute | solution.py:27
  40.0 3.1 %collective-permute-start.5 = (f32[32,2176]{1,0:T(8,128)S(1)}, f32[32,2176]{1,0:T(8,128)S(1)}, u32[]{:S(2)}, u32[]{:S(2)}) collective-permute-start(f32[32,2176]{1,0:T(8,128)S(1)} %get-tuple-element.32), channel_id=1, source_target_pairs={{0,32},{32,0},{64,96},{96,64},{128,160},{160,128},{192,224},{224,1... | collective-permute-start | bytes 835592 | tf_op jit(solution)/shard_map/ppermute | solution.py:27
  43.1 1.9 collective-permute-start.11
  45.0 4.6 %collective-permute-start.8 = (f32[32,2176]{1,0:T(8,128)}, f32[32,2176]{1,0:T(8,128)S(1)}, u32[]{:S(2)}, u32[]{:S(2)}) collective-permute-start(f32[32,2176]{1,0:T(8,128)} %get-tuple-element.36), channel_id=1, source_target_pairs={{0,448},{32,480},{64,0},{96,32},{128,64},{160,96},{192,128},{224,1... | collective-permute-start | bytes 835592 | tf_op jit(solution)/shard_map/ppermute | solution.py:27
  49.6 1.0 add.115
  50.6 1.9 collective-permute-start.4
  52.6 3.5 %collective-permute-start.7 = (f32[32,2176]{1,0:T(8,128)S(1)}, f32[32,2176]{1,0:T(8,128)S(1)}, u32[]{:S(2)}, u32[]{:S(2)}) collective-permute-start(f32[32,2176]{1,0:T(8,128)S(1)} %add.117), channel_id=1, source_target_pairs={{0,64},{32,96},{64,128},{96,160},{128,192},{160,224},{192,256},{22... | collective-permute-start | bytes 835592 | tf_op jit(solution)/shard_map/ppermute | solution.py:27
  56.2 1.9 collective-permute-start.12
  58.1 2.4 %collective-permute-done.4 = f32[32,2176]{1,0:T(8,128)S(1)} collective-permute-done((f32[32,2176]{1,0:T(8,128)S(1)}, f32[32,2176]{1,0:T(8,128)S(1)}, u32[]{:S(2)}, u32[]{:S(2)}) %collective-permute-start.4) | collective-permute-done | bytes 278560 | tf_op jit(solution)/shard_map/ppermute | solution.py:27
  60.5 2.0 %collective-permute-done.7 = f32[32,2176]{1,0:T(8,128)S(1)} collective-permute-done((f32[32,2176]{1,0:T(8,128)S(1)}, f32[32,2176]{1,0:T(8,128)S(1)}, u32[]{:S(2)}, u32[]{:S(2)}) %collective-permute-start.7) | collective-permute-done | bytes 278560 | tf_op jit(solution)/shard_map/ppermute | solution.py:27
  62.6 1.9 collective-permute-start.9
  64.6 2.3 %collective-permute-start.16 = (f32[32,2176]{1,0:T(8,128)S(1)}, f32[32,2176]{1,0:T(8,128)S(1)}, u32[]{:S(2)}, u32[]{:S(2)}) collective-permute-start(f32[32,2176]{1,0:T(8,128)S(1)} %add.127), channel_id=1, source_target_pairs={{0,32},{32,0},{64,96},{96,64},{128,160},{160,128},{192,224},{224,1... | collective-permute-start | bytes 835592 | tf_op jit(solution)/shard_map/ppermute | solution.py:27
  67.0 4.6 %collective-permute-start.15 = (f32[32,2176]{1,0:T(8,128)S(1)}, f32[32,2176]{1,0:T(8,128)S(1)}, u32[]{:S(2)}, u32[]{:S(2)}) collective-permute-start(f32[32,2176]{1,0:T(8,128)S(1)} %add.125), channel_id=1, source_target_pairs={{0,448},{32,480},{64,0},{96,32},{128,64},{160,96},{192,128},{224,1... | collective-permute-start | bytes 835592 | tf_op jit(solution)/shard_map/ppermute | solution.py:27
  71.6 3.1 %collective-permute-start.13 = (f32[32,2176]{1,0:T(8,128)S(1)}, f32[32,2176]{1,0:T(8,128)S(1)}, u32[]{:S(2)}, u32[]{:S(2)}) collective-permute-start(f32[32,2176]{1,0:T(8,128)S(1)} %add.122), channel_id=1, source_target_pairs={{0,32},{32,0},{64,96},{96,64},{128,160},{160,128},{192,224},{224,1... | collective-permute-start | bytes 835592 | tf_op jit(solution)/shard_map/ppermute | solution.py:27
  74.7 1.9 collective-permute-start.10
  76.7 4.6 %collective-permute-start.17 = (f32[32,2176]{1,0:T(8,128)S(1)}, f32[32,2176]{1,0:T(8,128)S(1)}, u32[]{:S(2)}, u32[]{:S(2)}) collective-permute-start(f32[32,2176]{1,0:T(8,128)S(1)} %add_add_fusion), channel_id=1, source_target_pairs={{0,448},{32,480},{64,0},{96,32},{128,64},{160,96},{192,128},{224,1... | collective-permute-start | bytes 835592 | tf_op jit(solution)/shard_map/ppermute | solution.py:27
  81.3 1.9 collective-permute-done.10
  83.3 1.9 collective-permute-start.14
  85.2 6.9 %collective-permute-done.14 = f32[32,2176]{1,0:T(8,128)S(1)} collective-permute-done((f32[32,2176]{1,0:T(8,128)S(1)}, f32[32,2176]{1,0:T(8,128)S(1)}, u32[]{:S(2)}, u32[]{:S(2)}) %collective-permute-start.14) | collective-permute-done | bytes 278560 | tf_op jit(solution)/shard_map/ppermute | solution.py:27
  93.7 26.6 %all_to_all.15 = f32[32,8,14]{2,1,0:T(8,128)S(1)} all-to-all(f32[32,8,14]{2,1,0:T(8,128)S(1)} %broadcast_in_dim.52), channel_id=1, replica_groups=mesh['dp'=16,'section'=4,'vocab'=8] {'section','vocab'}, dimensions={0} | all-to-all | bytes 28672 | tf_op jit(solution)/shard_map/all_to_all | solution.py:23
  122.5 44.5 %all_to_all.16 = bf16[16,24,2176]{2,1,0:T(8,128)(2,1)S(1)} all-to-all(bf16[16,24,2176]{2,1,0:T(8,128)(2,1)S(1)} %broadcast_in_dim.53), channel_id=1, replica_groups=mesh['dp'=16,'section'=4,'vocab'=8] {'dp'}, dimensions={0} | all-to-all | bytes 3342336 | tf_op jit(solution)/shard_map/all_to_all | solution.py:23
  167.1 5.4 %backward.1 = (f32[4,1024]{1,0:T(4,128)S(1)}, f32[128,128]{1,0:T(8,128)S(1)}) custom-call(s32[3]{0:T(128)S(1)} %pad_add_fusion.place_ref, bf16[384,2176]{1,0:T(8,128)(2,1)S(1)} %bitcast.83, bf16[2048,1024]{1,0:T(8,128)(2,1)} %head_ref.3, f32[4,1024]{1,0:T(4,128)S(1)} %concatenate.22.gains_ref, f32[1,1024]{1,0:T(1,128)S(1)} %bitcast.85, ...), custom_call_target="tpu_custom_call" | custom-call | tf_op jit(solution)/shard_map/backward/pallas_call | solution.py:337
  172.5 8.4 %all-gather.1 = f32[4,4,1024]{2,1,0:T(4,128)S(1)} all-gather(f32[1,4,1024]{2,1,0:T(4,128)S(1)} %bitcast.86), channel_id=2, replica_groups=mesh['dp'=16,'section'=4,'vocab'=8] {'section'}, dimensions={0}, use_global_device_ids=true | all-gather | bytes 81920 | tf_op jit(solution)/shard_map/all_gather | solution.py:355
  181.6 3.4 %all-to-all-start.2 = ((f32[8,4,1024]{2,1,0:T(4,128)}), f32[8,4,1024]{2,1,0:T(4,128)S(1)}, u32[]{:S(2)}, u32[]{:S(2)}) async-start(f32[8,4,1024]{2,1,0:T(4,128)} %broadcast_in_dim.54), calls=%async_computation.2 | async-start | bytes 262144 | tf_op jit(solution)/shard_map/all_to_all | solution.py:23
  185.6 7.9 %all-to-all-done.2 = f32[8,4,1024]{2,1,0:T(4,128)S(1)} async-done(((f32[8,4,1024]{2,1,0:T(4,128)}), f32[8,4,1024]{2,1,0:T(4,128)S(1)}, u32[]{:S(2)}, u32[]{:S(2)}) %all-to-all-start.2) | async-done | bytes 131104 | tf_op jit(solution)/shard_map/all_to_all | solution.py:23
  (77 shorter events, 8.5 us)
Async XLA Ops:
  0.6 19.3 %collective-permute-start.1 = (bf16[128,1024]{1,0:T(8,128)(2,1)}, bf16[128,1024]{1,0:T(8,128)(2,1)S(1)}, u32[]{:S(2)}, u32[]{:S(2)}) collective-permute-start(bf16[128,1024]{1,0:T(8,128)(2,1)} %bitcast.87), channel_id=1, source_target_pairs={{0,16},{8,24},{16,0},{24,8},{1,17},{9,25},{17,1},{25,9},{2,18},{10... | collective-permute-start | bytes 786440 | tf_op jit(solution)/shard_map/ppermute | solution.py:27
  6.1 13.8 %collective-permute-start = (bf16[128,1024]{1,0:T(8,128)(2,1)}, bf16[128,1024]{1,0:T(8,128)(2,1)S(1)}, u32[]{:S(2)}, u32[]{:S(2)}) collective-permute-start(bf16[128,1024]{1,0:T(8,128)(2,1)} %bitcast.88), channel_id=1, source_target_pairs={{0,8},{8,0},{16,24},{24,16},{1,9},{9,1},{17,25},{25,17},{2,10},{10... | collective-permute-start | bytes 786440 | tf_op jit(solution)/shard_map/ppermute | solution.py:27
  11.4 11.9 %collective-permute-start.2 = (bf16[128,1024]{1,0:T(8,128)(2,1)}, bf16[128,1024]{1,0:T(8,128)(2,1)S(1)}, u32[]{:S(2)}, u32[]{:S(2)}) collective-permute-start(bf16[128,1024]{1,0:T(8,128)(2,1)} %bitcast.89), channel_id=1, source_target_pairs={{0,24},{8,16},{16,8},{24,0},{1,25},{9,17},{17,9},{25,1},{2,26},{10... | collective-permute-start | bytes 786440 | tf_op jit(solution)/shard_map/ppermute | solution.py:27
  29.8 19.7 %collective-permute-start.3 = (f32[32,2176]{1,0:T(8,128)}, f32[32,2176]{1,0:T(8,128)S(1)}, u32[]{:S(2)}, u32[]{:S(2)}) collective-permute-start(f32[32,2176]{1,0:T(8,128)} %get-tuple-element.30), channel_id=1, source_target_pairs={{0,448},{32,480},{64,0},{96,32},{128,64},{160,96},{192,128},{224,1... | collective-permute-start | bytes 835592 | tf_op jit(solution)/shard_map/ppermute | solution.py:27
  37.8 14.8 %collective-permute-start.6 = (f32[32,2176]{1,0:T(8,128)S(1)}, f32[32,2176]{1,0:T(8,128)S(1)}, u32[]{:S(2)}, u32[]{:S(2)}) collective-permute-start(f32[32,2176]{1,0:T(8,128)S(1)} %get-tuple-element.34), channel_id=1, source_target_pairs={{0,32},{32,0},{64,96},{96,64},{128,160},{160,128},{192,224},{224,1... | collective-permute-start | bytes 835592 | tf_op jit(solution)/shard_map/ppermute | solution.py:27
  40.0 18.1 %collective-permute-start.5 = (f32[32,2176]{1,0:T(8,128)S(1)}, f32[32,2176]{1,0:T(8,128)S(1)}, u32[]{:S(2)}, u32[]{:S(2)}) collective-permute-start(f32[32,2176]{1,0:T(8,128)S(1)} %get-tuple-element.32), channel_id=1, source_target_pairs={{0,32},{32,0},{64,96},{96,64},{128,160},{160,128},{192,224},{224,1... | collective-permute-start | bytes 835592 | tf_op jit(solution)/shard_map/ppermute | solution.py:27
  43.1 13.1 %collective-permute-start.11 = (f32[32,2176]{1,0:T(8,128)S(1)}, f32[32,2176]{1,0:T(8,128)S(1)}, u32[]{:S(2)}, u32[]{:S(2)}) collective-permute-start(f32[32,2176]{1,0:T(8,128)S(1)} %get-tuple-element.41), channel_id=1, source_target_pairs={{0,64},{32,96},{64,128},{96,160},{128,192},{160,224},{192,256},{22... | collective-permute-start | bytes 835592 | tf_op jit(solution)/shard_map/ppermute | solution.py:27
  45.0 15.5 %collective-permute-start.8 = (f32[32,2176]{1,0:T(8,128)}, f32[32,2176]{1,0:T(8,128)S(1)}, u32[]{:S(2)}, u32[]{:S(2)}) collective-permute-start(f32[32,2176]{1,0:T(8,128)} %get-tuple-element.36), channel_id=1, source_target_pairs={{0,448},{32,480},{64,0},{96,32},{128,64},{160,96},{192,128},{224,1... | collective-permute-start | bytes 835592 | tf_op jit(solution)/shard_map/ppermute | solution.py:27
  49.6 14.9 %copy-start.2 = (f32[32,2176]{1,0:T(8,128)S(1)}, f32[32,2176]{1,0:T(8,128)}, u32[]{:S(2)}) copy-start(f32[32,2176]{1,0:T(8,128)} %get-tuple-element.48) | copy-start | bytes 835588
  50.6 9.9 %collective-permute-start.4 = (f32[32,2176]{1,0:T(8,128)S(1)}, f32[32,2176]{1,0:T(8,128)S(1)}, u32[]{:S(2)}, u32[]{:S(2)}) collective-permute-start(f32[32,2176]{1,0:T(8,128)S(1)} %add.115), channel_id=1, source_target_pairs={{0,448},{32,480},{64,0},{96,32},{128,64},{160,96},{192,128},{224,1... | collective-permute-start | bytes 835592 | tf_op jit(solution)/shard_map/ppermute | solution.py:27
  52.6 14.3 %copy-start.1 = (f32[32,2176]{1,0:T(8,128)S(1)}, f32[32,2176]{1,0:T(8,128)}, u32[]{:S(2)}) copy-start(f32[32,2176]{1,0:T(8,128)} %get-tuple-element.45) | copy-start | bytes 835588
  52.6 9.9 %collective-permute-start.7 = (f32[32,2176]{1,0:T(8,128)S(1)}, f32[32,2176]{1,0:T(8,128)S(1)}, u32[]{:S(2)}, u32[]{:S(2)}) collective-permute-start(f32[32,2176]{1,0:T(8,128)S(1)} %add.117), channel_id=1, source_target_pairs={{0,64},{32,96},{64,128},{96,160},{128,192},{160,224},{192,256},{22... | collective-permute-start | bytes 835592 | tf_op jit(solution)/shard_map/ppermute | solution.py:27
  56.2 15.4 %collective-permute-start.12 = (f32[32,2176]{1,0:T(8,128)S(1)}, f32[32,2176]{1,0:T(8,128)S(1)}, u32[]{:S(2)}, u32[]{:S(2)}) collective-permute-start(f32[32,2176]{1,0:T(8,128)S(1)} %add.121), channel_id=1, source_target_pairs={{0,64},{32,96},{64,128},{96,160},{128,192},{160,224},{192,256},{22... | collective-permute-start | bytes 835592 | tf_op jit(solution)/shard_map/ppermute | solution.py:27
  62.6 12.1 %collective-permute-start.9 = (f32[32,2176]{1,0:T(8,128)S(1)}, f32[32,2176]{1,0:T(8,128)S(1)}, u32[]{:S(2)}, u32[]{:S(2)}) collective-permute-start(f32[32,2176]{1,0:T(8,128)S(1)} %add.118), channel_id=1, source_target_pairs={{0,64},{32,96},{64,128},{96,160},{128,192},{160,224},{192,256},{22... | collective-permute-start | bytes 835592 | tf_op jit(solution)/shard_map/ppermute | solution.py:27
  64.5 12.2 %copy-start = (f32[32,2176]{1,0:T(8,128)S(1)}, f32[32,2176]{1,0:T(8,128)}, u32[]{:S(2)}) copy-start(f32[32,2176]{1,0:T(8,128)} %get-tuple-element.46) | copy-start | bytes 835588
  64.6 12.1 %collective-permute-start.16 = (f32[32,2176]{1,0:T(8,128)S(1)}, f32[32,2176]{1,0:T(8,128)S(1)}, u32[]{:S(2)}, u32[]{:S(2)}) collective-permute-start(f32[32,2176]{1,0:T(8,128)S(1)} %add.127), channel_id=1, source_target_pairs={{0,32},{32,0},{64,96},{96,64},{128,160},{160,128},{192,224},{224,1... | collective-permute-start | bytes 835592 | tf_op jit(solution)/shard_map/ppermute | solution.py:27
  67.0 9.7 %collective-permute-start.15 = (f32[32,2176]{1,0:T(8,128)S(1)}, f32[32,2176]{1,0:T(8,128)S(1)}, u32[]{:S(2)}, u32[]{:S(2)}) collective-permute-start(f32[32,2176]{1,0:T(8,128)S(1)} %add.125), channel_id=1, source_target_pairs={{0,448},{32,480},{64,0},{96,32},{128,64},{160,96},{192,128},{224,1... | collective-permute-start | bytes 835592 | tf_op jit(solution)/shard_map/ppermute | solution.py:27
  71.6 9.7 %collective-permute-start.13 = (f32[32,2176]{1,0:T(8,128)S(1)}, f32[32,2176]{1,0:T(8,128)S(1)}, u32[]{:S(2)}, u32[]{:S(2)}) collective-permute-start(f32[32,2176]{1,0:T(8,128)S(1)} %add.122), channel_id=1, source_target_pairs={{0,32},{32,0},{64,96},{96,64},{128,160},{160,128},{192,224},{224,1... | collective-permute-start | bytes 835592 | tf_op jit(solution)/shard_map/ppermute | solution.py:27
  74.7 8.5 %collective-permute-start.10 = (f32[32,2176]{1,0:T(8,128)S(1)}, f32[32,2176]{1,0:T(8,128)S(1)}, u32[]{:S(2)}, u32[]{:S(2)}) collective-permute-start(f32[32,2176]{1,0:T(8,128)S(1)} %add.119), channel_id=1, source_target_pairs={{0,64},{32,96},{64,128},{96,160},{128,192},{160,224},{192,256},{22... | collective-permute-start | bytes 835592 | tf_op jit(solution)/shard_map/ppermute | solution.py:27
  76.7 8.5 %collective-permute-start.17 = (f32[32,2176]{1,0:T(8,128)S(1)}, f32[32,2176]{1,0:T(8,128)S(1)}, u32[]{:S(2)}, u32[]{:S(2)}) collective-permute-start(f32[32,2176]{1,0:T(8,128)S(1)} %add_add_fusion), channel_id=1, source_target_pairs={{0,448},{32,480},{64,0},{96,32},{128,64},{160,96},{192,128},{224,1... | collective-permute-start | bytes 835592 | tf_op jit(solution)/shard_map/ppermute | solution.py:27
  83.3 8.9 %collective-permute-start.14 = (f32[32,2176]{1,0:T(8,128)S(1)}, f32[32,2176]{1,0:T(8,128)S(1)}, u32[]{:S(2)}, u32[]{:S(2)}) collective-permute-start(f32[32,2176]{1,0:T(8,128)S(1)} %add_add_fusion.2), channel_id=1, source_target_pairs={{0,64},{32,96},{64,128},{96,160},{128,192},{160,224},{192,256},{22... | collective-permute-start | bytes 835592 | tf_op jit(solution)/shard_map/ppermute | solution.py:27
  181.6 11.9 %all-to-all-start.2 = ((f32[8,4,1024]{2,1,0:T(4,128)}), f32[8,4,1024]{2,1,0:T(4,128)S(1)}, u32[]{:S(2)}, u32[]{:S(2)}) async-start(f32[8,4,1024]{2,1,0:T(4,128)} %broadcast_in_dim.54), calls=%async_computation.2 | async-start | bytes 262144 | tf_op jit(solution)/shard_map/all_to_all | solution.py:23
  193.5 0.6 copy-start.3

commit v12 on v9

--- a/solution.py
+++ b/solution.py
@@ -44,7 +44,9 @@
     far = n_z // 2
     ups, downs = [None, None], [None, None]
     ups[1], downs[1] = ring(term(far - 1, 1), 1), ring(term(far + 1, 1), -1)
-    half_way = swap(term(far, 1)) + term(far, 0)
+    crossed = swap(jnp.concatenate([term(far, 1), term(0, 1)], axis=0))
+    rows = crossed.shape[0] // 2
+    half_way, mine = crossed[:rows] + term(far, 0), crossed[rows:]
     downs[0] = ring(term(far + 1, 0), -1)
     ups[0] = ring(half_way, 1)
     for hops in range(far - 2, 0, -1):
@@ -59,7 +61,7 @@
             else:
                 ups[h], downs[h] = ring(ups[h], 1), ring(downs[h], -1)
     ups[0] = ring(ups[0] + term(1, 0) + ups[1], 1)
-    return term(0, 0) + swap(term(0, 1)) + ups[0] + downs[0]
+    return term(0, 0) + mine + ups[0] + downs[0]
 
 
 def parts(a):

time: 192 us -> 194 us (1.010)
  waiting for transfers between devices: 22.9 us -> 28.5 us
  starting transfers between devices: 67.7 us -> 64.2 us
    ppermute x18 -> x17, waiting for transfers between devices: 14.9 us -> 20.6 us  [permute(): lax.ppermute(a, axis, [(i, to(i)) for i in range(lax.axis_size(axis))])]
    ppermute x18 -> x17, starting transfers between devices: 64.3 us -> 60.8 us  [permute(): lax.ppermute(a, axis, [(i, to(i)) for i in range(lax.axis_size(axis))])]
  transfers between devices with their start and end apart: 19 -> 18, of which waited for: 5 -> 8; matrix products, arithmetic and copies ran while one was open for 3% -> 2% of each run, Pallas kernels for 0% -> 0%
where the time goes in v12:
time: 194 us; the launch traced here: 193 us
  blocking collectives  77.7 us (40%)
  starting transfers between devices  64.2 us (33%)
  waiting for transfers between devices  28.5 us (15%)
  Pallas kernels  12 us (6%)
  other arithmetic  5.92 us (3%)
  local copies, waits for them, and re-layouts  3.58 us (2%)
    all_to_all x2, blocking collectives, exchange(): return lax.all_to_all(jnp.broadcast_to(a[None], (n,) + a.shape), axis, 0, 0)  69.3 us
    ppermute x17, starting transfers between devices, permute(): lax.ppermute(a, axis, [(i, to(i)) for i in range(lax.axis_size(axis))])  60.8 us
    ppermute x17, waiting for transfers between devices, permute(): lax.ppermute(a, axis, [(i, to(i)) for i in range(lax.axis_size(axis))])  20.6 us
    all_gather x1, blocking collectives, on_device(): grads = jnp.sum(lax.all_gather(grads, 'section'), axis=0)  8.43 us
    all_to_all x1, waiting for transfers between devices, exchange(): return lax.all_to_all(jnp.broadcast_to(a[None], (n,) + a.shape), axis, 0, 0)  7.93 us
    pallas_call x1, Pallas kernels, on_device(): pl.pallas_call(functools.partial(forward, n_z, block, n_dp), out_shape=[j...  6.55 us
    pallas_call x1, Pallas kernels, on_device(): pl.pallas_call(functools.partial(backward, block, shards), out_shape=(jax...  5.44 us
  transfers between devices with their start and end apart: 18, of which 8 were waited for; matrix products, arithmetic and copies ran while one was open for 2% of the time, Pallas kernels for 0%

profile of v12, /device:TPU:1, one launch (start us, length us, event | category | flops | bytes accessed | tf_op | source)
XLA Modules:
  0.0 193.0 jit_solution(8917861210072090808)
XLA Ops:
  0.6 5.5 %collective-permute-start.1 = (bf16[128,1024]{1,0:T(8,128)(2,1)}, bf16[128,1024]{1,0:T(8,128)(2,1)S(1)}, u32[]{:S(2)}, u32[]{:S(2)}) collective-permute-start(bf16[128,1024]{1,0:T(8,128)(2,1)} %bitcast.87), channel_id=1, source_target_pairs={{0,16},{8,24},{16,0},{24,8},{1,17},{9,25},{17,1},{25,9},{2,18},{10... | collective-permute-start | bytes 786440 | tf_op jit(solution)/shard_map/ppermute | solution.py:27
  6.1 5.2 %collective-permute-start = (bf16[128,1024]{1,0:T(8,128)(2,1)}, bf16[128,1024]{1,0:T(8,128)(2,1)S(1)}, u32[]{:S(2)}, u32[]{:S(2)}) collective-permute-start(bf16[128,1024]{1,0:T(8,128)(2,1)} %bitcast.88), channel_id=1, source_target_pairs={{0,8},{8,0},{16,24},{24,16},{1,9},{9,1},{17,25},{25,17},{2,10},{10... | collective-permute-start | bytes 786440 | tf_op jit(solution)/shard_map/ppermute | solution.py:27
  11.4 5.0 %collective-permute-start.2 = (bf16[128,1024]{1,0:T(8,128)(2,1)}, bf16[128,1024]{1,0:T(8,128)(2,1)S(1)}, u32[]{:S(2)}, u32[]{:S(2)}) collective-permute-start(bf16[128,1024]{1,0:T(8,128)(2,1)} %bitcast.89), channel_id=1, source_target_pairs={{0,24},{8,16},{16,8},{24,0},{1,25},{9,17},{17,9},{25,1},{2,26},{10... | collective-permute-start | bytes 786440 | tf_op jit(solution)/shard_map/ppermute | solution.py:27
  16.4 0.8 slice_compare_fusion
  17.4 1.0 broadcast_select_fusion.refs_0_
  19.1 0.7 concatenate.25.gains_ref
  19.9 3.4 %collective-permute-done.2.refs_3_ = bf16[128,1024]{1,0:T(8,128)(2,1)S(1)} collective-permute-done((bf16[128,1024]{1,0:T(8,128)(2,1)}, bf16[128,1024]{1,0:T(8,128)(2,1)S(1)}, u32[]{:S(2)}, u32[]{:S(2)}) %collective-permute-start.2) | collective-permute-done | bytes 262176 | tf_op jit(solution)/shard_map/ppermute | solution.py:27
  23.3 6.5 %forward.1 = (f32[32,2176]{1,0:T(8,128)S(1)}, f32[32,2176]{1,0:T(8,128)S(1)}, f32[32,2176]{1,0:T(8,128)S(1)}, f32[32,2176]{1,0:T(8,128)S(1)}, f32[32,2176]{1,0:T...) custom-call(s32[3]{0:T(128)S(1)} %pad_add_fusion.place_ref, ...), custom_call_target="tpu_custom_call" | custom-call | tf_op jit(solution)/shard_map/forward/pallas_call | solution.py:264
  29.9 2.1 %collective-permute-start.3 = (f32[64,2176]{1,0:T(8,128)S(1)}, f32[64,2176]{1,0:T(8,128)S(1)}, u32[]{:S(2)}, u32[]{:S(2)}) collective-permute-start(f32[64,2176]{1,0:T(8,128)S(1)} %pad_maximum_fusion), channel_id=1, source_target_pairs={{0,32},{32,0},{64,96},{96,64},{128,160},{160,128},{192,224},{224,1... | collective-permute-start | bytes 1671176 | tf_op jit(solution)/shard_map/ppermute | solution.py:27
  32.0 1.9 collective-permute-start.7
  33.9 8.2 %collective-permute-start.11 = (f32[32,2176]{1,0:T(8,128)}, f32[32,2176]{1,0:T(8,128)S(1)}, u32[]{:S(2)}, u32[]{:S(2)}) collective-permute-start(f32[32,2176]{1,0:T(8,128)} %get-tuple-element.35), channel_id=1, source_target_pairs={{0,448},{32,480},{64,0},{96,32},{128,64},{160,96},{192,128},{224,1... | collective-permute-start | bytes 835592 | tf_op jit(solution)/shard_map/ppermute | solution.py:27
  42.1 3.4 %collective-permute-start.13 = (f32[32,2176]{1,0:T(8,128)}, f32[32,2176]{1,0:T(8,128)S(1)}, u32[]{:S(2)}, u32[]{:S(2)}) collective-permute-start(f32[32,2176]{1,0:T(8,128)} %get-tuple-element.38), channel_id=1, source_target_pairs={{0,448},{32,480},{64,0},{96,32},{128,64},{160,96},{192,128},{224,1... | collective-permute-start | bytes 835592 | tf_op jit(solution)/shard_map/ppermute | solution.py:27
  45.8 1.9 collective-permute-start.4
  47.7 6.4 %collective-permute-done.13 = f32[32,2176]{1,0:T(8,128)S(1)} collective-permute-done((f32[32,2176]{1,0:T(8,128)}, f32[32,2176]{1,0:T(8,128)S(1)}, u32[]{:S(2)}, u32[]{:S(2)}) %collective-permute-start.13) | collective-permute-done | bytes 278560 | tf_op jit(solution)/shard_map/ppermute | solution.py:27
  54.1 5.3 %collective-permute-start.14 = (f32[32,2176]{1,0:T(8,128)S(1)}, f32[32,2176]{1,0:T(8,128)S(1)}, u32[]{:S(2)}, u32[]{:S(2)}) collective-permute-start(f32[32,2176]{1,0:T(8,128)S(1)} %add.126), channel_id=1, source_target_pairs={{0,448},{32,480},{64,0},{96,32},{128,64},{160,96},{192,128},{224,1... | collective-permute-start | bytes 835592 | tf_op jit(solution)/shard_map/ppermute | solution.py:27
  59.5 1.9 collective-permute-start.8
  61.6 2.1 %collective-permute-start.5 = (f32[32,2176]{1,0:T(8,128)S(1)}, f32[32,2176]{1,0:T(8,128)S(1)}, u32[]{:S(2)}, u32[]{:S(2)}) collective-permute-start(f32[32,2176]{1,0:T(8,128)S(1)} %add.117), channel_id=1, source_target_pairs={{0,64},{32,96},{64,128},{96,160},{128,192},{160,224},{192,256},{22... | collective-permute-start | bytes 835592 | tf_op jit(solution)/shard_map/ppermute | solution.py:27
  63.6 4.6 %collective-permute-start.12 = (f32[32,2176]{1,0:T(8,128)S(1)}, f32[32,2176]{1,0:T(8,128)S(1)}, u32[]{:S(2)}, u32[]{:S(2)}) collective-permute-start(f32[32,2176]{1,0:T(8,128)S(1)} %add.124), channel_id=1, source_target_pairs={{0,448},{32,480},{64,0},{96,32},{128,64},{160,96},{192,128},{224,1... | collective-permute-start | bytes 835592 | tf_op jit(solution)/shard_map/ppermute | solution.py:27
  68.3 3.1 %collective-permute-start.15 = (f32[32,2176]{1,0:T(8,128)S(1)}, f32[32,2176]{1,0:T(8,128)S(1)}, u32[]{:S(2)}, u32[]{:S(2)}) collective-permute-start(f32[32,2176]{1,0:T(8,128)S(1)} %add.127), channel_id=1, source_target_pairs={{0,32},{32,0},{64,96},{96,64},{128,160},{160,128},{192,224},{224,1... | collective-permute-start | bytes 835592 | tf_op jit(solution)/shard_map/ppermute | solution.py:27
  71.4 2.2 %collective-permute-start.9 = (f32[32,2176]{1,0:T(8,128)S(1)}, f32[32,2176]{1,0:T(8,128)S(1)}, u32[]{:S(2)}, u32[]{:S(2)}) collective-permute-start(f32[32,2176]{1,0:T(8,128)S(1)} %add.121), channel_id=1, source_target_pairs={{0,32},{32,0},{64,96},{96,64},{128,160},{160,128},{192,224},{224,1... | collective-permute-start | bytes 835592 | tf_op jit(solution)/shard_map/ppermute | solution.py:27
  73.6 1.7 collective-permute-done.5
  75.3 1.9 collective-permute-start.6
  77.3 4.6 %collective-permute-start.16 = (f32[32,2176]{1,0:T(8,128)S(1)}, f32[32,2176]{1,0:T(8,128)S(1)}, u32[]{:S(2)}, u32[]{:S(2)}) collective-permute-start(f32[32,2176]{1,0:T(8,128)S(1)} %add_add_fusion), channel_id=1, source_target_pairs={{0,448},{32,480},{64,0},{96,32},{128,64},{160,96},{192,128},{224,1... | collective-permute-start | bytes 835592 | tf_op jit(solution)/shard_map/ppermute | solution.py:27
  82.3 1.9 %collective-permute-done.6 = f32[32,2176]{1,0:T(8,128)S(1)} collective-permute-done((f32[32,2176]{1,0:T(8,128)S(1)}, f32[32,2176]{1,0:T(8,128)S(1)}, u32[]{:S(2)}, u32[]{:S(2)}) %collective-permute-start.6) | collective-permute-done | bytes 278560 | tf_op jit(solution)/shard_map/ppermute | solution.py:27
  84.3 1.9 collective-permute-start.10
  86.2 6.6 %collective-permute-done.10 = f32[32,2176]{1,0:T(8,128)S(1)} collective-permute-done((f32[32,2176]{1,0:T(8,128)S(1)}, f32[32,2176]{1,0:T(8,128)S(1)}, u32[]{:S(2)}, u32[]{:S(2)}) %collective-permute-start.10) | collective-permute-done | bytes 278560 | tf_op jit(solution)/shard_map/ppermute | solution.py:27
  94.2 24.2 %all_to_all.15 = f32[32,8,14]{2,1,0:T(8,128)S(1)} all-to-all(f32[32,8,14]{2,1,0:T(8,128)S(1)} %broadcast_in_dim.52), channel_id=1, replica_groups=mesh['dp'=16,'section'=4,'vocab'=8] {'section','vocab'}, dimensions={0} | all-to-all | bytes 28672 | tf_op jit(solution)/shard_map/all_to_all | solution.py:23
  120.7 45.1 %all_to_all.16 = bf16[16,24,2176]{2,1,0:T(8,128)(2,1)S(1)} all-to-all(bf16[16,24,2176]{2,1,0:T(8,128)(2,1)S(1)} %broadcast_in_dim.53), channel_id=1, replica_groups=mesh['dp'=16,'section'=4,'vocab'=8] {'dp'}, dimensions={0} | all-to-all | bytes 3342336 | tf_op jit(solution)/shard_map/all_to_all | solution.py:23
  165.8 5.4 %backward.1 = (f32[4,1024]{1,0:T(4,128)S(1)}, f32[128,128]{1,0:T(8,128)S(1)}) custom-call(s32[3]{0:T(128)S(1)} %pad_add_fusion.place_ref, bf16[384,2176]{1,0:T(8,128)(2,1)S(1)} %bitcast.83, bf16[2048,1024]{1,0:T(8,128)(2,1)} %head_ref.3, f32[4,1024]{1,0:T(4,128)S(1)} %concatenate.25.gains_ref, f32[1,1024]{1,0:T(1,128)S(1)} %bitcast.85, ...), custom_call_target="tpu_custom_call" | custom-call | tf_op jit(solution)/shard_map/backward/pallas_call | solution.py:334
  171.3 8.4 %all-gather.1 = f32[4,4,1024]{2,1,0:T(4,128)S(1)} all-gather(f32[1,4,1024]{2,1,0:T(4,128)S(1)} %bitcast.86), channel_id=2, replica_groups=mesh['dp'=16,'section'=4,'vocab'=8] {'section'}, dimensions={0}, use_global_device_ids=true | all-gather | bytes 81920 | tf_op jit(solution)/shard_map/all_gather | solution.py:352
  180.4 3.4 %all-to-all-start.2 = ((f32[8,4,1024]{2,1,0:T(4,128)}), f32[8,4,1024]{2,1,0:T(4,128)S(1)}, u32[]{:S(2)}, u32[]{:S(2)}) async-start(f32[8,4,1024]{2,1,0:T(4,128)} %broadcast_in_dim.54), calls=%async_computation.2 | async-start | bytes 262144 | tf_op jit(solution)/shard_map/all_to_all | solution.py:23
  184.4 7.9 %all-to-all-done.2 = f32[8,4,1024]{2,1,0:T(4,128)S(1)} async-done(((f32[8,4,1024]{2,1,0:T(4,128)}), f32[8,4,1024]{2,1,0:T(4,128)S(1)}, u32[]{:S(2)}, u32[]{:S(2)}) %all-to-all-start.2) | async-done | bytes 131104 | tf_op jit(solution)/shard_map/all_to_all | solution.py:23
  (78 shorter events, 7.6 us)
Async XLA Ops:
  0.6 19.3 %collective-permute-start.1 = (bf16[128,1024]{1,0:T(8,128)(2,1)}, bf16[128,1024]{1,0:T(8,128)(2,1)S(1)}, u32[]{:S(2)}, u32[]{:S(2)}) collective-permute-start(bf16[128,1024]{1,0:T(8,128)(2,1)} %bitcast.87), channel_id=1, source_target_pairs={{0,16},{8,24},{16,0},{24,8},{1,17},{9,25},{17,1},{25,9},{2,18},{10... | collective-permute-start | bytes 786440 | tf_op jit(solution)/shard_map/ppermute | solution.py:27
  6.1 13.8 %collective-permute-start = (bf16[128,1024]{1,0:T(8,128)(2,1)}, bf16[128,1024]{1,0:T(8,128)(2,1)S(1)}, u32[]{:S(2)}, u32[]{:S(2)}) collective-permute-start(bf16[128,1024]{1,0:T(8,128)(2,1)} %bitcast.88), channel_id=1, source_target_pairs={{0,8},{8,0},{16,24},{24,16},{1,9},{9,1},{17,25},{25,17},{2,10},{10... | collective-permute-start | bytes 786440 | tf_op jit(solution)/shard_map/ppermute | solution.py:27
  11.4 11.9 %collective-permute-start.2 = (bf16[128,1024]{1,0:T(8,128)(2,1)}, bf16[128,1024]{1,0:T(8,128)(2,1)S(1)}, u32[]{:S(2)}, u32[]{:S(2)}) collective-permute-start(bf16[128,1024]{1,0:T(8,128)(2,1)} %bitcast.89), channel_id=1, source_target_pairs={{0,24},{8,16},{16,8},{24,0},{1,25},{9,17},{17,9},{25,1},{2,26},{10... | collective-permute-start | bytes 786440 | tf_op jit(solution)/shard_map/ppermute | solution.py:27
  29.8 24.2 %copy-start.3 = (f32[32,2176]{1,0:T(8,128)S(1)}, f32[32,2176]{1,0:T(8,128)}, u32[]{:S(2)}) copy-start(f32[32,2176]{1,0:T(8,128)} %get-tuple-element.39) | copy-start | bytes 835588
  29.8 31.6 %copy-start.2 = (f32[32,2176]{1,0:T(8,128)S(1)}, f32[32,2176]{1,0:T(8,128)}, u32[]{:S(2)}) copy-start(f32[32,2176]{1,0:T(8,128)} %get-tuple-element.36) | copy-start | bytes 835588
  29.9 15.8 %collective-permute-start.3 = (f32[64,2176]{1,0:T(8,128)S(1)}, f32[64,2176]{1,0:T(8,128)S(1)}, u32[]{:S(2)}, u32[]{:S(2)}) collective-permute-start(f32[64,2176]{1,0:T(8,128)S(1)} %pad_maximum_fusion), channel_id=1, source_target_pairs={{0,32},{32,0},{64,96},{96,64},{128,160},{160,128},{192,224},{224,1... | collective-permute-start | bytes 1671176 | tf_op jit(solution)/shard_map/ppermute | solution.py:27
  32.0 27.5 %collective-permute-start.7 = (f32[32,2176]{1,0:T(8,128)S(1)}, f32[32,2176]{1,0:T(8,128)S(1)}, u32[]{:S(2)}, u32[]{:S(2)}) collective-permute-start(f32[32,2176]{1,0:T(8,128)S(1)} %get-tuple-element.32), channel_id=1, source_target_pairs={{0,64},{32,96},{64,128},{96,160},{128,192},{160,224},{192,256},{22... | collective-permute-start | bytes 835592 | tf_op jit(solution)/shard_map/ppermute | solution.py:27
  33.9 27.6 %collective-permute-start.11 = (f32[32,2176]{1,0:T(8,128)}, f32[32,2176]{1,0:T(8,128)S(1)}, u32[]{:S(2)}, u32[]{:S(2)}) collective-permute-start(f32[32,2176]{1,0:T(8,128)} %get-tuple-element.35), channel_id=1, source_target_pairs={{0,448},{32,480},{64,0},{96,32},{128,64},{160,96},{192,128},{224,1... | collective-permute-start | bytes 835592 | tf_op jit(solution)/shard_map/ppermute | solution.py:27
  42.1 12.0 %collective-permute-start.13 = (f32[32,2176]{1,0:T(8,128)}, f32[32,2176]{1,0:T(8,128)S(1)}, u32[]{:S(2)}, u32[]{:S(2)}) collective-permute-start(f32[32,2176]{1,0:T(8,128)} %get-tuple-element.38), channel_id=1, source_target_pairs={{0,448},{32,480},{64,0},{96,32},{128,64},{160,96},{192,128},{224,1... | collective-permute-start | bytes 835592 | tf_op jit(solution)/shard_map/ppermute | solution.py:27
  45.8 15.7 %collective-permute-start.4 = (f32[32,2176]{1,0:T(8,128)S(1)}, f32[32,2176]{1,0:T(8,128)S(1)}, u32[]{:S(2)}, u32[]{:S(2)}) collective-permute-start(f32[32,2176]{1,0:T(8,128)S(1)} %slice_add_fusion), channel_id=1, source_target_pairs={{0,64},{32,96},{64,128},{96,160},{128,192},{160,224},{192,256},{22... | collective-permute-start | bytes 835592 | tf_op jit(solution)/shard_map/ppermute | solution.py:27
  54.1 14.1 %copy-start.1 = (f32[32,2176]{1,0:T(8,128)S(1)}, f32[32,2176]{1,0:T(8,128)}, u32[]{:S(2)}) copy-start(f32[32,2176]{1,0:T(8,128)} %get-tuple-element.40) | copy-start | bytes 835588
  54.1 14.1 %collective-permute-start.14 = (f32[32,2176]{1,0:T(8,128)S(1)}, f32[32,2176]{1,0:T(8,128)S(1)}, u32[]{:S(2)}, u32[]{:S(2)}) collective-permute-start(f32[32,2176]{1,0:T(8,128)S(1)} %add.126), channel_id=1, source_target_pairs={{0,448},{32,480},{64,0},{96,32},{128,64},{160,96},{192,128},{224,1... | collective-permute-start | bytes 835592 | tf_op jit(solution)/shard_map/ppermute | solution.py:27
  59.5 11.8 %collective-permute-start.8 = (f32[32,2176]{1,0:T(8,128)S(1)}, f32[32,2176]{1,0:T(8,128)S(1)}, u32[]{:S(2)}, u32[]{:S(2)}) collective-permute-start(f32[32,2176]{1,0:T(8,128)S(1)} %add.120), channel_id=1, source_target_pairs={{0,64},{32,96},{64,128},{96,160},{128,192},{160,224},{192,256},{22... | collective-permute-start | bytes 835592 | tf_op jit(solution)/shard_map/ppermute | solution.py:27
  61.5 15.8 %copy-start = (f32[32,2176]{1,0:T(8,128)S(1)}, f32[32,2176]{1,0:T(8,128)}, u32[]{:S(2)}) copy-start(f32[32,2176]{1,0:T(8,128)} %get-tuple-element.37) | copy-start | bytes 835588
  61.6 13.7 %collective-permute-start.5 = (f32[32,2176]{1,0:T(8,128)S(1)}, f32[32,2176]{1,0:T(8,128)S(1)}, u32[]{:S(2)}, u32[]{:S(2)}) collective-permute-start(f32[32,2176]{1,0:T(8,128)S(1)} %add.117), channel_id=1, source_target_pairs={{0,64},{32,96},{64,128},{96,160},{128,192},{160,224},{192,256},{22... | collective-permute-start | bytes 835592 | tf_op jit(solution)/shard_map/ppermute | solution.py:27
  63.6 13.6 %collective-permute-start.12 = (f32[32,2176]{1,0:T(8,128)S(1)}, f32[32,2176]{1,0:T(8,128)S(1)}, u32[]{:S(2)}, u32[]{:S(2)}) collective-permute-start(f32[32,2176]{1,0:T(8,128)S(1)} %add.124), channel_id=1, source_target_pairs={{0,448},{32,480},{64,0},{96,32},{128,64},{160,96},{192,128},{224,1... | collective-permute-start | bytes 835592 | tf_op jit(solution)/shard_map/ppermute | solution.py:27
  68.3 9.0 %collective-permute-start.15 = (f32[32,2176]{1,0:T(8,128)S(1)}, f32[32,2176]{1,0:T(8,128)S(1)}, u32[]{:S(2)}, u32[]{:S(2)}) collective-permute-start(f32[32,2176]{1,0:T(8,128)S(1)} %add.127), channel_id=1, source_target_pairs={{0,32},{32,0},{64,96},{96,64},{128,160},{160,128},{192,224},{224,1... | collective-permute-start | bytes 835592 | tf_op jit(solution)/shard_map/ppermute | solution.py:27
  71.4 10.9 %collective-permute-start.9 = (f32[32,2176]{1,0:T(8,128)S(1)}, f32[32,2176]{1,0:T(8,128)S(1)}, u32[]{:S(2)}, u32[]{:S(2)}) collective-permute-start(f32[32,2176]{1,0:T(8,128)S(1)} %add.121), channel_id=1, source_target_pairs={{0,32},{32,0},{64,96},{96,64},{128,160},{160,128},{192,224},{224,1... | collective-permute-start | bytes 835592 | tf_op jit(solution)/shard_map/ppermute | solution.py:27
  75.3 8.9 %collective-permute-start.6 = (f32[32,2176]{1,0:T(8,128)S(1)}, f32[32,2176]{1,0:T(8,128)S(1)}, u32[]{:S(2)}, u32[]{:S(2)}) collective-permute-start(f32[32,2176]{1,0:T(8,128)S(1)} %add.118), channel_id=1, source_target_pairs={{0,64},{32,96},{64,128},{96,160},{128,192},{160,224},{192,256},{22... | collective-permute-start | bytes 835592 | tf_op jit(solution)/shard_map/ppermute | solution.py:27
  77.3 8.8 %collective-permute-start.16 = (f32[32,2176]{1,0:T(8,128)S(1)}, f32[32,2176]{1,0:T(8,128)S(1)}, u32[]{:S(2)}, u32[]{:S(2)}) collective-permute-start(f32[32,2176]{1,0:T(8,128)S(1)} %add_add_fusion), channel_id=1, source_target_pairs={{0,448},{32,480},{64,0},{96,32},{128,64},{160,96},{192,128},{224,1... | collective-permute-start | bytes 835592 | tf_op jit(solution)/shard_map/ppermute | solution.py:27
  84.3 8.5 %collective-permute-start.10 = (f32[32,2176]{1,0:T(8,128)S(1)}, f32[32,2176]{1,0:T(8,128)S(1)}, u32[]{:S(2)}, u32[]{:S(2)}) collective-permute-start(f32[32,2176]{1,0:T(8,128)S(1)} %add_add_fusion.1), channel_id=1, source_target_pairs={{0,64},{32,96},{64,128},{96,160},{128,192},{160,224},{192,256},{22... | collective-permute-start | bytes 835592 | tf_op jit(solution)/shard_map/ppermute | solution.py:27
  180.4 11.9 %all-to-all-start.2 = ((f32[8,4,1024]{2,1,0:T(4,128)}), f32[8,4,1024]{2,1,0:T(4,128)S(1)}, u32[]{:S(2)}, u32[]{:S(2)}) async-start(f32[8,4,1024]{2,1,0:T(4,128)} %broadcast_in_dim.54), calls=%async_computation.2 | async-start | bytes 262144 | tf_op jit(solution)/shard_map/all_to_all | solution.py:23
  192.3 0.6 copy-start.4
